TPU v7x, 32 devices: a whole 2x2x4 slice. The times are simulated.
32 devices in a mesh: group: 2 (over y), tm: 4 (over z), tensor: 2 (over x), pair: 2 (over core).
Axes of the slice: x: 2, y: 2, z: 4, core: 2. Of those that a mesh axis runs over, the one named last changes fastest.
Arguments:
- frames: bfloat16 [12288, 1536], P(('group', 'tm'), ('tensor', 'pair')), parts along dimension 0, may hold values from -6 to 6
- router_weight: float32 [1536], replicated, may hold values from -0.15625 to 0.15625
- norm_gain: float32 [1536], replicated, may hold values from 0.25 to 1.75
- up_weight: bfloat16 [1536, 3072], P(None, ('tensor', 'pair')), may hold values from -0.15625 to 0.15625
- down_weight: bfloat16 [3072, 1536], P(('tensor', 'pair')), may hold values from -0.15625 to 0.15625
- picked_rows: int32 [3072], P(('group', 'tm')), parts along dimension 0, may hold values from 0 to 1535, as said below
- picked_count: int32 [8], P('group'), parts along dimension 0, may hold values from 1 to 384, 768 in all
- cotangent: bfloat16 [12288, 1536], P(('group', 'tm'), ('tensor', 'pair')), parts along dimension 0, may hold values from -6 to 6
Outputs:
- mixed: bfloat16 [12288, 1536], P(('group', 'tm'), ('tensor', 'pair')), parts along dimension 0
- frames_grad: bfloat16 [12288, 1536], P(('group', 'tm'), ('tensor', 'pair')), parts along dimension 0
There are 2 independent parts, one for each index of `group`. A program takes and returns all parts, laid end to end along the dimension named above; an argument that names none is the same for every part. Nothing has to cross between parts.
Inputs may be any that keep to these rules, and one draw needn't show every extreme that they name: `picked_rows`: the 384 entries of one index of tm are distinct frame indices among its own 1536 frames; the first picked_count of them are its routed frames, the others are not used. `picked_count`: the counts sum to 768.
All inputs are finite; a program needn't handle non-finite values.
Results may differ from a plain program's by a relative error of at most 0.0028.
Values may be sent and summed in bfloat16 or wider, within the bound.
No kernel may reach another device: no remote copies, remote signals or barrier semaphores. Data moves between devices by JAX's collectives and lax.ppermute only.
A program may use at most 64 MiB of HBM per device.

v0:
```python
import jax
import jax.numpy as jnp
from jax import lax
from jax.sharding import PartitionSpec as P

SEL = 192


def per_device(
    frames, router_weight, norm_gain, up_weight, down_weight, picked_rows, picked_count, cotangent
):
    width_dev = frames.shape[1]
    slots = picked_rows.shape[0]
    tm_count = lax.axis_size("tm")
    my_tm = lax.axis_index("tm")
    my_split = lax.axis_index(("tensor", "pair"))
    rank_ends = jnp.cumsum(picked_count)
    rank_starts = rank_ends - picked_count
    my_start = rank_starts[my_tm]
    is_live = jnp.arange(slots, dtype=jnp.int32) < picked_count[my_tm]
    rows_in = jnp.where(is_live[:, None], jnp.take(frames, picked_rows, axis=0), 0)
    rows_cot = jnp.where(is_live[:, None], jnp.take(cotangent, picked_rows, axis=0), 0)
    column_start = my_split * width_dev
    span = tm_count * SEL
    offset = tm_count // 2

    def spread(rows):
        padded = jnp.zeros((span + slots, width_dev), jnp.bfloat16)
        padded = lax.dynamic_update_slice_in_dim(padded, rows, my_start, 0)
        return jnp.roll(padded[:span].reshape(tm_count, SEL, width_dev), offset, axis=0)

    got_in, got_cot = (
        lax.all_to_all(spread(rows_in), "tm", split_axis=0, concat_axis=0, tiled=True),
        lax.all_to_all(spread(rows_cot), "tm", split_axis=0, concat_axis=0, tiled=True),
    )
    mine_in = jnp.sum(got_in.astype(jnp.float32), axis=0).astype(jnp.bfloat16)
    mine_cot = jnp.sum(got_cot.astype(jnp.float32), axis=0).astype(jnp.bfloat16)
    full_in = lax.all_gather(mine_in, ("tensor", "pair"), axis=1, tiled=True)
    full_cot = lax.all_gather(mine_cot, ("tensor", "pair"), axis=1, tiled=True)
    wide_in = full_in.astype(jnp.float32)
    gate_score = jax.nn.sigmoid(jnp.sum(wide_in * router_weight, axis=-1))
    row_mean = jnp.mean(wide_in, axis=-1, keepdims=True)
    deviate = wide_in - row_mean
    inv_std = lax.rsqrt(jnp.mean(deviate * deviate, axis=-1, keepdims=True) + 1e-05)
    centred = deviate * inv_std
    normed = (centred * norm_gain).astype(jnp.bfloat16)
    hidden_in = jnp.dot(normed, up_weight, preferred_element_type=jnp.float32)
    hidden = jax.nn.silu(hidden_in).astype(jnp.bfloat16)
    partial_out = jnp.dot(hidden, down_weight, preferred_element_type=jnp.float32)
    ffn_out = lax.psum_scatter(
        partial_out.astype(jnp.bfloat16), ("tensor", "pair"), scatter_dimension=1, tiled=True
    ).astype(jnp.float32)
    routed_out = (0.5 * gate_score[:, None] * ffn_out).astype(jnp.bfloat16)
    grad_hid = jnp.einsum("nd,fd->nf", full_cot, down_weight, preferred_element_type=jnp.float32)
    score_part = 0.5 * jnp.sum(grad_hid * hidden.astype(jnp.float32), axis=-1)
    swish_gate = jax.nn.sigmoid(hidden_in)
    grad_pre = (
        0.5 * gate_score[:, None] * grad_hid * swish_gate * (1.0 + hidden_in * (1.0 - swish_gate))
    ).astype(jnp.bfloat16)
    normed_part = jnp.einsum("nf,df->nd", grad_pre, up_weight, preferred_element_type=jnp.float32)
    grad_normed = lax.psum(normed_part.astype(jnp.bfloat16), ("tensor", "pair")).astype(jnp.float32)
    grad_score = lax.psum(score_part.astype(jnp.bfloat16), ("tensor", "pair")).astype(jnp.float32)
    grad_scaled = grad_normed * norm_gain
    plain_mean = jnp.mean(grad_scaled, axis=-1, keepdims=True)
    cross_mean = jnp.mean(grad_scaled * centred, axis=-1, keepdims=True)
    router_term = (grad_score * gate_score * (1.0 - gate_score))[:, None] * router_weight
    full_rows = inv_std * (grad_scaled - plain_mean - centred * cross_mean) + router_term
    grad_rows = lax.dynamic_slice_in_dim(full_rows, column_start, width_dev, 1).astype(jnp.bfloat16)
    routed_out, grad_rows = (routed_out, grad_rows)
    my_block = (my_tm + tm_count - offset) % tm_count
    my_ranks = my_block * SEL + jnp.arange(SEL, dtype=jnp.int32)
    owners = jnp.sum((rank_ends[None, :] <= my_ranks[:, None]).astype(jnp.int32), axis=1)
    to_source = owners[None, :] == jnp.arange(tm_count, dtype=jnp.int32)[:, None]

    def sort_back(rows):
        return jnp.where(to_source[:, :, None], rows[None, :, :], 0)

    back_out, back_grad = (
        lax.all_to_all(sort_back(routed_out), "tm", split_axis=0, concat_axis=0, tiled=True),
        lax.all_to_all(sort_back(grad_rows), "tm", split_axis=0, concat_axis=0, tiled=True),
    )

    def own_slots(got):
        ordered = jnp.roll(got, -offset, axis=0)
        flat = jnp.concatenate(
            [ordered.reshape(span, width_dev), jnp.zeros((slots, width_dev), jnp.bfloat16)], axis=0
        )
        return lax.dynamic_slice_in_dim(flat, my_start, slots, 0)

    out_home = own_slots(back_out)
    grad_home = own_slots(back_grad)
    mixed = (
        frames.astype(jnp.float32)
        .at[picked_rows]
        .add(out_home.astype(jnp.float32))
        .astype(jnp.bfloat16)
    )
    frames_grad = (
        cotangent.astype(jnp.float32)
        .at[picked_rows]
        .add(grad_home.astype(jnp.float32))
        .astype(jnp.bfloat16)
    )
    return (mixed, frames_grad)


def solution(mesh):
    return jax.shard_map(
        per_device,
        mesh=mesh,
        in_specs=(
            P(("group", "tm"), ("tensor", "pair")),
            P(),
            P(),
            P(None, ("tensor", "pair")),
            P(("tensor", "pair"), None),
            P(("group", "tm")),
            P("group"),
            P(("group", "tm"), ("tensor", "pair")),
        ),
        out_specs=(P(("group", "tm"), ("tensor", "pair")), P(("group", "tm"), ("tensor", "pair"))),
        check_vma=False,
    )
```

profile of v0, /device:TPU:0, one launch (start us, length us, event | category | flops | bytes accessed | tf_op | source)
XLA Modules:
  0.0 219.0 jit_solution(7401561236250738516)
XLA Ops:
  7.2 1.4 dynamic_slice.15
  8.6 0.8 reduce-window.8
  9.4 0.7 bitcast_subtract_fusion
  10.1 0.7 dynamic_slice.16
  12.1 0.7 compare_select_fusion
  12.8 1.3 iota_compare_fusion.1
  14.2 3.9 %gather_fusion.1 = bf16[384,384]{1,0:T(8,128)(2,1)} fusion(bf16[1536,384]{1,0:T(8,128)(2,1)} %param.17, s32[1024]{0:T(1024)S(1)} %pad_clamp_fusion), kind=kCustom, calls=%fused_computation.1.clone | custom fusion | bytes 591360 | tf_op jit(solution)/shard_map/jit(_take)/gather | solution.py:22
  18.1 2.5 %gather_fusion = bf16[384,384]{1,0:T(8,128)(2,1)} fusion(bf16[1536,384]{1,0:T(8,128)(2,1)S(1)} %copy-done.1, s32[1024]{0:T(1024)S(1)} %pad_clamp_fusion), kind=kCustom, calls=%fused_computation.clone | custom fusion | bytes 591360 | tf_op jit(solution)/shard_map/jit(_take)/gather | solution.py:21
  21.3 2.1 select_select_fusion
  23.4 1.0 broadcast.98.clone
  24.4 2.9 %dynamic_update_slice.6 = bf16[1152,384]{1,0:T(8,128)(2,1)} dynamic-update-slice(bf16[1152,384]{1,0:T(8,128)(2,1)} %broadcast.98.clone, bf16[384,384]{1,0:T(8,128)(2,1)} %get-tuple-element.22, s32[]{:T(128)S(6)} %select_n.49, s32[]{:T(128)} %constant.35.clone.1) | dynamic-update-slice | bytes 589828 | tf_op jit(solution)/shard_map/dynamic_update_slice | solution.py:29
  27.3 1.1 fusion.20
  28.4 0.9 pad_maximum_fusion
  29.3 6.3 %all-to-all-start = ((bf16[4,192,384]{2,1,0:T(8,128)(2,1)}), bf16[4,192,384]{2,1,0:T(8,128)(2,1)}, u32[]{:S(2)}, u32[]{:S(2)}) async-start(bf16[4,192,384]{2,1,0:T(8,128)(2,1)} %pad_maximum_fusion), calls=%async_computation | async-start | bytes 1179648 | tf_op jit(solution)/shard_map/all_to_all | solution.py:33
  35.6 0.6 dynamic-slice
  36.2 1.0 broadcast.98.clone.1
  37.2 2.9 %dynamic_update_slice.7 = bf16[1152,384]{1,0:T(8,128)(2,1)} dynamic-update-slice(bf16[1152,384]{1,0:T(8,128)(2,1)} %broadcast.98.clone.1, bf16[384,384]{1,0:T(8,128)(2,1)} %get-tuple-element.21, s32[]{:T(128)S(6)} %select_n.49, s32[]{:T(128)} %constant.35.clone.1) | dynamic-update-slice | bytes 589828 | tf_op jit(solution)/shard_map/dynamic_update_slice | solution.py:29
  40.1 0.6 convert_reduce_fusion.1
  40.7 1.1 fusion.19
  41.9 0.9 pad_maximum_fusion.2
  42.7 8.8 %all-to-all-done = bf16[4,192,384]{2,1,0:T(8,128)(2,1)} async-done(((bf16[4,192,384]{2,1,0:T(8,128)(2,1)}), bf16[4,192,384]{2,1,0:T(8,128)(2,1)}, u32[]{:S(2)}, u32[]{:S(2)}) %all-to-all-start) | async-done | bytes 589856 | tf_op jit(solution)/shard_map/all_to_all | solution.py:33
  51.6 4.1 %all-to-all-start.2 = ((bf16[4,192,384]{2,1,0:T(8,128)(2,1)}), bf16[4,192,384]{2,1,0:T(8,128)(2,1)}, u32[]{:S(2)}, u32[]{:S(2)}) async-start(bf16[4,192,384]{2,1,0:T(8,128)(2,1)} %pad_maximum_fusion.2), calls=%async_computation.2 | async-start | bytes 1179648 | tf_op jit(solution)/shard_map/all_to_all | solution.py:34
  55.7 0.0 all-reduce.4.cloned.1.call-start
  55.8 1.8 reduce_sum.88
  57.6 7.7 %all_gather.6 = bf16[192,1536]{1,0:T(8,128)(2,1)S(1)} all-gather(bf16[192,384]{1,0:T(8,128)(2,1)} %reduce_sum.88), channel_id=1, replica_groups=mesh['group'=2,'tm'=4,'tensor'=2,'pair'=2] {'tensor','pair'}, dimensions={1}, use_global_device_ids=true | all-gather | bytes 737280 | tf_op jit(solution)/shard_map/all_gather | solution.py:38
  65.4 0.8 fusion.3
  66.2 0.3 fusion.2
  66.5 4.7 %all-to-all-done.2 = bf16[4,192,384]{2,1,0:T(8,128)(2,1)} async-done(((bf16[4,192,384]{2,1,0:T(8,128)(2,1)}), bf16[4,192,384]{2,1,0:T(8,128)(2,1)}, u32[]{:S(2)}, u32[]{:S(2)}) %all-to-all-start.2) | async-done | bytes 589856 | tf_op jit(solution)/shard_map/all_to_all | solution.py:34
  71.2 1.8 reduce_sum.92
  73.1 7.7 %all_gather.7 = bf16[192,1536]{1,0:T(8,128)(2,1)S(1)} all-gather(bf16[192,384]{1,0:T(8,128)(2,1)} %reduce_sum.92), channel_id=1, replica_groups=mesh['group'=2,'tm'=4,'tensor'=2,'pair'=2] {'tensor','pair'}, dimensions={1}, use_global_device_ids=true | all-gather | bytes 737280 | tf_op jit(solution)/shard_map/all_gather | solution.py:39
  80.8 2.5 %fusion.4 = f32[192,768]{1,0:T(8,128)S(1)} fusion(bf16[1536,768]{1,0:T(8,128)(2,1)} %param.13, f32[1536]{0:T(1024)S(1)} %copy-done.6, bf16[192,1536]{1,0:T(8,128)(2,1)} %copy-done.3, f32[192]{0:T(256)S(1)} %add_rsqrt_fusion, f32[192]{0:T(256)S(1)} %broadcast_multiply_fusion.2), kind=kOutput, calls=%fused_computation.18 | convolution fusion | flops 454459392 | bytes 3546624 | tf_op jit(solution)/shard_map/dot_general | solution.py:47
  83.3 1.7 multiply_reduce_fusion.1
  85.1 0.5 multiply_convert_fusion.6
  85.6 6.9 %psum.15 = bf16[192]{0:T(256)(128)(2,1)} all-reduce(bf16[192]{0:T(256)(128)(2,1)} %multiply_convert_fusion.6), channel_id=1, replica_groups=mesh['group'=2,'tm'=4,'tensor'=2,'pair'=2] {'tensor','pair'}, use_global_device_ids=true, to_apply=%region_13.15 | all-reduce | flops 192 | bytes 768 | tf_op jit(solution)/shard_map/psum | solution.py:62
  92.5 1.3 subtract_multiply_fusion
  93.8 0.6 copy-done.10
  94.4 3.9 %convolution_convert_fusion = bf16[192,1536]{1,0:T(8,128)(2,1)} fusion(bf16[1536,768]{1,0:T(8,128)(2,1)} %param.13, f32[192,768]{1,0:T(8,128)} %copy-done.12, f32[192,768]{1,0:T(8,128)} %get-tuple-element.24, f32[192]{0:T(256)S(1)} %broadcast_multiply_fusion.3), kind=kOutput, calls=%fused_computation.4 | convolution fusion | flops 454754304 | bytes 4129536 | tf_op jit(solution)/shard_map/nf,df->nd/dot_general | solution.py:60
  98.3 0.0 all-reduce.4.cloned.1.call-update
  98.3 0.0 reduce-scatter.4.cloned.1.call-start
  98.3 2.6 %convolution_convert_fusion.1 = bf16[192,1536]{1,0:T(8,128)(2,1)} fusion(bf16[768,1536]{1,0:T(8,128)(2,1)S(1)} %copy-done, f32[192,768]{1,0:T(8,128)} %copy-done.12), kind=kOutput, calls=%fused_computation.5 | convolution fusion | flops 454017024 | bytes 3538944 | tf_op jit(solution)/shard_map/dot_general | solution.py:49
  100.9 2.2 %copy.10 = bf16[192,1536]{0,1:T(8,128)(2,1)} copy(bf16[192,1536]{1,0:T(8,128)(2,1)} %convolution_convert_fusion.1) | data formatting | bytes 1179648
  103.1 0.0 reduce-scatter.4.cloned.1.call-update
  103.2 1.2 iota_compare_fusion
  104.4 26.6 %all-reduce.4.cloned.1.call-done = bf16[192,1536]{1,0:T(8,128)(2,1)} async-done(((bf16[192,1536]{1,0:T(8,128)(2,1)}), bf16[192,1536]{1,0:T(8,128)(2,1)}) %all-reduce.4.cloned.1.call-update) | async-done | bytes 589840 | tf_op jit(solution)/shard_map/psum | solution.py:61
  131.0 1.6 fusion.10
  132.6 0.8 fusion.14
  133.5 23.9 %reduce-scatter.4.cloned.1.call-done = bf16[384,192]{1,0:T(8,128)(2,1)} async-done(((bf16[1536,192]{1,0:T(8,128)(2,1)}), bf16[384,192]{1,0:T(8,128)(2,1)}) %reduce-scatter.4.cloned.1.call-update) | async-done | bytes 147472
  157.4 1.7 copy.11
  159.1 1.0 multiply_convert_fusion.5
  160.1 2.0 broadcast_select_fusion
  162.1 20.4 %all_to_all.20 = bf16[4,192,384]{2,1,0:T(8,128)(2,1)} all-to-all(bf16[4,192,384]{2,1,0:T(8,128)(2,1)S(1)} %get-tuple-element.20), channel_id=1, replica_groups=mesh['group'=2,'tm'=4,'tensor'=2,'pair'=2] {'tm'}, dimensions={0} | all-to-all | bytes 1179648 | tf_op jit(solution)/shard_map/all_to_all | solution.py:79
  182.4 4.2 %all-to-all-start.3 = ((bf16[4,192,384]{2,1,0:T(8,128)(2,1)}), bf16[4,192,384]{2,1,0:T(8,128)(2,1)}, u32[]{:S(2)}, u32[]{:S(2)}) async-start(bf16[4,192,384]{2,1,0:T(8,128)(2,1)} %get-tuple-element.19), calls=%async_computation.3 | async-start | bytes 1179648 | tf_op jit(solution)/shard_map/all_to_all | solution.py:80
  186.6 1.5 convert_element_type.70
  188.2 0.1 copy-done.2
  188.3 1.6 convert_element_type.80
  189.9 0.1 fusion.22
  189.9 0.1 pad_maximum_fusion.1
  190.0 6.2 %scatter_custom_fusion = f32[1536,384]{1,0:T(8,128)} fusion(f32[1536,384]{1,0:T(8,128)} %convert_element_type.70, s32[384]{0:T(512)} %copy-done.8, s32[]{:T(128)S(6)} %select_n.49, s32[]{:T(128)} %constant.35.clone.1, bf16[768,384]{1,0:T(8,128)(2,1)S(1)} %bitcast.20, bf16[]{:T(256)} %constant.68.clone.1), kind=kCustom, calls=%fused_computation.27 | custom fusion | flops 294912 | bytes 2950148 | tf_op jit(solution)/shard_map/scatter-add | solution.py:95
  196.2 2.8 %convert_element_type.79 = bf16[1536,384]{1,0:T(8,128)(2,1)} convert(f32[1536,384]{1,0:T(8,128)} %scatter_custom_fusion) | non-fusion elementwise | flops 589824 | bytes 3538944 | tf_op jit(solution)/shard_map/convert_element_type | solution.py:96
  199.0 3.0 %all-to-all-done.3 = bf16[4,192,384]{2,1,0:T(8,128)(2,1)} async-done(((bf16[4,192,384]{2,1,0:T(8,128)(2,1)}), bf16[4,192,384]{2,1,0:T(8,128)(2,1)}, u32[]{:S(2)}, u32[]{:S(2)}) %all-to-all-start.3) | async-done | bytes 589856 | tf_op jit(solution)/shard_map/all_to_all | solution.py:80
  202.0 1.1 fusion.21
  203.1 0.1 pad_maximum_fusion.3
  203.2 6.2 %scatter_custom_fusion.1 = f32[1536,384]{1,0:T(8,128)} fusion(f32[1536,384]{1,0:T(8,128)} %convert_element_type.80, s32[384]{0:T(512)} %copy-done.8, s32[]{:T(128)S(6)} %select_n.49, s32[]{:T(128)} %constant.35.clone.1, bf16[768,384]{1,0:T(8,128)(2,1)S(1)} %bitcast.19, bf16[]{:T(256)} %constant.68.clone.1), kind=kCustom, calls=%fused_computation.23 | custom fusion | flops 294912 | bytes 2950148 | tf_op jit(solution)/shard_map/scatter-add | solution.py:101
  209.3 2.8 %convert_element_type.89 = bf16[1536,384]{1,0:T(8,128)(2,1)} convert(f32[1536,384]{1,0:T(8,128)} %scatter_custom_fusion.1) | non-fusion elementwise | flops 589824 | bytes 3538944 | tf_op jit(solution)/shard_map/convert_element_type | solution.py:102
  (31 shorter events, 0.1 us)
Async XLA Ops:
  7.2 76.2 %copy-start = (bf16[768,1536]{1,0:T(8,128)(2,1)S(1)}, bf16[768,1536]{1,0:T(8,128)(2,1)}, u32[]{:S(2)}) copy-start(bf16[768,1536]{1,0:T(8,128)(2,1)} %param.14) | copy-start | bytes 7077892
  12.8 1.3 copy-start.8
  14.1 3.9 %copy-start.1 = (bf16[1536,384]{1,0:T(8,128)(2,1)S(1)}, bf16[1536,384]{1,0:T(8,128)(2,1)}, u32[]{:S(2)}) copy-start(bf16[1536,384]{1,0:T(8,128)(2,1)} %param.10) | copy-start | bytes 3538948
  28.4 7.2 %copy-start.5 = (f32[1536]{0:T(1024)S(1)}, f32[1536]{0:T(1024)}, u32[]{:S(2)}) copy-start(f32[1536]{0:T(1024)} %param.11) | copy-start | bytes 18436
  29.3 22.3 %all-to-all-start = ((bf16[4,192,384]{2,1,0:T(8,128)(2,1)}), bf16[4,192,384]{2,1,0:T(8,128)(2,1)}, u32[]{:S(2)}, u32[]{:S(2)}) async-start(bf16[4,192,384]{2,1,0:T(8,128)(2,1)} %pad_maximum_fusion), calls=%async_computation | async-start | bytes 1179648 | tf_op jit(solution)/shard_map/all_to_all | solution.py:33
  51.6 19.6 %all-to-all-start.2 = ((bf16[4,192,384]{2,1,0:T(8,128)(2,1)}), bf16[4,192,384]{2,1,0:T(8,128)(2,1)}, u32[]{:S(2)}, u32[]{:S(2)}) async-start(bf16[4,192,384]{2,1,0:T(8,128)(2,1)} %pad_maximum_fusion.2), calls=%async_computation.2 | async-start | bytes 1179648 | tf_op jit(solution)/shard_map/all_to_all | solution.py:34
  55.7 75.2 %all-reduce.4.cloned.1.call-start = ((), (), s32[]{:S(2)}) async-start(), calls=%async_computation.5 | async-start | bytes 1179648 | tf_op jit(solution)/shard_map/psum | solution.py:61
  65.4 0.8 copy-start.3
  66.2 14.6 %copy-start.6 = (f32[1536]{0:T(1024)S(1)}, f32[1536]{0:T(1024)}, u32[]{:S(2)}) copy-start(f32[1536]{0:T(1024)} %param.12) | copy-start | bytes 18436
  83.3 1.8 copy-start.12
  93.8 0.6 copy-start.10
  98.3 59.1 %reduce-scatter.4.cloned.1.call-start = ((), (), s32[]{:S(2)}) async-start(), calls=%async_computation.6 | async-start | bytes 983040
  130.9 1.7 copy-start.7
  130.9 1.7 copy-start.9
  132.6 27.5 %copy-start.11 = (pred[4,192]{1,0:T(4,128)(4,1)S(1)}, pred[4,192]{1,0:T(4,128)(4,1)}, u32[]{:S(2)}) copy-start(pred[4,192]{1,0:T(4,128)(4,1)} %iota_compare_fusion) | copy-start | bytes 2308
  182.4 19.5 %all-to-all-start.3 = ((bf16[4,192,384]{2,1,0:T(8,128)(2,1)}), bf16[4,192,384]{2,1,0:T(8,128)(2,1)}, u32[]{:S(2)}, u32[]{:S(2)}) async-start(bf16[4,192,384]{2,1,0:T(8,128)(2,1)} %get-tuple-element.19), calls=%async_computation.3 | async-start | bytes 1179648 | tf_op jit(solution)/shard_map/all_to_all | solution.py:80
  186.6 1.7 copy-start.2
  188.3 1.6 copy-start.4
Sparse Core Ops, SparseCore 0:
  98.4 32.4 all-reduce.3
  134.1 23.2 reduce-scatter.3
where the time goes:
time: 220 us; the launch traced here: 219 us
  waiting for transfers between devices  67 us (30%)
  blocking collectives  42.7 us (19%)
  other arithmetic  42.5 us (19%)
  local copies, waits for them, and re-layouts  25 us (11%)
  between operations  16.3 us (7%)
  starting transfers between devices  14.7 us (7%)
  matrix products  10.7 us (5%)
    psum x1, waiting for transfers between devices, per_device(): lax.psum(normed_part.astype(jnp.bfloat16), ('tensor', 'pair'))  26.6 us
    unnamed x3, waiting for transfers between devices  23.9 us
    all_to_all x1, blocking collectives, per_device(): lax.all_to_all(sort_back(routed_out), 'tm', split_axis=0, concat_axis=0,...  20.4 us
    all_to_all x1, waiting for transfers between devices, per_device(): lax.all_to_all(spread(rows_in), 'tm', split_axis=0, concat_axis=0, tiled=...  8.85 us
    all_gather x1, blocking collectives, per_device(): full_in = lax.all_gather(mine_in, ('tensor', 'pair'), axis=1, tiled=True)  7.72 us
    all_gather x1, blocking collectives, per_device(): full_cot = lax.all_gather(mine_cot, ('tensor', 'pair'), axis=1, tiled=True)  7.72 us
    psum x1, blocking collectives, per_device(): lax.psum(score_part.astype(jnp.bfloat16), ('tensor', 'pair'))  6.89 us
    all_to_all x1, starting transfers between devices, per_device(): lax.all_to_all(spread(rows_in), 'tm', split_axis=0, concat_axis=0, tiled=...  6.32 us
  transfers between devices with their start and end apart: 5, of which 5 were waited for; matrix products, arithmetic and copies ran while one was open for 14% of the time, Pallas kernels for 0%

commit v1 on v0

v1 whole, which is shorter than its diff:
```python
import functools

import jax
import jax.numpy as jnp
from jax import lax
from jax.experimental import pallas as pl
from jax.experimental.pallas import tpu as pltpu
from jax.sharding import PartitionSpec as P

EPS = 1e-05
F32 = jnp.float32
BF16 = jnp.bfloat16
VMEM = pltpu.VMEM
SMEM = pltpu.SMEM


def params(limit=32):
    return pltpu.CompilerParams(vmem_limit_bytes=limit * 1024 * 1024)


def vspec():
    return pl.BlockSpec(memory_space=VMEM)


def tile_of(extent):
    for size in (256, 384, 128):
        if extent % size == 0:
            return size
    return extent


def live_count(count_ref):
    return count_ref[lax.axis_index("tm")]


def gather_body(count_ref, picked_ref, frames_ref, rows_ref):
    slots = picked_ref.shape[1]
    frames_dev = frames_ref.shape[0]
    live = lax.broadcasted_iota(jnp.int32, (1, slots), 1) < live_count(count_ref)
    wanted = jnp.where(live, picked_ref[...], -1).astype(F32)
    column = jnp.broadcast_to(wanted, (128, slots)).T[:, :1]
    place = lax.broadcasted_iota(jnp.int32, (1, frames_dev), 1).astype(F32)
    onehot = jnp.where(column == place, 1.0, 0.0).astype(BF16)
    rows_ref[...] = jnp.dot(onehot, frames_ref[...], preferred_element_type=F32).astype(BF16)


def gather_rows(count, picked, frames):
    slots, (frames_dev, width) = picked.shape[1], frames.shape
    return pl.pallas_call(
        gather_body,
        out_shape=jax.ShapeDtypeStruct((slots, width), BF16),
        in_specs=[pl.BlockSpec(memory_space=SMEM), vspec(), vspec()],
        out_specs=vspec(),
        compiler_params=params(),
        cost_estimate=pl.CostEstimate(
            flops=2 * slots * frames_dev * width, bytes_accessed=2 * frames_dev * width, transcendentals=0
        ),
        name="gather_rows",
    )(count, picked, frames)


def block_at(way, tensors, width):
    t, p = lax.axis_index("tensor"), lax.axis_index("pair")
    step, side = way
    index = ((t + tensors - step) % tensors) * 2 + (p + side) % 2
    return pl.multiple_of(index * width, 128)


def forward_body(ways, tensors, width, *refs):
    blocks = refs[: len(ways)]
    up_hbm, down_hbm, gain_ref, router_ref = refs[len(ways) : len(ways) + 4]
    full_ref, stats_ref, hidden_ref, slope_ref, part_ref = refs[len(ways) + 4 : len(ways) + 9]
    normed_ref, up_ref, down_ref, sems = refs[len(ways) + 9 :]
    slots, features = full_ref.shape
    hidden_dev = hidden_ref.shape[1]
    copy_up = pltpu.make_async_copy(up_hbm, up_ref, sems.at[0])
    copy_down = pltpu.make_async_copy(down_hbm, down_ref, sems.at[1])
    copy_up.start()
    copy_down.start()
    if len(ways) == 1:
        full_ref[...] = blocks[0][...]
    else:
        for way, block in zip(ways, blocks):
            full_ref[:, pl.ds(block_at(way, tensors, width), width)] = block[...]
    chunk = 32
    lane = lax.broadcasted_iota(jnp.int32, (chunk, 128), 1)

    def norm_chunk(i, _):
        rows = pl.ds(pl.multiple_of(i * chunk, chunk), chunk)
        wide = full_ref[rows, :].astype(F32)
        gate = jax.nn.sigmoid(jnp.sum(wide * router_ref[...], axis=1, keepdims=True))
        mean = jnp.sum(wide, axis=1, keepdims=True) * (1.0 / features)
        deviate = wide - mean
        inv = lax.rsqrt(jnp.sum(deviate * deviate, axis=1, keepdims=True) * (1.0 / features) + EPS)
        normed_ref[rows, :] = (deviate * inv * gain_ref[...]).astype(BF16)
        stats_ref[rows, :] = jnp.where(lane == 0, mean, jnp.where(lane == 1, inv, gate))
        return 0

    lax.fori_loop(0, slots // chunk, norm_chunk, 0)
    half_gate = 0.5 * stats_ref[:, 2:3]
    copy_up.wait()
    tile = tile_of(hidden_dev)

    def up_tile(i, _):
        cols = pl.ds(pl.multiple_of(i * tile, 128), tile)
        value = jnp.dot(normed_ref[...], up_ref[:, cols], preferred_element_type=F32)
        s = jax.nn.sigmoid(value)
        hidden_ref[:, cols] = (value * s).astype(BF16)
        slope_ref[:, cols] = half_gate * s * (1.0 + value * (1.0 - s))
        return 0

    lax.fori_loop(0, hidden_dev // tile, up_tile, 0)
    copy_down.wait()
    wide_tile = tile_of(features)

    def down_tile(i, _):
        cols = pl.ds(pl.multiple_of(i * wide_tile, 128), wide_tile)
        value = jnp.dot(hidden_ref[...], down_ref[:, cols], preferred_element_type=F32)
        part_ref[:, cols] = (value * half_gate).astype(BF16)
        return 0

    lax.fori_loop(0, features // wide_tile, down_tile, 0)


def forward(blocks, ways, tensors, up, down, gain, router):
    slots, width = blocks[0].shape
    features, hidden_dev = up.shape
    return pl.pallas_call(
        functools.partial(forward_body, ways, tensors, width),
        out_shape=(
            jax.ShapeDtypeStruct((slots, features), BF16),
            jax.ShapeDtypeStruct((slots, 128), F32),
            jax.ShapeDtypeStruct((slots, hidden_dev), BF16),
            jax.ShapeDtypeStruct((slots, hidden_dev), F32),
            jax.ShapeDtypeStruct((slots, features), BF16),
        ),
        in_specs=[vspec()] * len(blocks) + [pl.BlockSpec(memory_space=pl.ANY)] * 2 + [vspec()] * 2,
        out_specs=(vspec(),) * 5,
        scratch_shapes=[
            VMEM((slots, features), BF16),
            VMEM(up.shape, BF16),
            VMEM(down.shape, BF16),
            pltpu.SemaphoreType.DMA((2,)),
        ],
        compiler_params=params(),
        cost_estimate=pl.CostEstimate(
            flops=4 * slots * features * hidden_dev, bytes_accessed=4 * features * hidden_dev, transcendentals=0
        ),
        name="forward",
    )(*blocks, up, down, gain, router)


def backward_body(ways, tensors, width, *refs):
    blocks = refs[: len(ways)]
    up_hbm, down_hbm, gain_ref, full_ref, stats_ref, hidden_ref, slope_ref = refs[len(ways) : len(ways) + 7]
    part_ref, sums_ref = refs[len(ways) + 7 : len(ways) + 9]
    cot_ref, pre_ref, up_ref, down_ref, sems = refs[len(ways) + 9 :]
    slots, features = full_ref.shape
    hidden_dev = hidden_ref.shape[1]
    copy_up = pltpu.make_async_copy(up_hbm, up_ref, sems.at[0])
    copy_down = pltpu.make_async_copy(down_hbm, down_ref, sems.at[1])
    copy_down.start()
    copy_up.start()
    if len(ways) == 1:
        cot_ref[...] = blocks[0][...]
    else:
        for way, block in zip(ways, blocks):
            cot_ref[:, pl.ds(block_at(way, tensors, width), width)] = block[...]
    copy_down.wait()
    tile = tile_of(hidden_dev)
    over_lanes = (((1,), (1,)), ((), ()))

    def hidden_tile(i, score):
        cols = pl.ds(pl.multiple_of(i * tile, 128), tile)
        value = lax.dot_general(cot_ref[...], down_ref[cols, :], over_lanes, preferred_element_type=F32)
        pre_ref[:, cols] = (value * slope_ref[:, cols]).astype(BF16)
        return score + jnp.sum(value * hidden_ref[:, cols].astype(F32), axis=1, keepdims=True)

    score = lax.fori_loop(0, hidden_dev // tile, hidden_tile, jnp.zeros((slots, 1), F32))
    copy_up.wait()
    mean, inv = stats_ref[:, 0:1], stats_ref[:, 1:2]
    wide_tile = tile_of(features)

    def feature_tile(i, sums):
        plain, cross = sums
        cols = pl.ds(pl.multiple_of(i * wide_tile, 128), wide_tile)
        value = lax.dot_general(pre_ref[...], up_ref[cols, :], over_lanes, preferred_element_type=F32)
        scaled = value * gain_ref[:, cols]
        centred = (full_ref[:, cols].astype(F32) - mean) * inv
        part_ref[:, cols] = (scaled * inv).astype(BF16)
        return (
            plain + jnp.sum(scaled, axis=1, keepdims=True),
            cross + jnp.sum(scaled * centred, axis=1, keepdims=True),
        )

    zero = jnp.zeros((slots, 1), F32)
    plain, cross = lax.fori_loop(0, features // wide_tile, feature_tile, (zero, zero))
    lane = lax.broadcasted_iota(jnp.int32, (slots, 128), 1)
    table = jnp.where(lane == 0, plain, jnp.where(lane == 1, cross, score))
    sums_ref[...] = table.T[:8, :]


def backward(blocks, ways, tensors, up, down, gain, full, stats, hidden, slope):
    slots, width = blocks[0].shape
    features, hidden_dev = up.shape
    return pl.pallas_call(
        functools.partial(backward_body, ways, tensors, width),
        out_shape=(jax.ShapeDtypeStruct((slots, features), BF16), jax.ShapeDtypeStruct((8, slots), F32)),
        in_specs=[vspec()] * len(blocks) + [pl.BlockSpec(memory_space=pl.ANY)] * 2 + [vspec()] * 5,
        out_specs=(vspec(),) * 2,
        scratch_shapes=[
            VMEM((slots, features), BF16),
            VMEM((slots, hidden_dev), BF16),
            VMEM(up.shape, BF16),
            VMEM(down.shape, BF16),
            pltpu.SemaphoreType.DMA((2,)),
        ],
        compiler_params=params(),
        cost_estimate=pl.CostEstimate(
            flops=4 * slots * features * hidden_dev, bytes_accessed=4 * features * hidden_dev, transcendentals=0
        ),
        name="backward",
    )(*blocks, up, down, gain, full, stats, hidden, slope)


def place_rows(count_ref, picked_ref, frames_ref, rows, out_ref):
    slots = picked_ref.shape[1]
    tile = out_ref.shape[0]
    live = lax.broadcasted_iota(jnp.int32, (1, slots), 1) < live_count(count_ref)
    wanted = jnp.where(live, picked_ref[...], -1)
    place = lax.broadcasted_iota(jnp.int32, (tile, 1), 0) + pl.program_id(0) * tile
    onehot = jnp.where(wanted == place, 1.0, 0.0).astype(BF16)
    added = jnp.dot(onehot, rows, preferred_element_type=F32)
    out_ref[...] = (frames_ref[...].astype(F32) + added).astype(BF16)


def mixed_body(arrived, count_ref, picked_ref, frames_ref, keep_ref, got_ref, *refs):
    out_ref, rows_ref = refs[arrived:]

    @pl.when(pl.program_id(0) == 0)
    def _():
        total = keep_ref[...].astype(F32) + got_ref[...].astype(F32)
        for block in refs[:arrived]:
            total = total + block[...].astype(F32)
        rows_ref[...] = total.astype(BF16)

    place_rows(count_ref, picked_ref, frames_ref, rows_ref[...], out_ref)


def grads_body(
    arrived, sums_count, count_ref, picked_ref, frames_ref, keep_ref, got_ref, own_ref, stats_ref, gain_ref, router_ref, *refs
):
    blocks, sums_refs = refs[:arrived], refs[arrived : arrived + sums_count]
    out_ref, rows_ref = refs[arrived + sums_count :]

    @pl.when(pl.program_id(0) == 0)
    def _():
        slots = own_ref.shape[0]
        features = gain_ref.shape[1]
        sums = sums_refs[0][...]
        for ref in sums_refs[1:]:
            sums = sums + ref[...]
        columns = jnp.broadcast_to(sums[None], (16, 8, slots)).reshape(128, slots).T
        plain_mean = columns[:, 0:1] * (1.0 / features)
        cross_mean = columns[:, 1:2] * (1.0 / features)
        mean, inv, gate = stats_ref[:, 0:1], stats_ref[:, 1:2], stats_ref[:, 2:3]
        centred = (own_ref[...].astype(F32) - mean) * inv
        total = keep_ref[...].astype(F32) + got_ref[...].astype(F32)
        for block in blocks:
            total = total + block[...].astype(F32)
        score = 0.5 * columns[:, 2:3] * gate * (1.0 - gate)
        total = total - inv * (plain_mean + centred * cross_mean) + score * router_ref[...]
        rows_ref[...] = total.astype(BF16)

    place_rows(count_ref, picked_ref, frames_ref, rows_ref[...], out_ref)


def scatter_rows(body, name, count, picked, frames, others):
    slots, (frames_dev, width) = picked.shape[1], frames.shape
    tile = 256
    whole = [pl.BlockSpec(x.shape, lambda i: (0, 0)) for x in others]
    return pl.pallas_call(
        body,
        grid=(frames_dev // tile,),
        out_shape=jax.ShapeDtypeStruct(frames.shape, BF16),
        in_specs=[
            pl.BlockSpec(memory_space=SMEM),
            pl.BlockSpec(picked.shape, lambda i: (0, 0)),
            pl.BlockSpec((tile, width), lambda i: (i, 0)),
        ]
        + whole,
        out_specs=pl.BlockSpec((tile, width), lambda i: (i, 0)),
        scratch_shapes=[VMEM((slots, width), BF16)],
        compiler_params=params(),
        cost_estimate=pl.CostEstimate(
            flops=2 * slots * frames_dev * width, bytes_accessed=4 * frames_dev * width, transcendentals=0
        ),
        name=name,
    )(count, picked, frames, *others)


def per_device(frames, router_weight, norm_gain, up_weight, down_weight, picked_rows, picked_count, cotangent):
    width = frames.shape[1]
    features = up_weight.shape[0]
    tensors = lax.axis_size("tensor")
    t, p = lax.axis_index("tensor"), lax.axis_index("pair")
    picked = picked_rows.reshape(1, -1)
    gain, router = norm_gain.reshape(1, -1), router_weight.reshape(1, -1)
    steps = range(1, tensors)

    def shift(x, k):
        return lax.ppermute(x, "tensor", [(i, (i + k) % tensors) for i in range(tensors)])

    def swap(x):
        return lax.ppermute(x, "pair", [(0, 1), (1, 0)])

    def collect(rows):
        across = [shift(rows, k) for k in steps]
        near = [rows, swap(rows)]
        ways = [(0, 0), (0, 1)] + [(k, 0) for k in steps] + [(k, 1) for k in steps]
        blocks = near + across + [swap(x) for x in across]
        if width % 128 == 0:
            return blocks, ways
        full = jnp.zeros((rows.shape[0], features), BF16)
        for (k, side), block in zip(ways, blocks):
            start = (((t + tensors - k) % tensors) * 2 + (p + side) % 2) * width
            full = lax.dynamic_update_slice_in_dim(full, block, start, 1)
        return [full], [(0, 0)]

    def columns(part, k, side):
        start = (((t + k) % tensors) * 2 + (p + side) % 2) * width
        return lax.dynamic_slice_in_dim(part, start, width, 1)

    def reduce(part):
        sent = [columns(part, k, 0).astype(F32) + swap(columns(part, k, 1)).astype(F32) for k in steps]
        across = [shift(x.astype(BF16), k) for x, k in zip(sent, steps)]
        return columns(part, 0, 0), swap(columns(part, 0, 1)), across

    rows_in = gather_rows(picked_count, picked, frames)
    in_blocks, ways = collect(rows_in)
    rows_cot = gather_rows(picked_count, picked, cotangent)
    cot_blocks, _ = collect(rows_cot)
    full, stats, hidden, slope, out_part = forward(in_blocks, ways, tensors, up_weight, down_weight, gain, router)
    out_keep, out_got, out_across = reduce(out_part)
    grad_part, sums = backward(
        cot_blocks, ways, tensors, up_weight, down_weight, gain, full, stats, hidden, slope
    )
    sums = sums + swap(sums)
    sums_across = [shift(sums, k) for k in steps]
    grad_keep, grad_got, grad_across = reduce(grad_part)
    mixed = scatter_rows(
        functools.partial(mixed_body, len(out_across)),
        "mixed_rows",
        picked_count,
        picked,
        frames,
        [out_keep, out_got] + out_across,
    )
    router_own = lax.dynamic_slice_in_dim(router, (t * 2 + p) * width, width, 1)
    frames_grad = scatter_rows(
        functools.partial(grads_body, len(grad_across), len(sums_across) + 1),
        "grad_rows",
        picked_count,
        picked,
        cotangent,
        [grad_keep, grad_got, rows_in, stats, gain, router_own] + grad_across + [sums] + sums_across,
    )
    return (mixed, frames_grad)


def solution(mesh):
    return jax.shard_map(
        per_device,
        mesh=mesh,
        in_specs=(
            P(("group", "tm"), ("tensor", "pair")),
            P(),
            P(),
            P(None, ("tensor", "pair")),
            P(("tensor", "pair"), None),
            P(("group", "tm")),
            P("group"),
            P(("group", "tm"), ("tensor", "pair")),
        ),
        out_specs=(P(("group", "tm"), ("tensor", "pair")), P(("group", "tm"), ("tensor", "pair"))),
        check_vma=False,
    )
```

time: 220 us -> 68.1 us (0.31)
  waiting for transfers between devices: 67 us -> 13.1 us
  blocking collectives: 42.7 us -> 0 us
  other arithmetic: 42.5 us -> 2.08 us
  Pallas kernels: 0 us -> 26.9 us
  between operations: 16.3 us -> 0.79 us
  matrix products: 10.7 us -> 0 us
  local copies, waits for them, and re-layouts: 25 us -> 16 us
  starting transfers between devices: 14.7 us -> 8.57 us
    pallas_call x0 -> x6, Pallas kernels: none -> 26.9 us  [the longest x2 8.54 us: scatter_rows(): pl.pallas_call(body, grid=(frames_dev // tile,), out_shape=jax.ShapeDtype...]
    psum x1 -> x0, waiting for transfers between devices: 26.6 us -> none  [per_device(): lax.psum(normed_part.astype(jnp.bfloat16), ('tensor', 'pair'))]
    unnamed x3 -> x0, waiting for transfers between devices: 23.9 us -> none
    all_to_all x1 -> x0, blocking collectives: 20.4 us -> none  [per_device(): lax.all_to_all(sort_back(routed_out), 'tm', split_axis=0, concat_axis=0,...]
    all_to_all x3 -> x0, waiting for transfers between devices: 16.5 us -> none  [the longest x1 8.85 us: per_device(): lax.all_to_all(spread(rows_in), 'tm', split_axis=0, concat_axis=0, tiled=...]
    all_gather x2 -> x0, blocking collectives: 15.4 us -> none  [the longest x1 7.72 us: per_device(): full_in = lax.all_gather(mine_in, ('tensor', 'pair'), axis=1, tiled=True)]
    all_to_all x3 -> x0, starting transfers between devices: 14.6 us -> none  [the longest x1 6.32 us: per_device(): lax.all_to_all(spread(rows_in), 'tm', split_axis=0, concat_axis=0, tiled=...]
    ppermute x0 -> x14, waiting for transfers between devices: none -> 13.1 us  [the longest x5 12.7 us: shift(): lax.ppermute(x, 'tensor', [(i, (i + k) % tensors) for i in range(tensors)])]
  transfers between devices with their start and end apart: 5 -> 14, of which waited for: 5 -> 5; matrix products, arithmetic and copies ran while one was open for 14% -> 8% of each run, Pallas kernels for 0% -> 30%
where the time goes in v1:
time: 68.1 us; the launch traced here: 67.5 us
  Pallas kernels  26.9 us (40%)
  local copies, waits for them, and re-layouts  16 us (23%)
  waiting for transfers between devices  13.1 us (19%)
  starting transfers between devices  8.57 us (13%)
  other arithmetic  2.08 us (3%)
  between operations  0.79 us (1%)
    ppermute x5, waiting for transfers between devices, shift(): lax.ppermute(x, 'tensor', [(i, (i + k) % tensors) for i in range(tensors)])  12.7 us
    unnamed x50, local copies, waits for them, and re-layouts  12.2 us
    pallas_call x2, Pallas kernels, scatter_rows(): pl.pallas_call(body, grid=(frames_dev // tile,), out_shape=jax.ShapeDtype...  8.54 us
    pallas_call x1, Pallas kernels, forward(): pl.pallas_call(functools.partial(forward_body, ways, tensors, width), out...  7.54 us
    ppermute x5, starting transfers between devices, shift(): lax.ppermute(x, 'tensor', [(i, (i + k) % tensors) for i in range(tensors)])  6.89 us
    pallas_call x1, Pallas kernels, backward(): pl.pallas_call(functools.partial(backward_body, ways, tensors, width), ou...  6.81 us
    pallas_call x2, Pallas kernels, gather_rows(): pl.pallas_call(gather_body, out_shape=jax.ShapeDtypeStruct((slots, width)...  3.95 us
    convert_element_type x2, other arithmetic, reduce(): across = [shift(x.astype(BF16), k) for x, k in zip(sent, steps)]  2.08 us
  transfers between devices with their start and end apart: 14, of which 5 were waited for; matrix products, arithmetic and copies ran while one was open for 8% of the time, Pallas kernels for 30%

profile of v1, /device:TPU:0, one launch (start us, length us, event | category | flops | bytes accessed | tf_op | source)
XLA Modules:
  0.0 67.5 jit_solution(4896021623693433215)
XLA Ops:
  0.6 0.7 %reshape.14.picked_ref = s32[1,384]{1,0:T(1,128)S(1)} reshape(s32[384]{0:T(512)} %param.13) | data formatting | bytes 3072 | tf_op jit(solution)/shard_map/reshape | solution.py:307
  1.3 1.3 %copy-done.6 = bf16[1536,384]{1,0:T(8,128)(2,1)S(1)} copy-done((bf16[1536,384]{1,0:T(8,128)(2,1)S(1)}, bf16[1536,384]{1,0:T(8,128)(2,1)}, u32[]{:S(2)}) %copy-start.6) | copy-done | bytes 1179672
  2.6 0.7 copy-done.16
  3.2 1.6 %gather_rows.2.refs_0_.own_ref = bf16[384,384]{1,0:T(8,128)(2,1)S(1)} custom-call(s32[4]{0:T(128)S(1)} %copy-done.16, s32[1,384]{1,0:T(1,128)S(1)} %reshape.14.picked_ref, bf16[1536,384]{1,0:T(8,128)(2,1)S(1)} %copy-done.6), custom_call_target="tpu_custom_call" | custom-call | flops 452984832 | bytes 1179648 | tf_op jit(solution)/shard_map/gather_rows/pallas_call | solution.py:49
  4.9 0.0 copy-start.10
  4.9 3.0 %collective-permute-start.1 = (bf16[384,384]{1,0:T(8,128)(2,1)S(1)}, bf16[384,384]{1,0:T(8,128)(2,1)S(1)}, u32[]{:S(2)}, u32[]{:S(2)}) collective-permute-start(bf16[384,384]{1,0:T(8,128)(2,1)S(1)} %gather_rows.2.refs_0_.own_ref), channel_id=1, source_target_pairs={{0,2},{2,0},{1,3},{3,1},{4,6},{6,4},{5,7},{7,5},{8,10},{10,8},{9,1... | collective-permute-start | bytes 884744 | tf_op jit(solution)/shard_map/ppermute | solution.py:312
  7.9 1.3 %copy-done.2 = bf16[1536,384]{1,0:T(8,128)(2,1)S(1)} copy-done((bf16[1536,384]{1,0:T(8,128)(2,1)S(1)}, bf16[1536,384]{1,0:T(8,128)(2,1)}, u32[]{:S(2)}) %copy-start.2) | copy-done | bytes 1179672
  9.1 2.3 %gather_rows.3.refs_0_ = bf16[384,384]{1,0:T(8,128)(2,1)} custom-call(s32[4]{0:T(128)S(1)} %copy-done.16, s32[1,384]{1,0:T(1,128)S(1)} %reshape.14.picked_ref, bf16[1536,384]{1,0:T(8,128)(2,1)S(1)} %copy-done.2), custom_call_target="tpu_custom_call" | custom-call | flops 452984832 | bytes 1179648 | tf_op jit(solution)/shard_map/gather_rows/pallas_call | solution.py:49
  11.5 0.0 collective-permute-start.7
  11.5 0.0 collective-permute-start
  11.5 4.2 %collective-permute-done.1.refs_2_ = bf16[384,384]{1,0:T(8,128)(2,1)S(1)} collective-permute-done((bf16[384,384]{1,0:T(8,128)(2,1)S(1)}, bf16[384,384]{1,0:T(8,128)(2,1)S(1)}, u32[]{:S(2)}, u32[]{:S(2)}) %collective-permute-start.1) | collective-permute-done | bytes 294944 | tf_op jit(solution)/shard_map/ppermute | solution.py:312
  15.7 0.0 collective-permute-start.2
  15.7 0.7 %copy-done.18 = bf16[384,384]{1,0:T(8,128)(2,1)} copy-done((bf16[384,384]{1,0:T(8,128)(2,1)}, bf16[384,384]{1,0:T(8,128)(2,1)S(1)}, u32[]{:S(2)}) %copy-start.18) | copy-done | bytes 294936
  16.4 0.5 collective-permute-start.6
  16.9 0.0 copy-done.24
  16.9 0.0 copy-done.23
  17.0 0.6 reshape.16.refs_7_
  17.5 3.8 %collective-permute-done.7.refs_2_ = bf16[384,384]{1,0:T(8,128)(2,1)} collective-permute-done((bf16[384,384]{1,0:T(8,128)(2,1)}, bf16[384,384]{1,0:T(8,128)(2,1)}, u32[]{:S(2)}, u32[]{:S(2)}) %collective-permute-start.7) | collective-permute-done | bytes 294944 | tf_op jit(solution)/shard_map/ppermute | solution.py:312
  21.3 0.0 collective-permute-start.8
  21.3 0.0 collective-permute-done.refs_1_
  21.3 0.0 copy-done.10
  21.3 0.0 copy-start.20
  21.3 0.7 %copy-done.20 = bf16[384,384]{1,0:T(8,128)(2,1)} copy-done((bf16[384,384]{1,0:T(8,128)(2,1)}, bf16[384,384]{1,0:T(8,128)(2,1)S(1)}, u32[]{:S(2)}) %copy-start.20) | copy-done | bytes 294936
  22.0 0.0 collective-permute-done.2.refs_3_
  22.0 0.0 copy-done
  22.0 1.7 %copy-done.1 = bf16[768,1536]{1,0:T(8,128)(2,1)S(1)} copy-done((bf16[768,1536]{1,0:T(8,128)(2,1)S(1)}, bf16[768,1536]{1,0:T(8,128)(2,1)}, u32[]{:S(2)}) %copy-start.1) | copy-done | bytes 2359320
  23.7 1.0 %copy-done.11 = bf16[384,384]{1,0:T(8,128)(2,1)S(1)} copy-done((bf16[384,384]{1,0:T(8,128)(2,1)S(1)}, bf16[384,384]{1,0:T(8,128)(2,1)}, u32[]{:S(2)}) %copy-start.11) | copy-done | bytes 294936
  24.7 0.7 %copy-done.15 = f32[1,1536]{1,0:T(1,128)S(1)} copy-done((f32[1,1536]{1,0:T(1,128)S(1)}, f32[1,1536]{1,0:T(1,128)}, u32[]{:S(2)}) %copy-start.15) | copy-done | bytes 6168
  25.4 1.0 %copy-done.19 = bf16[384,384]{1,0:T(8,128)(2,1)S(1)} copy-done((bf16[384,384]{1,0:T(8,128)(2,1)S(1)}, bf16[384,384]{1,0:T(8,128)(2,1)}, u32[]{:S(2)}) %copy-start.19) | copy-done | bytes 294936
  26.3 1.0 %copy-done.21 = bf16[384,384]{1,0:T(8,128)(2,1)S(1)} copy-done((bf16[384,384]{1,0:T(8,128)(2,1)S(1)}, bf16[384,384]{1,0:T(8,128)(2,1)}, u32[]{:S(2)}) %copy-start.21) | copy-done | bytes 294936
  27.3 7.5 %forward.1 = (bf16[384,1536]{1,0:T(8,128)(2,1)S(1)}, f32[384,128]{1,0:T(8,128)S(1)}, bf16[384,768]{1,0:T(8,128)(2,1)S(1)}, f32[384,768]{1,0:T(8,128)S(1)}, bf16[384,1536]{1,0:T(8,128)(2,1)S(1)}) custom-call(bf16[384,384]{1,0:T(8,128)(2,1)S(1)} %copy-done.11, bf16[384,384]{1,0:T(8,128)(2,1)S(1)} %copy-done.21, bf16[384,384]{1,0:T(8,128)(2,1)S(1)} %copy-done.19, ...), custom_call_target="tpu_custom_call" | custom-call | flops 1811939328 | bytes 4718592 | tf_op jit(solution)/shard_map/forward/pallas_call | solution.py:128
  34.8 0.0 copy-start.8
  34.8 1.0 %constant_dynamic-slice_fusion.3 = (bf16[384,384]{1,0:T(8,128)(2,1)}, bf16[384,384]{1,0:T(8,128)(2,1)}, bf16[384,384]{1,0:T(8,128)(2,1)}) fusion(bf16[384,1536]{1,0:T(8,128)(2,1)S(1)} %get-tuple-element.9, s32[]{:T(128)S(6)} %select_n.69, s32[]{:T(128)S(6)} %select_n.66, s32[]{:T(128)S(6)} %select_n.64), kind=kLoop, calls=%fused_computation.5 | loop fusion | bytes 1769484 | tf_op jit(solution)/shard_map/dynamic_slice | solution.py:332
  35.8 0.5 collective-permute-start.4
  36.3 0.0 collective-permute-done.6.refs_1_
  36.3 0.0 collective-permute-done.8.refs_3_
  36.4 6.8 %backward.1 = (bf16[384,1536]{1,0:T(8,128)(2,1)S(1)}, f32[8,384]{1,0:T(8,128)S(1)}) custom-call(bf16[384,384]{1,0:T(8,128)(2,1)} %gather_rows.3.refs_0_, bf16[384,384]{1,0:T(8,128)(2,1)} %collective-permute-done.6.refs_1_, bf16[384,384]{1,0:T(8,128)(2,1)} %collective-permute-done.7.refs_2_, bf16[384,384]{1,0:T(8,128)(2,1)S(1)} %collective-permute-done.8.refs_3_, ...), custom_call_target="tpu_custom_call" | custom-call | flops 1811939328 | bytes 4718592 | tf_op jit(solution)/shard_map/backward/pallas_call | solution.py:206
  43.2 0.0 copy-start.4
  43.2 1.0 %copy-done.4 = bf16[384,1536]{1,0:T(8,128)(2,1)} copy-done((bf16[384,1536]{1,0:T(8,128)(2,1)}, bf16[384,1536]{1,0:T(8,128)(2,1)S(1)}, u32[]{:S(2)}) %copy-start.4) | copy-done | bytes 1179672
  44.2 0.8 %constant_dynamic-slice_fusion = (bf16[384,384]{1,0:T(8,128)(2,1)S(1)}, bf16[384,384]{1,0:T(8,128)(2,1)}, bf16[384,384]{1,0:T(8,128)(2,1)S(1)}) fusion(bf16[384,1536]{1,0:T(8,128)(2,1)S(1)} %get-tuple-element.14, s32[]{:T(128)S(6)} %select_n.69, s32[]{:T(128)S(6)} %select_n.66, s32[]{:T(128)S(6)} %select_n.64), kind=kLoop, calls=%fused_computation.2 | loop fusion | bytes 1769484 | tf_op jit(solution)/shard_map/dynamic_slice | solution.py:332
  45.0 0.1 collective-permute-start.10
  45.1 0.5 collective-permute-start.9
  45.6 0.1 collective-permute-start.3
  45.7 0.0 collective-permute-done.4
  45.7 1.0 %add_convert_fusion.1 = bf16[384,384]{1,0:T(8,128)(2,1)S(1)} fusion(bf16[384,384]{1,0:T(8,128)(2,1)} %collective-permute-done.4, bf16[384,1536]{1,0:T(8,128)(2,1)S(1)} %get-tuple-element.9, s32[]{:T(128)S(6)} %select_n.68), kind=kLoop, calls=%fused_computation.1 | loop fusion | flops 589824 | bytes 884740 | tf_op jit(solution)/shard_map/convert_element_type | solution.py:336
  46.7 1.7 %collective-permute-start.5 = (bf16[384,384]{1,0:T(8,128)(2,1)S(1)}, bf16[384,384]{1,0:T(8,128)(2,1)S(1)}, u32[]{:S(2)}, u32[]{:S(2)}) collective-permute-start(bf16[384,384]{1,0:T(8,128)(2,1)S(1)} %add_convert_fusion.1), channel_id=1, source_target_pairs={{0,2},{2,0},{1,3},{3,1},{4,6},{6,4},{5,7},{7,5},{8,10},{10,8},{9,1... | collective-permute-start | bytes 884744 | tf_op jit(solution)/shard_map/ppermute | solution.py:312
  48.5 0.0 collective-permute-done.10
  48.5 1.0 %add_convert_fusion = bf16[384,384]{1,0:T(8,128)(2,1)S(1)} fusion(bf16[384,384]{1,0:T(8,128)(2,1)S(1)} %collective-permute-done.10, bf16[384,1536]{1,0:T(8,128)(2,1)} %copy-done.4, s32[]{:T(128)S(6)} %select_n.68), kind=kLoop, calls=%fused_computation | loop fusion | flops 589824 | bytes 884740 | tf_op jit(solution)/shard_map/convert_element_type | solution.py:336
  49.5 0.4 collective-permute-start.11
  49.9 0.0 copy-done.14
  49.9 0.0 collective-permute-start.12
  49.9 0.8 %dynamic-slice.3 = f32[384]{0:T(512)S(1)} dynamic-slice(f32[1536]{0:T(1024)} %param.9, s32[]{:T(128)S(6)} %select_n.70), dynamic_slice_sizes={384} | dynamic-slice | bytes 3076 | tf_op jit(solution)/shard_map/dynamic-slice
  50.7 0.4 collective-permute-done.12
  51.1 1.7 %collective-permute-start.13 = (f32[8,384]{1,0:T(8,128)S(1)}, f32[8,384]{1,0:T(8,128)S(1)}, u32[]{:S(2)}, u32[]{:S(2)}) collective-permute-start(f32[8,384]{1,0:T(8,128)S(1)} %add.102.refs_1_), channel_id=1, source_target_pairs={{0,2},{2,0},{1,3},{3,1},{4,6},{6,4},{5,7},{7,5},{8,10},{10,8},{9,1... | collective-permute-start | bytes 36872 | tf_op jit(solution)/shard_map/ppermute | solution.py:312
  52.8 0.0 collective-permute-done.3.got_ref
  52.8 3.8 %collective-permute-done.5.refs_0_ = bf16[384,384]{1,0:T(8,128)(2,1)S(1)} collective-permute-done((bf16[384,384]{1,0:T(8,128)(2,1)S(1)}, bf16[384,384]{1,0:T(8,128)(2,1)S(1)}, u32[]{:S(2)}, u32[]{:S(2)}) %collective-permute-start.5) | collective-permute-done | bytes 294944 | tf_op jit(solution)/shard_map/ppermute | solution.py:312
  56.6 1.3 %copy-done.7 = bf16[1536,384]{1,0:T(8,128)(2,1)S(1)} copy-done((bf16[1536,384]{1,0:T(8,128)(2,1)S(1)}, bf16[1536,384]{1,0:T(8,128)(2,1)}, u32[]{:S(2)}) %copy-start.7) | copy-done | bytes 1179672
  57.9 3.8 %mixed_rows.1 = bf16[1536,384]{1,0:T(8,128)(2,1)} custom-call(s32[4]{0:T(128)S(1)} %copy-done.17, s32[1,384]{1,0:T(1,128)S(1)} %reshape.14.picked_ref, bf16[1536,384]{1,0:T(8,128)(2,1)S(1)} %copy-done.7, bf16[384,384]{1,0:T(8,128)(2,1)S(1)} %copy-done.5, bf16[384,384]{1,0:T(8,128)(2,1)S(1)} %collective-permute-done.3.got_ref, ...), custom_call_target="tpu_custom_call" | custom-call | flops 452984832 | bytes 2359296 | tf_op jit(solution)/shard_map/mixed_rows/pallas_call | solution.py:282
  61.7 1.0 %collective-permute-done.13.refs_2_ = f32[8,384]{1,0:T(8,128)S(1)} collective-permute-done((f32[8,384]{1,0:T(8,128)S(1)}, f32[8,384]{1,0:T(8,128)S(1)}, u32[]{:S(2)}, u32[]{:S(2)}) %collective-permute-start.13) | collective-permute-done | bytes 12320 | tf_op jit(solution)/shard_map/ppermute | solution.py:312
  62.7 0.0 collective-permute-done.9.got_ref
  62.7 0.0 collective-permute-done.11.refs_0_
  62.7 0.0 copy-done.9
  62.7 0.0 copy-done.12
  62.8 4.7 %grad_rows.1 = bf16[1536,384]{1,0:T(8,128)(2,1)} custom-call(s32[4]{0:T(128)S(1)} %copy-done.17, s32[1,384]{1,0:T(1,128)S(1)} %reshape.14.picked_ref, bf16[1536,384]{1,0:T(8,128)(2,1)S(1)} %copy-done.3, bf16[384,384]{1,0:T(8,128)(2,1)S(1)} %get-tuple-element.18.keep_ref, bf16[384,384]{1,0:T(8,128)(2,1)} %collective-permute-done.9.got_ref, ...), custom_call_target="tpu_custom_call" | custom-call | flops 452984832 | bytes 2359296 | tf_op jit(solution)/shard_map/grad_rows/pallas_call | solution.py:282
  (30 shorter events, 0.1 us)
Async XLA Ops:
  1.3 1.3 %copy-start.6 = (bf16[1536,384]{1,0:T(8,128)(2,1)S(1)}, bf16[1536,384]{1,0:T(8,128)(2,1)}, u32[]{:S(2)}) copy-start(bf16[1536,384]{1,0:T(8,128)(2,1)} %frames_ref.5) | copy-start | bytes 3538948
  2.6 0.7 copy-start.16
  3.2 18.8 %copy-start = (bf16[1536,768]{1,0:T(8,128)(2,1)S(1)}, bf16[1536,768]{1,0:T(8,128)(2,1)}, u32[]{:S(2)}) copy-start(bf16[1536,768]{1,0:T(8,128)(2,1)} %refs_4_.3) | copy-start | bytes 7077892
  4.9 16.5 %copy-start.10 = (bf16[384,384]{1,0:T(8,128)(2,1)}, bf16[384,384]{1,0:T(8,128)(2,1)S(1)}, u32[]{:S(2)}) copy-start(bf16[384,384]{1,0:T(8,128)(2,1)S(1)} %gather_rows.2.refs_0_.own_ref) | copy-start | bytes 884740
  4.9 10.8 %collective-permute-start.1 = (bf16[384,384]{1,0:T(8,128)(2,1)S(1)}, bf16[384,384]{1,0:T(8,128)(2,1)S(1)}, u32[]{:S(2)}, u32[]{:S(2)}) collective-permute-start(bf16[384,384]{1,0:T(8,128)(2,1)S(1)} %gather_rows.2.refs_0_.own_ref), channel_id=1, source_target_pairs={{0,2},{2,0},{1,3},{3,1},{4,6},{6,4},{5,7},{7,5},{8,10},{10,8},{9,1... | collective-permute-start | bytes 884744 | tf_op jit(solution)/shard_map/ppermute | solution.py:312
  7.9 1.3 %copy-start.2 = (bf16[1536,384]{1,0:T(8,128)(2,1)S(1)}, bf16[1536,384]{1,0:T(8,128)(2,1)}, u32[]{:S(2)}) copy-start(bf16[1536,384]{1,0:T(8,128)(2,1)} %frames_ref.7) | copy-start | bytes 3538948
  9.1 7.8 %copy-start.24 = (f32[1536]{0:T(1024)S(1)}, f32[1536]{0:T(1024)}, u32[]{:S(2)}) copy-start(f32[1536]{0:T(1024)} %param.10) | copy-start | bytes 18436
  9.1 7.8 %copy-start.23 = (f32[1536]{0:T(1024)S(1)}, f32[1536]{0:T(1024)}, u32[]{:S(2)}) copy-start(f32[1536]{0:T(1024)} %param.9) | copy-start | bytes 18436
  11.5 9.8 %collective-permute-start.7 = (bf16[384,384]{1,0:T(8,128)(2,1)}, bf16[384,384]{1,0:T(8,128)(2,1)}, u32[]{:S(2)}, u32[]{:S(2)}) collective-permute-start(bf16[384,384]{1,0:T(8,128)(2,1)} %gather_rows.3.refs_0_), channel_id=1, source_target_pairs={{0,2},{2,0},{1,3},{3,1},{4,6},{6,4},{5,7},{7,5},{8,10},{10,8},{9,1... | collective-permute-start | bytes 884744 | tf_op jit(solution)/shard_map/ppermute | solution.py:312
  11.5 9.8 %collective-permute-start = (bf16[384,384]{1,0:T(8,128)(2,1)S(1)}, bf16[384,384]{1,0:T(8,128)(2,1)S(1)}, u32[]{:S(2)}, u32[]{:S(2)}) collective-permute-start(bf16[384,384]{1,0:T(8,128)(2,1)S(1)} %gather_rows.2.refs_0_.own_ref), channel_id=1, source_target_pairs={{0,1},{1,0},{2,3},{3,2},{4,5},{5,4},{6,7},{7,6},{8,9},{9,8},{10,11... | collective-permute-start | bytes 884744 | tf_op jit(solution)/shard_map/ppermute | solution.py:315
  15.7 6.3 %collective-permute-start.2 = (bf16[384,384]{1,0:T(8,128)(2,1)S(1)}, bf16[384,384]{1,0:T(8,128)(2,1)}, u32[]{:S(2)}, u32[]{:S(2)}) collective-permute-start(bf16[384,384]{1,0:T(8,128)(2,1)S(1)} %collective-permute-done.1.refs_2_), channel_id=1, source_target_pairs={{0,1},{1,0},{2,3},{3,2},{4,5},{5,4},{6,7},{7,6},{8,9},{9,8},{10,11... | collective-permute-start | bytes 884744 | tf_op jit(solution)/shard_map/ppermute | solution.py:315
  15.7 0.7 %copy-start.18 = (bf16[384,384]{1,0:T(8,128)(2,1)}, bf16[384,384]{1,0:T(8,128)(2,1)S(1)}, u32[]{:S(2)}) copy-start(bf16[384,384]{1,0:T(8,128)(2,1)S(1)} %collective-permute-done.1.refs_2_) | copy-start | bytes 884740
  16.4 19.9 %collective-permute-start.6 = (bf16[384,384]{1,0:T(8,128)(2,1)}, bf16[384,384]{1,0:T(8,128)(2,1)}, u32[]{:S(2)}, u32[]{:S(2)}) collective-permute-start(bf16[384,384]{1,0:T(8,128)(2,1)} %gather_rows.3.refs_0_), channel_id=1, source_target_pairs={{0,1},{1,0},{2,3},{3,2},{4,5},{5,4},{6,7},{7,6},{8,9},{9,8},{10,11... | collective-permute-start | bytes 884744 | tf_op jit(solution)/shard_map/ppermute | solution.py:315
  21.3 15.0 %collective-permute-start.8 = (bf16[384,384]{1,0:T(8,128)(2,1)}, bf16[384,384]{1,0:T(8,128)(2,1)S(1)}, u32[]{:S(2)}, u32[]{:S(2)}) collective-permute-start(bf16[384,384]{1,0:T(8,128)(2,1)} %collective-permute-done.7.refs_2_), channel_id=1, source_target_pairs={{0,1},{1,0},{2,3},{3,2},{4,5},{5,4},{6,7},{7,6},{8,9},{9,8},{10,11... | collective-permute-start | bytes 884744 | tf_op jit(solution)/shard_map/ppermute | solution.py:315
  21.3 0.7 %copy-start.20 = (bf16[384,384]{1,0:T(8,128)(2,1)}, bf16[384,384]{1,0:T(8,128)(2,1)S(1)}, u32[]{:S(2)}) copy-start(bf16[384,384]{1,0:T(8,128)(2,1)S(1)} %collective-permute-done.refs_1_) | copy-start | bytes 884740
  22.0 1.7 %copy-start.1 = (bf16[768,1536]{1,0:T(8,128)(2,1)S(1)}, bf16[768,1536]{1,0:T(8,128)(2,1)}, u32[]{:S(2)}) copy-start(bf16[768,1536]{1,0:T(8,128)(2,1)} %refs_5_.3) | copy-start | bytes 7077892
  23.7 1.0 %copy-start.11 = (bf16[384,384]{1,0:T(8,128)(2,1)S(1)}, bf16[384,384]{1,0:T(8,128)(2,1)}, u32[]{:S(2)}) copy-start(bf16[384,384]{1,0:T(8,128)(2,1)} %copy-done.10) | copy-start | bytes 884740
  24.7 0.7 %copy-start.15 = (f32[1,1536]{1,0:T(1,128)S(1)}, f32[1,1536]{1,0:T(1,128)}, u32[]{:S(2)}) copy-start(f32[1,1536]{1,0:T(1,128)} %reshape.16.refs_7_) | copy-start | bytes 18436
  25.4 1.0 %copy-start.19 = (bf16[384,384]{1,0:T(8,128)(2,1)S(1)}, bf16[384,384]{1,0:T(8,128)(2,1)}, u32[]{:S(2)}) copy-start(bf16[384,384]{1,0:T(8,128)(2,1)} %copy-done.18) | copy-start | bytes 884740
  26.3 1.0 %copy-start.21 = (bf16[384,384]{1,0:T(8,128)(2,1)S(1)}, bf16[384,384]{1,0:T(8,128)(2,1)}, u32[]{:S(2)}) copy-start(bf16[384,384]{1,0:T(8,128)(2,1)} %copy-done.20) | copy-start | bytes 884740
  34.8 8.3 %copy-start.8 = (f32[384,128]{1,0:T(8,128)}, f32[384,128]{1,0:T(8,128)S(1)}, u32[]{:S(2)}) copy-start(f32[384,128]{1,0:T(8,128)S(1)} %get-tuple-element.11.refs_8_.stats_ref) | copy-start | bytes 589828
  35.8 9.8 %collective-permute-start.4 = (bf16[384,384]{1,0:T(8,128)(2,1)}, bf16[384,384]{1,0:T(8,128)(2,1)}, u32[]{:S(2)}, u32[]{:S(2)}) collective-permute-start(bf16[384,384]{1,0:T(8,128)(2,1)} %get-tuple-element.19), channel_id=1, source_target_pairs={{0,1},{1,0},{2,3},{3,2},{4,5},{5,4},{6,7},{7,6},{8,9},{9,8},{10,11... | collective-permute-start | bytes 884744 | tf_op jit(solution)/shard_map/ppermute | solution.py:315
  43.2 1.0 %copy-start.4 = (bf16[384,1536]{1,0:T(8,128)(2,1)}, bf16[384,1536]{1,0:T(8,128)(2,1)S(1)}, u32[]{:S(2)}) copy-start(bf16[384,1536]{1,0:T(8,128)(2,1)S(1)} %get-tuple-element.14) | copy-start | bytes 3538948
  43.2 1.8 %copy-start.13 = (f32[8,384]{1,0:T(8,128)}, f32[8,384]{1,0:T(8,128)S(1)}, u32[]{:S(2)}) copy-start(f32[8,384]{1,0:T(8,128)S(1)} %get-tuple-element.15) | copy-start | bytes 36868
  43.2 2.4 %copy-start.22 = (bf16[384,384]{1,0:T(8,128)(2,1)S(1)}, bf16[384,384]{1,0:T(8,128)(2,1)}, u32[]{:S(2)}) copy-start(bf16[384,384]{1,0:T(8,128)(2,1)} %get-tuple-element.20) | copy-start | bytes 884740
  45.0 11.6 %copy-start.5 = (bf16[384,384]{1,0:T(8,128)(2,1)S(1)}, bf16[384,384]{1,0:T(8,128)(2,1)}, u32[]{:S(2)}) copy-start(bf16[384,384]{1,0:T(8,128)(2,1)} %get-tuple-element.21.keep_ref) | copy-start | bytes 884740
  45.0 11.6 %copy-start.17 = (s32[4]{0:T(128)S(1)}, s32[4]{0:T(128)}, u32[]{:S(2)}) copy-start(s32[4]{0:T(128)} %count_ref.7) | copy-start | bytes 52
  45.0 4.9 %copy-start.14 = (f32[8,384]{1,0:T(8,128)S(1)}, f32[8,384]{1,0:T(8,128)}, u32[]{:S(2)}) copy-start(f32[8,384]{1,0:T(8,128)} %copy-done.13) | copy-start | bytes 36868
  45.0 3.5 %collective-permute-start.10 = (bf16[384,384]{1,0:T(8,128)(2,1)S(1)}, bf16[384,384]{1,0:T(8,128)(2,1)S(1)}, u32[]{:S(2)}, u32[]{:S(2)}) collective-permute-start(bf16[384,384]{1,0:T(8,128)(2,1)S(1)} %get-tuple-element.16), channel_id=1, source_target_pairs={{0,1},{1,0},{2,3},{3,2},{4,5},{5,4},{6,7},{7,6},{8,9},{9,8},{10,11... | collective-permute-start | bytes 884744 | tf_op jit(solution)/shard_map/ppermute | solution.py:315
  45.1 17.6 %collective-permute-start.9 = (bf16[384,384]{1,0:T(8,128)(2,1)}, bf16[384,384]{1,0:T(8,128)(2,1)}, u32[]{:S(2)}, u32[]{:S(2)}) collective-permute-start(bf16[384,384]{1,0:T(8,128)(2,1)} %get-tuple-element.17), channel_id=1, source_target_pairs={{0,1},{1,0},{2,3},{3,2},{4,5},{5,4},{6,7},{7,6},{8,9},{9,8},{10,11... | collective-permute-start | bytes 884744 | tf_op jit(solution)/shard_map/ppermute | solution.py:315
  45.6 7.2 %collective-permute-start.3 = (bf16[384,384]{1,0:T(8,128)(2,1)S(1)}, bf16[384,384]{1,0:T(8,128)(2,1)S(1)}, u32[]{:S(2)}, u32[]{:S(2)}) collective-permute-start(bf16[384,384]{1,0:T(8,128)(2,1)S(1)} %copy-done.22), channel_id=1, source_target_pairs={{0,1},{1,0},{2,3},{3,2},{4,5},{5,4},{6,7},{7,6},{8,9},{9,8},{10,11... | collective-permute-start | bytes 884744 | tf_op jit(solution)/shard_map/ppermute | solution.py:315
  46.7 9.9 %collective-permute-start.5 = (bf16[384,384]{1,0:T(8,128)(2,1)S(1)}, bf16[384,384]{1,0:T(8,128)(2,1)S(1)}, u32[]{:S(2)}, u32[]{:S(2)}) collective-permute-start(bf16[384,384]{1,0:T(8,128)(2,1)S(1)} %add_convert_fusion.1), channel_id=1, source_target_pairs={{0,2},{2,0},{1,3},{3,1},{4,6},{6,4},{5,7},{7,5},{8,10},{10,8},{9,1... | collective-permute-start | bytes 884744 | tf_op jit(solution)/shard_map/ppermute | solution.py:312
  49.5 13.2 %collective-permute-start.11 = (bf16[384,384]{1,0:T(8,128)(2,1)S(1)}, bf16[384,384]{1,0:T(8,128)(2,1)S(1)}, u32[]{:S(2)}, u32[]{:S(2)}) collective-permute-start(bf16[384,384]{1,0:T(8,128)(2,1)S(1)} %add_convert_fusion), channel_id=1, source_target_pairs={{0,2},{2,0},{1,3},{3,1},{4,6},{6,4},{5,7},{7,5},{8,10},{10,8},{9,1... | collective-permute-start | bytes 884744 | tf_op jit(solution)/shard_map/ppermute | solution.py:312
  49.9 1.2 %collective-permute-start.12 = (f32[8,384]{1,0:T(8,128)S(1)}, f32[8,384]{1,0:T(8,128)S(1)}, u32[]{:S(2)}, u32[]{:S(2)}) collective-permute-start(f32[8,384]{1,0:T(8,128)S(1)} %copy-done.14), channel_id=1, source_target_pairs={{0,1},{1,0},{2,3},{3,2},{4,5},{5,4},{6,7},{7,6},{8,9},{9,8},{10,11... | collective-permute-start | bytes 36872 | tf_op jit(solution)/shard_map/ppermute | solution.py:315
  51.1 11.6 %collective-permute-start.13 = (f32[8,384]{1,0:T(8,128)S(1)}, f32[8,384]{1,0:T(8,128)S(1)}, u32[]{:S(2)}, u32[]{:S(2)}) collective-permute-start(f32[8,384]{1,0:T(8,128)S(1)} %add.102.refs_1_), channel_id=1, source_target_pairs={{0,2},{2,0},{1,3},{3,1},{4,6},{6,4},{5,7},{7,5},{8,10},{10,8},{9,1... | collective-permute-start | bytes 36872 | tf_op jit(solution)/shard_map/ppermute | solution.py:312
  56.6 1.3 %copy-start.7 = (bf16[1536,384]{1,0:T(8,128)(2,1)S(1)}, bf16[1536,384]{1,0:T(8,128)(2,1)}, u32[]{:S(2)}) copy-start(bf16[1536,384]{1,0:T(8,128)(2,1)} %frames_ref.5) | copy-start | bytes 3538948
  57.9 4.8 %copy-start.3 = (bf16[1536,384]{1,0:T(8,128)(2,1)S(1)}, bf16[1536,384]{1,0:T(8,128)(2,1)}, u32[]{:S(2)}) copy-start(bf16[1536,384]{1,0:T(8,128)(2,1)} %frames_ref.7) | copy-start | bytes 3538948
  57.9 4.9 %copy-start.9 = (f32[384,128]{1,0:T(8,128)S(1)}, f32[384,128]{1,0:T(8,128)}, u32[]{:S(2)}) copy-start(f32[384,128]{1,0:T(8,128)} %copy-done.8) | copy-start | bytes 589828
  57.9 4.9 %copy-start.12 = (bf16[384,384]{1,0:T(8,128)(2,1)S(1)}, bf16[384,384]{1,0:T(8,128)(2,1)}, u32[]{:S(2)}) copy-start(bf16[384,384]{1,0:T(8,128)(2,1)} %copy-done.10) | copy-start | bytes 884740

commit v2 on v0

v2 whole, which is shorter than its diff:
```python
import functools

import jax
import jax.numpy as jnp
from jax import lax
from jax.experimental import pallas as pl
from jax.experimental.pallas import tpu as pltpu
from jax.sharding import PartitionSpec as P

EPS = 1e-05
F32 = jnp.float32
BF16 = jnp.bfloat16
VMEM = pltpu.VMEM
ANY = pl.BlockSpec(memory_space=pl.ANY)
OVER_ROWS = (((0,), (0,)), ((), ()))
OVER_LANES = (((1,), (1,)), ((), ()))


def vspec():
    return pl.BlockSpec(memory_space=VMEM)


def call(body, name, outs, ins, specs, scratch, flops, moved, limit):
    return pl.pallas_call(
        body,
        out_shape=outs,
        in_specs=specs,
        out_specs=jax.tree.map(lambda _: vspec(), outs),
        scratch_shapes=scratch,
        compiler_params=pltpu.CompilerParams(vmem_limit_bytes=limit * 1024 * 1024),
        cost_estimate=pl.CostEstimate(flops=flops, bytes_accessed=moved, transcendentals=0),
        name=name,
    )(*ins)


def chunks_of(extent):
    size = 512 if extent % 512 == 0 else extent
    return [(start, size) for start in range(0, extent, size)]


def wanted_slots(count_ref, picked_ref):
    slots = picked_ref.shape[1]
    live = lax.broadcasted_iota(jnp.int32, (8, slots), 1) < count_ref[lax.axis_index("tm")]
    wanted = jnp.where(live, jnp.broadcast_to(picked_ref[...], (8, slots)), -1)
    swapped = pltpu.roll(wanted, slots // 2, 1)
    return jnp.where(lax.axis_index("pair") == 0, wanted, swapped)[:1]


def onehot_rows(wanted, start, size):
    place = lax.broadcasted_iota(jnp.int32, (size, 1), 0) + start
    return jnp.where(wanted == place, 1.0, 0.0).astype(BF16)


def gather_body(count_ref, picked_ref, frames_hbm, mine_ref, sib_ref, frames_ref, sems):
    cuts = chunks_of(frames_ref.shape[0])
    copies = [
        pltpu.make_async_copy(frames_hbm.at[pl.ds(a, n)], frames_ref.at[pl.ds(a, n)], sems.at[i])
        for i, (a, n) in enumerate(cuts)
    ]
    for copy in copies:
        copy.start()
    wanted = wanted_slots(count_ref, picked_ref)
    total = None
    for copy, (a, n) in zip(copies, cuts):
        onehot = onehot_rows(wanted, a, n)
        copy.wait()
        part = lax.dot_general(onehot, frames_ref[a : a + n, :], OVER_ROWS, preferred_element_type=F32)
        total = part if total is None else total + part
    half = mine_ref.shape[0]
    mine_ref[...] = total[:half].astype(BF16)
    sib_ref[...] = total[half:].astype(BF16)


def gather_rows(count, picked, frames):
    slots, (frames_dev, width) = picked.shape[1], frames.shape
    out = jax.ShapeDtypeStruct((slots // 2, width), BF16)
    return call(
        gather_body,
        "gather_rows",
        (out, out),
        (count, picked, frames),
        [pl.BlockSpec(memory_space=pltpu.SMEM), vspec(), ANY],
        [VMEM(frames.shape, BF16), pltpu.SemaphoreType.DMA((len(chunks_of(frames_dev)),))],
        2 * slots * frames_dev * width,
        2 * frames_dev * width,
        10,
    )


def scatter_body(mines, sibs, count_ref, picked_ref, frames_hbm, *refs):
    parts, (out_hbm, frames_ref, out_ref, sems) = refs[: mines + sibs], refs[mines + sibs :]
    cuts = chunks_of(frames_ref.shape[0])
    loads = [
        pltpu.make_async_copy(frames_hbm.at[pl.ds(a, n)], frames_ref.at[pl.ds(a, n)], sems.at[0, i])
        for i, (a, n) in enumerate(cuts)
    ]
    stores = [
        pltpu.make_async_copy(out_ref.at[pl.ds(a, n)], out_hbm.at[pl.ds(a, n)], sems.at[1, i])
        for i, (a, n) in enumerate(cuts)
    ]
    for load in loads:
        load.start()
    wanted = wanted_slots(count_ref, picked_ref)

    def added(blocks):
        total = blocks[0][...].astype(F32)
        for block in blocks[1:]:
            total = total + block[...].astype(F32)
        return total.astype(BF16)

    rows = jnp.concatenate([added(parts[:mines]), added(parts[mines:])], axis=0)
    for load, store, (a, n) in zip(loads, stores, cuts):
        put = jnp.dot(onehot_rows(wanted, a, n), rows, preferred_element_type=F32)
        load.wait()
        out_ref[a : a + n, :] = (frames_ref[a : a + n, :].astype(F32) + put).astype(BF16)
        store.start()
    for store in stores:
        store.wait()


def scatter_rows(name, count, picked, frames, mine_parts, sib_parts):
    slots, (frames_dev, width) = picked.shape[1], frames.shape
    parts = list(mine_parts) + list(sib_parts)
    return pl.pallas_call(
        functools.partial(scatter_body, len(mine_parts), len(sib_parts)),
        out_shape=jax.ShapeDtypeStruct(frames.shape, BF16),
        in_specs=[pl.BlockSpec(memory_space=pltpu.SMEM), vspec(), ANY] + [vspec()] * len(parts),
        out_specs=ANY,
        scratch_shapes=[
            VMEM(frames.shape, BF16),
            VMEM(frames.shape, BF16),
            pltpu.SemaphoreType.DMA((2, len(chunks_of(frames_dev)))),
        ],
        compiler_params=pltpu.CompilerParams(vmem_limit_bytes=10 * 1024 * 1024),
        cost_estimate=pl.CostEstimate(
            flops=2 * slots * frames_dev * width, bytes_accessed=4 * frames_dev * width, transcendentals=0
        ),
        name=name,
    )(count, picked, frames, *parts)


def block_start(step, side, width):
    tensors = lax.axis_size("tensor")
    chip = (lax.axis_index("tensor") + tensors + step) % tensors
    return (chip * 2 + (lax.axis_index("pair") + side) % 2) * width


def assemble(full_ref, blocks, ways, width):
    if len(ways) == 1:
        full_ref[...] = blocks[0][...]
        return
    for (step, side), block in zip(ways, blocks):
        start = pl.multiple_of(block_start(-step, side, width), 128)
        full_ref[:, pl.ds(start, width)] = block[...]


def dissect(total_ref, outs, ways, width):
    if len(ways) == 1:
        outs[0][...] = total_ref[...]
        return
    for (step, side), out in zip(ways, outs):
        start = pl.multiple_of(block_start(step, side, width), 128)
        out[...] = total_ref[:, pl.ds(start, width)]


def forward_body(ways, width, *refs):
    n = len(ways)
    blocks = refs[:n]
    up_own, up_sib, down_own, down_sib, gain_ref, router_ref = refs[n : n + 6]
    outs = refs[n + 6 : 2 * n + 6]
    full_ref, stats_ref, hidden_ref, slope_ref = refs[2 * n + 6 : 2 * n + 10]
    up0, up1, down0, down1, total_ref, sems = refs[2 * n + 10 :]
    copies = [
        pltpu.make_async_copy(src, dst, sems.at[i])
        for i, (src, dst) in enumerate([(up_own, up0), (up_sib, up1), (down_own, down0), (down_sib, down1)])
    ]
    for copy in copies:
        copy.start()
    assemble(full_ref, blocks, ways, width)
    half, features = full_ref.shape
    hidden_dev = up0.shape[1]
    wide = full_ref[...].astype(F32)
    gate = jax.nn.sigmoid(jnp.sum(wide * router_ref[...], axis=1, keepdims=True))
    mean = jnp.sum(wide, axis=1, keepdims=True) * (1.0 / features)
    deviate = wide - mean
    inv = lax.rsqrt(jnp.sum(deviate * deviate, axis=1, keepdims=True) * (1.0 / features) + EPS)
    normed = (deviate * inv * gain_ref[...]).astype(BF16)
    lane = lax.broadcasted_iota(jnp.int32, (half, 128), 1)
    stats_ref[...] = jnp.where(lane == 0, mean, jnp.where(lane == 1, inv, gate))
    half_gate = 0.5 * gate
    for i, (copy, up) in enumerate(zip(copies[:2], (up0, up1))):
        copy.wait()
        value = jnp.dot(normed, up[...], preferred_element_type=F32)
        s = jax.nn.sigmoid(value)
        cols = slice(i * hidden_dev, (i + 1) * hidden_dev)
        hidden_ref[:, cols] = (value * s).astype(BF16)
        slope_ref[:, cols] = half_gate * s * (1.0 + value * (1.0 - s))
    copies[2].wait()
    total = jnp.dot(hidden_ref[:, :hidden_dev], down0[...], preferred_element_type=F32)
    copies[3].wait()
    total = total + jnp.dot(hidden_ref[:, hidden_dev:], down1[...], preferred_element_type=F32)
    total_ref[...] = (total * half_gate).astype(BF16)
    dissect(total_ref, outs, ways, width)


def forward(blocks, ways, weights, gain, router):
    half, width = blocks[0].shape
    features, hidden_dev = weights[0].shape
    piece = jax.ShapeDtypeStruct((half, width), BF16)
    got = call(
        functools.partial(forward_body, ways, width),
        "forward",
        (piece,) * len(ways)
        + (
            jax.ShapeDtypeStruct((half, features), BF16),
            jax.ShapeDtypeStruct((half, 128), F32),
            jax.ShapeDtypeStruct((half, 2 * hidden_dev), BF16),
            jax.ShapeDtypeStruct((half, 2 * hidden_dev), F32),
        ),
        (*blocks, *weights, gain, router),
        [vspec()] * len(blocks) + [ANY] * 4 + [vspec()] * 2,
        [VMEM(w.shape, BF16) for w in weights] + [VMEM((half, features), BF16), pltpu.SemaphoreType.DMA((4,))],
        8 * half * features * hidden_dev,
        8 * features * hidden_dev,
        28,
    )
    return got[: len(ways)], got[len(ways) :]


def backward_body(ways, width, *refs):
    n = len(ways)
    blocks = refs[:n]
    up_own, up_sib, down_own, down_sib, gain_ref, router_ref = refs[n : n + 6]
    full_ref, stats_ref, hidden_ref, slope_ref = refs[n + 6 : n + 10]
    outs = refs[n + 10 : 2 * n + 10]
    up0, up1, down0, down1, cot_ref, sems = refs[2 * n + 10 :]
    copies = [
        pltpu.make_async_copy(src, dst, sems.at[i])
        for i, (src, dst) in enumerate([(down_own, down0), (down_sib, down1), (up_own, up0), (up_sib, up1)])
    ]
    for copy in copies:
        copy.start()
    assemble(cot_ref, blocks, ways, width)
    half, features = full_ref.shape
    hidden_dev = up0.shape[1]
    score, pre = 0.0, []
    for i, (copy, down) in enumerate(zip(copies[:2], (down0, down1))):
        copy.wait()
        value = lax.dot_general(cot_ref[...], down[...], OVER_LANES, preferred_element_type=F32)
        cols = slice(i * hidden_dev, (i + 1) * hidden_dev)
        pre.append((value * slope_ref[:, cols]).astype(BF16))
        score = score + jnp.sum(value * hidden_ref[:, cols].astype(F32), axis=1, keepdims=True)
    copies[2].wait()
    scaled = lax.dot_general(pre[0], up0[...], OVER_LANES, preferred_element_type=F32)
    copies[3].wait()
    scaled = scaled + lax.dot_general(pre[1], up1[...], OVER_LANES, preferred_element_type=F32)
    scaled = scaled * gain_ref[...]
    mean, inv, gate = stats_ref[:, 0:1], stats_ref[:, 1:2], stats_ref[:, 2:3]
    centred = (full_ref[...].astype(F32) - mean) * inv
    plain = jnp.sum(scaled, axis=1, keepdims=True) * (1.0 / features)
    cross = jnp.sum(scaled * centred, axis=1, keepdims=True) * (1.0 / features)
    term = 0.5 * score * gate * (1.0 - gate)
    cot_ref[...] = (inv * (scaled - plain - centred * cross) + term * router_ref[...]).astype(BF16)
    dissect(cot_ref, outs, ways, width)


def backward(blocks, ways, weights, gain, router, saved):
    half, width = blocks[0].shape
    features, hidden_dev = weights[0].shape
    return call(
        functools.partial(backward_body, ways, width),
        "backward",
        (jax.ShapeDtypeStruct((half, width), BF16),) * len(ways),
        (*blocks, *weights, gain, router, *saved),
        [vspec()] * len(blocks) + [ANY] * 4 + [vspec()] * 6,
        [VMEM(w.shape, BF16) for w in weights] + [VMEM((half, features), BF16), pltpu.SemaphoreType.DMA((4,))],
        8 * half * features * hidden_dev,
        8 * features * hidden_dev,
        28,
    )


def after(value, *others):
    return lax.optimization_barrier((value, *others))[0]


def per_device(frames, router_weight, norm_gain, up_weight, down_weight, picked_rows, picked_count, cotangent):
    width = frames.shape[1]
    features = up_weight.shape[0]
    half = picked_rows.shape[0] // 2
    tensors = lax.axis_size("tensor")
    picked = picked_rows.reshape(1, -1)
    gain, router = norm_gain.reshape(1, -1), router_weight.reshape(1, -1)
    steps = range(1, tensors)
    aligned = width % 128 == 0
    pieces = [(0, 0), (0, 1)] + [(k, 0) for k in steps] + [(k, 1) for k in steps]
    ways = pieces if aligned else [(0, 0)]

    def shift(x, k):
        return lax.ppermute(x, "tensor", [(i, (i + k) % tensors) for i in range(tensors)])

    def swap(x):
        return lax.ppermute(x, "pair", [(0, 1), (1, 0)])

    def joined(blocks):
        if aligned:
            return blocks
        full = jnp.zeros((half, features), BF16)
        for (k, side), block in zip(pieces, blocks):
            full = lax.dynamic_update_slice_in_dim(full, block, block_start(-k, side, width), 1)
        return [full]

    def cut(outs):
        if aligned:
            return outs
        return [lax.dynamic_slice_in_dim(outs[0], block_start(k, side, width), width, 1) for k, side in pieces]

    def collect(mine, sib):
        far_sib = [shift(sib, k) for k in steps]
        far_mine = [shift(after(mine, sib), k) for k in steps]
        near = swap(sib)
        return [mine, near] + far_mine + [swap(x) for x in far_sib], far_sib

    def deliver(parts):
        count = tensors - 1
        far_mine = [shift(x, k) for x, k in zip(parts[2 : 2 + count], steps)]
        through = [swap(x) for x in parts[2 + count :]]
        far_sib = [shift(x, k) for x, k in zip(through, steps)]
        return [parts[0]] + far_mine, [swap(parts[1])] + far_sib

    up_sib, down_sib = swap(up_weight), swap(down_weight)
    weights = (up_weight, up_sib, down_weight, down_sib)
    mine, sib = gather_rows(picked_count, picked, frames)
    blocks, arrived = collect(mine, sib)
    cot_mine, cot_sib = gather_rows(picked_count, picked, cotangent)
    cot_sib = after(cot_sib, *arrived)
    cot_blocks, _ = collect(cot_mine, cot_sib)
    parts, saved = forward(joined(blocks), ways, weights, gain, router)
    out_mine, out_sib = deliver(cut(parts))
    grads = backward(joined(cot_blocks), ways, weights, gain, router, saved)
    grad_mine, grad_sib = deliver(cut(grads))
    mixed = scatter_rows("mixed_rows", picked_count, picked, frames, out_mine, out_sib)
    frames_grad = scatter_rows("grad_rows", picked_count, picked, cotangent, grad_mine, grad_sib)
    return (mixed, frames_grad)


def solution(mesh):
    return jax.shard_map(
        per_device,
        mesh=mesh,
        in_specs=(
            P(("group", "tm"), ("tensor", "pair")),
            P(),
            P(),
            P(None, ("tensor", "pair")),
            P(("tensor", "pair"), None),
            P(("group", "tm")),
            P("group"),
            P(("group", "tm"), ("tensor", "pair")),
        ),
        out_specs=(P(("group", "tm"), ("tensor", "pair")), P(("group", "tm"), ("tensor", "pair"))),
        check_vma=False,
    )
```

time: 220 us -> 52.6 us (0.24)
  waiting for transfers between devices: 67 us -> 13.2 us
  blocking collectives: 42.7 us -> 0 us
  other arithmetic: 42.5 us -> 0 us
  Pallas kernels: 0 us -> 21.3 us
  local copies, waits for them, and re-layouts: 25 us -> 5.58 us
  between operations: 16.3 us -> 0.81 us
  matrix products: 10.7 us -> 0 us
  starting transfers between devices: 14.7 us -> 11.6 us
    psum x1 -> x0, waiting for transfers between devices: 26.6 us -> none  [per_device(): lax.psum(normed_part.astype(jnp.bfloat16), ('tensor', 'pair'))]
    unnamed x3 -> x0, waiting for transfers between devices: 23.9 us -> none
    pallas_call x0 -> x6, Pallas kernels: none -> 21.3 us  [the longest x4 14.1 us: call(): pl.pallas_call(body, out_shape=outs, in_specs=specs, out_specs=jax.tree.m...]
    all_to_all x1 -> x0, blocking collectives: 20.4 us -> none  [per_device(): lax.all_to_all(sort_back(routed_out), 'tm', split_axis=0, concat_axis=0,...]
    all_to_all x3 -> x0, waiting for transfers between devices: 16.5 us -> none  [the longest x1 8.85 us: per_device(): lax.all_to_all(spread(rows_in), 'tm', split_axis=0, concat_axis=0, tiled=...]
    all_gather x2 -> x0, blocking collectives: 15.4 us -> none  [the longest x1 7.72 us: per_device(): full_in = lax.all_gather(mine_in, ('tensor', 'pair'), axis=1, tiled=True)]
    all_to_all x3 -> x0, starting transfers between devices: 14.6 us -> none  [the longest x1 6.32 us: per_device(): lax.all_to_all(spread(rows_in), 'tm', split_axis=0, concat_axis=0, tiled=...]
    ppermute x0 -> x18, waiting for transfers between devices: none -> 13.2 us  [the longest x8 12.7 us: shift(): lax.ppermute(x, 'tensor', [(i, (i + k) % tensors) for i in range(tensors)])]
  transfers between devices with their start and end apart: 5 -> 18, of which waited for: 5 -> 7; matrix products, arithmetic and copies ran while one was open for 14% -> 1% of each run, Pallas kernels for 0% -> 24%
where the time goes in v2:
time: 52.6 us; the launch traced here: 52.4 us
  Pallas kernels  21.3 us (40%)
  waiting for transfers between devices  13.2 us (25%)
  starting transfers between devices  11.6 us (22%)
  local copies, waits for them, and re-layouts  5.58 us (11%)
  between operations  0.81 us (2%)
    pallas_call x4, Pallas kernels, call(): pl.pallas_call(body, out_shape=outs, in_specs=specs, out_specs=jax.tree.m...  14.1 us
    ppermute x8, waiting for transfers between devices, shift(): lax.ppermute(x, 'tensor', [(i, (i + k) % tensors) for i in range(tensors)])  12.7 us
    ppermute x8, starting transfers between devices, shift(): lax.ppermute(x, 'tensor', [(i, (i + k) % tensors) for i in range(tensors)])  9.57 us
    pallas_call x2, Pallas kernels, scatter_rows(): pl.pallas_call(functools.partial(scatter_body, len(mine_parts), len(sib_p...  7.18 us
    unnamed x22, local copies, waits for them, and re-layouts  4.89 us
    ppermute x10, starting transfers between devices, swap(): return lax.ppermute(x, 'pair', [(0, 1), (1, 0)])  1.98 us
  transfers between devices with their start and end apart: 18, of which 7 were waited for; matrix products, arithmetic and copies ran while one was open for 1% of the time, Pallas kernels for 24%

profile of v2, /device:TPU:0, one launch (start us, length us, event | category | flops | bytes accessed | tf_op | source)
XLA Modules:
  0.0 52.4 jit_solution(3862214784386788844)
XLA Ops:
  0.6 0.5 collective-permute-start.4
  1.1 0.1 collective-permute-start.5
  1.2 0.7 %reshape.13.picked_ref = s32[1,384]{1,0:T(1,128)S(1)} reshape(s32[384]{0:T(512)} %param.13) | data formatting | bytes 3072 | tf_op jit(solution)/shard_map/reshape | solution.py:292
  1.9 0.0 copy-start.5
  1.9 1.3 %copy-done.5 = bf16[1536,384]{1,0:T(8,128)(2,1)S(1)} copy-done((bf16[1536,384]{1,0:T(8,128)(2,1)S(1)}, bf16[1536,384]{1,0:T(8,128)(2,1)}, u32[]{:S(2)}) %copy-start.5) | copy-done | bytes 1179672
  3.2 0.0 copy-start.7
  3.2 0.7 %copy-done.7 = s32[4]{0:T(128)S(1)} copy-done((s32[4]{0:T(128)S(1)}, s32[4]{0:T(128)}, u32[]{:S(2)}) %copy-start.7) | copy-done | bytes 40
  3.8 0.0 copy-start
  3.8 2.4 %gather_rows.2 = (bf16[192,384]{1,0:T(8,128)(2,1)S(1)}, bf16[192,384]{1,0:T(8,128)(2,1)S(1)}) custom-call(s32[4]{0:T(128)S(1)} %copy-done.7, s32[1,384]{1,0:T(1,128)S(1)} %reshape.13.picked_ref, bf16[1536,384]{1,0:T(8,128)(2,1)S(1)} %copy-done.5), custom_call_target="tpu_custom_call" | custom-call | flops 452984832 | bytes 1179648 | tf_op jit(solution)/shard_map/gather_rows/pallas_call | solution.py:24
  6.3 3.0 %collective-permute-start.2 = (bf16[192,384]{1,0:T(8,128)(2,1)S(1)}, bf16[192,384]{1,0:T(8,128)(2,1)S(1)}, u32[]{:S(2)}, u32[]{:S(2)}) collective-permute-start(bf16[192,384]{1,0:T(8,128)(2,1)S(1)} %get-tuple-element.22), channel_id=1, source_target_pairs={{0,2},{2,0},{1,3},{3,1},{4,6},{6,4},{5,7},{7,5},{8,10},{10,8},{9,1... | collective-permute-start | bytes 442376 | tf_op jit(solution)/shard_map/ppermute | solution.py:300
  9.2 0.1 collective-permute-start.1
  9.3 0.0 collective-permute-start
  9.3 0.0 copy-start.3
  9.3 1.3 %copy-done.3 = bf16[1536,384]{1,0:T(8,128)(2,1)S(1)} copy-done((bf16[1536,384]{1,0:T(8,128)(2,1)S(1)}, bf16[1536,384]{1,0:T(8,128)(2,1)}, u32[]{:S(2)}) %copy-start.3) | copy-done | bytes 1179672
  10.6 0.0 copy-start.9
  10.6 0.0 copy-start.10
  10.6 2.4 %gather_rows.3 = (bf16[192,384]{1,0:T(8,128)(2,1)S(1)}, bf16[192,384]{1,0:T(8,128)(2,1)S(1)}) custom-call(s32[4]{0:T(128)S(1)} %copy-done.7, s32[1,384]{1,0:T(1,128)S(1)} %reshape.13.picked_ref, bf16[1536,384]{1,0:T(8,128)(2,1)S(1)} %copy-done.3), custom_call_target="tpu_custom_call" | custom-call | flops 452984832 | bytes 1179648 | tf_op jit(solution)/shard_map/gather_rows/pallas_call | solution.py:24
  13.0 0.9 %collective-permute-done.2 = bf16[192,384]{1,0:T(8,128)(2,1)S(1)} collective-permute-done((bf16[192,384]{1,0:T(8,128)(2,1)S(1)}, bf16[192,384]{1,0:T(8,128)(2,1)S(1)}, u32[]{:S(2)}, u32[]{:S(2)}) %collective-permute-start.2) | collective-permute-done | bytes 147488 | tf_op jit(solution)/shard_map/ppermute | solution.py:300
  13.9 2.1 %collective-permute-start.12 = (bf16[192,384]{1,0:T(8,128)(2,1)S(1)}, bf16[192,384]{1,0:T(8,128)(2,1)S(1)}, u32[]{:S(2)}, u32[]{:S(2)}) collective-permute-start(bf16[192,384]{1,0:T(8,128)(2,1)S(1)} %get-tuple-element.29), channel_id=1, source_target_pairs={{0,2},{2,0},{1,3},{3,1},{4,6},{6,4},{5,7},{7,5},{8,10},{10,8},{9,1... | collective-permute-start | bytes 442376 | tf_op jit(solution)/shard_map/ppermute | solution.py:300
  15.9 0.6 %collective-permute-done.1.refs_2_ = bf16[192,384]{1,0:T(8,128)(2,1)S(1)} collective-permute-done((bf16[192,384]{1,0:T(8,128)(2,1)S(1)}, bf16[192,384]{1,0:T(8,128)(2,1)S(1)}, u32[]{:S(2)}, u32[]{:S(2)}) %collective-permute-start.1) | collective-permute-done | bytes 147488 | tf_op jit(solution)/shard_map/ppermute | solution.py:300
  16.5 0.0 collective-permute-start.3
  16.5 0.0 copy-done.9
  16.5 0.0 copy-done.10
  16.6 0.0 collective-permute-done.refs_1_
  16.6 0.6 %collective-permute-start.10 = (bf16[192,384]{1,0:T(8,128)(2,1)S(1)}, bf16[192,384]{1,0:T(8,128)(2,1)S(1)}, u32[]{:S(2)}, u32[]{:S(2)}) collective-permute-start(bf16[192,384]{1,0:T(8,128)(2,1)S(1)} %get-tuple-element.29), channel_id=1, source_target_pairs={{0,1},{1,0},{2,3},{3,2},{4,5},{5,4},{6,7},{7,6},{8,9},{9,8},{10,11... | collective-permute-start | bytes 442376 | tf_op jit(solution)/shard_map/ppermute | solution.py:303
  17.1 2.5 %collective-permute-done.12 = bf16[192,384]{1,0:T(8,128)(2,1)S(1)} collective-permute-done((bf16[192,384]{1,0:T(8,128)(2,1)S(1)}, bf16[192,384]{1,0:T(8,128)(2,1)S(1)}, u32[]{:S(2)}, u32[]{:S(2)}) %collective-permute-start.12) | collective-permute-done | bytes 147488 | tf_op jit(solution)/shard_map/ppermute | solution.py:300
  19.7 1.7 %collective-permute-start.11 = (bf16[192,384]{1,0:T(8,128)(2,1)S(1)}, bf16[192,384]{1,0:T(8,128)(2,1)S(1)}, u32[]{:S(2)}, u32[]{:S(2)}) collective-permute-start(bf16[192,384]{1,0:T(8,128)(2,1)S(1)} %get-tuple-element.27.refs_0_), channel_id=1, source_target_pairs={{0,2},{2,0},{1,3},{3,1},{4,6},{6,4},{5,7},{7,5},{8,10},{10,8},{9,1... | collective-permute-start | bytes 442376 | tf_op jit(solution)/shard_map/ppermute | solution.py:300
  21.4 0.0 collective-permute-done.3.refs_3_
  21.4 0.0 collective-permute-start.13
  21.4 0.0 collective-permute-done.4.refs_5_
  21.4 0.0 collective-permute-done.5.refs_7_
  21.4 0.0 copy-done
  21.4 0.0 copy-start.1
  21.4 1.7 %copy-done.1 = bf16[768,1536]{1,0:T(8,128)(2,1)S(1)} copy-done((bf16[768,1536]{1,0:T(8,128)(2,1)S(1)}, bf16[768,1536]{1,0:T(8,128)(2,1)}, u32[]{:S(2)}) %copy-start.1) | copy-done | bytes 2359320
  23.1 0.0 copy-start.2
  23.1 4.1 %forward.1 = (bf16[192,384]{1,0:T(8,128)(2,1)S(1)}, bf16[192,384]{1,0:T(8,128)(2,1)S(1)}, bf16[192,384]{1,0:T(8,128)(2,1)S(1)}, bf16[192,384]{1,0:T(8,128)(2,1)S...) custom-call(bf16[192,384]{1,0:T(8,128)(2,1)S(1)} %get-tuple-element., ...), custom_call_target="tpu_custom_call" | custom-call | flops 1811939328 | bytes 9437184 | tf_op jit(solution)/shard_map/forward/pallas_call | solution.py:24
  27.2 0.0 collective-permute-done.11.refs_2_
  27.2 0.0 collective-permute-done.10.refs_1_
  27.2 0.0 collective-permute-done.13.refs_3_
  27.2 0.0 copy-done.2
  27.2 0.0 copy-start.4
  27.2 0.0 copy-start.8
  27.3 5.2 %backward.1 = (bf16[192,384]{1,0:T(8,128)(2,1)S(1)}, bf16[192,384]{1,0:T(8,128)(2,1)S(1)}, bf16[192,384]{1,0:T(8,128)(2,1)S(1)}, bf16[192,384]{1,0:T(8,128)(2,1)S(1)}) custom-call(bf16[192,384]{1,0:T(8,128)(2,1)S(1)} %get-tuple-element.27.refs_0_, bf16[192,384]{1,0:T(8,128)(2,1)S(1)} %collective-permute-done.10.refs_1_, ...), custom_call_target="tpu_custom_call" | custom-call | flops 1811939328 | bytes 9437184 | tf_op jit(solution)/shard_map/backward/pallas_call | solution.py:24
  32.5 0.6 %collective-permute-start.16 = (bf16[192,384]{1,0:T(8,128)(2,1)S(1)}, bf16[192,384]{1,0:T(8,128)(2,1)S(1)}, u32[]{:S(2)}, u32[]{:S(2)}) collective-permute-start(bf16[192,384]{1,0:T(8,128)(2,1)S(1)} %get-tuple-element.38), channel_id=1, source_target_pairs={{0,1},{1,0},{2,3},{3,2},{4,5},{5,4},{6,7},{7,6},{8,9},{9,8},{10,11... | collective-permute-start | bytes 442376 | tf_op jit(solution)/shard_map/ppermute | solution.py:303
  33.0 0.1 collective-permute-start.8
  33.1 0.3 collective-permute-start.14
  33.5 0.2 collective-permute-start.15
  33.6 0.4 collective-permute-done.16
  34.0 1.3 %collective-permute-start.17 = (bf16[192,384]{1,0:T(8,128)(2,1)S(1)}, bf16[192,384]{1,0:T(8,128)(2,1)S(1)}, u32[]{:S(2)}, u32[]{:S(2)}) collective-permute-start(bf16[192,384]{1,0:T(8,128)(2,1)S(1)} %collective-permute-done.16), channel_id=1, source_target_pairs={{0,2},{2,0},{1,3},{3,1},{4,6},{6,4},{5,7},{7,5},{8,10},{10,8},{9,1... | collective-permute-start | bytes 442376 | tf_op jit(solution)/shard_map/ppermute | solution.py:300
  35.3 0.8 %collective-permute-start.6 = (bf16[192,384]{1,0:T(8,128)(2,1)S(1)}, bf16[192,384]{1,0:T(8,128)(2,1)S(1)}, u32[]{:S(2)}, u32[]{:S(2)}) collective-permute-start(bf16[192,384]{1,0:T(8,128)(2,1)S(1)} %get-tuple-element.24), channel_id=1, source_target_pairs={{0,2},{2,0},{1,3},{3,1},{4,6},{6,4},{5,7},{7,5},{8,10},{10,8},{9,1... | collective-permute-start | bytes 442376 | tf_op jit(solution)/shard_map/ppermute | solution.py:300
  36.1 0.0 collective-permute-done.8
  36.1 0.0 collective-permute-start.7
  36.1 3.7 %collective-permute-done.14.refs_1_ = bf16[192,384]{1,0:T(8,128)(2,1)S(1)} collective-permute-done((bf16[192,384]{1,0:T(8,128)(2,1)S(1)}, bf16[192,384]{1,0:T(8,128)(2,1)S(1)}, u32[]{:S(2)}, u32[]{:S(2)}) %collective-permute-start.14) | collective-permute-done | bytes 147488 | tf_op jit(solution)/shard_map/ppermute | solution.py:300
  39.8 0.3 collective-permute-start.9
  40.1 0.0 collective-permute-done.15.refs_2_
  40.1 2.8 %collective-permute-done.17.refs_3_ = bf16[192,384]{1,0:T(8,128)(2,1)S(1)} collective-permute-done((bf16[192,384]{1,0:T(8,128)(2,1)S(1)}, bf16[192,384]{1,0:T(8,128)(2,1)S(1)}, u32[]{:S(2)}, u32[]{:S(2)}) %collective-permute-start.17) | collective-permute-done | bytes 147488 | tf_op jit(solution)/shard_map/ppermute | solution.py:300
  42.9 0.0 copy-done.4
  42.9 0.0 copy-done.8
  42.9 3.6 %grad_rows.1 = bf16[1536,384]{1,0:T(8,128)(2,1)} custom-call(s32[4]{0:T(128)S(1)} %copy-done.8, s32[1,384]{1,0:T(1,128)S(1)} %reshape.13.picked_ref, bf16[1536,384]{1,0:T(8,128)(2,1)S(1)} %copy-done.4, bf16[192,384]{1,0:T(8,128)(2,1)S(1)} %get-tuple-element.35.refs_0_, bf16[192,384]{1,0:T(8,128)(2,1)S(1)} %collective-permute-done.14.refs_1_, ...), custom_call_target="tpu_custom_call" | custom-call | flops 452984832 | bytes 2359296 | tf_op jit(solution)/shard_map/grad_rows/pallas_call | solution.py:124
  46.5 0.0 collective-permute-done.6.refs_1_
  46.5 0.0 collective-permute-done.7.refs_2_
  46.6 2.2 %collective-permute-done.9.refs_3_ = bf16[192,384]{1,0:T(8,128)(2,1)S(1)} collective-permute-done((bf16[192,384]{1,0:T(8,128)(2,1)S(1)}, bf16[192,384]{1,0:T(8,128)(2,1)S(1)}, u32[]{:S(2)}, u32[]{:S(2)}) %collective-permute-start.9) | collective-permute-done | bytes 147488 | tf_op jit(solution)/shard_map/ppermute | solution.py:300
  48.8 0.0 copy-done.6
  48.8 3.6 %mixed_rows.1 = bf16[1536,384]{1,0:T(8,128)(2,1)} custom-call(s32[4]{0:T(128)S(1)} %copy-done.8, s32[1,384]{1,0:T(1,128)S(1)} %reshape.13.picked_ref, bf16[1536,384]{1,0:T(8,128)(2,1)S(1)} %copy-done.6, bf16[192,384]{1,0:T(8,128)(2,1)S(1)} %get-tuple-element.23.refs_0_, bf16[192,384]{1,0:T(8,128)(2,1)S(1)} %collective-permute-done.6.refs_1_, ...), custom_call_target="tpu_custom_call" | custom-call | flops 452984832 | bytes 2359296 | tf_op jit(solution)/shard_map/mixed_rows/pallas_call | solution.py:124
  (3 shorter events, 0.0 us)
Async XLA Ops:
  0.6 20.8 %collective-permute-start.4 = (bf16[1536,768]{1,0:T(8,128)(2,1)}, bf16[1536,768]{1,0:T(8,128)(2,1)S(1)}, u32[]{:S(2)}, u32[]{:S(2)}) collective-permute-start(bf16[1536,768]{1,0:T(8,128)(2,1)} %refs_4_.3), channel_id=1, source_target_pairs={{0,1},{1,0},{2,3},{3,2},{4,5},{5,4},{6,7},{7,6},{8,9},{9,8},{10,11... | collective-permute-start | bytes 7077896 | tf_op jit(solution)/shard_map/ppermute | solution.py:303
  1.1 20.3 %collective-permute-start.5 = (bf16[768,1536]{1,0:T(8,128)(2,1)}, bf16[768,1536]{1,0:T(8,128)(2,1)S(1)}, u32[]{:S(2)}, u32[]{:S(2)}) collective-permute-start(bf16[768,1536]{1,0:T(8,128)(2,1)} %refs_6_.3), channel_id=1, source_target_pairs={{0,1},{1,0},{2,3},{3,2},{4,5},{5,4},{6,7},{7,6},{8,9},{9,8},{10,11... | collective-permute-start | bytes 7077896 | tf_op jit(solution)/shard_map/ppermute | solution.py:303
  1.9 1.3 %copy-start.5 = (bf16[1536,384]{1,0:T(8,128)(2,1)S(1)}, bf16[1536,384]{1,0:T(8,128)(2,1)}, u32[]{:S(2)}) copy-start(bf16[1536,384]{1,0:T(8,128)(2,1)} %frames_hbm.5) | copy-start | bytes 3538948
  3.2 0.7 %copy-start.7 = (s32[4]{0:T(128)S(1)}, s32[4]{0:T(128)}, u32[]{:S(2)}) copy-start(s32[4]{0:T(128)} %count_ref.7) | copy-start | bytes 52
  3.8 17.6 %copy-start = (bf16[1536,768]{1,0:T(8,128)(2,1)S(1)}, bf16[1536,768]{1,0:T(8,128)(2,1)}, u32[]{:S(2)}) copy-start(bf16[1536,768]{1,0:T(8,128)(2,1)} %refs_4_.3) | copy-start | bytes 7077892
  6.3 7.6 %collective-permute-start.2 = (bf16[192,384]{1,0:T(8,128)(2,1)S(1)}, bf16[192,384]{1,0:T(8,128)(2,1)S(1)}, u32[]{:S(2)}, u32[]{:S(2)}) collective-permute-start(bf16[192,384]{1,0:T(8,128)(2,1)S(1)} %get-tuple-element.22), channel_id=1, source_target_pairs={{0,2},{2,0},{1,3},{3,1},{4,6},{6,4},{5,7},{7,5},{8,10},{10,8},{9,1... | collective-permute-start | bytes 442376 | tf_op jit(solution)/shard_map/ppermute | solution.py:300
  9.2 7.3 %collective-permute-start.1 = (bf16[192,384]{1,0:T(8,128)(2,1)S(1)}, bf16[192,384]{1,0:T(8,128)(2,1)S(1)}, u32[]{:S(2)}, u32[]{:S(2)}) collective-permute-start(bf16[192,384]{1,0:T(8,128)(2,1)S(1)} %get-tuple-element.21.refs_0_), channel_id=1, source_target_pairs={{0,2},{2,0},{1,3},{3,1},{4,6},{6,4},{5,7},{7,5},{8,10},{10,8},{9,1... | collective-permute-start | bytes 442376 | tf_op jit(solution)/shard_map/ppermute | solution.py:300
  9.3 7.2 %collective-permute-start = (bf16[192,384]{1,0:T(8,128)(2,1)S(1)}, bf16[192,384]{1,0:T(8,128)(2,1)S(1)}, u32[]{:S(2)}, u32[]{:S(2)}) collective-permute-start(bf16[192,384]{1,0:T(8,128)(2,1)S(1)} %get-tuple-element.22), channel_id=1, source_target_pairs={{0,1},{1,0},{2,3},{3,2},{4,5},{5,4},{6,7},{7,6},{8,9},{9,8},{10,11... | collective-permute-start | bytes 442376 | tf_op jit(solution)/shard_map/ppermute | solution.py:303
  9.3 1.3 %copy-start.3 = (bf16[1536,384]{1,0:T(8,128)(2,1)S(1)}, bf16[1536,384]{1,0:T(8,128)(2,1)}, u32[]{:S(2)}) copy-start(bf16[1536,384]{1,0:T(8,128)(2,1)} %frames_hbm.7) | copy-start | bytes 3538948
  10.6 5.9 %copy-start.9 = (f32[1536]{0:T(1024)S(1)}, f32[1536]{0:T(1024)}, u32[]{:S(2)}) copy-start(f32[1536]{0:T(1024)} %param.9) | copy-start | bytes 18436
  10.6 5.9 %copy-start.10 = (f32[1536]{0:T(1024)S(1)}, f32[1536]{0:T(1024)}, u32[]{:S(2)}) copy-start(f32[1536]{0:T(1024)} %param.10) | copy-start | bytes 18436
  13.9 5.8 %collective-permute-start.12 = (bf16[192,384]{1,0:T(8,128)(2,1)S(1)}, bf16[192,384]{1,0:T(8,128)(2,1)S(1)}, u32[]{:S(2)}, u32[]{:S(2)}) collective-permute-start(bf16[192,384]{1,0:T(8,128)(2,1)S(1)} %get-tuple-element.29), channel_id=1, source_target_pairs={{0,2},{2,0},{1,3},{3,1},{4,6},{6,4},{5,7},{7,5},{8,10},{10,8},{9,1... | collective-permute-start | bytes 442376 | tf_op jit(solution)/shard_map/ppermute | solution.py:300
  16.5 4.9 %collective-permute-start.3 = (bf16[192,384]{1,0:T(8,128)(2,1)S(1)}, bf16[192,384]{1,0:T(8,128)(2,1)S(1)}, u32[]{:S(2)}, u32[]{:S(2)}) collective-permute-start(bf16[192,384]{1,0:T(8,128)(2,1)S(1)} %collective-permute-done.2), channel_id=1, source_target_pairs={{0,1},{1,0},{2,3},{3,2},{4,5},{5,4},{6,7},{7,6},{8,9},{9,8},{10,11... | collective-permute-start | bytes 442376 | tf_op jit(solution)/shard_map/ppermute | solution.py:303
  16.6 10.6 %collective-permute-start.10 = (bf16[192,384]{1,0:T(8,128)(2,1)S(1)}, bf16[192,384]{1,0:T(8,128)(2,1)S(1)}, u32[]{:S(2)}, u32[]{:S(2)}) collective-permute-start(bf16[192,384]{1,0:T(8,128)(2,1)S(1)} %get-tuple-element.29), channel_id=1, source_target_pairs={{0,1},{1,0},{2,3},{3,2},{4,5},{5,4},{6,7},{7,6},{8,9},{9,8},{10,11... | collective-permute-start | bytes 442376 | tf_op jit(solution)/shard_map/ppermute | solution.py:303
  19.7 7.5 %collective-permute-start.11 = (bf16[192,384]{1,0:T(8,128)(2,1)S(1)}, bf16[192,384]{1,0:T(8,128)(2,1)S(1)}, u32[]{:S(2)}, u32[]{:S(2)}) collective-permute-start(bf16[192,384]{1,0:T(8,128)(2,1)S(1)} %get-tuple-element.27.refs_0_), channel_id=1, source_target_pairs={{0,2},{2,0},{1,3},{3,1},{4,6},{6,4},{5,7},{7,5},{8,10},{10,8},{9,1... | collective-permute-start | bytes 442376 | tf_op jit(solution)/shard_map/ppermute | solution.py:300
  21.4 5.8 %collective-permute-start.13 = (bf16[192,384]{1,0:T(8,128)(2,1)S(1)}, bf16[192,384]{1,0:T(8,128)(2,1)S(1)}, u32[]{:S(2)}, u32[]{:S(2)}) collective-permute-start(bf16[192,384]{1,0:T(8,128)(2,1)S(1)} %collective-permute-done.12), channel_id=1, source_target_pairs={{0,1},{1,0},{2,3},{3,2},{4,5},{5,4},{6,7},{7,6},{8,9},{9,8},{10,11... | collective-permute-start | bytes 442376 | tf_op jit(solution)/shard_map/ppermute | solution.py:303
  21.4 1.7 %copy-start.1 = (bf16[768,1536]{1,0:T(8,128)(2,1)S(1)}, bf16[768,1536]{1,0:T(8,128)(2,1)}, u32[]{:S(2)}) copy-start(bf16[768,1536]{1,0:T(8,128)(2,1)} %refs_6_.3) | copy-start | bytes 7077892
  23.1 4.1 %copy-start.2 = (bf16[768,1536]{1,0:T(8,128)(2,1)S(1)}, bf16[768,1536]{1,0:T(8,128)(2,1)}, u32[]{:S(2)}) copy-start(bf16[768,1536]{1,0:T(8,128)(2,1)} %refs_6_.3) | copy-start | bytes 7077892
  27.2 15.7 %copy-start.4 = (bf16[1536,384]{1,0:T(8,128)(2,1)S(1)}, bf16[1536,384]{1,0:T(8,128)(2,1)}, u32[]{:S(2)}) copy-start(bf16[1536,384]{1,0:T(8,128)(2,1)} %frames_hbm.7) | copy-start | bytes 3538948
  27.2 15.7 %copy-start.8 = (s32[4]{0:T(128)S(1)}, s32[4]{0:T(128)}, u32[]{:S(2)}) copy-start(s32[4]{0:T(128)} %count_ref.7) | copy-start | bytes 52
  32.5 1.6 %collective-permute-start.16 = (bf16[192,384]{1,0:T(8,128)(2,1)S(1)}, bf16[192,384]{1,0:T(8,128)(2,1)S(1)}, u32[]{:S(2)}, u32[]{:S(2)}) collective-permute-start(bf16[192,384]{1,0:T(8,128)(2,1)S(1)} %get-tuple-element.38), channel_id=1, source_target_pairs={{0,1},{1,0},{2,3},{3,2},{4,5},{5,4},{6,7},{7,6},{8,9},{9,8},{10,11... | collective-permute-start | bytes 442376 | tf_op jit(solution)/shard_map/ppermute | solution.py:303
  33.0 3.1 %collective-permute-start.8 = (bf16[192,384]{1,0:T(8,128)(2,1)S(1)}, bf16[192,384]{1,0:T(8,128)(2,1)S(1)}, u32[]{:S(2)}, u32[]{:S(2)}) collective-permute-start(bf16[192,384]{1,0:T(8,128)(2,1)S(1)} %get-tuple-element.26), channel_id=1, source_target_pairs={{0,1},{1,0},{2,3},{3,2},{4,5},{5,4},{6,7},{7,6},{8,9},{9,8},{10,11... | collective-permute-start | bytes 442376 | tf_op jit(solution)/shard_map/ppermute | solution.py:303
  33.1 6.6 %collective-permute-start.14 = (bf16[192,384]{1,0:T(8,128)(2,1)S(1)}, bf16[192,384]{1,0:T(8,128)(2,1)S(1)}, u32[]{:S(2)}, u32[]{:S(2)}) collective-permute-start(bf16[192,384]{1,0:T(8,128)(2,1)S(1)} %get-tuple-element.36), channel_id=1, source_target_pairs={{0,2},{2,0},{1,3},{3,1},{4,6},{6,4},{5,7},{7,5},{8,10},{10,8},{9,1... | collective-permute-start | bytes 442376 | tf_op jit(solution)/shard_map/ppermute | solution.py:300
  33.5 6.7 %collective-permute-start.15 = (bf16[192,384]{1,0:T(8,128)(2,1)S(1)}, bf16[192,384]{1,0:T(8,128)(2,1)S(1)}, u32[]{:S(2)}, u32[]{:S(2)}) collective-permute-start(bf16[192,384]{1,0:T(8,128)(2,1)S(1)} %get-tuple-element.37), channel_id=1, source_target_pairs={{0,1},{1,0},{2,3},{3,2},{4,5},{5,4},{6,7},{7,6},{8,9},{9,8},{10,11... | collective-permute-start | bytes 442376 | tf_op jit(solution)/shard_map/ppermute | solution.py:303
  34.0 8.9 %collective-permute-start.17 = (bf16[192,384]{1,0:T(8,128)(2,1)S(1)}, bf16[192,384]{1,0:T(8,128)(2,1)S(1)}, u32[]{:S(2)}, u32[]{:S(2)}) collective-permute-start(bf16[192,384]{1,0:T(8,128)(2,1)S(1)} %collective-permute-done.16), channel_id=1, source_target_pairs={{0,2},{2,0},{1,3},{3,1},{4,6},{6,4},{5,7},{7,5},{8,10},{10,8},{9,1... | collective-permute-start | bytes 442376 | tf_op jit(solution)/shard_map/ppermute | solution.py:300
  35.3 11.2 %collective-permute-start.6 = (bf16[192,384]{1,0:T(8,128)(2,1)S(1)}, bf16[192,384]{1,0:T(8,128)(2,1)S(1)}, u32[]{:S(2)}, u32[]{:S(2)}) collective-permute-start(bf16[192,384]{1,0:T(8,128)(2,1)S(1)} %get-tuple-element.24), channel_id=1, source_target_pairs={{0,2},{2,0},{1,3},{3,1},{4,6},{6,4},{5,7},{7,5},{8,10},{10,8},{9,1... | collective-permute-start | bytes 442376 | tf_op jit(solution)/shard_map/ppermute | solution.py:300
  36.1 10.5 %collective-permute-start.7 = (bf16[192,384]{1,0:T(8,128)(2,1)S(1)}, bf16[192,384]{1,0:T(8,128)(2,1)S(1)}, u32[]{:S(2)}, u32[]{:S(2)}) collective-permute-start(bf16[192,384]{1,0:T(8,128)(2,1)S(1)} %get-tuple-element.25), channel_id=1, source_target_pairs={{0,1},{1,0},{2,3},{3,2},{4,5},{5,4},{6,7},{7,6},{8,9},{9,8},{10,11... | collective-permute-start | bytes 442376 | tf_op jit(solution)/shard_map/ppermute | solution.py:303
  39.8 9.0 %collective-permute-start.9 = (bf16[192,384]{1,0:T(8,128)(2,1)S(1)}, bf16[192,384]{1,0:T(8,128)(2,1)S(1)}, u32[]{:S(2)}, u32[]{:S(2)}) collective-permute-start(bf16[192,384]{1,0:T(8,128)(2,1)S(1)} %collective-permute-done.8), channel_id=1, source_target_pairs={{0,2},{2,0},{1,3},{3,1},{4,6},{6,4},{5,7},{7,5},{8,10},{10,8},{9,1... | collective-permute-start | bytes 442376 | tf_op jit(solution)/shard_map/ppermute | solution.py:300
  42.9 5.9 %copy-start.6 = (bf16[1536,384]{1,0:T(8,128)(2,1)S(1)}, bf16[1536,384]{1,0:T(8,128)(2,1)}, u32[]{:S(2)}) copy-start(bf16[1536,384]{1,0:T(8,128)(2,1)} %frames_hbm.5) | copy-start | bytes 3538948

commit v3 on v2

v3 whole, which is shorter than its diff:
```python
import functools

import jax
import jax.numpy as jnp
from jax import lax
from jax.experimental import pallas as pl
from jax.experimental.pallas import tpu as pltpu
from jax.sharding import PartitionSpec as P

EPS = 1e-05
F32 = jnp.float32
BF16 = jnp.bfloat16
VMEM = pltpu.VMEM
ANY = pl.BlockSpec(memory_space=pl.ANY)
OVER_ROWS = (((0,), (0,)), ((), ()))
OVER_LANES = (((1,), (1,)), ((), ()))


def vspec():
    return pl.BlockSpec(memory_space=VMEM)


def fetch(sources, targets, sems):
    copies = [pltpu.make_async_copy(s, t, sems.at[i]) for i, (s, t) in enumerate(zip(sources, targets))]
    for copy in copies:
        copy.start()
    return copies


def call_in_hbm(body, name, outs, ins, scratch, flops, moved):
    return pl.pallas_call(
        body,
        out_shape=outs,
        in_specs=[ANY] * len(ins),
        out_specs=jax.tree.map(lambda _: ANY, outs),
        scratch_shapes=scratch,
        compiler_params=pltpu.CompilerParams(vmem_limit_bytes=56 * 1024 * 1024),
        cost_estimate=pl.CostEstimate(flops=flops, bytes_accessed=moved, transcendentals=0),
        name=name,
    )(*ins)


def wanted_slots(count, picked):
    slots = picked.shape[0]
    live = lax.broadcasted_iota(jnp.int32, (8, slots), 1) < count
    wanted = jnp.where(live, jnp.broadcast_to(picked.reshape(1, slots), (8, slots)), -1)
    swapped = pltpu.roll(wanted, slots // 2, 1)
    return jnp.where(lax.axis_index("pair") == 0, wanted, swapped)[:1]


def gather_body(count_hbm, picked_hbm, frames_hbm, mine_hbm, sib_hbm, frames, picked, count, mine, sib, sems):
    slots = picked.shape[0]
    frames_dev = frames.shape[0]
    copies = fetch((frames_hbm, picked_hbm, count_hbm), (frames, picked, count), sems)
    copies[1].wait()
    copies[2].wait()
    wanted = wanted_slots(count[lax.axis_index("tm")], picked[...])
    column = jnp.broadcast_to(wanted.astype(F32), (128, slots)).T[:, :1]
    place = lax.broadcasted_iota(jnp.int32, (1, frames_dev), 1).astype(F32)
    onehot = jnp.where(column == place, 1.0, 0.0).astype(BF16)
    copies[0].wait()
    rows = jnp.dot(onehot, frames[...], preferred_element_type=F32).astype(BF16)
    half = mine.shape[0]
    mine[...] = rows[:half]
    sib[...] = rows[half:]
    for copy in fetch((mine, sib), (mine_hbm, sib_hbm), sems):
        copy.wait()


def gather_rows(count, picked, frames):
    slots, (frames_dev, width) = picked.shape[0], frames.shape
    out = jax.ShapeDtypeStruct((slots // 2, width), BF16)
    return call_in_hbm(
        gather_body,
        "gather_rows",
        (out, out),
        (count, picked, frames),
        [
            VMEM(frames.shape, BF16),
            VMEM(picked.shape, jnp.int32),
            pltpu.SMEM(count.shape, jnp.int32),
            VMEM(out.shape, BF16),
            VMEM(out.shape, BF16),
            pltpu.SemaphoreType.DMA((3,)),
        ],
        2 * slots * frames_dev * width,
        2 * frames_dev * width,
    )


def scatter_body(mines, sibs, count_ref, picked_ref, frames_ref, *refs):
    parts, (out_hbm, out_ref, sems) = refs[: mines + sibs], refs[mines + sibs :]
    wanted = wanted_slots(count_ref[lax.axis_index("tm")], picked_ref[...])

    def added(blocks):
        total = blocks[0][...].astype(F32)
        for block in blocks[1:]:
            total = total + block[...].astype(F32)
        return total.astype(BF16)

    rows = jnp.concatenate([added(parts[:mines]), added(parts[mines:])], axis=0)
    stores = []
    for i, (start, size) in enumerate(chunks_of(frames_ref.shape[0])):
        place = lax.broadcasted_iota(jnp.int32, (size, 1), 0) + start
        onehot = jnp.where(wanted == place, 1.0, 0.0).astype(BF16)
        put = jnp.dot(onehot, rows, preferred_element_type=F32)
        out_ref[start : start + size, :] = (frames_ref[start : start + size, :].astype(F32) + put).astype(BF16)
        cut = pl.ds(start, size)
        store = pltpu.make_async_copy(out_ref.at[cut], out_hbm.at[cut], sems.at[i])
        store.start()
        stores.append(store)
    for store in stores:
        store.wait()


def chunks_of(extent):
    size = 512 if extent % 512 == 0 else extent
    return [(start, size) for start in range(0, extent, size)]


def scatter_rows(name, count, picked, frames, mine_parts, sib_parts):
    slots, (frames_dev, width) = picked.shape[0], frames.shape
    parts = list(mine_parts) + list(sib_parts)
    return pl.pallas_call(
        functools.partial(scatter_body, len(mine_parts), len(sib_parts)),
        out_shape=jax.ShapeDtypeStruct(frames.shape, BF16),
        in_specs=[pl.BlockSpec(memory_space=pltpu.SMEM), vspec(), vspec()] + [vspec()] * len(parts),
        out_specs=ANY,
        scratch_shapes=[VMEM(frames.shape, BF16), pltpu.SemaphoreType.DMA((len(chunks_of(frames_dev)),))],
        compiler_params=pltpu.CompilerParams(vmem_limit_bytes=8 * 1024 * 1024),
        cost_estimate=pl.CostEstimate(
            flops=2 * slots * frames_dev * width, bytes_accessed=4 * frames_dev * width, transcendentals=0
        ),
        name=name,
    )(count, picked, frames, *parts)


def block_start(step, side, width):
    tensors = lax.axis_size("tensor")
    chip = (lax.axis_index("tensor") + tensors + step) % tensors
    return (chip * 2 + (lax.axis_index("pair") + side) % 2) * width


def places(full, ways, width):
    if len(ways) == 1:
        return [full]
    return [full.at[:, pl.ds(pl.multiple_of(block_start(-k, side, width), 128), width)] for k, side in ways]


def pieces_of(total, ways, width):
    if len(ways) == 1:
        return [total]
    return [total.at[:, pl.ds(pl.multiple_of(block_start(k, side, width), 128), width)] for k, side in ways]


def forward_body(ways, width, *refs):
    n = len(ways)
    blocks, weights = refs[:n], refs[n : n + 4]
    gain_hbm, router_hbm = refs[n + 4 : n + 6]
    outs, saved = refs[n + 6 : 2 * n + 6], refs[2 * n + 6 : 2 * n + 10]
    full, gain, router, stats, hidden, slope, total, up0, up1, down0, down1, in_sems, out_sems = refs[2 * n + 10 :]
    copies = fetch(
        (*blocks, gain_hbm, router_hbm, *weights),
        (*places(full, ways, width), gain, router, up0, up1, down0, down1),
        in_sems,
    )
    half, features = full.shape
    hidden_dev = up0.shape[1]
    for copy in copies[: n + 2]:
        copy.wait()
    wide = full[...].astype(F32)
    gate = jax.nn.sigmoid(jnp.sum(wide * router[...].reshape(1, features), axis=1, keepdims=True))
    mean = jnp.sum(wide, axis=1, keepdims=True) * (1.0 / features)
    deviate = wide - mean
    inv = lax.rsqrt(jnp.sum(deviate * deviate, axis=1, keepdims=True) * (1.0 / features) + EPS)
    normed = (deviate * inv * gain[...].reshape(1, features)).astype(BF16)
    lane = lax.broadcasted_iota(jnp.int32, (half, 128), 1)
    stats[...] = jnp.where(lane == 0, mean, jnp.where(lane == 1, inv, gate))
    half_gate = 0.5 * gate
    for i, (copy, up) in enumerate(zip(copies[n + 2 : n + 4], (up0, up1))):
        copy.wait()
        value = jnp.dot(normed, up[...], preferred_element_type=F32)
        s = jax.nn.sigmoid(value)
        cols = slice(i * hidden_dev, (i + 1) * hidden_dev)
        hidden[:, cols] = (value * s).astype(BF16)
        slope[:, cols] = half_gate * s * (1.0 + value * (1.0 - s))
    saving = fetch((full, stats, hidden, slope), saved, out_sems)
    copies[n + 4].wait()
    value = jnp.dot(hidden[:, :hidden_dev], down0[...], preferred_element_type=F32)
    copies[n + 5].wait()
    value = value + jnp.dot(hidden[:, hidden_dev:], down1[...], preferred_element_type=F32)
    total[...] = (value * half_gate).astype(BF16)
    for copy in fetch(pieces_of(total, ways, width), outs, in_sems) + saving:
        copy.wait()


def forward(blocks, ways, weights, gain, router):
    half, block = blocks[0].shape
    features, hidden_dev = weights[0].shape
    saved = (
        ((half, features), BF16),
        ((half, 128), F32),
        ((half, 2 * hidden_dev), BF16),
        ((half, 2 * hidden_dev), F32),
    )
    got = call_in_hbm(
        functools.partial(forward_body, ways, block),
        "forward",
        (jax.ShapeDtypeStruct((half, block), BF16),) * len(ways) + tuple(jax.ShapeDtypeStruct(*x) for x in saved),
        (*blocks, *weights, gain, router),
        [
            VMEM(*saved[0]),
            VMEM(gain.shape, F32),
            VMEM(router.shape, F32),
            *[VMEM(*x) for x in saved[1:]],
            VMEM(*saved[0]),
            *[VMEM(w.shape, BF16) for w in weights],
            pltpu.SemaphoreType.DMA((len(ways) + 6,)),
            pltpu.SemaphoreType.DMA((4,)),
        ],
        8 * half * features * hidden_dev,
        8 * features * hidden_dev,
    )
    return got[: len(ways)], got[len(ways) :]


def backward_body(ways, width, *refs):
    n = len(ways)
    blocks, (up_own, up_sib, down_own, down_sib) = refs[:n], refs[n : n + 4]
    smalls, saved, outs = refs[n + 4 : n + 6], refs[n + 6 : n + 10], refs[n + 10 : 2 * n + 10]
    cot, gain, router, full, stats, hidden, slope, up0, up1, down0, down1, sems = refs[2 * n + 10 :]
    copies = fetch(
        (*blocks, down_own, saved[2], saved[3], down_sib, up_own, up_sib, *smalls, saved[0], saved[1]),
        (*places(cot, ways, width), down0, hidden, slope, down1, up0, up1, gain, router, full, stats),
        sems,
    )
    half, features = full.shape
    hidden_dev = up0.shape[1]
    for copy in copies[: n + 3]:
        copy.wait()
    score, pre = 0.0, []
    for i, down in enumerate((down0, down1)):
        if i:
            copies[n + 3].wait()
        value = lax.dot_general(cot[...], down[...], OVER_LANES, preferred_element_type=F32)
        cols = slice(i * hidden_dev, (i + 1) * hidden_dev)
        pre.append((value * slope[:, cols]).astype(BF16))
        score = score + jnp.sum(value * hidden[:, cols].astype(F32), axis=1, keepdims=True)
    copies[n + 4].wait()
    scaled = lax.dot_general(pre[0], up0[...], OVER_LANES, preferred_element_type=F32)
    copies[n + 5].wait()
    scaled = scaled + lax.dot_general(pre[1], up1[...], OVER_LANES, preferred_element_type=F32)
    for copy in copies[n + 6 :]:
        copy.wait()
    scaled = scaled * gain[...].reshape(1, features)
    mean, inv, gate = stats[:, 0:1], stats[:, 1:2], stats[:, 2:3]
    centred = (full[...].astype(F32) - mean) * inv
    plain = jnp.sum(scaled, axis=1, keepdims=True) * (1.0 / features)
    cross = jnp.sum(scaled * centred, axis=1, keepdims=True) * (1.0 / features)
    term = 0.5 * score * gate * (1.0 - gate)
    cot[...] = (inv * (scaled - plain - centred * cross) + term * router[...].reshape(1, features)).astype(BF16)
    for copy in fetch(pieces_of(cot, ways, width), outs, sems):
        copy.wait()


def backward(blocks, ways, weights, gain, router, saved):
    half, block = blocks[0].shape
    features, hidden_dev = weights[0].shape
    return call_in_hbm(
        functools.partial(backward_body, ways, block),
        "backward",
        (jax.ShapeDtypeStruct((half, block), BF16),) * len(ways),
        (*blocks, *weights, gain, router, *saved),
        [
            VMEM((half, features), BF16),
            VMEM(gain.shape, F32),
            VMEM(router.shape, F32),
            *[VMEM(x.shape, x.dtype) for x in saved],
            *[VMEM(w.shape, BF16) for w in weights],
            pltpu.SemaphoreType.DMA((len(ways) + 10,)),
        ],
        8 * half * features * hidden_dev,
        8 * features * hidden_dev,
    )


def after(value, *others):
    return lax.optimization_barrier((value, *others))[0]


def per_device(frames, router_weight, norm_gain, up_weight, down_weight, picked_rows, picked_count, cotangent):
    width = frames.shape[1]
    features = up_weight.shape[0]
    half = picked_rows.shape[0] // 2
    tensors = lax.axis_size("tensor")
    picked, gain, router = picked_rows, norm_gain, router_weight
    steps = range(1, tensors)
    aligned = width % 128 == 0
    pieces = [(0, 0), (0, 1)] + [(k, 0) for k in steps] + [(k, 1) for k in steps]
    ways = pieces if aligned else [(0, 0)]

    def shift(x, k):
        return lax.ppermute(x, "tensor", [(i, (i + k) % tensors) for i in range(tensors)])

    def swap(x):
        return lax.ppermute(x, "pair", [(0, 1), (1, 0)])

    def joined(blocks):
        if aligned:
            return blocks
        full = jnp.zeros((half, features), BF16)
        for (k, side), block in zip(pieces, blocks):
            full = lax.dynamic_update_slice_in_dim(full, block, block_start(-k, side, width), 1)
        return [full]

    def cut(outs):
        if aligned:
            return outs
        return [lax.dynamic_slice_in_dim(outs[0], block_start(k, side, width), width, 1) for k, side in pieces]

    def collect(mine, sib):
        far_sib = [shift(sib, k) for k in steps]
        far_mine = [shift(after(mine, sib), k) for k in steps]
        near = swap(sib)
        return [mine, near] + far_mine + [swap(x) for x in far_sib], far_sib

    def deliver(parts):
        count = tensors - 1
        far_mine = [shift(x, k) for x, k in zip(parts[2 : 2 + count], steps)]
        through = [swap(x) for x in parts[2 + count :]]
        far_sib = [shift(x, k) for x, k in zip(through, steps)]
        return [parts[0]] + far_mine, [swap(parts[1])] + far_sib, through

    up_sib, down_sib = swap(up_weight), swap(down_weight)
    weights = (up_weight, up_sib, down_weight, down_sib)
    mine, sib = gather_rows(picked_count, picked, frames)
    blocks, arrived = collect(mine, sib)
    cot_mine, cot_sib = gather_rows(picked_count, picked, cotangent)
    cot_sib = after(cot_sib, *arrived)
    cot_blocks, _ = collect(cot_mine, cot_sib)
    parts, saved = forward(joined(blocks), ways, weights, gain, router)
    out_mine, out_sib, through = deliver(cut(parts))
    cot_full = joined(cot_blocks)
    cot_full[0] = after(cot_full[0], *through)
    grads = backward(cot_full, ways, weights, gain, router, saved)
    grad_mine, grad_sib, _ = deliver(cut(grads))
    mixed = scatter_rows("mixed_rows", picked_count, picked, frames, out_mine, out_sib)
    grad_mine[0] = after(grad_mine[0], mixed)
    frames_grad = scatter_rows("grad_rows", picked_count, picked, cotangent, grad_mine, grad_sib)
    return (mixed, frames_grad)


def solution(mesh):
    return jax.shard_map(
        per_device,
        mesh=mesh,
        in_specs=(
            P(("group", "tm"), ("tensor", "pair")),
            P(),
            P(),
            P(None, ("tensor", "pair")),
            P(("tensor", "pair"), None),
            P(("group", "tm")),
            P("group"),
            P(("group", "tm"), ("tensor", "pair")),
        ),
        out_specs=(P(("group", "tm"), ("tensor", "pair")), P(("group", "tm"), ("tensor", "pair"))),
        check_vma=False,
    )
```

time: 52.6 us -> 57.8 us (1.099)
  waiting for transfers between devices: 13.2 us -> 17 us
  Pallas kernels: 21.3 us -> 25 us
  local copies, waits for them, and re-layouts: 5.58 us -> 3.62 us
    pallas_call x4, Pallas kernels: 14.1 us -> 20.4 us  [call_in_hbm(): pl.pallas_call(body, out_shape=outs, in_specs=[ANY] * len(ins), out_specs...]
    ppermute x8, waiting for transfers between devices: 12.7 us -> 17 us  [shift(): lax.ppermute(x, 'tensor', [(i, (i + k) % tensors) for i in range(tensors)])]
    pallas_call x2, Pallas kernels: 7.18 us -> 4.62 us  [scatter_rows(): pl.pallas_call(functools.partial(scatter_body, len(mine_parts), len(sib_p...]
    unnamed x22 -> x32, local copies, waits for them, and re-layouts: 4.89 us -> 3.62 us
    reshape x3 -> x0, local copies, waits for them, and re-layouts: 0.69 us -> none  [the longest x1 0.68 us: per_device(): picked = picked_rows.reshape(1, -1)]
  transfers between devices with their start and end apart: 18 -> 18, of which waited for: 7 -> 5; matrix products, arithmetic and copies ran while one was open for 1% -> 0% of each run, Pallas kernels for 24% -> 39%
where the time goes in v3:
time: 57.8 us; the launch traced here: 57.6 us
  Pallas kernels  25 us (43%)
  waiting for transfers between devices  17 us (29%)
  starting transfers between devices  11.2 us (19%)
  local copies, waits for them, and re-layouts  3.62 us (6%)
  between operations  0.81 us (1%)
    pallas_call x4, Pallas kernels, call_in_hbm(): pl.pallas_call(body, out_shape=outs, in_specs=[ANY] * len(ins), out_specs...  20.4 us
    ppermute x8, waiting for transfers between devices, shift(): lax.ppermute(x, 'tensor', [(i, (i + k) % tensors) for i in range(tensors)])  17 us
    ppermute x8, starting transfers between devices, shift(): lax.ppermute(x, 'tensor', [(i, (i + k) % tensors) for i in range(tensors)])  9.3 us
    pallas_call x2, Pallas kernels, scatter_rows(): pl.pallas_call(functools.partial(scatter_body, len(mine_parts), len(sib_p...  4.62 us
    unnamed x32, local copies, waits for them, and re-layouts  3.62 us
    ppermute x10, starting transfers between devices, swap(): return lax.ppermute(x, 'pair', [(0, 1), (1, 0)])  1.9 us
  transfers between devices with their start and end apart: 18, of which 5 were waited for; matrix products, arithmetic and copies ran while one was open for 0% of the time, Pallas kernels for 39%

profile of v3, /device:TPU:0, one launch (start us, length us, event | category | flops | bytes accessed | tf_op | source)
XLA Modules:
  0.0 57.6 jit_solution(4133949971083018487)
XLA Ops:
  0.6 0.5 collective-permute-start.4
  1.1 0.1 collective-permute-start.5
  1.2 2.8 %gather_rows.2 = (bf16[192,384]{1,0:T(8,128)(2,1)}, bf16[192,384]{1,0:T(8,128)(2,1)}) custom-call(s32[4]{0:T(128)} %count_ref.3, s32[384]{0:T(512)} %picked_ref.3, bf16[1536,384]{1,0:T(8,128)(2,1)} %frames_ref.2), custom_call_target="tpu_custom_call" | custom-call | flops 452984832 | bytes 1179648 | tf_op jit(solution)/shard_map/gather_rows/pallas_call | solution.py:31
  4.1 3.0 %collective-permute-start.2 = (bf16[192,384]{1,0:T(8,128)(2,1)}, bf16[192,384]{1,0:T(8,128)(2,1)S(1)}, u32[]{:S(2)}, u32[]{:S(2)}) collective-permute-start(bf16[192,384]{1,0:T(8,128)(2,1)} %get-tuple-element.24), channel_id=1, source_target_pairs={{0,2},{2,0},{1,3},{3,1},{4,6},{6,4},{5,7},{7,5},{8,10},{10,8},{9,1... | collective-permute-start | bytes 442376 | tf_op jit(solution)/shard_map/ppermute | solution.py:303
  7.0 0.1 collective-permute-start.1
  7.1 0.0 collective-permute-start
  7.1 4.8 %collective-permute-done.2 = bf16[192,384]{1,0:T(8,128)(2,1)S(1)} collective-permute-done((bf16[192,384]{1,0:T(8,128)(2,1)}, bf16[192,384]{1,0:T(8,128)(2,1)S(1)}, u32[]{:S(2)}, u32[]{:S(2)}) %collective-permute-start.2) | collective-permute-done | bytes 147488 | tf_op jit(solution)/shard_map/ppermute | solution.py:303
  11.9 0.0 collective-permute-start.3
  11.9 2.8 %gather_rows.3 = (bf16[192,384]{1,0:T(8,128)(2,1)}, bf16[192,384]{1,0:T(8,128)(2,1)}) custom-call(s32[4]{0:T(128)} %count_ref.3, s32[384]{0:T(512)} %picked_ref.3, bf16[1536,384]{1,0:T(8,128)(2,1)} %frames_ref.3), custom_call_target="tpu_custom_call" | custom-call | flops 452984832 | bytes 1179648 | tf_op jit(solution)/shard_map/gather_rows/pallas_call | solution.py:31
  14.7 0.0 copy-start.8
  14.7 0.0 collective-permute-done.1.refs_2_
  14.8 0.0 copy-start.10
  14.8 2.1 %collective-permute-start.12 = (bf16[192,384]{1,0:T(8,128)(2,1)}, bf16[192,384]{1,0:T(8,128)(2,1)S(1)}, u32[]{:S(2)}, u32[]{:S(2)}) collective-permute-start(bf16[192,384]{1,0:T(8,128)(2,1)} %get-tuple-element.32), channel_id=1, source_target_pairs={{0,2},{2,0},{1,3},{3,1},{4,6},{6,4},{5,7},{7,5},{8,10},{10,8},{9,1... | collective-permute-start | bytes 442376 | tf_op jit(solution)/shard_map/ppermute | solution.py:303
  16.9 0.0 collective-permute-done.refs_1_
  16.9 0.2 collective-permute-start.10
  17.1 0.0 collective-permute-done.3.refs_3_
  17.1 0.0 collective-permute-done.4.refs_5_
  17.1 0.0 copy-start.6
  17.1 0.0 collective-permute-done.5.refs_7_
  17.2 0.0 copy-done.10
  17.2 0.4 copy-done.11
  17.6 0.2 copy-done.12
  17.8 0.8 %copy-done.6 = bf16[1536,768]{1,0:T(8,128)(2,1)} copy-done((bf16[1536,768]{1,0:T(8,128)(2,1)}, bf16[1536,768]{1,0:T(8,128)(2,1)S(1)}, u32[]{:S(2)}) %copy-start.6) | copy-done | bytes 2359320
  18.6 1.4 %copy-done.7 = bf16[768,1536]{1,0:T(8,128)(2,1)} copy-done((bf16[768,1536]{1,0:T(8,128)(2,1)}, bf16[768,1536]{1,0:T(8,128)(2,1)S(1)}, u32[]{:S(2)}) %copy-start.7) | copy-done | bytes 2359320
  20.0 6.4 %forward.1 = (bf16[192,384]{1,0:T(8,128)(2,1)}, bf16[192,384]{1,0:T(8,128)(2,1)}, bf16[192,384]{1,0:T(8,128)(2,1)}, bf16[192,384]{1,0:T(8,128)(2,1)}, bf16[192,1...) custom-call(bf16[192,384]{1,0:T(8,128)(2,1)} %get-tuple-element.23.refs_0_, ...), custom_call_target="tpu_custom_call" | custom-call | flops 1811939328 | bytes 9437184 | tf_op jit(solution)/shard_map/forward/pallas_call | solution.py:31
  26.4 0.3 collective-permute-start.8
  26.7 0.0 copy-done.8
  26.7 0.2 collective-permute-start.11
  26.9 0.0 collective-permute-done.12
  26.9 0.2 collective-permute-start.13
  27.1 1.7 %collective-permute-start.6 = (bf16[192,384]{1,0:T(8,128)(2,1)}, bf16[192,384]{1,0:T(8,128)(2,1)S(1)}, u32[]{:S(2)}, u32[]{:S(2)}) collective-permute-start(bf16[192,384]{1,0:T(8,128)(2,1)} %get-tuple-element.26), channel_id=1, source_target_pairs={{0,2},{2,0},{1,3},{3,1},{4,6},{6,4},{5,7},{7,5},{8,10},{10,8},{9,1... | collective-permute-start | bytes 442376 | tf_op jit(solution)/shard_map/ppermute | solution.py:303
  28.8 0.0 collective-permute-done.8
  28.8 4.6 %collective-permute-done.11.refs_2_ = bf16[192,384]{1,0:T(8,128)(2,1)S(1)} collective-permute-done((bf16[192,384]{1,0:T(8,128)(2,1)S(1)}, bf16[192,384]{1,0:T(8,128)(2,1)S(1)}, u32[]{:S(2)}, u32[]{:S(2)}) %collective-permute-start.11) | collective-permute-done | bytes 147488 | tf_op jit(solution)/shard_map/ppermute | solution.py:303
  33.4 0.0 collective-permute-done.10.refs_1_
  33.4 0.0 collective-permute-done.13.refs_3_
  33.4 0.0 copy-start.14
  33.5 0.6 %copy-done.13 = bf16[192,384]{1,0:T(8,128)(2,1)} copy-done((bf16[192,384]{1,0:T(8,128)(2,1)}, bf16[192,384]{1,0:T(8,128)(2,1)S(1)}, u32[]{:S(2)}) %copy-start.13) | copy-done | bytes 147480
  34.1 0.1 copy-done.9
  34.2 0.0 copy-done.14
  34.2 0.0 copy-start.5
  34.2 8.3 %backward.1 = (bf16[192,384]{1,0:T(8,128)(2,1)}, bf16[192,384]{1,0:T(8,128)(2,1)}, bf16[192,384]{1,0:T(8,128)(2,1)}, bf16[192,384]{1,0:T(8,128)(2,1)}) custom-call(bf16[192,384]{1,0:T(8,128)(2,1)} %get-tuple-element.30.refs_0_, bf16[192,384]{1,0:T(8,128)(2,1)} %copy-done.9, bf16[192,384]{1,0:T(8,128)(2,1)} %copy-done.13, bf16[192,384]{1,0:T(8,128)(2,1)} %copy-done.14, ...), custom_call_target="tpu_custom_call" | custom-call | flops 1811939328 | bytes 9437184 | tf_op jit(solution)/shard_map/backward/pallas_call | solution.py:31
  42.6 0.1 collective-permute-start.16
  42.6 0.0 copy-done.15
  42.7 0.5 collective-permute-start.7
  43.1 0.2 collective-permute-start.9
  43.3 1.9 %collective-permute-start.14 = (bf16[192,384]{1,0:T(8,128)(2,1)}, bf16[192,384]{1,0:T(8,128)(2,1)S(1)}, u32[]{:S(2)}, u32[]{:S(2)}) collective-permute-start(bf16[192,384]{1,0:T(8,128)(2,1)} %get-tuple-element.40), channel_id=1, source_target_pairs={{0,2},{2,0},{1,3},{3,1},{4,6},{6,4},{5,7},{7,5},{8,10},{10,8},{9,1... | collective-permute-start | bytes 442376 | tf_op jit(solution)/shard_map/ppermute | solution.py:303
  45.2 0.0 collective-permute-done.6.refs_1_
  45.2 0.0 collective-permute-start.15
  45.2 0.0 collective-permute-done.16
  45.2 0.2 collective-permute-start.17
  45.4 0.0 collective-permute-done.7.refs_2_
  45.4 4.4 %collective-permute-done.9.refs_3_ = bf16[192,384]{1,0:T(8,128)(2,1)S(1)} collective-permute-done((bf16[192,384]{1,0:T(8,128)(2,1)S(1)}, bf16[192,384]{1,0:T(8,128)(2,1)S(1)}, u32[]{:S(2)}, u32[]{:S(2)}) %collective-permute-start.9) | collective-permute-done | bytes 147488 | tf_op jit(solution)/shard_map/ppermute | solution.py:303
  49.9 0.0 copy-done
  49.9 0.0 copy-done.2
  49.9 0.0 copy-done.4
  49.9 0.0 copy-done.5
  49.9 0.0 copy-start.1
  49.9 0.0 copy-start.3
  49.9 2.3 %mixed_rows.1 = bf16[1536,384]{1,0:T(8,128)(2,1)} custom-call(s32[4]{0:T(128)S(1)} %copy-done.5, s32[384]{0:T(512)S(1)} %copy-done.4, bf16[1536,384]{1,0:T(8,128)(2,1)S(1)} %copy-done, bf16[192,384]{1,0:T(8,128)(2,1)S(1)} %copy-done.2, bf16[192,384]{1,0:T(8,128)(2,1)S(1)} %collective-permute-done.6.refs_1_, ...), custom_call_target="tpu_custom_call" | custom-call | flops 452984832 | bytes 2359296 | tf_op jit(solution)/shard_map/mixed_rows/pallas_call | solution.py:124
  52.2 0.8 %collective-permute-done.14.refs_1_ = bf16[192,384]{1,0:T(8,128)(2,1)S(1)} collective-permute-done((bf16[192,384]{1,0:T(8,128)(2,1)}, bf16[192,384]{1,0:T(8,128)(2,1)S(1)}, u32[]{:S(2)}, u32[]{:S(2)}) %collective-permute-start.14) | collective-permute-done | bytes 147488 | tf_op jit(solution)/shard_map/ppermute | solution.py:303
  53.0 0.0 collective-permute-done.15.refs_2_
  53.0 2.3 %collective-permute-done.17.refs_3_ = bf16[192,384]{1,0:T(8,128)(2,1)S(1)} collective-permute-done((bf16[192,384]{1,0:T(8,128)(2,1)S(1)}, bf16[192,384]{1,0:T(8,128)(2,1)S(1)}, u32[]{:S(2)}, u32[]{:S(2)}) %collective-permute-start.17) | collective-permute-done | bytes 147488 | tf_op jit(solution)/shard_map/ppermute | solution.py:303
  55.3 0.0 copy-done.3
  55.3 2.3 %grad_rows.1 = bf16[1536,384]{1,0:T(8,128)(2,1)} custom-call(s32[4]{0:T(128)S(1)} %copy-done.5, s32[384]{0:T(512)S(1)} %copy-done.4, bf16[1536,384]{1,0:T(8,128)(2,1)S(1)} %copy-done.1, bf16[192,384]{1,0:T(8,128)(2,1)S(1)} %copy-done.3, bf16[192,384]{1,0:T(8,128)(2,1)S(1)} %collective-permute-done.14.refs_1_, ...), custom_call_target="tpu_custom_call" | custom-call | flops 452984832 | bytes 2359296 | tf_op jit(solution)/shard_map/grad_rows/pallas_call | solution.py:124
  (10 shorter events, 0.0 us)
Async XLA Ops:
  0.6 16.5 %collective-permute-start.4 = (bf16[1536,768]{1,0:T(8,128)(2,1)}, bf16[1536,768]{1,0:T(8,128)(2,1)S(1)}, u32[]{:S(2)}, u32[]{:S(2)}) collective-permute-start(bf16[1536,768]{1,0:T(8,128)(2,1)} %refs_4_.3), channel_id=1, source_target_pairs={{0,1},{1,0},{2,3},{3,2},{4,5},{5,4},{6,7},{7,6},{8,9},{9,8},{10,11... | collective-permute-start | bytes 7077896 | tf_op jit(solution)/shard_map/ppermute | solution.py:306
  1.1 16.0 %collective-permute-start.5 = (bf16[768,1536]{1,0:T(8,128)(2,1)}, bf16[768,1536]{1,0:T(8,128)(2,1)S(1)}, u32[]{:S(2)}, u32[]{:S(2)}) collective-permute-start(bf16[768,1536]{1,0:T(8,128)(2,1)} %refs_6_.3), channel_id=1, source_target_pairs={{0,1},{1,0},{2,3},{3,2},{4,5},{5,4},{6,7},{7,6},{8,9},{9,8},{10,11... | collective-permute-start | bytes 7077896 | tf_op jit(solution)/shard_map/ppermute | solution.py:306
  4.1 7.8 %collective-permute-start.2 = (bf16[192,384]{1,0:T(8,128)(2,1)}, bf16[192,384]{1,0:T(8,128)(2,1)S(1)}, u32[]{:S(2)}, u32[]{:S(2)}) collective-permute-start(bf16[192,384]{1,0:T(8,128)(2,1)} %get-tuple-element.24), channel_id=1, source_target_pairs={{0,2},{2,0},{1,3},{3,1},{4,6},{6,4},{5,7},{7,5},{8,10},{10,8},{9,1... | collective-permute-start | bytes 442376 | tf_op jit(solution)/shard_map/ppermute | solution.py:303
  7.0 7.7 %collective-permute-start.1 = (bf16[192,384]{1,0:T(8,128)(2,1)}, bf16[192,384]{1,0:T(8,128)(2,1)S(1)}, u32[]{:S(2)}, u32[]{:S(2)}) collective-permute-start(bf16[192,384]{1,0:T(8,128)(2,1)} %get-tuple-element.23.refs_0_), channel_id=1, source_target_pairs={{0,2},{2,0},{1,3},{3,1},{4,6},{6,4},{5,7},{7,5},{8,10},{10,8},{9,1... | collective-permute-start | bytes 442376 | tf_op jit(solution)/shard_map/ppermute | solution.py:303
  7.1 9.8 %collective-permute-start = (bf16[192,384]{1,0:T(8,128)(2,1)}, bf16[192,384]{1,0:T(8,128)(2,1)S(1)}, u32[]{:S(2)}, u32[]{:S(2)}) collective-permute-start(bf16[192,384]{1,0:T(8,128)(2,1)} %get-tuple-element.24), channel_id=1, source_target_pairs={{0,1},{1,0},{2,3},{3,2},{4,5},{5,4},{6,7},{7,6},{8,9},{9,8},{10,11... | collective-permute-start | bytes 442376 | tf_op jit(solution)/shard_map/ppermute | solution.py:306
  11.9 5.2 %collective-permute-start.3 = (bf16[192,384]{1,0:T(8,128)(2,1)S(1)}, bf16[192,384]{1,0:T(8,128)(2,1)S(1)}, u32[]{:S(2)}, u32[]{:S(2)}) collective-permute-start(bf16[192,384]{1,0:T(8,128)(2,1)S(1)} %collective-permute-done.2), channel_id=1, source_target_pairs={{0,1},{1,0},{2,3},{3,2},{4,5},{5,4},{6,7},{7,6},{8,9},{9,8},{10,11... | collective-permute-start | bytes 442376 | tf_op jit(solution)/shard_map/ppermute | solution.py:306
  14.7 12.0 %copy-start.8 = (bf16[192,384]{1,0:T(8,128)(2,1)S(1)}, bf16[192,384]{1,0:T(8,128)(2,1)}, u32[]{:S(2)}) copy-start(bf16[192,384]{1,0:T(8,128)(2,1)} %get-tuple-element.30.refs_0_) | copy-start | bytes 442372
  14.8 2.4 %copy-start.10 = (bf16[192,384]{1,0:T(8,128)(2,1)}, bf16[192,384]{1,0:T(8,128)(2,1)S(1)}, u32[]{:S(2)}) copy-start(bf16[192,384]{1,0:T(8,128)(2,1)S(1)} %collective-permute-done.1.refs_2_) | copy-start | bytes 442372
  14.8 12.2 %collective-permute-start.12 = (bf16[192,384]{1,0:T(8,128)(2,1)}, bf16[192,384]{1,0:T(8,128)(2,1)S(1)}, u32[]{:S(2)}, u32[]{:S(2)}) collective-permute-start(bf16[192,384]{1,0:T(8,128)(2,1)} %get-tuple-element.32), channel_id=1, source_target_pairs={{0,2},{2,0},{1,3},{3,1},{4,6},{6,4},{5,7},{7,5},{8,10},{10,8},{9,1... | collective-permute-start | bytes 442376 | tf_op jit(solution)/shard_map/ppermute | solution.py:303
  16.9 0.7 %copy-start.11 = (bf16[192,384]{1,0:T(8,128)(2,1)}, bf16[192,384]{1,0:T(8,128)(2,1)S(1)}, u32[]{:S(2)}) copy-start(bf16[192,384]{1,0:T(8,128)(2,1)S(1)} %collective-permute-done.refs_1_) | copy-start | bytes 442372
  16.9 16.5 %collective-permute-start.10 = (bf16[192,384]{1,0:T(8,128)(2,1)}, bf16[192,384]{1,0:T(8,128)(2,1)S(1)}, u32[]{:S(2)}, u32[]{:S(2)}) collective-permute-start(bf16[192,384]{1,0:T(8,128)(2,1)} %get-tuple-element.32), channel_id=1, source_target_pairs={{0,1},{1,0},{2,3},{3,2},{4,5},{5,4},{6,7},{7,6},{8,9},{9,8},{10,11... | collective-permute-start | bytes 442376 | tf_op jit(solution)/shard_map/ppermute | solution.py:306
  17.1 0.7 %copy-start.12 = (bf16[192,384]{1,0:T(8,128)(2,1)}, bf16[192,384]{1,0:T(8,128)(2,1)S(1)}, u32[]{:S(2)}) copy-start(bf16[192,384]{1,0:T(8,128)(2,1)S(1)} %collective-permute-done.3.refs_3_) | copy-start | bytes 442372
  17.1 1.4 %copy-start.6 = (bf16[1536,768]{1,0:T(8,128)(2,1)}, bf16[1536,768]{1,0:T(8,128)(2,1)S(1)}, u32[]{:S(2)}) copy-start(bf16[1536,768]{1,0:T(8,128)(2,1)S(1)} %collective-permute-done.4.refs_5_) | copy-start | bytes 7077892
  18.6 1.4 %copy-start.7 = (bf16[768,1536]{1,0:T(8,128)(2,1)}, bf16[768,1536]{1,0:T(8,128)(2,1)S(1)}, u32[]{:S(2)}) copy-start(bf16[768,1536]{1,0:T(8,128)(2,1)S(1)} %collective-permute-done.5.refs_7_) | copy-start | bytes 7077892
  26.4 2.4 %collective-permute-start.8 = (bf16[192,384]{1,0:T(8,128)(2,1)}, bf16[192,384]{1,0:T(8,128)(2,1)S(1)}, u32[]{:S(2)}, u32[]{:S(2)}) collective-permute-start(bf16[192,384]{1,0:T(8,128)(2,1)} %get-tuple-element.28), channel_id=1, source_target_pairs={{0,1},{1,0},{2,3},{3,2},{4,5},{5,4},{6,7},{7,6},{8,9},{9,8},{10,11... | collective-permute-start | bytes 442376 | tf_op jit(solution)/shard_map/ppermute | solution.py:306
  26.7 6.7 %collective-permute-start.11 = (bf16[192,384]{1,0:T(8,128)(2,1)S(1)}, bf16[192,384]{1,0:T(8,128)(2,1)S(1)}, u32[]{:S(2)}, u32[]{:S(2)}) collective-permute-start(bf16[192,384]{1,0:T(8,128)(2,1)S(1)} %copy-done.8), channel_id=1, source_target_pairs={{0,2},{2,0},{1,3},{3,1},{4,6},{6,4},{5,7},{7,5},{8,10},{10,8},{9,1... | collective-permute-start | bytes 442376 | tf_op jit(solution)/shard_map/ppermute | solution.py:303
  26.9 6.5 %collective-permute-start.13 = (bf16[192,384]{1,0:T(8,128)(2,1)S(1)}, bf16[192,384]{1,0:T(8,128)(2,1)S(1)}, u32[]{:S(2)}, u32[]{:S(2)}) collective-permute-start(bf16[192,384]{1,0:T(8,128)(2,1)S(1)} %collective-permute-done.12), channel_id=1, source_target_pairs={{0,1},{1,0},{2,3},{3,2},{4,5},{5,4},{6,7},{7,6},{8,9},{9,8},{10,11... | collective-permute-start | bytes 442376 | tf_op jit(solution)/shard_map/ppermute | solution.py:306
  27.1 18.1 %collective-permute-start.6 = (bf16[192,384]{1,0:T(8,128)(2,1)}, bf16[192,384]{1,0:T(8,128)(2,1)S(1)}, u32[]{:S(2)}, u32[]{:S(2)}) collective-permute-start(bf16[192,384]{1,0:T(8,128)(2,1)} %get-tuple-element.26), channel_id=1, source_target_pairs={{0,2},{2,0},{1,3},{3,1},{4,6},{6,4},{5,7},{7,5},{8,10},{10,8},{9,1... | collective-permute-start | bytes 442376 | tf_op jit(solution)/shard_map/ppermute | solution.py:303
  33.4 0.7 %copy-start.13 = (bf16[192,384]{1,0:T(8,128)(2,1)}, bf16[192,384]{1,0:T(8,128)(2,1)S(1)}, u32[]{:S(2)}) copy-start(bf16[192,384]{1,0:T(8,128)(2,1)S(1)} %collective-permute-done.11.refs_2_) | copy-start | bytes 442372
  33.4 0.7 %copy-start.9 = (bf16[192,384]{1,0:T(8,128)(2,1)}, bf16[192,384]{1,0:T(8,128)(2,1)S(1)}, u32[]{:S(2)}) copy-start(bf16[192,384]{1,0:T(8,128)(2,1)S(1)} %collective-permute-done.10.refs_1_) | copy-start | bytes 442372
  33.4 0.7 %copy-start.14 = (bf16[192,384]{1,0:T(8,128)(2,1)}, bf16[192,384]{1,0:T(8,128)(2,1)S(1)}, u32[]{:S(2)}) copy-start(bf16[192,384]{1,0:T(8,128)(2,1)S(1)} %collective-permute-done.13.refs_3_) | copy-start | bytes 442372
  34.2 8.5 %copy-start.15 = (bf16[192,384]{1,0:T(8,128)(2,1)S(1)}, bf16[192,384]{1,0:T(8,128)(2,1)}, u32[]{:S(2)}) copy-start(bf16[192,384]{1,0:T(8,128)(2,1)} %get-tuple-element.27) | copy-start | bytes 442372
  34.2 15.7 %copy-start = (bf16[1536,384]{1,0:T(8,128)(2,1)S(1)}, bf16[1536,384]{1,0:T(8,128)(2,1)}, u32[]{:S(2)}) copy-start(bf16[1536,384]{1,0:T(8,128)(2,1)} %frames_ref.2) | copy-start | bytes 3538948
  34.2 15.7 %copy-start.2 = (bf16[192,384]{1,0:T(8,128)(2,1)S(1)}, bf16[192,384]{1,0:T(8,128)(2,1)}, u32[]{:S(2)}) copy-start(bf16[192,384]{1,0:T(8,128)(2,1)} %get-tuple-element.25.refs_0_) | copy-start | bytes 442372
  34.2 15.7 %copy-start.4 = (s32[384]{0:T(512)S(1)}, s32[384]{0:T(512)}, u32[]{:S(2)}) copy-start(s32[384]{0:T(512)} %picked_ref.3) | copy-start | bytes 4612
  34.2 15.7 %copy-start.5 = (s32[4]{0:T(128)S(1)}, s32[4]{0:T(128)}, u32[]{:S(2)}) copy-start(s32[4]{0:T(128)} %count_ref.3) | copy-start | bytes 52
  42.6 2.6 %collective-permute-start.16 = (bf16[192,384]{1,0:T(8,128)(2,1)}, bf16[192,384]{1,0:T(8,128)(2,1)S(1)}, u32[]{:S(2)}, u32[]{:S(2)}) collective-permute-start(bf16[192,384]{1,0:T(8,128)(2,1)} %get-tuple-element.42), channel_id=1, source_target_pairs={{0,1},{1,0},{2,3},{3,2},{4,5},{5,4},{6,7},{7,6},{8,9},{9,8},{10,11... | collective-permute-start | bytes 442376 | tf_op jit(solution)/shard_map/ppermute | solution.py:306
  42.7 2.8 %collective-permute-start.7 = (bf16[192,384]{1,0:T(8,128)(2,1)S(1)}, bf16[192,384]{1,0:T(8,128)(2,1)S(1)}, u32[]{:S(2)}, u32[]{:S(2)}) collective-permute-start(bf16[192,384]{1,0:T(8,128)(2,1)S(1)} %copy-done.15), channel_id=1, source_target_pairs={{0,1},{1,0},{2,3},{3,2},{4,5},{5,4},{6,7},{7,6},{8,9},{9,8},{10,11... | collective-permute-start | bytes 442376 | tf_op jit(solution)/shard_map/ppermute | solution.py:306
  43.1 6.7 %collective-permute-start.9 = (bf16[192,384]{1,0:T(8,128)(2,1)S(1)}, bf16[192,384]{1,0:T(8,128)(2,1)S(1)}, u32[]{:S(2)}, u32[]{:S(2)}) collective-permute-start(bf16[192,384]{1,0:T(8,128)(2,1)S(1)} %collective-permute-done.8), channel_id=1, source_target_pairs={{0,2},{2,0},{1,3},{3,1},{4,6},{6,4},{5,7},{7,5},{8,10},{10,8},{9,1... | collective-permute-start | bytes 442376 | tf_op jit(solution)/shard_map/ppermute | solution.py:303
  43.3 9.7 %collective-permute-start.14 = (bf16[192,384]{1,0:T(8,128)(2,1)}, bf16[192,384]{1,0:T(8,128)(2,1)S(1)}, u32[]{:S(2)}, u32[]{:S(2)}) collective-permute-start(bf16[192,384]{1,0:T(8,128)(2,1)} %get-tuple-element.40), channel_id=1, source_target_pairs={{0,2},{2,0},{1,3},{3,1},{4,6},{6,4},{5,7},{7,5},{8,10},{10,8},{9,1... | collective-permute-start | bytes 442376 | tf_op jit(solution)/shard_map/ppermute | solution.py:303
  45.2 7.8 %collective-permute-start.15 = (bf16[192,384]{1,0:T(8,128)(2,1)}, bf16[192,384]{1,0:T(8,128)(2,1)S(1)}, u32[]{:S(2)}, u32[]{:S(2)}) collective-permute-start(bf16[192,384]{1,0:T(8,128)(2,1)} %get-tuple-element.41), channel_id=1, source_target_pairs={{0,1},{1,0},{2,3},{3,2},{4,5},{5,4},{6,7},{7,6},{8,9},{9,8},{10,11... | collective-permute-start | bytes 442376 | tf_op jit(solution)/shard_map/ppermute | solution.py:306
  45.2 10.1 %collective-permute-start.17 = (bf16[192,384]{1,0:T(8,128)(2,1)S(1)}, bf16[192,384]{1,0:T(8,128)(2,1)S(1)}, u32[]{:S(2)}, u32[]{:S(2)}) collective-permute-start(bf16[192,384]{1,0:T(8,128)(2,1)S(1)} %collective-permute-done.16), channel_id=1, source_target_pairs={{0,2},{2,0},{1,3},{3,1},{4,6},{6,4},{5,7},{7,5},{8,10},{10,8},{9,1... | collective-permute-start | bytes 442376 | tf_op jit(solution)/shard_map/ppermute | solution.py:303
  49.9 5.4 %copy-start.1 = (bf16[1536,384]{1,0:T(8,128)(2,1)S(1)}, bf16[1536,384]{1,0:T(8,128)(2,1)}, u32[]{:S(2)}) copy-start(bf16[1536,384]{1,0:T(8,128)(2,1)} %frames_ref.3) | copy-start | bytes 3538948
  49.9 5.4 %copy-start.3 = (bf16[192,384]{1,0:T(8,128)(2,1)S(1)}, bf16[192,384]{1,0:T(8,128)(2,1)}, u32[]{:S(2)}) copy-start(bf16[192,384]{1,0:T(8,128)(2,1)} %get-tuple-element.39.refs_0_) | copy-start | bytes 442372

commit v4 on v2

v4 whole, which is shorter than its diff:
```python
import functools

import jax
import jax.numpy as jnp
from jax import lax
from jax.experimental import pallas as pl
from jax.experimental.pallas import tpu as pltpu
from jax.sharding import PartitionSpec as P

EPS = 1e-05
F32 = jnp.float32
BF16 = jnp.bfloat16
VMEM = pltpu.VMEM
ANY = pl.BlockSpec(memory_space=pl.ANY)
OVER_LANES = (((1,), (1,)), ((), ()))


def vspec():
    return pl.BlockSpec(memory_space=VMEM)


def call(body, name, outs, ins, specs, scratch, flops, moved, limit):
    return pl.pallas_call(
        body,
        out_shape=outs,
        in_specs=specs,
        out_specs=jax.tree.map(lambda _: vspec(), outs),
        scratch_shapes=scratch,
        compiler_params=pltpu.CompilerParams(vmem_limit_bytes=limit * 1024 * 1024),
        cost_estimate=pl.CostEstimate(flops=flops, bytes_accessed=moved, transcendentals=0),
        name=name,
    )(*ins)


def chunks_of(extent):
    size = 512 if extent % 512 == 0 else extent
    return [(start, size) for start in range(0, extent, size)]


def fetch(sources, targets, sems):
    copies = [pltpu.make_async_copy(s, t, sems.at[i]) for i, (s, t) in enumerate(zip(sources, targets))]
    for copy in copies:
        copy.start()
    return copies


def call_in_hbm(body, name, outs, ins, scratch, flops, moved):
    return pl.pallas_call(
        body,
        out_shape=outs,
        in_specs=[ANY] * len(ins),
        out_specs=jax.tree.map(lambda _: ANY, outs),
        scratch_shapes=scratch,
        compiler_params=pltpu.CompilerParams(vmem_limit_bytes=56 * 1024 * 1024),
        cost_estimate=pl.CostEstimate(flops=flops, bytes_accessed=moved, transcendentals=0),
        name=name,
    )(*ins)


def wanted_slots(count, picked):
    slots = picked.shape[0]
    live = lax.broadcasted_iota(jnp.int32, (8, slots), 1) < count
    wanted = jnp.where(live, jnp.broadcast_to(picked.reshape(1, slots), (8, slots)), -1)
    swapped = pltpu.roll(wanted, slots // 2, 1)
    return jnp.where(lax.axis_index("pair") == 0, wanted, swapped)[:1]


def gather_body(count_hbm, picked_hbm, frames_hbm, mine_hbm, sib_hbm, wanted_hbm, frames, picked, count, mine, sib, sems):
    slots = picked.shape[0]
    frames_dev = frames.shape[0]
    copies = fetch((frames_hbm, picked_hbm, count_hbm), (frames, picked, count), sems)
    copies[1].wait()
    copies[2].wait()
    wanted = wanted_slots(count[lax.axis_index("tm")], picked[...])
    picked[...] = wanted.reshape(slots)
    column = jnp.broadcast_to(wanted.astype(F32), (128, slots)).T[:, :1]
    place = lax.broadcasted_iota(jnp.int32, (1, frames_dev), 1).astype(F32)
    onehot = jnp.where(column == place, 1.0, 0.0).astype(BF16)
    copies[0].wait()
    rows = jnp.dot(onehot, frames[...], preferred_element_type=F32).astype(BF16)
    half = mine.shape[0]
    mine[...] = rows[:half]
    sib[...] = rows[half:]
    for copy in fetch((sib, mine, picked), (sib_hbm, mine_hbm, wanted_hbm), sems):
        copy.wait()


def gather_rows(count, picked, frames, moved):
    slots, (frames_dev, width) = picked.shape[0], frames.shape
    out = jax.ShapeDtypeStruct((slots // 2, width), BF16)
    return call_in_hbm(
        gather_body,
        "gather_rows",
        (out, out, jax.ShapeDtypeStruct(picked.shape, jnp.int32)),
        (count, picked, frames),
        [
            VMEM(frames.shape, BF16),
            VMEM(picked.shape, jnp.int32),
            pltpu.SMEM(count.shape, jnp.int32),
            VMEM(out.shape, BF16),
            VMEM(out.shape, BF16),
            pltpu.SemaphoreType.DMA((3,)),
        ],
        2 * slots * frames_dev * width,
        moved,
    )


def scatter_body(mines, sibs, wanted_ref, frames_ref, *refs):
    parts, (out_hbm, out_ref, sems) = refs[: mines + sibs], refs[mines + sibs :]
    wanted = wanted_ref[...].reshape(1, wanted_ref.shape[0])

    def added(blocks):
        total = blocks[0][...].astype(F32)
        for block in blocks[1:]:
            total = total + block[...].astype(F32)
        return total.astype(BF16)

    rows = jnp.concatenate([added(parts[:mines]), added(parts[mines:])], axis=0)
    stores = []
    for i, (start, size) in enumerate(chunks_of(frames_ref.shape[0])):
        place = lax.broadcasted_iota(jnp.int32, (size, 1), 0) + start
        onehot = jnp.where(wanted == place, 1.0, 0.0).astype(BF16)
        put = jnp.dot(onehot, rows, preferred_element_type=F32)
        out_ref[start : start + size, :] = (frames_ref[start : start + size, :].astype(F32) + put).astype(BF16)
        cut = pl.ds(start, size)
        store = pltpu.make_async_copy(out_ref.at[cut], out_hbm.at[cut], sems.at[i])
        store.start()
        stores.append(store)
    for store in stores:
        store.wait()


def scatter_rows(name, wanted, frames, mine_parts, sib_parts):
    slots, (frames_dev, width) = wanted.shape[0], frames.shape
    parts = list(mine_parts) + list(sib_parts)
    return pl.pallas_call(
        functools.partial(scatter_body, len(mine_parts), len(sib_parts)),
        out_shape=jax.ShapeDtypeStruct(frames.shape, BF16),
        in_specs=[vspec(), vspec()] + [vspec()] * len(parts),
        out_specs=ANY,
        scratch_shapes=[VMEM(frames.shape, BF16), pltpu.SemaphoreType.DMA((len(chunks_of(frames_dev)),))],
        compiler_params=pltpu.CompilerParams(vmem_limit_bytes=8 * 1024 * 1024),
        cost_estimate=pl.CostEstimate(
            flops=2 * slots * frames_dev * width, bytes_accessed=4 * frames_dev * width, transcendentals=0
        ),
        name=name,
    )(wanted, frames, *parts)


def block_start(step, side, width):
    tensors = lax.axis_size("tensor")
    chip = (lax.axis_index("tensor") + tensors + step) % tensors
    return (chip * 2 + (lax.axis_index("pair") + side) % 2) * width


def assemble(full_ref, blocks, ways, width):
    if len(ways) == 1:
        full_ref[...] = blocks[0][...]
        return
    for (step, side), block in zip(ways, blocks):
        start = pl.multiple_of(block_start(-step, side, width), 128)
        full_ref[:, pl.ds(start, width)] = block[...]


def dissect(total_ref, outs, ways, width):
    if len(ways) == 1:
        outs[0][...] = total_ref[...]
        return
    for (step, side), out in zip(ways, outs):
        start = pl.multiple_of(block_start(step, side, width), 128)
        out[...] = total_ref[:, pl.ds(start, width)]


def forward_body(ways, width, *refs):
    n = len(ways)
    blocks = refs[:n]
    up_own, up_sib, down_own, down_sib, gain_ref, router_ref = refs[n : n + 6]
    outs = refs[n + 6 : 2 * n + 6]
    full_ref, stats_ref, hidden_ref, slope_ref = refs[2 * n + 6 : 2 * n + 10]
    (total_ref,) = refs[2 * n + 10 :]
    assemble(full_ref, blocks, ways, width)
    half, features = full_ref.shape
    hidden_dev = up_own.shape[1]
    wide = full_ref[...].astype(F32)
    gate = jax.nn.sigmoid(jnp.sum(wide * router_ref[...].reshape(1, features), axis=1, keepdims=True))
    mean = jnp.sum(wide, axis=1, keepdims=True) * (1.0 / features)
    deviate = wide - mean
    inv = lax.rsqrt(jnp.sum(deviate * deviate, axis=1, keepdims=True) * (1.0 / features) + EPS)
    normed = (deviate * inv * gain_ref[...].reshape(1, features)).astype(BF16)
    lane = lax.broadcasted_iota(jnp.int32, (half, 128), 1)
    stats_ref[...] = jnp.where(lane == 0, mean, jnp.where(lane == 1, inv, gate))
    half_gate = 0.5 * gate
    for i, up in enumerate((up_own, up_sib)):
        value = jnp.dot(normed, up[...], preferred_element_type=F32)
        s = jax.nn.sigmoid(value)
        cols = slice(i * hidden_dev, (i + 1) * hidden_dev)
        hidden_ref[:, cols] = (value * s).astype(BF16)
        slope_ref[:, cols] = half_gate * s * (1.0 + value * (1.0 - s))
    total = jnp.dot(hidden_ref[:, :hidden_dev], down_own[...], preferred_element_type=F32)
    total = total + jnp.dot(hidden_ref[:, hidden_dev:], down_sib[...], preferred_element_type=F32)
    total_ref[...] = (total * half_gate).astype(BF16)
    dissect(total_ref, outs, ways, width)


def forward(blocks, ways, weights, gain, router):
    half, width = blocks[0].shape
    features, hidden_dev = weights[0].shape
    piece = jax.ShapeDtypeStruct((half, width), BF16)
    got = call(
        functools.partial(forward_body, ways, width),
        "forward",
        (piece,) * len(ways)
        + (
            jax.ShapeDtypeStruct((half, features), BF16),
            jax.ShapeDtypeStruct((half, 128), F32),
            jax.ShapeDtypeStruct((half, 2 * hidden_dev), BF16),
            jax.ShapeDtypeStruct((half, 2 * hidden_dev), F32),
        ),
        (*blocks, *weights, gain, router),
        [vspec()] * (len(blocks) + 6),
        [VMEM((half, features), BF16)],
        1,
        1,
        16,
    )
    return got[: len(ways)], got[len(ways) :]


def backward_body(ways, width, *refs):
    n = len(ways)
    blocks = refs[:n]
    up_own, up_sib, down_own, down_sib, gain_ref, router_ref = refs[n : n + 6]
    full_ref, stats_ref, hidden_ref, slope_ref = refs[n + 6 : n + 10]
    outs = refs[n + 10 : 2 * n + 10]
    (cot_ref,) = refs[2 * n + 10 :]
    assemble(cot_ref, blocks, ways, width)
    half, features = full_ref.shape
    hidden_dev = up_own.shape[1]
    score, pre = 0.0, []
    for i, down in enumerate((down_own, down_sib)):
        value = lax.dot_general(cot_ref[...], down[...], OVER_LANES, preferred_element_type=F32)
        cols = slice(i * hidden_dev, (i + 1) * hidden_dev)
        pre.append((value * slope_ref[:, cols]).astype(BF16))
        score = score + jnp.sum(value * hidden_ref[:, cols].astype(F32), axis=1, keepdims=True)
    scaled = lax.dot_general(pre[0], up_own[...], OVER_LANES, preferred_element_type=F32)
    scaled = scaled + lax.dot_general(pre[1], up_sib[...], OVER_LANES, preferred_element_type=F32)
    scaled = scaled * gain_ref[...].reshape(1, features)
    mean, inv, gate = stats_ref[:, 0:1], stats_ref[:, 1:2], stats_ref[:, 2:3]
    centred = (full_ref[...].astype(F32) - mean) * inv
    plain = jnp.sum(scaled, axis=1, keepdims=True) * (1.0 / features)
    cross = jnp.sum(scaled * centred, axis=1, keepdims=True) * (1.0 / features)
    term = 0.5 * score * gate * (1.0 - gate)
    cot_ref[...] = (inv * (scaled - plain - centred * cross) + term * router_ref[...].reshape(1, features)).astype(BF16)
    dissect(cot_ref, outs, ways, width)


def backward(blocks, ways, weights, gain, router, saved):
    half, width = blocks[0].shape
    features, hidden_dev = weights[0].shape
    return call(
        functools.partial(backward_body, ways, width),
        "backward",
        (jax.ShapeDtypeStruct((half, width), BF16),) * len(ways),
        (*blocks, *weights, gain, router, *saved),
        [vspec()] * (len(blocks) + 10),
        [VMEM((half, features), BF16)],
        1,
        1,
        16,
    )


def after(value, *others):
    return lax.optimization_barrier((value, *others))[0]


def per_device(frames, router_weight, norm_gain, up_weight, down_weight, picked_rows, picked_count, cotangent):
    width = frames.shape[1]
    features = up_weight.shape[0]
    half = picked_rows.shape[0] // 2
    tensors = lax.axis_size("tensor")
    gain, router = norm_gain, router_weight
    steps = range(1, tensors)
    aligned = width % 128 == 0
    pieces = [(0, 0), (0, 1)] + [(k, 0) for k in steps] + [(k, 1) for k in steps]
    ways = pieces if aligned else [(0, 0)]

    def send(x, k, side):
        pairs = [
            (chip * 2 + core, (chip + k) % tensors * 2 + (core + side) % 2) for chip in range(tensors) for core in (0, 1)
        ]
        return lax.ppermute(x, ("tensor", "pair"), pairs)

    def swap(x):
        return lax.ppermute(x, "pair", [(0, 1), (1, 0)])

    def joined(blocks):
        if aligned:
            return blocks
        full = jnp.zeros((half, features), BF16)
        for (k, side), block in zip(pieces, blocks):
            full = lax.dynamic_update_slice_in_dim(full, block, block_start(-k, side, width), 1)
        return [full]

    def cut(outs):
        if aligned:
            return outs
        return [lax.dynamic_slice_in_dim(outs[0], block_start(k, side, width), width, 1) for k, side in pieces]

    def collect(mine, sib):
        return [mine, swap(sib)] + [send(mine, k, 0) for k in steps] + [send(sib, k, 1) for k in steps]

    def deliver(parts):
        count = tensors - 1
        far_mine = [send(x, k, 0) for x, k in zip(parts[2 : 2 + count], steps)]
        far_sib = [send(x, k, 1) for x, k in zip(parts[2 + count :], steps)]
        return [parts[0]] + far_mine, [swap(parts[1])] + far_sib

    up_sib, down_sib = swap(up_weight), swap(down_weight)
    weights = (up_weight, up_sib, down_weight, down_sib)
    mine, sib, wanted = gather_rows(picked_count, picked_rows, frames, 1)
    blocks = collect(mine, sib)
    cot_mine, cot_sib, _ = gather_rows(picked_count, picked_rows, cotangent, 1)
    cot_mine, cot_sib = lax.optimization_barrier((cot_mine, cot_sib, blocks[2]))[:2]
    cot_blocks = collect(cot_mine, cot_sib)
    parts, saved = forward(joined(blocks), ways, weights, gain, router)
    out_mine, out_sib = deliver(cut(parts))
    grads = backward(joined(cot_blocks), ways, weights, gain, router, saved)
    grad_mine, grad_sib = deliver(cut(grads))
    mixed = scatter_rows("mixed_rows", wanted, frames, out_mine, out_sib)
    grad_mine[0] = after(grad_mine[0], mixed)
    frames_grad = scatter_rows("grad_rows", wanted, cotangent, grad_mine, grad_sib)
    return (mixed, frames_grad)


def solution(mesh):
    return jax.shard_map(
        per_device,
        mesh=mesh,
        in_specs=(
            P(("group", "tm"), ("tensor", "pair")),
            P(),
            P(),
            P(None, ("tensor", "pair")),
            P(("tensor", "pair"), None),
            P(("group", "tm")),
            P("group"),
            P(("group", "tm"), ("tensor", "pair")),
        ),
        out_specs=(P(("group", "tm"), ("tensor", "pair")), P(("group", "tm"), ("tensor", "pair"))),
        check_vma=False,
    )
```

time: 52.6 us -> 38.3 us (0.73)
  Pallas kernels: 21.3 us -> 15.4 us
  waiting for transfers between devices: 13.2 us -> 8.61 us
  local copies, waits for them, and re-layouts: 5.58 us -> 1.7 us
    pallas_call x4 -> x2, Pallas kernels: 14.1 us -> 6.13 us  [call(): pl.pallas_call(body, out_shape=outs, in_specs=specs, out_specs=jax.tree.m...]
    pallas_call x0 -> x2, Pallas kernels: none -> 5.9 us  [call_in_hbm(): pl.pallas_call(body, out_shape=outs, in_specs=[ANY] * len(ins), out_specs...]
    ppermute x8, waiting for transfers between devices: 12.7 us -> 8.6 us  [send(): return lax.ppermute(x, ('tensor', 'pair'), pairs)]
    pallas_call x2, Pallas kernels: 7.18 us -> 3.36 us  [scatter_rows(): pl.pallas_call(functools.partial(scatter_body, len(mine_parts), len(sib_p...]
    unnamed x22 -> x20, local copies, waits for them, and re-layouts: 4.89 us -> 1.7 us
    ppermute x8, starting transfers between devices: 9.57 us -> 10.7 us  [send(): return lax.ppermute(x, ('tensor', 'pair'), pairs)]
    ppermute x10 -> x6, starting transfers between devices: 1.98 us -> 0.98 us  [swap(): return lax.ppermute(x, 'pair', [(0, 1), (1, 0)])]
    reshape x3 -> x0, local copies, waits for them, and re-layouts: 0.69 us -> none  [the longest x1 0.68 us: per_device(): picked = picked_rows.reshape(1, -1)]
  transfers between devices with their start and end apart: 18 -> 14, of which waited for: 7 -> 6; matrix products, arithmetic and copies ran while one was open for 1% -> 0% of each run, Pallas kernels for 24% -> 36%
where the time goes in v4:
time: 38.3 us; the launch traced here: 38.1 us
  Pallas kernels  15.4 us (40%)
  starting transfers between devices  11.6 us (30%)
  waiting for transfers between devices  8.61 us (22%)
  local copies, waits for them, and re-layouts  1.7 us (4%)
  between operations  0.79 us (2%)
    ppermute x8, starting transfers between devices, send(): return lax.ppermute(x, ('tensor', 'pair'), pairs)  10.7 us
    ppermute x8, waiting for transfers between devices, send(): return lax.ppermute(x, ('tensor', 'pair'), pairs)  8.6 us
    pallas_call x2, Pallas kernels, call(): pl.pallas_call(body, out_shape=outs, in_specs=specs, out_specs=jax.tree.m...  6.13 us
    pallas_call x2, Pallas kernels, call_in_hbm(): pl.pallas_call(body, out_shape=outs, in_specs=[ANY] * len(ins), out_specs...  5.9 us
    pallas_call x2, Pallas kernels, scatter_rows(): pl.pallas_call(functools.partial(scatter_body, len(mine_parts), len(sib_p...  3.36 us
    unnamed x20, local copies, waits for them, and re-layouts  1.7 us
    ppermute x6, starting transfers between devices, swap(): return lax.ppermute(x, 'pair', [(0, 1), (1, 0)])  0.98 us
  transfers between devices with their start and end apart: 14, of which 6 were waited for; matrix products, arithmetic and copies ran while one was open for 0% of the time, Pallas kernels for 36%

profile of v4, /device:TPU:0, one launch (start us, length us, event | category | flops | bytes accessed | tf_op | source)
XLA Modules:
  0.0 38.1 jit_solution(6594000266795572229)
XLA Ops:
  0.6 0.5 %collective-permute-start.3 = (bf16[1536,768]{1,0:T(8,128)(2,1)}, bf16[1536,768]{1,0:T(8,128)(2,1)S(1)}, u32[]{:S(2)}, u32[]{:S(2)}) collective-permute-start(bf16[1536,768]{1,0:T(8,128)(2,1)} %refs_4_.3), channel_id=1, source_target_pairs={{0,1},{1,0},{2,3},{3,2},{4,5},{5,4},{6,7},{7,6},{8,9},{9,8},{10,11... | collective-permute-start | bytes 7077896 | tf_op jit(solution)/shard_map/ppermute | solution.py:296
  1.1 0.1 collective-permute-start.4
  1.2 0.0 copy-start
  1.2 3.0 %gather_rows.2 = (bf16[192,384]{1,0:T(8,128)(2,1)}, bf16[192,384]{1,0:T(8,128)(2,1)}, s32[384]{0:T(512)}) custom-call(s32[4]{0:T(128)} %count_hbm.3, s32[384]{0:T(512)} %picked_hbm.3, bf16[1536,384]{1,0:T(8,128)(2,1)} %frames_ref.2), custom_call_target="tpu_custom_call" | custom-call | flops 452984832 | bytes 1 | tf_op jit(solution)/shard_map/gather_rows/pallas_call | solution.py:48
  4.3 0.0 copy-start.6
  4.3 0.0 copy-start.7
  4.3 0.0 copy-start.8
  4.3 3.0 %collective-permute-start.1 = (bf16[192,384]{1,0:T(8,128)(2,1)}, bf16[192,384]{1,0:T(8,128)(2,1)S(1)}, u32[]{:S(2)}, u32[]{:S(2)}) collective-permute-start(bf16[192,384]{1,0:T(8,128)(2,1)} %get-tuple-element.23.refs_0_), channel_id=1, source_target_pairs={{0,2},{1,3},{2,0},{3,1},{4,6},{5,7},{6,4},{7,5},{8,10},{9,11},{10,... | collective-permute-start | bytes 442376 | tf_op jit(solution)/shard_map/ppermute | solution.py:293
  7.3 0.0 collective-permute-start.2
  7.3 0.2 collective-permute-start
  7.5 2.9 %gather_rows.3 = (bf16[192,384]{1,0:T(8,128)(2,1)}, bf16[192,384]{1,0:T(8,128)(2,1)}, s32[384]{0:T(512)}) custom-call(s32[4]{0:T(128)} %count_hbm.3, s32[384]{0:T(512)} %picked_hbm.3, bf16[1536,384]{1,0:T(8,128)(2,1)} %frames_ref.3), custom_call_target="tpu_custom_call" | custom-call | flops 452984832 | bytes 1 | tf_op jit(solution)/shard_map/gather_rows/pallas_call | solution.py:48
  10.4 1.8 %collective-permute-done.1.refs_2_ = bf16[192,384]{1,0:T(8,128)(2,1)S(1)} collective-permute-done((bf16[192,384]{1,0:T(8,128)(2,1)}, bf16[192,384]{1,0:T(8,128)(2,1)S(1)}, u32[]{:S(2)}, u32[]{:S(2)}) %collective-permute-start.1) | collective-permute-done | bytes 147488 | tf_op jit(solution)/shard_map/ppermute | solution.py:293
  12.1 2.1 %collective-permute-start.9 = (bf16[192,384]{1,0:T(8,128)(2,1)}, bf16[192,384]{1,0:T(8,128)(2,1)S(1)}, u32[]{:S(2)}, u32[]{:S(2)}) collective-permute-start(bf16[192,384]{1,0:T(8,128)(2,1)} %get-tuple-element.31.refs_0_), channel_id=1, source_target_pairs={{0,2},{1,3},{2,0},{3,1},{4,6},{5,7},{6,4},{7,5},{8,10},{9,11},{10,... | collective-permute-start | bytes 442376 | tf_op jit(solution)/shard_map/ppermute | solution.py:293
  14.2 0.8 %collective-permute-done.2.refs_3_ = bf16[192,384]{1,0:T(8,128)(2,1)S(1)} collective-permute-done((bf16[192,384]{1,0:T(8,128)(2,1)}, bf16[192,384]{1,0:T(8,128)(2,1)S(1)}, u32[]{:S(2)}, u32[]{:S(2)}) %collective-permute-start.2) | collective-permute-done | bytes 147488 | tf_op jit(solution)/shard_map/ppermute | solution.py:293
  15.0 1.8 %collective-permute-start.10 = (bf16[192,384]{1,0:T(8,128)(2,1)}, bf16[192,384]{1,0:T(8,128)(2,1)S(1)}, u32[]{:S(2)}, u32[]{:S(2)}) collective-permute-start(bf16[192,384]{1,0:T(8,128)(2,1)} %get-tuple-element.32), channel_id=1, source_target_pairs={{0,3},{1,2},{2,1},{3,0},{4,7},{5,6},{6,5},{7,4},{8,11},{9,10},{10,... | collective-permute-start | bytes 442376 | tf_op jit(solution)/shard_map/ppermute | solution.py:293
  16.8 0.0 collective-permute-done.refs_1_
  16.8 0.0 collective-permute-start.8
  16.8 0.0 collective-permute-done.3.refs_5_
  16.8 0.0 collective-permute-done.4.refs_7_
  16.8 0.0 copy-done
  16.8 0.0 copy-done.6
  16.8 0.0 copy-done.7
  16.8 0.0 copy-done.8
  16.8 0.0 copy-start.1
  16.8 1.7 %copy-done.1 = bf16[768,1536]{1,0:T(8,128)(2,1)S(1)} copy-done((bf16[768,1536]{1,0:T(8,128)(2,1)S(1)}, bf16[768,1536]{1,0:T(8,128)(2,1)}, u32[]{:S(2)}) %copy-start.1) | copy-done | bytes 2359320
  18.5 0.0 copy-start.2
  18.5 0.0 copy-start.5
  18.5 2.6 %forward.1 = (bf16[192,384]{1,0:T(8,128)(2,1)S(1)}, bf16[192,384]{1,0:T(8,128)(2,1)S(1)}, bf16[192,384]{1,0:T(8,128)(2,1)S(1)}, bf16[192,384]{1,0:T(8,128)(2,1)S...) custom-call(bf16[192,384]{1,0:T(8,128)(2,1)S(1)} %copy-done.6, ...), custom_call_target="tpu_custom_call" | custom-call | flops 1 | bytes 1 | tf_op jit(solution)/shard_map/forward/pallas_call | solution.py:23
  21.1 0.5 %collective-permute-start.5 = (bf16[192,384]{1,0:T(8,128)(2,1)S(1)}, bf16[192,384]{1,0:T(8,128)(2,1)S(1)}, u32[]{:S(2)}, u32[]{:S(2)}) collective-permute-start(bf16[192,384]{1,0:T(8,128)(2,1)S(1)} %get-tuple-element.26), channel_id=1, source_target_pairs={{0,2},{1,3},{2,0},{3,1},{4,6},{5,7},{6,4},{7,5},{8,10},{9,11},{10,... | collective-permute-start | bytes 442376 | tf_op jit(solution)/shard_map/ppermute | solution.py:293
  21.5 0.2 collective-permute-start.6
  21.7 0.0 collective-permute-done.9.refs_2_
  21.7 1.6 %collective-permute-start.7 = (bf16[192,384]{1,0:T(8,128)(2,1)S(1)}, bf16[192,384]{1,0:T(8,128)(2,1)S(1)}, u32[]{:S(2)}, u32[]{:S(2)}) collective-permute-start(bf16[192,384]{1,0:T(8,128)(2,1)S(1)} %get-tuple-element.28), channel_id=1, source_target_pairs={{0,3},{1,2},{2,1},{3,0},{4,7},{5,6},{6,5},{7,4},{8,11},{9,10},{10,... | collective-permute-start | bytes 442376 | tf_op jit(solution)/shard_map/ppermute | solution.py:293
  23.3 0.0 collective-permute-done.10.refs_3_
  23.3 0.0 collective-permute-done.8.refs_1_
  23.3 0.0 copy-done.2
  23.3 0.0 copy-done.5
  23.3 0.0 copy-start.3
  23.3 0.0 copy-start.9
  23.3 3.6 %backward.1 = (bf16[192,384]{1,0:T(8,128)(2,1)S(1)}, bf16[192,384]{1,0:T(8,128)(2,1)S(1)}, bf16[192,384]{1,0:T(8,128)(2,1)S(1)}, bf16[192,384]{1,0:T(8,128)(2,1)S(1)}) custom-call(bf16[192,384]{1,0:T(8,128)(2,1)S(1)} %copy-done.5, bf16[192,384]{1,0:T(8,128)(2,1)S(1)} %collective-permute-done.8.refs_1_, bf16[192,384]{1,0:T(8,128)(2,1)S(1)} %collective-permute-done.9.refs_2_, ...), custom_call_target="tpu_custom_call" | custom-call | flops 1 | bytes 1 | tf_op jit(solution)/shard_map/backward/pallas_call | solution.py:23
  26.9 0.5 %collective-permute-start.11 = (bf16[192,384]{1,0:T(8,128)(2,1)S(1)}, bf16[192,384]{1,0:T(8,128)(2,1)S(1)}, u32[]{:S(2)}, u32[]{:S(2)}) collective-permute-start(bf16[192,384]{1,0:T(8,128)(2,1)S(1)} %get-tuple-element.39), channel_id=1, source_target_pairs={{0,2},{1,3},{2,0},{3,1},{4,6},{5,7},{6,4},{7,5},{8,10},{9,11},{10,... | collective-permute-start | bytes 442376 | tf_op jit(solution)/shard_map/ppermute | solution.py:293
  27.4 0.0 collective-permute-start.12
  27.4 0.4 %collective-permute-done.5.refs_1_ = bf16[192,384]{1,0:T(8,128)(2,1)S(1)} collective-permute-done((bf16[192,384]{1,0:T(8,128)(2,1)S(1)}, bf16[192,384]{1,0:T(8,128)(2,1)S(1)}, u32[]{:S(2)}, u32[]{:S(2)}) %collective-permute-start.5) | collective-permute-done | bytes 147488 | tf_op jit(solution)/shard_map/ppermute | solution.py:293
  27.8 1.3 %collective-permute-start.13 = (bf16[192,384]{1,0:T(8,128)(2,1)S(1)}, bf16[192,384]{1,0:T(8,128)(2,1)S(1)}, u32[]{:S(2)}, u32[]{:S(2)}) collective-permute-start(bf16[192,384]{1,0:T(8,128)(2,1)S(1)} %get-tuple-element.41), channel_id=1, source_target_pairs={{0,3},{1,2},{2,1},{3,0},{4,7},{5,6},{6,5},{7,4},{8,11},{9,10},{10,... | collective-permute-start | bytes 442376 | tf_op jit(solution)/shard_map/ppermute | solution.py:293
  29.1 0.0 collective-permute-done.6.refs_2_
  29.1 1.0 %collective-permute-done.7.refs_3_ = bf16[192,384]{1,0:T(8,128)(2,1)S(1)} collective-permute-done((bf16[192,384]{1,0:T(8,128)(2,1)S(1)}, bf16[192,384]{1,0:T(8,128)(2,1)S(1)}, u32[]{:S(2)}, u32[]{:S(2)}) %collective-permute-start.7) | collective-permute-done | bytes 147488 | tf_op jit(solution)/shard_map/ppermute | solution.py:293
  30.1 0.0 copy-done.3
  30.1 0.0 copy-done.9
  30.1 0.0 copy-start.4
  30.1 1.7 %mixed_rows.1 = bf16[1536,384]{1,0:T(8,128)(2,1)} custom-call(s32[384]{0:T(512)S(1)} %copy-done.9, bf16[1536,384]{1,0:T(8,128)(2,1)S(1)} %copy-done.3, bf16[192,384]{1,0:T(8,128)(2,1)S(1)} %get-tuple-element.25.refs_0_, bf16[192,384]{1,0:T(8,128)(2,1)S(1)} %collective-permute-done.5.refs_1_, bf16[192,384]{1,0:T(8,128)(2,1)S(1)} %collective-permute-done.6.refs_2_, ...), custom_call_target="tpu_custom_call" | custom-call | flops 452984832 | bytes 2359296 | tf_op jit(solution)/shard_map/mixed_rows/pallas_call | solution.py:137
  31.8 2.3 %collective-permute-done.11.refs_1_ = bf16[192,384]{1,0:T(8,128)(2,1)S(1)} collective-permute-done((bf16[192,384]{1,0:T(8,128)(2,1)S(1)}, bf16[192,384]{1,0:T(8,128)(2,1)S(1)}, u32[]{:S(2)}, u32[]{:S(2)}) %collective-permute-start.11) | collective-permute-done | bytes 147488 | tf_op jit(solution)/shard_map/ppermute | solution.py:293
  34.1 0.0 collective-permute-done.12.refs_2_
  34.1 2.4 %collective-permute-done.13.refs_3_ = bf16[192,384]{1,0:T(8,128)(2,1)S(1)} collective-permute-done((bf16[192,384]{1,0:T(8,128)(2,1)S(1)}, bf16[192,384]{1,0:T(8,128)(2,1)S(1)}, u32[]{:S(2)}, u32[]{:S(2)}) %collective-permute-start.13) | collective-permute-done | bytes 147488 | tf_op jit(solution)/shard_map/ppermute | solution.py:293
  36.5 0.0 copy-done.4
  36.5 1.7 %grad_rows.1 = bf16[1536,384]{1,0:T(8,128)(2,1)} custom-call(s32[384]{0:T(512)S(1)} %copy-done.9, bf16[1536,384]{1,0:T(8,128)(2,1)S(1)} %copy-done.4, bf16[192,384]{1,0:T(8,128)(2,1)S(1)} %get-tuple-element.38.refs_0_, bf16[192,384]{1,0:T(8,128)(2,1)S(1)} %collective-permute-done.11.refs_1_, bf16[192,384]{1,0:T(8,128)(2,1)S(1)} %collective-permute-done.12.refs_2_, ...), custom_call_target="tpu_custom_call" | custom-call | flops 452984832 | bytes 2359296 | tf_op jit(solution)/shard_map/grad_rows/pallas_call | solution.py:137
Async XLA Ops:
  0.6 16.2 %collective-permute-start.3 = (bf16[1536,768]{1,0:T(8,128)(2,1)}, bf16[1536,768]{1,0:T(8,128)(2,1)S(1)}, u32[]{:S(2)}, u32[]{:S(2)}) collective-permute-start(bf16[1536,768]{1,0:T(8,128)(2,1)} %refs_4_.3), channel_id=1, source_target_pairs={{0,1},{1,0},{2,3},{3,2},{4,5},{5,4},{6,7},{7,6},{8,9},{9,8},{10,11... | collective-permute-start | bytes 7077896 | tf_op jit(solution)/shard_map/ppermute | solution.py:296
  1.1 15.6 %collective-permute-start.4 = (bf16[768,1536]{1,0:T(8,128)(2,1)}, bf16[768,1536]{1,0:T(8,128)(2,1)S(1)}, u32[]{:S(2)}, u32[]{:S(2)}) collective-permute-start(bf16[768,1536]{1,0:T(8,128)(2,1)} %refs_6_.3), channel_id=1, source_target_pairs={{0,1},{1,0},{2,3},{3,2},{4,5},{5,4},{6,7},{7,6},{8,9},{9,8},{10,11... | collective-permute-start | bytes 7077896 | tf_op jit(solution)/shard_map/ppermute | solution.py:296
  1.2 15.6 %copy-start = (bf16[1536,768]{1,0:T(8,128)(2,1)S(1)}, bf16[1536,768]{1,0:T(8,128)(2,1)}, u32[]{:S(2)}) copy-start(bf16[1536,768]{1,0:T(8,128)(2,1)} %refs_4_.3) | copy-start | bytes 7077892
  4.3 12.6 %copy-start.6 = (bf16[192,384]{1,0:T(8,128)(2,1)S(1)}, bf16[192,384]{1,0:T(8,128)(2,1)}, u32[]{:S(2)}) copy-start(bf16[192,384]{1,0:T(8,128)(2,1)} %get-tuple-element.23.refs_0_) | copy-start | bytes 442372
  4.3 12.6 %copy-start.7 = (f32[1536]{0:T(1024)S(1)}, f32[1536]{0:T(1024)}, u32[]{:S(2)}) copy-start(f32[1536]{0:T(1024)} %refs_8_.3) | copy-start | bytes 18436
  4.3 12.6 %copy-start.8 = (f32[1536]{0:T(1024)S(1)}, f32[1536]{0:T(1024)}, u32[]{:S(2)}) copy-start(f32[1536]{0:T(1024)} %refs_9_.3) | copy-start | bytes 18436
  4.3 7.8 %collective-permute-start.1 = (bf16[192,384]{1,0:T(8,128)(2,1)}, bf16[192,384]{1,0:T(8,128)(2,1)S(1)}, u32[]{:S(2)}, u32[]{:S(2)}) collective-permute-start(bf16[192,384]{1,0:T(8,128)(2,1)} %get-tuple-element.23.refs_0_), channel_id=1, source_target_pairs={{0,2},{1,3},{2,0},{3,1},{4,6},{5,7},{6,4},{7,5},{8,10},{9,11},{10,... | collective-permute-start | bytes 442376 | tf_op jit(solution)/shard_map/ppermute | solution.py:293
  7.3 7.7 %collective-permute-start.2 = (bf16[192,384]{1,0:T(8,128)(2,1)}, bf16[192,384]{1,0:T(8,128)(2,1)S(1)}, u32[]{:S(2)}, u32[]{:S(2)}) collective-permute-start(bf16[192,384]{1,0:T(8,128)(2,1)} %get-tuple-element.24), channel_id=1, source_target_pairs={{0,3},{1,2},{2,1},{3,0},{4,7},{5,6},{6,5},{7,4},{8,11},{9,10},{10,... | collective-permute-start | bytes 442376 | tf_op jit(solution)/shard_map/ppermute | solution.py:293
  7.3 9.5 %collective-permute-start = (bf16[192,384]{1,0:T(8,128)(2,1)}, bf16[192,384]{1,0:T(8,128)(2,1)S(1)}, u32[]{:S(2)}, u32[]{:S(2)}) collective-permute-start(bf16[192,384]{1,0:T(8,128)(2,1)} %get-tuple-element.24), channel_id=1, source_target_pairs={{0,1},{1,0},{2,3},{3,2},{4,5},{5,4},{6,7},{7,6},{8,9},{9,8},{10,11... | collective-permute-start | bytes 442376 | tf_op jit(solution)/shard_map/ppermute | solution.py:296
  12.1 9.6 %collective-permute-start.9 = (bf16[192,384]{1,0:T(8,128)(2,1)}, bf16[192,384]{1,0:T(8,128)(2,1)S(1)}, u32[]{:S(2)}, u32[]{:S(2)}) collective-permute-start(bf16[192,384]{1,0:T(8,128)(2,1)} %get-tuple-element.31.refs_0_), channel_id=1, source_target_pairs={{0,2},{1,3},{2,0},{3,1},{4,6},{5,7},{6,4},{7,5},{8,10},{9,11},{10,... | collective-permute-start | bytes 442376 | tf_op jit(solution)/shard_map/ppermute | solution.py:293
  15.0 8.3 %collective-permute-start.10 = (bf16[192,384]{1,0:T(8,128)(2,1)}, bf16[192,384]{1,0:T(8,128)(2,1)S(1)}, u32[]{:S(2)}, u32[]{:S(2)}) collective-permute-start(bf16[192,384]{1,0:T(8,128)(2,1)} %get-tuple-element.32), channel_id=1, source_target_pairs={{0,3},{1,2},{2,1},{3,0},{4,7},{5,6},{6,5},{7,4},{8,11},{9,10},{10,... | collective-permute-start | bytes 442376 | tf_op jit(solution)/shard_map/ppermute | solution.py:293
  16.8 6.5 %collective-permute-start.8 = (bf16[192,384]{1,0:T(8,128)(2,1)}, bf16[192,384]{1,0:T(8,128)(2,1)S(1)}, u32[]{:S(2)}, u32[]{:S(2)}) collective-permute-start(bf16[192,384]{1,0:T(8,128)(2,1)} %get-tuple-element.32), channel_id=1, source_target_pairs={{0,1},{1,0},{2,3},{3,2},{4,5},{5,4},{6,7},{7,6},{8,9},{9,8},{10,11... | collective-permute-start | bytes 442376 | tf_op jit(solution)/shard_map/ppermute | solution.py:296
  16.8 1.7 %copy-start.1 = (bf16[768,1536]{1,0:T(8,128)(2,1)S(1)}, bf16[768,1536]{1,0:T(8,128)(2,1)}, u32[]{:S(2)}) copy-start(bf16[768,1536]{1,0:T(8,128)(2,1)} %refs_6_.3) | copy-start | bytes 7077892
  18.5 4.8 %copy-start.2 = (bf16[768,1536]{1,0:T(8,128)(2,1)S(1)}, bf16[768,1536]{1,0:T(8,128)(2,1)}, u32[]{:S(2)}) copy-start(bf16[768,1536]{1,0:T(8,128)(2,1)} %refs_6_.3) | copy-start | bytes 7077892
  18.5 4.8 %copy-start.5 = (bf16[192,384]{1,0:T(8,128)(2,1)S(1)}, bf16[192,384]{1,0:T(8,128)(2,1)}, u32[]{:S(2)}) copy-start(bf16[192,384]{1,0:T(8,128)(2,1)} %get-tuple-element.31.refs_0_) | copy-start | bytes 442372
  21.1 6.7 %collective-permute-start.5 = (bf16[192,384]{1,0:T(8,128)(2,1)S(1)}, bf16[192,384]{1,0:T(8,128)(2,1)S(1)}, u32[]{:S(2)}, u32[]{:S(2)}) collective-permute-start(bf16[192,384]{1,0:T(8,128)(2,1)S(1)} %get-tuple-element.26), channel_id=1, source_target_pairs={{0,2},{1,3},{2,0},{3,1},{4,6},{5,7},{6,4},{7,5},{8,10},{9,11},{10,... | collective-permute-start | bytes 442376 | tf_op jit(solution)/shard_map/ppermute | solution.py:293
  21.5 7.6 %collective-permute-start.6 = (bf16[192,384]{1,0:T(8,128)(2,1)S(1)}, bf16[192,384]{1,0:T(8,128)(2,1)S(1)}, u32[]{:S(2)}, u32[]{:S(2)}) collective-permute-start(bf16[192,384]{1,0:T(8,128)(2,1)S(1)} %get-tuple-element.27), channel_id=1, source_target_pairs={{0,1},{1,0},{2,3},{3,2},{4,5},{5,4},{6,7},{7,6},{8,9},{9,8},{10,11... | collective-permute-start | bytes 442376 | tf_op jit(solution)/shard_map/ppermute | solution.py:296
  21.7 8.4 %collective-permute-start.7 = (bf16[192,384]{1,0:T(8,128)(2,1)S(1)}, bf16[192,384]{1,0:T(8,128)(2,1)S(1)}, u32[]{:S(2)}, u32[]{:S(2)}) collective-permute-start(bf16[192,384]{1,0:T(8,128)(2,1)S(1)} %get-tuple-element.28), channel_id=1, source_target_pairs={{0,3},{1,2},{2,1},{3,0},{4,7},{5,6},{6,5},{7,4},{8,11},{9,10},{10,... | collective-permute-start | bytes 442376 | tf_op jit(solution)/shard_map/ppermute | solution.py:293
  23.3 6.8 %copy-start.3 = (bf16[1536,384]{1,0:T(8,128)(2,1)S(1)}, bf16[1536,384]{1,0:T(8,128)(2,1)}, u32[]{:S(2)}) copy-start(bf16[1536,384]{1,0:T(8,128)(2,1)} %frames_ref.2) | copy-start | bytes 3538948
  23.3 6.8 %copy-start.9 = (s32[384]{0:T(512)S(1)}, s32[384]{0:T(512)}, u32[]{:S(2)}) copy-start(s32[384]{0:T(512)} %get-tuple-element.22.wanted_ref) | copy-start | bytes 4612
  26.9 7.2 %collective-permute-start.11 = (bf16[192,384]{1,0:T(8,128)(2,1)S(1)}, bf16[192,384]{1,0:T(8,128)(2,1)S(1)}, u32[]{:S(2)}, u32[]{:S(2)}) collective-permute-start(bf16[192,384]{1,0:T(8,128)(2,1)S(1)} %get-tuple-element.39), channel_id=1, source_target_pairs={{0,2},{1,3},{2,0},{3,1},{4,6},{5,7},{6,4},{7,5},{8,10},{9,11},{10,... | collective-permute-start | bytes 442376 | tf_op jit(solution)/shard_map/ppermute | solution.py:293
  27.4 6.7 %collective-permute-start.12 = (bf16[192,384]{1,0:T(8,128)(2,1)S(1)}, bf16[192,384]{1,0:T(8,128)(2,1)S(1)}, u32[]{:S(2)}, u32[]{:S(2)}) collective-permute-start(bf16[192,384]{1,0:T(8,128)(2,1)S(1)} %get-tuple-element.40), channel_id=1, source_target_pairs={{0,1},{1,0},{2,3},{3,2},{4,5},{5,4},{6,7},{7,6},{8,9},{9,8},{10,11... | collective-permute-start | bytes 442376 | tf_op jit(solution)/shard_map/ppermute | solution.py:296
  27.8 8.7 %collective-permute-start.13 = (bf16[192,384]{1,0:T(8,128)(2,1)S(1)}, bf16[192,384]{1,0:T(8,128)(2,1)S(1)}, u32[]{:S(2)}, u32[]{:S(2)}) collective-permute-start(bf16[192,384]{1,0:T(8,128)(2,1)S(1)} %get-tuple-element.41), channel_id=1, source_target_pairs={{0,3},{1,2},{2,1},{3,0},{4,7},{5,6},{6,5},{7,4},{8,11},{9,10},{10,... | collective-permute-start | bytes 442376 | tf_op jit(solution)/shard_map/ppermute | solution.py:293
  30.1 6.3 %copy-start.4 = (bf16[1536,384]{1,0:T(8,128)(2,1)S(1)}, bf16[1536,384]{1,0:T(8,128)(2,1)}, u32[]{:S(2)}) copy-start(bf16[1536,384]{1,0:T(8,128)(2,1)} %frames_ref.3) | copy-start | bytes 3538948

commit v5 on v4

--- a/solution.py
+++ b/solution.py
@@ -322,7 +322,7 @@
     mine, sib, wanted = gather_rows(picked_count, picked_rows, frames, 1)
     blocks = collect(mine, sib)
     cot_mine, cot_sib, _ = gather_rows(picked_count, picked_rows, cotangent, 1)
-    cot_mine, cot_sib = lax.optimization_barrier((cot_mine, cot_sib, blocks[2]))[:2]
+    cot_mine, cot_sib = lax.optimization_barrier((cot_mine, cot_sib, blocks[1], up_sib, down_sib))[:2]
     cot_blocks = collect(cot_mine, cot_sib)
     parts, saved = forward(joined(blocks), ways, weights, gain, router)
     out_mine, out_sib = deliver(cut(parts))

time: 38.3 us -> 36.4 us (0.950)
  starting transfers between devices: 11.6 us -> 10.3 us
  waiting for transfers between devices: 8.61 us -> 8 us
    ppermute x8, starting transfers between devices: 10.7 us -> 8.23 us  [send(): return lax.ppermute(x, ('tensor', 'pair'), pairs)]
    ppermute x6, starting transfers between devices: 0.98 us -> 2.12 us  [swap(): return lax.ppermute(x, 'pair', [(0, 1), (1, 0)])]
    ppermute x8, waiting for transfers between devices: 8.6 us -> 7.98 us  [send(): return lax.ppermute(x, ('tensor', 'pair'), pairs)]
  transfers between devices with their start and end apart: 14 -> 14, of which waited for: 6 -> 4; matrix products, arithmetic and copies ran while one was open for 0% -> 0% of each run, Pallas kernels for 36% -> 38%
where the time goes in v5:
time: 36.4 us; the launch traced here: 36.3 us
  Pallas kernels  15.4 us (42%)
  starting transfers between devices  10.3 us (28%)
  waiting for transfers between devices  8 us (22%)
  local copies, waits for them, and re-layouts  1.7 us (5%)
  between operations  0.77 us (2%)
    ppermute x8, starting transfers between devices, send(): return lax.ppermute(x, ('tensor', 'pair'), pairs)  8.23 us
    ppermute x8, waiting for transfers between devices, send(): return lax.ppermute(x, ('tensor', 'pair'), pairs)  7.98 us
    pallas_call x2, Pallas kernels, call(): pl.pallas_call(body, out_shape=outs, in_specs=specs, out_specs=jax.tree.m...  6.17 us
    pallas_call x2, Pallas kernels, call_in_hbm(): pl.pallas_call(body, out_shape=outs, in_specs=[ANY] * len(ins), out_specs...  5.9 us
    pallas_call x2, Pallas kernels, scatter_rows(): pl.pallas_call(functools.partial(scatter_body, len(mine_parts), len(sib_p...  3.36 us
    ppermute x6, starting transfers between devices, swap(): return lax.ppermute(x, 'pair', [(0, 1), (1, 0)])  2.12 us
    unnamed x20, local copies, waits for them, and re-layouts  1.7 us
  transfers between devices with their start and end apart: 14, of which 4 were waited for; matrix products, arithmetic and copies ran while one was open for 0% of the time, Pallas kernels for 38%

profile of v5, /device:TPU:0, one launch (start us, length us, event | category | flops | bytes accessed | tf_op | source)
XLA Modules:
  0.0 36.3 jit_solution(14960859565073102335)
XLA Ops:
  0.6 0.5 %collective-permute-start.3 = (bf16[1536,768]{1,0:T(8,128)(2,1)}, bf16[1536,768]{1,0:T(8,128)(2,1)S(1)}, u32[]{:S(2)}, u32[]{:S(2)}) collective-permute-start(bf16[1536,768]{1,0:T(8,128)(2,1)} %refs_4_.3), channel_id=1, source_target_pairs={{0,1},{1,0},{2,3},{3,2},{4,5},{5,4},{6,7},{7,6},{8,9},{9,8},{10,11... | collective-permute-start | bytes 7077896 | tf_op jit(solution)/shard_map/ppermute | solution.py:296
  1.1 0.1 collective-permute-start.4
  1.2 0.0 copy-start
  1.2 3.0 %gather_rows.2 = (bf16[192,384]{1,0:T(8,128)(2,1)}, bf16[192,384]{1,0:T(8,128)(2,1)}, s32[384]{0:T(512)}) custom-call(s32[4]{0:T(128)} %count_hbm.3, s32[384]{0:T(512)} %picked_hbm.3, bf16[1536,384]{1,0:T(8,128)(2,1)} %frames_ref.2), custom_call_target="tpu_custom_call" | custom-call | flops 452984832 | bytes 1 | tf_op jit(solution)/shard_map/gather_rows/pallas_call | solution.py:48
  4.3 0.0 copy-start.6
  4.3 0.0 copy-start.7
  4.3 0.0 copy-start.8
  4.3 0.5 %collective-permute-start = (bf16[192,384]{1,0:T(8,128)(2,1)}, bf16[192,384]{1,0:T(8,128)(2,1)S(1)}, u32[]{:S(2)}, u32[]{:S(2)}) collective-permute-start(bf16[192,384]{1,0:T(8,128)(2,1)} %get-tuple-element.24), channel_id=1, source_target_pairs={{0,1},{1,0},{2,3},{3,2},{4,5},{5,4},{6,7},{7,6},{8,9},{9,8},{10,11... | collective-permute-start | bytes 442376 | tf_op jit(solution)/shard_map/ppermute | solution.py:296
  4.8 2.6 %collective-permute-start.1 = (bf16[192,384]{1,0:T(8,128)(2,1)}, bf16[192,384]{1,0:T(8,128)(2,1)S(1)}, u32[]{:S(2)}, u32[]{:S(2)}) collective-permute-start(bf16[192,384]{1,0:T(8,128)(2,1)} %get-tuple-element.23.refs_0_), channel_id=1, source_target_pairs={{0,2},{1,3},{2,0},{3,1},{4,6},{5,7},{6,4},{7,5},{8,10},{9,11},{10,... | collective-permute-start | bytes 442376 | tf_op jit(solution)/shard_map/ppermute | solution.py:293
  7.4 0.1 collective-permute-start.2
  7.4 2.9 %gather_rows.3 = (bf16[192,384]{1,0:T(8,128)(2,1)}, bf16[192,384]{1,0:T(8,128)(2,1)}, s32[384]{0:T(512)}) custom-call(s32[4]{0:T(128)} %count_hbm.3, s32[384]{0:T(512)} %picked_hbm.3, bf16[1536,384]{1,0:T(8,128)(2,1)} %frames_ref.3), custom_call_target="tpu_custom_call" | custom-call | flops 452984832 | bytes 1 | tf_op jit(solution)/shard_map/gather_rows/pallas_call | solution.py:48
  10.3 0.0 collective-permute-done.refs_1_
  10.3 0.0 collective-permute-done.3.refs_5_
  10.3 0.0 collective-permute-done.4.refs_7_
  10.3 1.8 %collective-permute-start.9 = (bf16[192,384]{1,0:T(8,128)(2,1)}, bf16[192,384]{1,0:T(8,128)(2,1)S(1)}, u32[]{:S(2)}, u32[]{:S(2)}) collective-permute-start(bf16[192,384]{1,0:T(8,128)(2,1)} %get-tuple-element.31.refs_0_), channel_id=1, source_target_pairs={{0,2},{1,3},{2,0},{3,1},{4,6},{5,7},{6,4},{7,5},{8,10},{9,11},{10,... | collective-permute-start | bytes 442376 | tf_op jit(solution)/shard_map/ppermute | solution.py:293
  12.1 0.0 collective-permute-start.10
  12.2 0.4 %collective-permute-start.8 = (bf16[192,384]{1,0:T(8,128)(2,1)}, bf16[192,384]{1,0:T(8,128)(2,1)S(1)}, u32[]{:S(2)}, u32[]{:S(2)}) collective-permute-start(bf16[192,384]{1,0:T(8,128)(2,1)} %get-tuple-element.32), channel_id=1, source_target_pairs={{0,1},{1,0},{2,3},{3,2},{4,5},{5,4},{6,7},{7,6},{8,9},{9,8},{10,11... | collective-permute-start | bytes 442376 | tf_op jit(solution)/shard_map/ppermute | solution.py:296
  12.6 0.0 collective-permute-done.1.refs_2_
  12.6 2.4 %collective-permute-done.2.refs_3_ = bf16[192,384]{1,0:T(8,128)(2,1)S(1)} collective-permute-done((bf16[192,384]{1,0:T(8,128)(2,1)}, bf16[192,384]{1,0:T(8,128)(2,1)S(1)}, u32[]{:S(2)}, u32[]{:S(2)}) %collective-permute-start.2) | collective-permute-done | bytes 147488 | tf_op jit(solution)/shard_map/ppermute | solution.py:293
  15.0 0.0 copy-done
  15.0 0.0 copy-done.6
  15.0 0.0 copy-done.7
  15.0 0.0 copy-done.8
  15.0 0.0 copy-start.1
  15.0 1.7 %copy-done.1 = bf16[768,1536]{1,0:T(8,128)(2,1)S(1)} copy-done((bf16[768,1536]{1,0:T(8,128)(2,1)S(1)}, bf16[768,1536]{1,0:T(8,128)(2,1)}, u32[]{:S(2)}) %copy-start.1) | copy-done | bytes 2359320
  16.7 0.0 copy-start.2
  16.7 0.0 copy-start.5
  16.7 2.6 %forward.1 = (bf16[192,384]{1,0:T(8,128)(2,1)S(1)}, bf16[192,384]{1,0:T(8,128)(2,1)S(1)}, bf16[192,384]{1,0:T(8,128)(2,1)S(1)}, bf16[192,384]{1,0:T(8,128)(2,1)S...) custom-call(bf16[192,384]{1,0:T(8,128)(2,1)S(1)} %copy-done.6, ...), custom_call_target="tpu_custom_call" | custom-call | flops 1 | bytes 1 | tf_op jit(solution)/shard_map/forward/pallas_call | solution.py:23
  19.2 1.5 %collective-permute-start.5 = (bf16[192,384]{1,0:T(8,128)(2,1)S(1)}, bf16[192,384]{1,0:T(8,128)(2,1)S(1)}, u32[]{:S(2)}, u32[]{:S(2)}) collective-permute-start(bf16[192,384]{1,0:T(8,128)(2,1)S(1)} %get-tuple-element.26), channel_id=1, source_target_pairs={{0,2},{1,3},{2,0},{3,1},{4,6},{5,7},{6,4},{7,5},{8,10},{9,11},{10,... | collective-permute-start | bytes 442376 | tf_op jit(solution)/shard_map/ppermute | solution.py:293
  20.8 0.4 %collective-permute-start.6 = (bf16[192,384]{1,0:T(8,128)(2,1)S(1)}, bf16[192,384]{1,0:T(8,128)(2,1)S(1)}, u32[]{:S(2)}, u32[]{:S(2)}) collective-permute-start(bf16[192,384]{1,0:T(8,128)(2,1)S(1)} %get-tuple-element.27), channel_id=1, source_target_pairs={{0,1},{1,0},{2,3},{3,2},{4,5},{5,4},{6,7},{7,6},{8,9},{9,8},{10,11... | collective-permute-start | bytes 442376 | tf_op jit(solution)/shard_map/ppermute | solution.py:296
  21.2 0.0 collective-permute-done.9.refs_2_
  21.2 0.2 collective-permute-start.7
  21.5 0.0 collective-permute-done.10.refs_3_
  21.5 0.0 collective-permute-done.8.refs_1_
  21.5 0.0 copy-done.2
  21.5 0.0 copy-done.5
  21.5 0.0 copy-start.3
  21.5 0.0 copy-start.9
  21.5 3.6 %backward.1 = (bf16[192,384]{1,0:T(8,128)(2,1)S(1)}, bf16[192,384]{1,0:T(8,128)(2,1)S(1)}, bf16[192,384]{1,0:T(8,128)(2,1)S(1)}, bf16[192,384]{1,0:T(8,128)(2,1)S(1)}) custom-call(bf16[192,384]{1,0:T(8,128)(2,1)S(1)} %copy-done.5, bf16[192,384]{1,0:T(8,128)(2,1)S(1)} %collective-permute-done.8.refs_1_, bf16[192,384]{1,0:T(8,128)(2,1)S(1)} %collective-permute-done.9.refs_2_, ...), custom_call_target="tpu_custom_call" | custom-call | flops 1 | bytes 1 | tf_op jit(solution)/shard_map/backward/pallas_call | solution.py:23
  25.1 1.5 %collective-permute-start.11 = (bf16[192,384]{1,0:T(8,128)(2,1)S(1)}, bf16[192,384]{1,0:T(8,128)(2,1)S(1)}, u32[]{:S(2)}, u32[]{:S(2)}) collective-permute-start(bf16[192,384]{1,0:T(8,128)(2,1)S(1)} %get-tuple-element.39), channel_id=1, source_target_pairs={{0,2},{1,3},{2,0},{3,1},{4,6},{5,7},{6,4},{7,5},{8,10},{9,11},{10,... | collective-permute-start | bytes 442376 | tf_op jit(solution)/shard_map/ppermute | solution.py:293
  26.6 0.2 collective-permute-start.12
  26.8 0.0 collective-permute-done.5.refs_1_
  26.8 0.5 %collective-permute-start.13 = (bf16[192,384]{1,0:T(8,128)(2,1)S(1)}, bf16[192,384]{1,0:T(8,128)(2,1)S(1)}, u32[]{:S(2)}, u32[]{:S(2)}) collective-permute-start(bf16[192,384]{1,0:T(8,128)(2,1)S(1)} %get-tuple-element.41), channel_id=1, source_target_pairs={{0,3},{1,2},{2,1},{3,0},{4,7},{5,6},{6,5},{7,4},{8,11},{9,10},{10,... | collective-permute-start | bytes 442376 | tf_op jit(solution)/shard_map/ppermute | solution.py:293
  27.3 0.0 collective-permute-done.6.refs_2_
  27.3 0.9 %collective-permute-done.7.refs_3_ = bf16[192,384]{1,0:T(8,128)(2,1)S(1)} collective-permute-done((bf16[192,384]{1,0:T(8,128)(2,1)S(1)}, bf16[192,384]{1,0:T(8,128)(2,1)S(1)}, u32[]{:S(2)}, u32[]{:S(2)}) %collective-permute-start.7) | collective-permute-done | bytes 147488 | tf_op jit(solution)/shard_map/ppermute | solution.py:293
  28.2 0.0 copy-done.3
  28.2 0.0 copy-done.9
  28.3 0.0 copy-start.4
  28.3 1.7 %mixed_rows.1 = bf16[1536,384]{1,0:T(8,128)(2,1)} custom-call(s32[384]{0:T(512)S(1)} %copy-done.9, bf16[1536,384]{1,0:T(8,128)(2,1)S(1)} %copy-done.3, bf16[192,384]{1,0:T(8,128)(2,1)S(1)} %get-tuple-element.25.refs_0_, bf16[192,384]{1,0:T(8,128)(2,1)S(1)} %collective-permute-done.5.refs_1_, bf16[192,384]{1,0:T(8,128)(2,1)S(1)} %collective-permute-done.6.refs_2_, ...), custom_call_target="tpu_custom_call" | custom-call | flops 452984832 | bytes 2359296 | tf_op jit(solution)/shard_map/mixed_rows/pallas_call | solution.py:137
  29.9 2.3 %collective-permute-done.11.refs_1_ = bf16[192,384]{1,0:T(8,128)(2,1)S(1)} collective-permute-done((bf16[192,384]{1,0:T(8,128)(2,1)S(1)}, bf16[192,384]{1,0:T(8,128)(2,1)S(1)}, u32[]{:S(2)}, u32[]{:S(2)}) %collective-permute-start.11) | collective-permute-done | bytes 147488 | tf_op jit(solution)/shard_map/ppermute | solution.py:293
  32.3 0.0 collective-permute-done.12.refs_2_
  32.3 2.3 %collective-permute-done.13.refs_3_ = bf16[192,384]{1,0:T(8,128)(2,1)S(1)} collective-permute-done((bf16[192,384]{1,0:T(8,128)(2,1)S(1)}, bf16[192,384]{1,0:T(8,128)(2,1)S(1)}, u32[]{:S(2)}, u32[]{:S(2)}) %collective-permute-start.13) | collective-permute-done | bytes 147488 | tf_op jit(solution)/shard_map/ppermute | solution.py:293
  34.6 0.0 copy-done.4
  34.6 1.7 %grad_rows.1 = bf16[1536,384]{1,0:T(8,128)(2,1)} custom-call(s32[384]{0:T(512)S(1)} %copy-done.9, bf16[1536,384]{1,0:T(8,128)(2,1)S(1)} %copy-done.4, bf16[192,384]{1,0:T(8,128)(2,1)S(1)} %get-tuple-element.38.refs_0_, bf16[192,384]{1,0:T(8,128)(2,1)S(1)} %collective-permute-done.11.refs_1_, bf16[192,384]{1,0:T(8,128)(2,1)S(1)} %collective-permute-done.12.refs_2_, ...), custom_call_target="tpu_custom_call" | custom-call | flops 452984832 | bytes 2359296 | tf_op jit(solution)/shard_map/grad_rows/pallas_call | solution.py:137
Async XLA Ops:
  0.6 9.7 %collective-permute-start.3 = (bf16[1536,768]{1,0:T(8,128)(2,1)}, bf16[1536,768]{1,0:T(8,128)(2,1)S(1)}, u32[]{:S(2)}, u32[]{:S(2)}) collective-permute-start(bf16[1536,768]{1,0:T(8,128)(2,1)} %refs_4_.3), channel_id=1, source_target_pairs={{0,1},{1,0},{2,3},{3,2},{4,5},{5,4},{6,7},{7,6},{8,9},{9,8},{10,11... | collective-permute-start | bytes 7077896 | tf_op jit(solution)/shard_map/ppermute | solution.py:296
  1.1 9.2 %collective-permute-start.4 = (bf16[768,1536]{1,0:T(8,128)(2,1)}, bf16[768,1536]{1,0:T(8,128)(2,1)S(1)}, u32[]{:S(2)}, u32[]{:S(2)}) collective-permute-start(bf16[768,1536]{1,0:T(8,128)(2,1)} %refs_6_.3), channel_id=1, source_target_pairs={{0,1},{1,0},{2,3},{3,2},{4,5},{5,4},{6,7},{7,6},{8,9},{9,8},{10,11... | collective-permute-start | bytes 7077896 | tf_op jit(solution)/shard_map/ppermute | solution.py:296
  1.2 13.8 %copy-start = (bf16[1536,768]{1,0:T(8,128)(2,1)S(1)}, bf16[1536,768]{1,0:T(8,128)(2,1)}, u32[]{:S(2)}) copy-start(bf16[1536,768]{1,0:T(8,128)(2,1)} %refs_4_.3) | copy-start | bytes 7077892
  4.3 10.7 %copy-start.6 = (bf16[192,384]{1,0:T(8,128)(2,1)S(1)}, bf16[192,384]{1,0:T(8,128)(2,1)}, u32[]{:S(2)}) copy-start(bf16[192,384]{1,0:T(8,128)(2,1)} %get-tuple-element.23.refs_0_) | copy-start | bytes 442372
  4.3 10.7 %copy-start.7 = (f32[1536]{0:T(1024)S(1)}, f32[1536]{0:T(1024)}, u32[]{:S(2)}) copy-start(f32[1536]{0:T(1024)} %refs_8_.3) | copy-start | bytes 18436
  4.3 10.7 %copy-start.8 = (f32[1536]{0:T(1024)S(1)}, f32[1536]{0:T(1024)}, u32[]{:S(2)}) copy-start(f32[1536]{0:T(1024)} %refs_9_.3) | copy-start | bytes 18436
  4.3 6.0 %collective-permute-start = (bf16[192,384]{1,0:T(8,128)(2,1)}, bf16[192,384]{1,0:T(8,128)(2,1)S(1)}, u32[]{:S(2)}, u32[]{:S(2)}) collective-permute-start(bf16[192,384]{1,0:T(8,128)(2,1)} %get-tuple-element.24), channel_id=1, source_target_pairs={{0,1},{1,0},{2,3},{3,2},{4,5},{5,4},{6,7},{7,6},{8,9},{9,8},{10,11... | collective-permute-start | bytes 442376 | tf_op jit(solution)/shard_map/ppermute | solution.py:296
  4.8 7.8 %collective-permute-start.1 = (bf16[192,384]{1,0:T(8,128)(2,1)}, bf16[192,384]{1,0:T(8,128)(2,1)S(1)}, u32[]{:S(2)}, u32[]{:S(2)}) collective-permute-start(bf16[192,384]{1,0:T(8,128)(2,1)} %get-tuple-element.23.refs_0_), channel_id=1, source_target_pairs={{0,2},{1,3},{2,0},{3,1},{4,6},{5,7},{6,4},{7,5},{8,10},{9,11},{10,... | collective-permute-start | bytes 442376 | tf_op jit(solution)/shard_map/ppermute | solution.py:293
  7.4 7.6 %collective-permute-start.2 = (bf16[192,384]{1,0:T(8,128)(2,1)}, bf16[192,384]{1,0:T(8,128)(2,1)S(1)}, u32[]{:S(2)}, u32[]{:S(2)}) collective-permute-start(bf16[192,384]{1,0:T(8,128)(2,1)} %get-tuple-element.24), channel_id=1, source_target_pairs={{0,3},{1,2},{2,1},{3,0},{4,7},{5,6},{6,5},{7,4},{8,11},{9,10},{10,... | collective-permute-start | bytes 442376 | tf_op jit(solution)/shard_map/ppermute | solution.py:293
  10.3 10.9 %collective-permute-start.9 = (bf16[192,384]{1,0:T(8,128)(2,1)}, bf16[192,384]{1,0:T(8,128)(2,1)S(1)}, u32[]{:S(2)}, u32[]{:S(2)}) collective-permute-start(bf16[192,384]{1,0:T(8,128)(2,1)} %get-tuple-element.31.refs_0_), channel_id=1, source_target_pairs={{0,2},{1,3},{2,0},{3,1},{4,6},{5,7},{6,4},{7,5},{8,10},{9,11},{10,... | collective-permute-start | bytes 442376 | tf_op jit(solution)/shard_map/ppermute | solution.py:293
  12.1 9.3 %collective-permute-start.10 = (bf16[192,384]{1,0:T(8,128)(2,1)}, bf16[192,384]{1,0:T(8,128)(2,1)S(1)}, u32[]{:S(2)}, u32[]{:S(2)}) collective-permute-start(bf16[192,384]{1,0:T(8,128)(2,1)} %get-tuple-element.32), channel_id=1, source_target_pairs={{0,3},{1,2},{2,1},{3,0},{4,7},{5,6},{6,5},{7,4},{8,11},{9,10},{10,... | collective-permute-start | bytes 442376 | tf_op jit(solution)/shard_map/ppermute | solution.py:293
  12.2 9.3 %collective-permute-start.8 = (bf16[192,384]{1,0:T(8,128)(2,1)}, bf16[192,384]{1,0:T(8,128)(2,1)S(1)}, u32[]{:S(2)}, u32[]{:S(2)}) collective-permute-start(bf16[192,384]{1,0:T(8,128)(2,1)} %get-tuple-element.32), channel_id=1, source_target_pairs={{0,1},{1,0},{2,3},{3,2},{4,5},{5,4},{6,7},{7,6},{8,9},{9,8},{10,11... | collective-permute-start | bytes 442376 | tf_op jit(solution)/shard_map/ppermute | solution.py:296
  15.0 1.7 %copy-start.1 = (bf16[768,1536]{1,0:T(8,128)(2,1)S(1)}, bf16[768,1536]{1,0:T(8,128)(2,1)}, u32[]{:S(2)}) copy-start(bf16[768,1536]{1,0:T(8,128)(2,1)} %refs_6_.3) | copy-start | bytes 7077892
  16.7 4.8 %copy-start.2 = (bf16[768,1536]{1,0:T(8,128)(2,1)S(1)}, bf16[768,1536]{1,0:T(8,128)(2,1)}, u32[]{:S(2)}) copy-start(bf16[768,1536]{1,0:T(8,128)(2,1)} %refs_6_.3) | copy-start | bytes 7077892
  16.7 4.8 %copy-start.5 = (bf16[192,384]{1,0:T(8,128)(2,1)S(1)}, bf16[192,384]{1,0:T(8,128)(2,1)}, u32[]{:S(2)}) copy-start(bf16[192,384]{1,0:T(8,128)(2,1)} %get-tuple-element.31.refs_0_) | copy-start | bytes 442372
  19.2 7.6 %collective-permute-start.5 = (bf16[192,384]{1,0:T(8,128)(2,1)S(1)}, bf16[192,384]{1,0:T(8,128)(2,1)S(1)}, u32[]{:S(2)}, u32[]{:S(2)}) collective-permute-start(bf16[192,384]{1,0:T(8,128)(2,1)S(1)} %get-tuple-element.26), channel_id=1, source_target_pairs={{0,2},{1,3},{2,0},{3,1},{4,6},{5,7},{6,4},{7,5},{8,10},{9,11},{10,... | collective-permute-start | bytes 442376 | tf_op jit(solution)/shard_map/ppermute | solution.py:293
  20.8 6.5 %collective-permute-start.6 = (bf16[192,384]{1,0:T(8,128)(2,1)S(1)}, bf16[192,384]{1,0:T(8,128)(2,1)S(1)}, u32[]{:S(2)}, u32[]{:S(2)}) collective-permute-start(bf16[192,384]{1,0:T(8,128)(2,1)S(1)} %get-tuple-element.27), channel_id=1, source_target_pairs={{0,1},{1,0},{2,3},{3,2},{4,5},{5,4},{6,7},{7,6},{8,9},{9,8},{10,11... | collective-permute-start | bytes 442376 | tf_op jit(solution)/shard_map/ppermute | solution.py:296
  21.2 7.0 %collective-permute-start.7 = (bf16[192,384]{1,0:T(8,128)(2,1)S(1)}, bf16[192,384]{1,0:T(8,128)(2,1)S(1)}, u32[]{:S(2)}, u32[]{:S(2)}) collective-permute-start(bf16[192,384]{1,0:T(8,128)(2,1)S(1)} %get-tuple-element.28), channel_id=1, source_target_pairs={{0,3},{1,2},{2,1},{3,0},{4,7},{5,6},{6,5},{7,4},{8,11},{9,10},{10,... | collective-permute-start | bytes 442376 | tf_op jit(solution)/shard_map/ppermute | solution.py:293
  21.5 6.8 %copy-start.3 = (bf16[1536,384]{1,0:T(8,128)(2,1)S(1)}, bf16[1536,384]{1,0:T(8,128)(2,1)}, u32[]{:S(2)}) copy-start(bf16[1536,384]{1,0:T(8,128)(2,1)} %frames_ref.2) | copy-start | bytes 3538948
  21.5 6.8 %copy-start.9 = (s32[384]{0:T(512)S(1)}, s32[384]{0:T(512)}, u32[]{:S(2)}) copy-start(s32[384]{0:T(512)} %get-tuple-element.22.wanted_ref) | copy-start | bytes 4612
  25.1 7.2 %collective-permute-start.11 = (bf16[192,384]{1,0:T(8,128)(2,1)S(1)}, bf16[192,384]{1,0:T(8,128)(2,1)S(1)}, u32[]{:S(2)}, u32[]{:S(2)}) collective-permute-start(bf16[192,384]{1,0:T(8,128)(2,1)S(1)} %get-tuple-element.39), channel_id=1, source_target_pairs={{0,2},{1,3},{2,0},{3,1},{4,6},{5,7},{6,4},{7,5},{8,10},{9,11},{10,... | collective-permute-start | bytes 442376 | tf_op jit(solution)/shard_map/ppermute | solution.py:293
  26.6 5.7 %collective-permute-start.12 = (bf16[192,384]{1,0:T(8,128)(2,1)S(1)}, bf16[192,384]{1,0:T(8,128)(2,1)S(1)}, u32[]{:S(2)}, u32[]{:S(2)}) collective-permute-start(bf16[192,384]{1,0:T(8,128)(2,1)S(1)} %get-tuple-element.40), channel_id=1, source_target_pairs={{0,1},{1,0},{2,3},{3,2},{4,5},{5,4},{6,7},{7,6},{8,9},{9,8},{10,11... | collective-permute-start | bytes 442376 | tf_op jit(solution)/shard_map/ppermute | solution.py:296
  26.8 7.7 %collective-permute-start.13 = (bf16[192,384]{1,0:T(8,128)(2,1)S(1)}, bf16[192,384]{1,0:T(8,128)(2,1)S(1)}, u32[]{:S(2)}, u32[]{:S(2)}) collective-permute-start(bf16[192,384]{1,0:T(8,128)(2,1)S(1)} %get-tuple-element.41), channel_id=1, source_target_pairs={{0,3},{1,2},{2,1},{3,0},{4,7},{5,6},{6,5},{7,4},{8,11},{9,10},{10,... | collective-permute-start | bytes 442376 | tf_op jit(solution)/shard_map/ppermute | solution.py:293
  28.3 6.3 %copy-start.4 = (bf16[1536,384]{1,0:T(8,128)(2,1)S(1)}, bf16[1536,384]{1,0:T(8,128)(2,1)}, u32[]{:S(2)}) copy-start(bf16[1536,384]{1,0:T(8,128)(2,1)} %frames_ref.3) | copy-start | bytes 3538948

commit v6 on v5

--- a/solution.py
+++ b/solution.py
@@ -317,12 +317,12 @@
         far_sib = [send(x, k, 1) for x, k in zip(parts[2 + count :], steps)]
         return [parts[0]] + far_mine, [swap(parts[1])] + far_sib
 
-    up_sib, down_sib = swap(up_weight), swap(down_weight)
-    weights = (up_weight, up_sib, down_weight, down_sib)
     mine, sib, wanted = gather_rows(picked_count, picked_rows, frames, 1)
     blocks = collect(mine, sib)
+    up_sib, down_sib = swap(after(up_weight, mine)), swap(after(down_weight, mine))
+    weights = (up_weight, up_sib, down_weight, down_sib)
     cot_mine, cot_sib, _ = gather_rows(picked_count, picked_rows, cotangent, 1)
-    cot_mine, cot_sib = lax.optimization_barrier((cot_mine, cot_sib, blocks[1], up_sib, down_sib))[:2]
+    cot_mine, cot_sib = lax.optimization_barrier((cot_mine, cot_sib, up_sib))[:2]
     cot_blocks = collect(cot_mine, cot_sib)
     parts, saved = forward(joined(blocks), ways, weights, gain, router)
     out_mine, out_sib = deliver(cut(parts))

time: 36.4 us -> 35.7 us (0.981)
  waiting for transfers between devices: 8 us -> 6.24 us
  starting transfers between devices: 10.3 us -> 11.2 us
    ppermute x8, starting transfers between devices: 8.23 us -> 10 us  [send(): return lax.ppermute(x, ('tensor', 'pair'), pairs)]
    ppermute x8, waiting for transfers between devices: 7.98 us -> 6.22 us  [send(): return lax.ppermute(x, ('tensor', 'pair'), pairs)]
    ppermute x6, starting transfers between devices: 2.12 us -> 1.2 us  [swap(): return lax.ppermute(x, 'pair', [(0, 1), (1, 0)])]
  transfers between devices with their start and end apart: 14 -> 14, of which waited for: 4 -> 3; matrix products, arithmetic and copies ran while one was open for 0% -> 0% of each run, Pallas kernels for 38% -> 30%
where the time goes in v6:
time: 35.7 us; the launch traced here: 35.4 us
  Pallas kernels  15.4 us (43%)
  starting transfers between devices  11.2 us (31%)
  waiting for transfers between devices  6.24 us (17%)
  local copies, waits for them, and re-layouts  1.71 us (5%)
  between operations  0.8 us (2%)
    ppermute x8, starting transfers between devices, send(): return lax.ppermute(x, ('tensor', 'pair'), pairs)  10 us
    ppermute x8, waiting for transfers between devices, send(): return lax.ppermute(x, ('tensor', 'pair'), pairs)  6.22 us
    pallas_call x2, Pallas kernels, call(): pl.pallas_call(body, out_shape=outs, in_specs=specs, out_specs=jax.tree.m...  6.13 us
    pallas_call x2, Pallas kernels, call_in_hbm(): pl.pallas_call(body, out_shape=outs, in_specs=[ANY] * len(ins), out_specs...  5.91 us
    pallas_call x2, Pallas kernels, scatter_rows(): pl.pallas_call(functools.partial(scatter_body, len(mine_parts), len(sib_p...  3.36 us
    unnamed x20, local copies, waits for them, and re-layouts  1.71 us
    ppermute x6, starting transfers between devices, swap(): return lax.ppermute(x, 'pair', [(0, 1), (1, 0)])  1.2 us
  transfers between devices with their start and end apart: 14, of which 3 were waited for; matrix products, arithmetic and copies ran while one was open for 0% of the time, Pallas kernels for 30%

profile of v6, /device:TPU:0, one launch (start us, length us, event | category | flops | bytes accessed | tf_op | source)
XLA Modules:
  0.0 35.4 jit_solution(16557909599778164460)
XLA Ops:
  0.6 0.0 copy-start
  0.6 3.0 %gather_rows.2 = (bf16[192,384]{1,0:T(8,128)(2,1)}, bf16[192,384]{1,0:T(8,128)(2,1)}, s32[384]{0:T(512)}) custom-call(s32[4]{0:T(128)} %count_hbm.3, s32[384]{0:T(512)} %picked_hbm.3, bf16[1536,384]{1,0:T(8,128)(2,1)} %frames_ref.2), custom_call_target="tpu_custom_call" | custom-call | flops 452984832 | bytes 1 | tf_op jit(solution)/shard_map/gather_rows/pallas_call | solution.py:48
  3.7 0.0 copy-start.6
  3.7 0.0 copy-start.7
  3.7 0.0 copy-start.8
  3.7 0.5 %collective-permute-start.3 = (bf16[1536,768]{1,0:T(8,128)(2,1)}, bf16[1536,768]{1,0:T(8,128)(2,1)S(1)}, u32[]{:S(2)}, u32[]{:S(2)}) collective-permute-start(bf16[1536,768]{1,0:T(8,128)(2,1)} %refs_4_.3), channel_id=1, source_target_pairs={{0,1},{1,0},{2,3},{3,2},{4,5},{5,4},{6,7},{7,6},{8,9},{9,8},{10,11... | collective-permute-start | bytes 7077896 | tf_op jit(solution)/shard_map/ppermute | solution.py:296
  4.2 0.1 collective-permute-start.4
  4.3 2.6 %collective-permute-start.2 = (bf16[192,384]{1,0:T(8,128)(2,1)}, bf16[192,384]{1,0:T(8,128)(2,1)S(1)}, u32[]{:S(2)}, u32[]{:S(2)}) collective-permute-start(bf16[192,384]{1,0:T(8,128)(2,1)} %get-tuple-element.26), channel_id=1, source_target_pairs={{0,3},{1,2},{2,1},{3,0},{4,7},{5,6},{6,5},{7,4},{8,11},{9,10},{10,... | collective-permute-start | bytes 442376 | tf_op jit(solution)/shard_map/ppermute | solution.py:293
  6.9 0.4 %collective-permute-start = (bf16[192,384]{1,0:T(8,128)(2,1)}, bf16[192,384]{1,0:T(8,128)(2,1)S(1)}, u32[]{:S(2)}, u32[]{:S(2)}) collective-permute-start(bf16[192,384]{1,0:T(8,128)(2,1)} %get-tuple-element.26), channel_id=1, source_target_pairs={{0,1},{1,0},{2,3},{3,2},{4,5},{5,4},{6,7},{7,6},{8,9},{9,8},{10,11... | collective-permute-start | bytes 442376 | tf_op jit(solution)/shard_map/ppermute | solution.py:296
  7.3 0.0 collective-permute-start.1
  7.3 2.9 %gather_rows.3 = (bf16[192,384]{1,0:T(8,128)(2,1)}, bf16[192,384]{1,0:T(8,128)(2,1)}, s32[384]{0:T(512)}) custom-call(s32[4]{0:T(128)} %count_hbm.3, s32[384]{0:T(512)} %picked_hbm.3, bf16[1536,384]{1,0:T(8,128)(2,1)} %frames_ref.3), custom_call_target="tpu_custom_call" | custom-call | flops 452984832 | bytes 1 | tf_op jit(solution)/shard_map/gather_rows/pallas_call | solution.py:48
  10.2 0.0 collective-permute-done.3.refs_5_
  10.2 2.1 %collective-permute-start.9 = (bf16[192,384]{1,0:T(8,128)(2,1)}, bf16[192,384]{1,0:T(8,128)(2,1)S(1)}, u32[]{:S(2)}, u32[]{:S(2)}) collective-permute-start(bf16[192,384]{1,0:T(8,128)(2,1)} %get-tuple-element.35.refs_0_), channel_id=1, source_target_pairs={{0,2},{1,3},{2,0},{3,1},{4,6},{5,7},{6,4},{7,5},{8,10},{9,11},{10,... | collective-permute-start | bytes 442376 | tf_op jit(solution)/shard_map/ppermute | solution.py:293
  12.3 0.0 collective-permute-done.2.refs_3_
  12.3 0.9 %collective-permute-start.10 = (bf16[192,384]{1,0:T(8,128)(2,1)}, bf16[192,384]{1,0:T(8,128)(2,1)S(1)}, u32[]{:S(2)}, u32[]{:S(2)}) collective-permute-start(bf16[192,384]{1,0:T(8,128)(2,1)} %get-tuple-element.36), channel_id=1, source_target_pairs={{0,3},{1,2},{2,1},{3,0},{4,7},{5,6},{6,5},{7,4},{8,11},{9,10},{10,... | collective-permute-start | bytes 442376 | tf_op jit(solution)/shard_map/ppermute | solution.py:293
  13.3 0.0 collective-permute-done.refs_1_
  13.3 0.2 collective-permute-start.8
  13.4 1.8 %collective-permute-done.1.refs_2_ = bf16[192,384]{1,0:T(8,128)(2,1)S(1)} collective-permute-done((bf16[192,384]{1,0:T(8,128)(2,1)}, bf16[192,384]{1,0:T(8,128)(2,1)S(1)}, u32[]{:S(2)}, u32[]{:S(2)}) %collective-permute-start.1) | collective-permute-done | bytes 147488 | tf_op jit(solution)/shard_map/ppermute | solution.py:293
  15.2 0.0 collective-permute-done.4.refs_7_
  15.2 0.0 copy-done
  15.2 0.0 copy-done.6
  15.2 0.0 copy-done.7
  15.3 0.0 copy-done.8
  15.3 0.0 copy-start.1
  15.3 1.7 %copy-done.1 = bf16[768,1536]{1,0:T(8,128)(2,1)S(1)} copy-done((bf16[768,1536]{1,0:T(8,128)(2,1)S(1)}, bf16[768,1536]{1,0:T(8,128)(2,1)}, u32[]{:S(2)}) %copy-start.1) | copy-done | bytes 2359320
  16.9 0.0 copy-start.2
  16.9 0.0 copy-start.5
  16.9 2.6 %forward.1 = (bf16[192,384]{1,0:T(8,128)(2,1)S(1)}, bf16[192,384]{1,0:T(8,128)(2,1)S(1)}, bf16[192,384]{1,0:T(8,128)(2,1)S(1)}, bf16[192,384]{1,0:T(8,128)(2,1)S...) custom-call(bf16[192,384]{1,0:T(8,128)(2,1)S(1)} %copy-done.6, ...), custom_call_target="tpu_custom_call" | custom-call | flops 1 | bytes 1 | tf_op jit(solution)/shard_map/forward/pallas_call | solution.py:23
  19.5 1.8 %collective-permute-start.5 = (bf16[192,384]{1,0:T(8,128)(2,1)S(1)}, bf16[192,384]{1,0:T(8,128)(2,1)S(1)}, u32[]{:S(2)}, u32[]{:S(2)}) collective-permute-start(bf16[192,384]{1,0:T(8,128)(2,1)S(1)} %get-tuple-element.30), channel_id=1, source_target_pairs={{0,2},{1,3},{2,0},{3,1},{4,6},{5,7},{6,4},{7,5},{8,10},{9,11},{10,... | collective-permute-start | bytes 442376 | tf_op jit(solution)/shard_map/ppermute | solution.py:293
  21.3 0.0 collective-permute-start.6
  21.3 0.0 collective-permute-done.9.refs_2_
  21.3 0.4 %collective-permute-start.7 = (bf16[192,384]{1,0:T(8,128)(2,1)S(1)}, bf16[192,384]{1,0:T(8,128)(2,1)S(1)}, u32[]{:S(2)}, u32[]{:S(2)}) collective-permute-start(bf16[192,384]{1,0:T(8,128)(2,1)S(1)} %get-tuple-element.32), channel_id=1, source_target_pairs={{0,3},{1,2},{2,1},{3,0},{4,7},{5,6},{6,5},{7,4},{8,11},{9,10},{10,... | collective-permute-start | bytes 442376 | tf_op jit(solution)/shard_map/ppermute | solution.py:293
  21.7 0.0 collective-permute-done.10.refs_3_
  21.7 0.0 collective-permute-done.8.refs_1_
  21.7 0.0 copy-done.2
  21.7 0.0 copy-done.5
  21.7 0.0 copy-start.3
  21.7 0.0 copy-start.9
  21.8 3.6 %backward.1 = (bf16[192,384]{1,0:T(8,128)(2,1)S(1)}, bf16[192,384]{1,0:T(8,128)(2,1)S(1)}, bf16[192,384]{1,0:T(8,128)(2,1)S(1)}, bf16[192,384]{1,0:T(8,128)(2,1)S(1)}) custom-call(bf16[192,384]{1,0:T(8,128)(2,1)S(1)} %copy-done.5, bf16[192,384]{1,0:T(8,128)(2,1)S(1)} %collective-permute-done.8.refs_1_, bf16[192,384]{1,0:T(8,128)(2,1)S(1)} %collective-permute-done.9.refs_2_, ...), custom_call_target="tpu_custom_call" | custom-call | flops 1 | bytes 1 | tf_op jit(solution)/shard_map/backward/pallas_call | solution.py:23
  25.3 1.9 %collective-permute-start.11 = (bf16[192,384]{1,0:T(8,128)(2,1)S(1)}, bf16[192,384]{1,0:T(8,128)(2,1)S(1)}, u32[]{:S(2)}, u32[]{:S(2)}) collective-permute-start(bf16[192,384]{1,0:T(8,128)(2,1)S(1)} %get-tuple-element.43), channel_id=1, source_target_pairs={{0,2},{1,3},{2,0},{3,1},{4,6},{5,7},{6,4},{7,5},{8,10},{9,11},{10,... | collective-permute-start | bytes 442376 | tf_op jit(solution)/shard_map/ppermute | solution.py:293
  27.2 0.0 collective-permute-start.12
  27.2 0.0 collective-permute-done.5.refs_1_
  27.2 0.3 collective-permute-start.13
  27.6 0.0 collective-permute-done.6.refs_2_
  27.6 0.0 collective-permute-done.7.refs_3_
  27.6 0.0 copy-done.3
  27.6 0.0 copy-done.9
  27.6 0.0 copy-start.4
  27.6 1.7 %mixed_rows.1 = bf16[1536,384]{1,0:T(8,128)(2,1)} custom-call(s32[384]{0:T(512)S(1)} %copy-done.9, bf16[1536,384]{1,0:T(8,128)(2,1)S(1)} %copy-done.3, bf16[192,384]{1,0:T(8,128)(2,1)S(1)} %get-tuple-element.29.refs_0_, bf16[192,384]{1,0:T(8,128)(2,1)S(1)} %collective-permute-done.5.refs_1_, bf16[192,384]{1,0:T(8,128)(2,1)S(1)} %collective-permute-done.6.refs_2_, ...), custom_call_target="tpu_custom_call" | custom-call | flops 452984832 | bytes 2359296 | tf_op jit(solution)/shard_map/mixed_rows/pallas_call | solution.py:137
  29.3 2.8 %collective-permute-done.11.refs_1_ = bf16[192,384]{1,0:T(8,128)(2,1)S(1)} collective-permute-done((bf16[192,384]{1,0:T(8,128)(2,1)S(1)}, bf16[192,384]{1,0:T(8,128)(2,1)S(1)}, u32[]{:S(2)}, u32[]{:S(2)}) %collective-permute-start.11) | collective-permute-done | bytes 147488 | tf_op jit(solution)/shard_map/ppermute | solution.py:293
  32.1 0.0 collective-permute-done.12.refs_2_
  32.1 1.6 %collective-permute-done.13.refs_3_ = bf16[192,384]{1,0:T(8,128)(2,1)S(1)} collective-permute-done((bf16[192,384]{1,0:T(8,128)(2,1)S(1)}, bf16[192,384]{1,0:T(8,128)(2,1)S(1)}, u32[]{:S(2)}, u32[]{:S(2)}) %collective-permute-start.13) | collective-permute-done | bytes 147488 | tf_op jit(solution)/shard_map/ppermute | solution.py:293
  33.7 0.0 copy-done.4
  33.7 1.7 %grad_rows.1 = bf16[1536,384]{1,0:T(8,128)(2,1)} custom-call(s32[384]{0:T(512)S(1)} %copy-done.9, bf16[1536,384]{1,0:T(8,128)(2,1)S(1)} %copy-done.4, bf16[192,384]{1,0:T(8,128)(2,1)S(1)} %get-tuple-element.42.refs_0_, bf16[192,384]{1,0:T(8,128)(2,1)S(1)} %collective-permute-done.11.refs_1_, bf16[192,384]{1,0:T(8,128)(2,1)S(1)} %collective-permute-done.12.refs_2_, ...), custom_call_target="tpu_custom_call" | custom-call | flops 452984832 | bytes 2359296 | tf_op jit(solution)/shard_map/grad_rows/pallas_call | solution.py:137
Async XLA Ops:
  0.6 14.6 %copy-start = (bf16[1536,768]{1,0:T(8,128)(2,1)S(1)}, bf16[1536,768]{1,0:T(8,128)(2,1)}, u32[]{:S(2)}) copy-start(bf16[1536,768]{1,0:T(8,128)(2,1)} %refs_4_.3) | copy-start | bytes 7077892
  3.7 11.6 %copy-start.6 = (bf16[192,384]{1,0:T(8,128)(2,1)S(1)}, bf16[192,384]{1,0:T(8,128)(2,1)}, u32[]{:S(2)}) copy-start(bf16[192,384]{1,0:T(8,128)(2,1)} %get-tuple-element.25.refs_0_) | copy-start | bytes 442372
  3.7 11.6 %copy-start.7 = (f32[1536]{0:T(1024)S(1)}, f32[1536]{0:T(1024)}, u32[]{:S(2)}) copy-start(f32[1536]{0:T(1024)} %refs_8_.3) | copy-start | bytes 18436
  3.7 11.6 %copy-start.8 = (f32[1536]{0:T(1024)S(1)}, f32[1536]{0:T(1024)}, u32[]{:S(2)}) copy-start(f32[1536]{0:T(1024)} %refs_9_.3) | copy-start | bytes 18436
  3.7 6.5 %collective-permute-start.3 = (bf16[1536,768]{1,0:T(8,128)(2,1)}, bf16[1536,768]{1,0:T(8,128)(2,1)S(1)}, u32[]{:S(2)}, u32[]{:S(2)}) collective-permute-start(bf16[1536,768]{1,0:T(8,128)(2,1)} %refs_4_.3), channel_id=1, source_target_pairs={{0,1},{1,0},{2,3},{3,2},{4,5},{5,4},{6,7},{7,6},{8,9},{9,8},{10,11... | collective-permute-start | bytes 7077896 | tf_op jit(solution)/shard_map/ppermute | solution.py:296
  4.2 11.0 %collective-permute-start.4 = (bf16[768,1536]{1,0:T(8,128)(2,1)}, bf16[768,1536]{1,0:T(8,128)(2,1)S(1)}, u32[]{:S(2)}, u32[]{:S(2)}) collective-permute-start(bf16[768,1536]{1,0:T(8,128)(2,1)} %refs_6_.3), channel_id=1, source_target_pairs={{0,1},{1,0},{2,3},{3,2},{4,5},{5,4},{6,7},{7,6},{8,9},{9,8},{10,11... | collective-permute-start | bytes 7077896 | tf_op jit(solution)/shard_map/ppermute | solution.py:296
  4.3 8.0 %collective-permute-start.2 = (bf16[192,384]{1,0:T(8,128)(2,1)}, bf16[192,384]{1,0:T(8,128)(2,1)S(1)}, u32[]{:S(2)}, u32[]{:S(2)}) collective-permute-start(bf16[192,384]{1,0:T(8,128)(2,1)} %get-tuple-element.26), channel_id=1, source_target_pairs={{0,3},{1,2},{2,1},{3,0},{4,7},{5,6},{6,5},{7,4},{8,11},{9,10},{10,... | collective-permute-start | bytes 442376 | tf_op jit(solution)/shard_map/ppermute | solution.py:293
  6.9 6.4 %collective-permute-start = (bf16[192,384]{1,0:T(8,128)(2,1)}, bf16[192,384]{1,0:T(8,128)(2,1)S(1)}, u32[]{:S(2)}, u32[]{:S(2)}) collective-permute-start(bf16[192,384]{1,0:T(8,128)(2,1)} %get-tuple-element.26), channel_id=1, source_target_pairs={{0,1},{1,0},{2,3},{3,2},{4,5},{5,4},{6,7},{7,6},{8,9},{9,8},{10,11... | collective-permute-start | bytes 442376 | tf_op jit(solution)/shard_map/ppermute | solution.py:296
  7.3 7.9 %collective-permute-start.1 = (bf16[192,384]{1,0:T(8,128)(2,1)}, bf16[192,384]{1,0:T(8,128)(2,1)S(1)}, u32[]{:S(2)}, u32[]{:S(2)}) collective-permute-start(bf16[192,384]{1,0:T(8,128)(2,1)} %get-tuple-element.25.refs_0_), channel_id=1, source_target_pairs={{0,2},{1,3},{2,0},{3,1},{4,6},{5,7},{6,4},{7,5},{8,10},{9,11},{10,... | collective-permute-start | bytes 442376 | tf_op jit(solution)/shard_map/ppermute | solution.py:293
  10.2 11.1 %collective-permute-start.9 = (bf16[192,384]{1,0:T(8,128)(2,1)}, bf16[192,384]{1,0:T(8,128)(2,1)S(1)}, u32[]{:S(2)}, u32[]{:S(2)}) collective-permute-start(bf16[192,384]{1,0:T(8,128)(2,1)} %get-tuple-element.35.refs_0_), channel_id=1, source_target_pairs={{0,2},{1,3},{2,0},{3,1},{4,6},{5,7},{6,4},{7,5},{8,10},{9,11},{10,... | collective-permute-start | bytes 442376 | tf_op jit(solution)/shard_map/ppermute | solution.py:293
  12.3 9.4 %collective-permute-start.10 = (bf16[192,384]{1,0:T(8,128)(2,1)}, bf16[192,384]{1,0:T(8,128)(2,1)S(1)}, u32[]{:S(2)}, u32[]{:S(2)}) collective-permute-start(bf16[192,384]{1,0:T(8,128)(2,1)} %get-tuple-element.36), channel_id=1, source_target_pairs={{0,3},{1,2},{2,1},{3,0},{4,7},{5,6},{6,5},{7,4},{8,11},{9,10},{10,... | collective-permute-start | bytes 442376 | tf_op jit(solution)/shard_map/ppermute | solution.py:293
  13.3 8.5 %collective-permute-start.8 = (bf16[192,384]{1,0:T(8,128)(2,1)}, bf16[192,384]{1,0:T(8,128)(2,1)S(1)}, u32[]{:S(2)}, u32[]{:S(2)}) collective-permute-start(bf16[192,384]{1,0:T(8,128)(2,1)} %get-tuple-element.36), channel_id=1, source_target_pairs={{0,1},{1,0},{2,3},{3,2},{4,5},{5,4},{6,7},{7,6},{8,9},{9,8},{10,11... | collective-permute-start | bytes 442376 | tf_op jit(solution)/shard_map/ppermute | solution.py:296
  15.3 1.7 %copy-start.1 = (bf16[768,1536]{1,0:T(8,128)(2,1)S(1)}, bf16[768,1536]{1,0:T(8,128)(2,1)}, u32[]{:S(2)}) copy-start(bf16[768,1536]{1,0:T(8,128)(2,1)} %refs_6_.3) | copy-start | bytes 7077892
  16.9 4.8 %copy-start.2 = (bf16[768,1536]{1,0:T(8,128)(2,1)S(1)}, bf16[768,1536]{1,0:T(8,128)(2,1)}, u32[]{:S(2)}) copy-start(bf16[768,1536]{1,0:T(8,128)(2,1)} %refs_6_.3) | copy-start | bytes 7077892
  16.9 4.8 %copy-start.5 = (bf16[192,384]{1,0:T(8,128)(2,1)S(1)}, bf16[192,384]{1,0:T(8,128)(2,1)}, u32[]{:S(2)}) copy-start(bf16[192,384]{1,0:T(8,128)(2,1)} %get-tuple-element.35.refs_0_) | copy-start | bytes 442372
  19.5 7.7 %collective-permute-start.5 = (bf16[192,384]{1,0:T(8,128)(2,1)S(1)}, bf16[192,384]{1,0:T(8,128)(2,1)S(1)}, u32[]{:S(2)}, u32[]{:S(2)}) collective-permute-start(bf16[192,384]{1,0:T(8,128)(2,1)S(1)} %get-tuple-element.30), channel_id=1, source_target_pairs={{0,2},{1,3},{2,0},{3,1},{4,6},{5,7},{6,4},{7,5},{8,10},{9,11},{10,... | collective-permute-start | bytes 442376 | tf_op jit(solution)/shard_map/ppermute | solution.py:293
  21.3 6.2 %collective-permute-start.6 = (bf16[192,384]{1,0:T(8,128)(2,1)S(1)}, bf16[192,384]{1,0:T(8,128)(2,1)S(1)}, u32[]{:S(2)}, u32[]{:S(2)}) collective-permute-start(bf16[192,384]{1,0:T(8,128)(2,1)S(1)} %get-tuple-element.31), channel_id=1, source_target_pairs={{0,1},{1,0},{2,3},{3,2},{4,5},{5,4},{6,7},{7,6},{8,9},{9,8},{10,11... | collective-permute-start | bytes 442376 | tf_op jit(solution)/shard_map/ppermute | solution.py:296
  21.3 6.2 %collective-permute-start.7 = (bf16[192,384]{1,0:T(8,128)(2,1)S(1)}, bf16[192,384]{1,0:T(8,128)(2,1)S(1)}, u32[]{:S(2)}, u32[]{:S(2)}) collective-permute-start(bf16[192,384]{1,0:T(8,128)(2,1)S(1)} %get-tuple-element.32), channel_id=1, source_target_pairs={{0,3},{1,2},{2,1},{3,0},{4,7},{5,6},{6,5},{7,4},{8,11},{9,10},{10,... | collective-permute-start | bytes 442376 | tf_op jit(solution)/shard_map/ppermute | solution.py:293
  21.7 5.8 %copy-start.3 = (bf16[1536,384]{1,0:T(8,128)(2,1)S(1)}, bf16[1536,384]{1,0:T(8,128)(2,1)}, u32[]{:S(2)}) copy-start(bf16[1536,384]{1,0:T(8,128)(2,1)} %frames_ref.2) | copy-start | bytes 3538948
  21.7 5.8 %copy-start.9 = (s32[384]{0:T(512)S(1)}, s32[384]{0:T(512)}, u32[]{:S(2)}) copy-start(s32[384]{0:T(512)} %get-tuple-element.24.wanted_ref) | copy-start | bytes 4612
  25.3 6.8 %collective-permute-start.11 = (bf16[192,384]{1,0:T(8,128)(2,1)S(1)}, bf16[192,384]{1,0:T(8,128)(2,1)S(1)}, u32[]{:S(2)}, u32[]{:S(2)}) collective-permute-start(bf16[192,384]{1,0:T(8,128)(2,1)S(1)} %get-tuple-element.43), channel_id=1, source_target_pairs={{0,2},{1,3},{2,0},{3,1},{4,6},{5,7},{6,4},{7,5},{8,10},{9,11},{10,... | collective-permute-start | bytes 442376 | tf_op jit(solution)/shard_map/ppermute | solution.py:293
  27.2 4.9 %collective-permute-start.12 = (bf16[192,384]{1,0:T(8,128)(2,1)S(1)}, bf16[192,384]{1,0:T(8,128)(2,1)S(1)}, u32[]{:S(2)}, u32[]{:S(2)}) collective-permute-start(bf16[192,384]{1,0:T(8,128)(2,1)S(1)} %get-tuple-element.44), channel_id=1, source_target_pairs={{0,1},{1,0},{2,3},{3,2},{4,5},{5,4},{6,7},{7,6},{8,9},{9,8},{10,11... | collective-permute-start | bytes 442376 | tf_op jit(solution)/shard_map/ppermute | solution.py:296
  27.2 6.5 %collective-permute-start.13 = (bf16[192,384]{1,0:T(8,128)(2,1)S(1)}, bf16[192,384]{1,0:T(8,128)(2,1)S(1)}, u32[]{:S(2)}, u32[]{:S(2)}) collective-permute-start(bf16[192,384]{1,0:T(8,128)(2,1)S(1)} %get-tuple-element.45), channel_id=1, source_target_pairs={{0,3},{1,2},{2,1},{3,0},{4,7},{5,6},{6,5},{7,4},{8,11},{9,10},{10,... | collective-permute-start | bytes 442376 | tf_op jit(solution)/shard_map/ppermute | solution.py:293
  27.6 6.1 %copy-start.4 = (bf16[1536,384]{1,0:T(8,128)(2,1)S(1)}, bf16[1536,384]{1,0:T(8,128)(2,1)}, u32[]{:S(2)}) copy-start(bf16[1536,384]{1,0:T(8,128)(2,1)} %frames_ref.3) | copy-start | bytes 3538948

commit v7 on v6

--- a/solution.py
+++ b/solution.py
@@ -65,45 +65,29 @@
     return jnp.where(lax.axis_index("pair") == 0, wanted, swapped)[:1]
 
 
-def gather_body(count_hbm, picked_hbm, frames_hbm, mine_hbm, sib_hbm, wanted_hbm, frames, picked, count, mine, sib, sems):
-    slots = picked.shape[0]
-    frames_dev = frames.shape[0]
-    copies = fetch((frames_hbm, picked_hbm, count_hbm), (frames, picked, count), sems)
-    copies[1].wait()
-    copies[2].wait()
-    wanted = wanted_slots(count[lax.axis_index("tm")], picked[...])
-    picked[...] = wanted.reshape(slots)
-    column = jnp.broadcast_to(wanted.astype(F32), (128, slots)).T[:, :1]
-    place = lax.broadcasted_iota(jnp.int32, (1, frames_dev), 1).astype(F32)
-    onehot = jnp.where(column == place, 1.0, 0.0).astype(BF16)
-    copies[0].wait()
-    rows = jnp.dot(onehot, frames[...], preferred_element_type=F32).astype(BF16)
-    half = mine.shape[0]
-    mine[...] = rows[:half]
-    sib[...] = rows[half:]
-    for copy in fetch((sib, mine, picked), (sib_hbm, mine_hbm, wanted_hbm), sems):
+def slots_body(count_hbm, picked_hbm, wanted_hbm, count, picked, sems):
+    for copy in fetch((count_hbm, picked_hbm), (count, picked), sems):
         copy.wait()
-
-
-def gather_rows(count, picked, frames, moved):
-    slots, (frames_dev, width) = picked.shape[0], frames.shape
-    out = jax.ShapeDtypeStruct((slots // 2, width), BF16)
+    picked[...] = wanted_slots(count[lax.axis_index("tm")], picked[...]).reshape(picked.shape)
+    for copy in fetch((picked,), (wanted_hbm,), sems):
+        copy.wait()
+
+
+def live_slots(count, picked):
     return call_in_hbm(
-        gather_body,
-        "gather_rows",
-        (out, out, jax.ShapeDtypeStruct(picked.shape, jnp.int32)),
-        (count, picked, frames),
-        [
-            VMEM(frames.shape, BF16),
-            VMEM(picked.shape, jnp.int32),
-            pltpu.SMEM(count.shape, jnp.int32),
-            VMEM(out.shape, BF16),
-            VMEM(out.shape, BF16),
-            pltpu.SemaphoreType.DMA((3,)),
-        ],
-        2 * slots * frames_dev * width,
-        moved,
+        slots_body,
+        "live_slots",
+        jax.ShapeDtypeStruct(picked.shape, jnp.int32),
+        (count, picked),
+        [pltpu.SMEM(count.shape, jnp.int32), VMEM(picked.shape, jnp.int32), pltpu.SemaphoreType.DMA((2,))],
+        1,
+        1,
     )
+
+
+def gather_rows(places, frames):
+    onehot = (lax.broadcasted_iota(jnp.int32, (frames.shape[0], 1), 0) == places).astype(BF16)
+    return lax.dot_general(onehot, frames, (((0,), (0,)), ((), ())), preferred_element_type=F32).astype(BF16)
 
 
 def scatter_body(mines, sibs, wanted_ref, frames_ref, *refs):
@@ -317,11 +301,16 @@
         far_sib = [send(x, k, 1) for x, k in zip(parts[2 + count :], steps)]
         return [parts[0]] + far_mine, [swap(parts[1])] + far_sib
 
-    mine, sib, wanted = gather_rows(picked_count, picked_rows, frames, 1)
+    wanted = live_slots(picked_count, picked_rows)
+    first = lax.axis_index("pair") == 0
+    places_mine = jnp.where(first, picked_rows[:half], picked_rows[half:])
+    places_sib = jnp.where(first, picked_rows[half:], picked_rows[:half])
+    mine, sib = gather_rows(places_mine, frames), gather_rows(places_sib, frames)
     blocks = collect(mine, sib)
     up_sib, down_sib = swap(after(up_weight, mine)), swap(after(down_weight, mine))
     weights = (up_weight, up_sib, down_weight, down_sib)
-    cot_mine, cot_sib, _ = gather_rows(picked_count, picked_rows, cotangent, 1)
+    rows = gather_rows(jnp.concatenate([places_mine, places_sib]), cotangent)
+    cot_mine, cot_sib = lax.optimization_barrier((rows[:half], rows[half:]))
     cot_mine, cot_sib = lax.optimization_barrier((cot_mine, cot_sib, up_sib))[:2]
     cot_blocks = collect(cot_mine, cot_sib)
     parts, saved = forward(joined(blocks), ways, weights, gain, router)

time: 35.7 us -> 34.4 us (0.964)
  Pallas kernels: 15.4 us -> 10.8 us
  matrix products: 0 us -> 3.39 us
  waiting for transfers between devices: 6.24 us -> 4.92 us
  starting transfers between devices: 11.2 us -> 12.5 us
  local copies, waits for them, and re-layouts: 1.71 us -> 0.74 us
  other arithmetic: 0 us -> 0.94 us
    pallas_call x2 -> x1, Pallas kernels: 5.91 us -> 1.34 us  [call_in_hbm(): pl.pallas_call(body, out_shape=outs, in_specs=[ANY] * len(ins), out_specs...]
    dot_general x0 -> x3, matrix products: none -> 3.39 us  [gather_rows(): lax.dot_general(onehot, frames, (((0,), (0,)), ((), ())), preferred_eleme...]
    ppermute x8, waiting for transfers between devices: 6.22 us -> 4.52 us  [send(): return lax.ppermute(x, ('tensor', 'pair'), pairs)]
    ppermute x6, starting transfers between devices: 1.2 us -> 2.28 us  [swap(): return lax.ppermute(x, 'pair', [(0, 1), (1, 0)])]
    unnamed x20 -> x14, local copies, waits for them, and re-layouts: 1.71 us -> 0.7 us
    select_n x0 -> x1, other arithmetic: none -> 0.87 us  [per_device(): places_sib = jnp.where(first, picked_rows[half:], picked_rows[:half])]
    ppermute x6, waiting for transfers between devices: 0.02 us -> 0.41 us  [swap(): return lax.ppermute(x, 'pair', [(0, 1), (1, 0)])]
  transfers between devices with their start and end apart: 14 -> 14, of which waited for: 3 -> 6; matrix products, arithmetic and copies ran while one was open for 0% -> 5% of each run, Pallas kernels for 30% -> 27%
where the time goes in v7:
time: 34.4 us; the launch traced here: 34.1 us
  starting transfers between devices  12.5 us (36%)
  Pallas kernels  10.8 us (31%)
  waiting for transfers between devices  4.92 us (14%)
  matrix products  3.39 us (10%)
  other arithmetic  0.94 us (3%)
  between operations  0.77 us (2%)
  local copies, waits for them, and re-layouts  0.74 us (2%)
    ppermute x8, starting transfers between devices, send(): return lax.ppermute(x, ('tensor', 'pair'), pairs)  10.2 us
    pallas_call x2, Pallas kernels, call(): pl.pallas_call(body, out_shape=outs, in_specs=specs, out_specs=jax.tree.m...  6.14 us
    ppermute x8, waiting for transfers between devices, send(): return lax.ppermute(x, ('tensor', 'pair'), pairs)  4.52 us
    dot_general x3, matrix products, gather_rows(): lax.dot_general(onehot, frames, (((0,), (0,)), ((), ())), preferred_eleme...  3.39 us
    pallas_call x2, Pallas kernels, scatter_rows(): pl.pallas_call(functools.partial(scatter_body, len(mine_parts), len(sib_p...  3.35 us
    ppermute x6, starting transfers between devices, swap(): return lax.ppermute(x, 'pair', [(0, 1), (1, 0)])  2.28 us
    pallas_call x1, Pallas kernels, call_in_hbm(): pl.pallas_call(body, out_shape=outs, in_specs=[ANY] * len(ins), out_specs...  1.34 us
    select_n x1, other arithmetic, per_device(): places_sib = jnp.where(first, picked_rows[half:], picked_rows[:half])  0.87 us
  transfers between devices with their start and end apart: 14, of which 6 were waited for; matrix products, arithmetic and copies ran while one was open for 5% of the time, Pallas kernels for 27%

profile of v7, /device:TPU:0, one launch (start us, length us, event | category | flops | bytes accessed | tf_op | source)
XLA Modules:
  0.0 34.1 jit_solution(2835233822083886724)
XLA Ops:
  0.6 0.0 copy-start.2
  0.6 0.9 %broadcast_select_fusion = (s32[192]{0:T(256)S(1)}, s32[192]{0:T(256)S(1)}) fusion(pred[]{:T(512)S(6)} %eq.21, s32[384]{0:T(512)} %picked_hbm.1), kind=kLoop, calls=%fused_computation.13 | loop fusion | flops 384 | bytes 3073 | tf_op jit(solution)/shard_map/jit(_where)/select_n | solution.py:307
  1.5 1.9 %fusion.6.refs_0_ = bf16[192,384]{1,0:T(8,128)(2,1)S(1)} fusion(bf16[1536,384]{1,0:T(8,128)(2,1)} %frames_ref.2, s32[192]{0:T(256)S(1)} %get-tuple-element.43), kind=kOutput, calls=%fused_computation.9 | convolution fusion | flops 226861056 | bytes 1327872 | tf_op jit(solution)/shard_map/dot_general | solution.py:90
  3.4 0.0 copy-start.3
  3.4 0.5 %collective-permute-start.3 = (bf16[1536,768]{1,0:T(8,128)(2,1)}, bf16[1536,768]{1,0:T(8,128)(2,1)S(1)}, u32[]{:S(2)}, u32[]{:S(2)}) collective-permute-start(bf16[1536,768]{1,0:T(8,128)(2,1)} %refs_4_.3), channel_id=1, source_target_pairs={{0,1},{1,0},{2,3},{3,2},{4,5},{5,4},{6,7},{7,6},{8,9},{9,8},{10,11... | collective-permute-start | bytes 7077896 | tf_op jit(solution)/shard_map/ppermute | solution.py:280
  4.0 0.1 collective-permute-start.4
  4.0 2.9 %collective-permute-start.1 = (bf16[192,384]{1,0:T(8,128)(2,1)S(1)}, bf16[192,384]{1,0:T(8,128)(2,1)S(1)}, u32[]{:S(2)}, u32[]{:S(2)}) collective-permute-start(bf16[192,384]{1,0:T(8,128)(2,1)S(1)} %fusion.6.refs_0_), channel_id=1, source_target_pairs={{0,2},{1,3},{2,0},{3,1},{4,6},{5,7},{6,4},{7,5},{8,10},{9,11},{10,... | collective-permute-start | bytes 442376 | tf_op jit(solution)/shard_map/ppermute | solution.py:277
  7.0 0.0 copy-done.2
  7.0 0.0 copy-start.1
  7.0 0.6 %fusion.5 = bf16[192,384]{1,0:T(8,128)(2,1)S(1)} fusion(bf16[1536,384]{1,0:T(8,128)(2,1)S(1)} %copy-done.2, s32[192]{0:T(256)S(1)} %get-tuple-element.42), kind=kOutput, calls=%fused_computation.8 | convolution fusion | flops 226861056 | bytes 1327872 | tf_op jit(solution)/shard_map/dot_general | solution.py:90
  7.6 0.1 collective-permute-start
  7.7 0.1 collective-permute-start.2
  7.8 0.1 pad_add_fusion
  7.9 0.0 copy-done.3
  7.9 0.0 copy-start
  7.9 0.0 copy-start.4
  7.9 0.0 copy-start.5
  7.9 0.8 %fusion.3 = bf16[384,384]{1,0:T(8,128)(2,1)S(1)} fusion(bf16[1536,384]{1,0:T(8,128)(2,1)S(1)} %copy-done.3, s32[384]{0:T(512)S(1)} %pad_add_fusion), kind=kOutput, calls=%fused_computation.6 | convolution fusion | flops 453722112 | bytes 1476096 | tf_op jit(solution)/shard_map/dot_general | solution.py:90
  8.8 0.0 collective-permute-done.3.refs_5_
  8.8 2.2 %collective-permute-start.10 = (bf16[192,384]{1,0:T(8,128)(2,1)S(1)}, bf16[192,384]{1,0:T(8,128)(2,1)S(1)}, u32[]{:S(2)}, u32[]{:S(2)}) collective-permute-start(bf16[192,384]{1,0:T(8,128)(2,1)S(1)} %get-tuple-element.30), channel_id=1, source_target_pairs={{0,3},{1,2},{2,1},{3,0},{4,7},{5,6},{6,5},{7,4},{8,11},{9,10},{10,... | collective-permute-start | bytes 442376 | tf_op jit(solution)/shard_map/ppermute | solution.py:277
  10.9 0.3 %collective-permute-done.1.refs_2_ = bf16[192,384]{1,0:T(8,128)(2,1)S(1)} collective-permute-done((bf16[192,384]{1,0:T(8,128)(2,1)S(1)}, bf16[192,384]{1,0:T(8,128)(2,1)S(1)}, u32[]{:S(2)}, u32[]{:S(2)}) %collective-permute-start.1) | collective-permute-done | bytes 147488 | tf_op jit(solution)/shard_map/ppermute | solution.py:277
  11.3 0.0 collective-permute-start.8
  11.3 0.4 %collective-permute-done.refs_1_ = bf16[192,384]{1,0:T(8,128)(2,1)S(1)} collective-permute-done((bf16[192,384]{1,0:T(8,128)(2,1)S(1)}, bf16[192,384]{1,0:T(8,128)(2,1)S(1)}, u32[]{:S(2)}, u32[]{:S(2)}) %collective-permute-start) | collective-permute-done | bytes 147488 | tf_op jit(solution)/shard_map/ppermute | solution.py:280
  11.7 2.0 %collective-permute-start.9 = (bf16[192,384]{1,0:T(8,128)(2,1)S(1)}, bf16[192,384]{1,0:T(8,128)(2,1)S(1)}, u32[]{:S(2)}, u32[]{:S(2)}) collective-permute-start(bf16[192,384]{1,0:T(8,128)(2,1)S(1)} %get-tuple-element.29.refs_0_), channel_id=1, source_target_pairs={{0,2},{1,3},{2,0},{3,1},{4,6},{5,7},{6,4},{7,5},{8,10},{9,11},{10,... | collective-permute-start | bytes 442376 | tf_op jit(solution)/shard_map/ppermute | solution.py:277
  13.7 0.7 %collective-permute-done.2.refs_3_ = bf16[192,384]{1,0:T(8,128)(2,1)S(1)} collective-permute-done((bf16[192,384]{1,0:T(8,128)(2,1)S(1)}, bf16[192,384]{1,0:T(8,128)(2,1)S(1)}, u32[]{:S(2)}, u32[]{:S(2)}) %collective-permute-start.2) | collective-permute-done | bytes 147488 | tf_op jit(solution)/shard_map/ppermute | solution.py:277
  14.3 0.0 collective-permute-done.4.refs_7_
  14.3 0.0 copy-done.1
  14.3 0.0 copy-done
  14.4 0.0 copy-done.4
  14.4 0.0 copy-done.5
  14.4 2.6 %forward.1 = (bf16[192,384]{1,0:T(8,128)(2,1)S(1)}, bf16[192,384]{1,0:T(8,128)(2,1)S(1)}, bf16[192,384]{1,0:T(8,128)(2,1)S(1)}, bf16[192,384]{1,0:T(8,128)(2,1)S...) custom-call(bf16[192,384]{1,0:T(8,128)(2,1)S(1)} %fusion.6.refs_0_, ...), custom_call_target="tpu_custom_call" | custom-call | flops 1 | bytes 1 | tf_op jit(solution)/shard_map/forward/pallas_call | solution.py:23
  16.9 0.8 %collective-permute-start.5 = (bf16[192,384]{1,0:T(8,128)(2,1)S(1)}, bf16[192,384]{1,0:T(8,128)(2,1)S(1)}, u32[]{:S(2)}, u32[]{:S(2)}) collective-permute-start(bf16[192,384]{1,0:T(8,128)(2,1)S(1)} %get-tuple-element.24), channel_id=1, source_target_pairs={{0,2},{1,3},{2,0},{3,1},{4,6},{5,7},{6,4},{7,5},{8,10},{9,11},{10,... | collective-permute-start | bytes 442376 | tf_op jit(solution)/shard_map/ppermute | solution.py:277
  17.8 1.6 %collective-permute-start.6 = (bf16[192,384]{1,0:T(8,128)(2,1)S(1)}, bf16[192,384]{1,0:T(8,128)(2,1)S(1)}, u32[]{:S(2)}, u32[]{:S(2)}) collective-permute-start(bf16[192,384]{1,0:T(8,128)(2,1)S(1)} %get-tuple-element.25), channel_id=1, source_target_pairs={{0,1},{1,0},{2,3},{3,2},{4,5},{5,4},{6,7},{7,6},{8,9},{9,8},{10,11... | collective-permute-start | bytes 442376 | tf_op jit(solution)/shard_map/ppermute | solution.py:280
  19.3 0.0 collective-permute-done.10.refs_3_
  19.3 0.1 collective-permute-start.7
  19.4 0.0 collective-permute-done.8.refs_1_
  19.4 1.1 %collective-permute-done.9.refs_2_ = bf16[192,384]{1,0:T(8,128)(2,1)S(1)} collective-permute-done((bf16[192,384]{1,0:T(8,128)(2,1)S(1)}, bf16[192,384]{1,0:T(8,128)(2,1)S(1)}, u32[]{:S(2)}, u32[]{:S(2)}) %collective-permute-start.9) | collective-permute-done | bytes 147488 | tf_op jit(solution)/shard_map/ppermute | solution.py:277
  20.5 3.6 %backward.1 = (bf16[192,384]{1,0:T(8,128)(2,1)S(1)}, bf16[192,384]{1,0:T(8,128)(2,1)S(1)}, bf16[192,384]{1,0:T(8,128)(2,1)S(1)}, bf16[192,384]{1,0:T(8,128)(2,1)S(1)}) custom-call(bf16[192,384]{1,0:T(8,128)(2,1)S(1)} %get-tuple-element.29.refs_0_, bf16[192,384]{1,0:T(8,128)(2,1)S(1)} %collective-permute-done.8.refs_1_, ...), custom_call_target="tpu_custom_call" | custom-call | flops 1 | bytes 1 | tf_op jit(solution)/shard_map/backward/pallas_call | solution.py:23
  24.1 1.8 %collective-permute-start.11 = (bf16[192,384]{1,0:T(8,128)(2,1)S(1)}, bf16[192,384]{1,0:T(8,128)(2,1)S(1)}, u32[]{:S(2)}, u32[]{:S(2)}) collective-permute-start(bf16[192,384]{1,0:T(8,128)(2,1)S(1)} %get-tuple-element.37), channel_id=1, source_target_pairs={{0,2},{1,3},{2,0},{3,1},{4,6},{5,7},{6,4},{7,5},{8,10},{9,11},{10,... | collective-permute-start | bytes 442376 | tf_op jit(solution)/shard_map/ppermute | solution.py:277
  25.9 0.0 collective-permute-start.12
  25.9 0.0 collective-permute-done.5.refs_1_
  25.9 0.4 %collective-permute-start.13 = (bf16[192,384]{1,0:T(8,128)(2,1)S(1)}, bf16[192,384]{1,0:T(8,128)(2,1)S(1)}, u32[]{:S(2)}, u32[]{:S(2)}) collective-permute-start(bf16[192,384]{1,0:T(8,128)(2,1)S(1)} %get-tuple-element.39), channel_id=1, source_target_pairs={{0,3},{1,2},{2,1},{3,0},{4,7},{5,6},{6,5},{7,4},{8,11},{9,10},{10,... | collective-permute-start | bytes 442376 | tf_op jit(solution)/shard_map/ppermute | solution.py:277
  26.3 1.3 %live_slots.1.wanted_ref = s32[384]{0:T(512)} custom-call(s32[4]{0:T(128)} %count_hbm.1, s32[384]{0:T(512)} %picked_hbm.1), custom_call_target="tpu_custom_call" | custom-call | flops 1 | bytes 1 | tf_op jit(solution)/shard_map/live_slots/pallas_call | solution.py:48
  27.7 0.0 collective-permute-done.6.refs_2_
  27.7 0.0 collective-permute-done.7.refs_3_
  27.7 0.0 copy-start.6
  27.7 0.7 %copy-done.6 = s32[384]{0:T(512)S(1)} copy-done((s32[384]{0:T(512)S(1)}, s32[384]{0:T(512)}, u32[]{:S(2)}) %copy-start.6) | copy-done | bytes 1560
  28.4 1.7 %mixed_rows.1 = bf16[1536,384]{1,0:T(8,128)(2,1)} custom-call(s32[384]{0:T(512)S(1)} %copy-done.6, bf16[1536,384]{1,0:T(8,128)(2,1)S(1)} %copy-done.2, bf16[192,384]{1,0:T(8,128)(2,1)S(1)} %get-tuple-element.23.refs_0_, bf16[192,384]{1,0:T(8,128)(2,1)S(1)} %collective-permute-done.5.refs_1_, bf16[192,384]{1,0:T(8,128)(2,1)S(1)} %collective-permute-done.6.refs_2_, ...), custom_call_target="tpu_custom_call" | custom-call | flops 452984832 | bytes 2359296 | tf_op jit(solution)/shard_map/mixed_rows/pallas_call | solution.py:121
  30.1 0.9 %collective-permute-done.11.refs_1_ = bf16[192,384]{1,0:T(8,128)(2,1)S(1)} collective-permute-done((bf16[192,384]{1,0:T(8,128)(2,1)S(1)}, bf16[192,384]{1,0:T(8,128)(2,1)S(1)}, u32[]{:S(2)}, u32[]{:S(2)}) %collective-permute-start.11) | collective-permute-done | bytes 147488 | tf_op jit(solution)/shard_map/ppermute | solution.py:277
  31.0 0.0 collective-permute-done.12.refs_2_
  31.0 1.5 %collective-permute-done.13.refs_3_ = bf16[192,384]{1,0:T(8,128)(2,1)S(1)} collective-permute-done((bf16[192,384]{1,0:T(8,128)(2,1)S(1)}, bf16[192,384]{1,0:T(8,128)(2,1)S(1)}, u32[]{:S(2)}, u32[]{:S(2)}) %collective-permute-start.13) | collective-permute-done | bytes 147488 | tf_op jit(solution)/shard_map/ppermute | solution.py:277
  32.4 1.7 %grad_rows.1 = bf16[1536,384]{1,0:T(8,128)(2,1)} custom-call(s32[384]{0:T(512)S(1)} %copy-done.6, bf16[1536,384]{1,0:T(8,128)(2,1)S(1)} %copy-done.3, bf16[192,384]{1,0:T(8,128)(2,1)S(1)} %get-tuple-element.36.refs_0_, bf16[192,384]{1,0:T(8,128)(2,1)S(1)} %collective-permute-done.11.refs_1_, bf16[192,384]{1,0:T(8,128)(2,1)S(1)} %collective-permute-done.12.refs_2_, ...), custom_call_target="tpu_custom_call" | custom-call | flops 452984832 | bytes 2359296 | tf_op jit(solution)/shard_map/grad_rows/pallas_call | solution.py:121
  (1 shorter events, 0.0 us)
Async XLA Ops:
  0.6 6.3 %copy-start.2 = (bf16[1536,384]{1,0:T(8,128)(2,1)S(1)}, bf16[1536,384]{1,0:T(8,128)(2,1)}, u32[]{:S(2)}) copy-start(bf16[1536,384]{1,0:T(8,128)(2,1)} %frames_ref.2) | copy-start | bytes 3538948
  3.4 4.5 %copy-start.3 = (bf16[1536,384]{1,0:T(8,128)(2,1)S(1)}, bf16[1536,384]{1,0:T(8,128)(2,1)}, u32[]{:S(2)}) copy-start(bf16[1536,384]{1,0:T(8,128)(2,1)} %frames_ref.3) | copy-start | bytes 3538948
  3.4 5.3 %collective-permute-start.3 = (bf16[1536,768]{1,0:T(8,128)(2,1)}, bf16[1536,768]{1,0:T(8,128)(2,1)S(1)}, u32[]{:S(2)}, u32[]{:S(2)}) collective-permute-start(bf16[1536,768]{1,0:T(8,128)(2,1)} %refs_4_.3), channel_id=1, source_target_pairs={{0,1},{1,0},{2,3},{3,2},{4,5},{5,4},{6,7},{7,6},{8,9},{9,8},{10,11... | collective-permute-start | bytes 7077896 | tf_op jit(solution)/shard_map/ppermute | solution.py:280
  4.0 10.4 %collective-permute-start.4 = (bf16[768,1536]{1,0:T(8,128)(2,1)}, bf16[768,1536]{1,0:T(8,128)(2,1)S(1)}, u32[]{:S(2)}, u32[]{:S(2)}) collective-permute-start(bf16[768,1536]{1,0:T(8,128)(2,1)} %refs_6_.3), channel_id=1, source_target_pairs={{0,1},{1,0},{2,3},{3,2},{4,5},{5,4},{6,7},{7,6},{8,9},{9,8},{10,11... | collective-permute-start | bytes 7077896 | tf_op jit(solution)/shard_map/ppermute | solution.py:280
  4.0 7.2 %collective-permute-start.1 = (bf16[192,384]{1,0:T(8,128)(2,1)S(1)}, bf16[192,384]{1,0:T(8,128)(2,1)S(1)}, u32[]{:S(2)}, u32[]{:S(2)}) collective-permute-start(bf16[192,384]{1,0:T(8,128)(2,1)S(1)} %fusion.6.refs_0_), channel_id=1, source_target_pairs={{0,2},{1,3},{2,0},{3,1},{4,6},{5,7},{6,4},{7,5},{8,10},{9,11},{10,... | collective-permute-start | bytes 442376 | tf_op jit(solution)/shard_map/ppermute | solution.py:277
  7.0 7.4 %copy-start.1 = (bf16[768,1536]{1,0:T(8,128)(2,1)S(1)}, bf16[768,1536]{1,0:T(8,128)(2,1)}, u32[]{:S(2)}) copy-start(bf16[768,1536]{1,0:T(8,128)(2,1)} %refs_6_.3) | copy-start | bytes 7077892
  7.6 4.1 %collective-permute-start = (bf16[192,384]{1,0:T(8,128)(2,1)S(1)}, bf16[192,384]{1,0:T(8,128)(2,1)S(1)}, u32[]{:S(2)}, u32[]{:S(2)}) collective-permute-start(bf16[192,384]{1,0:T(8,128)(2,1)S(1)} %fusion.5), channel_id=1, source_target_pairs={{0,1},{1,0},{2,3},{3,2},{4,5},{5,4},{6,7},{7,6},{8,9},{9,8},{10,11... | collective-permute-start | bytes 442376 | tf_op jit(solution)/shard_map/ppermute | solution.py:280
  7.7 6.7 %collective-permute-start.2 = (bf16[192,384]{1,0:T(8,128)(2,1)S(1)}, bf16[192,384]{1,0:T(8,128)(2,1)S(1)}, u32[]{:S(2)}, u32[]{:S(2)}) collective-permute-start(bf16[192,384]{1,0:T(8,128)(2,1)S(1)} %fusion.5), channel_id=1, source_target_pairs={{0,3},{1,2},{2,1},{3,0},{4,7},{5,6},{6,5},{7,4},{8,11},{9,10},{10,... | collective-permute-start | bytes 442376 | tf_op jit(solution)/shard_map/ppermute | solution.py:277
  7.9 6.5 %copy-start = (bf16[1536,768]{1,0:T(8,128)(2,1)S(1)}, bf16[1536,768]{1,0:T(8,128)(2,1)}, u32[]{:S(2)}) copy-start(bf16[1536,768]{1,0:T(8,128)(2,1)} %refs_4_.3) | copy-start | bytes 7077892
  7.9 6.5 %copy-start.4 = (f32[1536]{0:T(1024)S(1)}, f32[1536]{0:T(1024)}, u32[]{:S(2)}) copy-start(f32[1536]{0:T(1024)} %refs_8_.3) | copy-start | bytes 18436
  7.9 6.5 %copy-start.5 = (f32[1536]{0:T(1024)S(1)}, f32[1536]{0:T(1024)}, u32[]{:S(2)}) copy-start(f32[1536]{0:T(1024)} %refs_9_.3) | copy-start | bytes 18436
  8.8 10.6 %collective-permute-start.10 = (bf16[192,384]{1,0:T(8,128)(2,1)S(1)}, bf16[192,384]{1,0:T(8,128)(2,1)S(1)}, u32[]{:S(2)}, u32[]{:S(2)}) collective-permute-start(bf16[192,384]{1,0:T(8,128)(2,1)S(1)} %get-tuple-element.30), channel_id=1, source_target_pairs={{0,3},{1,2},{2,1},{3,0},{4,7},{5,6},{6,5},{7,4},{8,11},{9,10},{10,... | collective-permute-start | bytes 442376 | tf_op jit(solution)/shard_map/ppermute | solution.py:277
  11.3 8.1 %collective-permute-start.8 = (bf16[192,384]{1,0:T(8,128)(2,1)S(1)}, bf16[192,384]{1,0:T(8,128)(2,1)S(1)}, u32[]{:S(2)}, u32[]{:S(2)}) collective-permute-start(bf16[192,384]{1,0:T(8,128)(2,1)S(1)} %get-tuple-element.30), channel_id=1, source_target_pairs={{0,1},{1,0},{2,3},{3,2},{4,5},{5,4},{6,7},{7,6},{8,9},{9,8},{10,11... | collective-permute-start | bytes 442376 | tf_op jit(solution)/shard_map/ppermute | solution.py:280
  11.7 8.8 %collective-permute-start.9 = (bf16[192,384]{1,0:T(8,128)(2,1)S(1)}, bf16[192,384]{1,0:T(8,128)(2,1)S(1)}, u32[]{:S(2)}, u32[]{:S(2)}) collective-permute-start(bf16[192,384]{1,0:T(8,128)(2,1)S(1)} %get-tuple-element.29.refs_0_), channel_id=1, source_target_pairs={{0,2},{1,3},{2,0},{3,1},{4,6},{5,7},{6,4},{7,5},{8,10},{9,11},{10,... | collective-permute-start | bytes 442376 | tf_op jit(solution)/shard_map/ppermute | solution.py:277
  16.9 9.0 %collective-permute-start.5 = (bf16[192,384]{1,0:T(8,128)(2,1)S(1)}, bf16[192,384]{1,0:T(8,128)(2,1)S(1)}, u32[]{:S(2)}, u32[]{:S(2)}) collective-permute-start(bf16[192,384]{1,0:T(8,128)(2,1)S(1)} %get-tuple-element.24), channel_id=1, source_target_pairs={{0,2},{1,3},{2,0},{3,1},{4,6},{5,7},{6,4},{7,5},{8,10},{9,11},{10,... | collective-permute-start | bytes 442376 | tf_op jit(solution)/shard_map/ppermute | solution.py:277
  17.8 9.9 %collective-permute-start.6 = (bf16[192,384]{1,0:T(8,128)(2,1)S(1)}, bf16[192,384]{1,0:T(8,128)(2,1)S(1)}, u32[]{:S(2)}, u32[]{:S(2)}) collective-permute-start(bf16[192,384]{1,0:T(8,128)(2,1)S(1)} %get-tuple-element.25), channel_id=1, source_target_pairs={{0,1},{1,0},{2,3},{3,2},{4,5},{5,4},{6,7},{7,6},{8,9},{9,8},{10,11... | collective-permute-start | bytes 442376 | tf_op jit(solution)/shard_map/ppermute | solution.py:280
  19.3 8.3 %collective-permute-start.7 = (bf16[192,384]{1,0:T(8,128)(2,1)S(1)}, bf16[192,384]{1,0:T(8,128)(2,1)S(1)}, u32[]{:S(2)}, u32[]{:S(2)}) collective-permute-start(bf16[192,384]{1,0:T(8,128)(2,1)S(1)} %get-tuple-element.26), channel_id=1, source_target_pairs={{0,3},{1,2},{2,1},{3,0},{4,7},{5,6},{6,5},{7,4},{8,11},{9,10},{10,... | collective-permute-start | bytes 442376 | tf_op jit(solution)/shard_map/ppermute | solution.py:277
  24.1 6.9 %collective-permute-start.11 = (bf16[192,384]{1,0:T(8,128)(2,1)S(1)}, bf16[192,384]{1,0:T(8,128)(2,1)S(1)}, u32[]{:S(2)}, u32[]{:S(2)}) collective-permute-start(bf16[192,384]{1,0:T(8,128)(2,1)S(1)} %get-tuple-element.37), channel_id=1, source_target_pairs={{0,2},{1,3},{2,0},{3,1},{4,6},{5,7},{6,4},{7,5},{8,10},{9,11},{10,... | collective-permute-start | bytes 442376 | tf_op jit(solution)/shard_map/ppermute | solution.py:277
  25.9 5.0 %collective-permute-start.12 = (bf16[192,384]{1,0:T(8,128)(2,1)S(1)}, bf16[192,384]{1,0:T(8,128)(2,1)S(1)}, u32[]{:S(2)}, u32[]{:S(2)}) collective-permute-start(bf16[192,384]{1,0:T(8,128)(2,1)S(1)} %get-tuple-element.38), channel_id=1, source_target_pairs={{0,1},{1,0},{2,3},{3,2},{4,5},{5,4},{6,7},{7,6},{8,9},{9,8},{10,11... | collective-permute-start | bytes 442376 | tf_op jit(solution)/shard_map/ppermute | solution.py:280
  25.9 6.5 %collective-permute-start.13 = (bf16[192,384]{1,0:T(8,128)(2,1)S(1)}, bf16[192,384]{1,0:T(8,128)(2,1)S(1)}, u32[]{:S(2)}, u32[]{:S(2)}) collective-permute-start(bf16[192,384]{1,0:T(8,128)(2,1)S(1)} %get-tuple-element.39), channel_id=1, source_target_pairs={{0,3},{1,2},{2,1},{3,0},{4,7},{5,6},{6,5},{7,4},{8,11},{9,10},{10,... | collective-permute-start | bytes 442376 | tf_op jit(solution)/shard_map/ppermute | solution.py:277
  27.7 0.7 %copy-start.6 = (s32[384]{0:T(512)S(1)}, s32[384]{0:T(512)}, u32[]{:S(2)}) copy-start(s32[384]{0:T(512)} %live_slots.1.wanted_ref) | copy-start | bytes 4612

commit v8 on v7

--- a/solution.py
+++ b/solution.py
@@ -33,56 +33,19 @@
 
 
 def chunks_of(extent):
-    size = 512 if extent % 512 == 0 else extent
+    size = 256 if extent % 256 == 0 else extent
     return [(start, size) for start in range(0, extent, size)]
 
 
-def fetch(sources, targets, sems):
-    copies = [pltpu.make_async_copy(s, t, sems.at[i]) for i, (s, t) in enumerate(zip(sources, targets))]
-    for copy in copies:
-        copy.start()
-    return copies
-
-
-def call_in_hbm(body, name, outs, ins, scratch, flops, moved):
-    return pl.pallas_call(
-        body,
-        out_shape=outs,
-        in_specs=[ANY] * len(ins),
-        out_specs=jax.tree.map(lambda _: ANY, outs),
-        scratch_shapes=scratch,
-        compiler_params=pltpu.CompilerParams(vmem_limit_bytes=56 * 1024 * 1024),
-        cost_estimate=pl.CostEstimate(flops=flops, bytes_accessed=moved, transcendentals=0),
-        name=name,
-    )(*ins)
-
-
-def wanted_slots(count, picked):
-    slots = picked.shape[0]
+def wanted_slots(count_ref, picked_ref):
+    slots, indices = picked_ref.shape[0], count_ref.shape[0]
+    here = lax.broadcasted_iota(jnp.int32, (1, indices), 1) == lax.axis_index("tm")
+    count = jnp.sum(jnp.where(here, count_ref[...].reshape(1, indices), 0), axis=1, keepdims=True)
     live = lax.broadcasted_iota(jnp.int32, (8, slots), 1) < count
-    wanted = jnp.where(live, jnp.broadcast_to(picked.reshape(1, slots), (8, slots)), -1)
+    wanted = jnp.where(live, jnp.broadcast_to(picked_ref[...].reshape(1, slots), (8, slots)), -1)
     swapped = pltpu.roll(wanted, slots // 2, 1)
-    return jnp.where(lax.axis_index("pair") == 0, wanted, swapped)[:1]
-
-
-def slots_body(count_hbm, picked_hbm, wanted_hbm, count, picked, sems):
-    for copy in fetch((count_hbm, picked_hbm), (count, picked), sems):
-        copy.wait()
-    picked[...] = wanted_slots(count[lax.axis_index("tm")], picked[...]).reshape(picked.shape)
-    for copy in fetch((picked,), (wanted_hbm,), sems):
-        copy.wait()
-
-
-def live_slots(count, picked):
-    return call_in_hbm(
-        slots_body,
-        "live_slots",
-        jax.ShapeDtypeStruct(picked.shape, jnp.int32),
-        (count, picked),
-        [pltpu.SMEM(count.shape, jnp.int32), VMEM(picked.shape, jnp.int32), pltpu.SemaphoreType.DMA((2,))],
-        1,
-        1,
-    )
+    first = lax.axis_index("pair") == 0
+    return [jnp.where(first, x, y)[:1, : slots // 2] for x, y in ((wanted, swapped), (swapped, wanted))]
 
 
 def gather_rows(places, frames):
@@ -90,46 +53,47 @@
     return lax.dot_general(onehot, frames, (((0,), (0,)), ((), ())), preferred_element_type=F32).astype(BF16)
 
 
-def scatter_body(mines, sibs, wanted_ref, frames_ref, *refs):
-    parts, (out_hbm, out_ref, sems) = refs[: mines + sibs], refs[mines + sibs :]
-    wanted = wanted_ref[...].reshape(1, wanted_ref.shape[0])
-
-    def added(blocks):
-        total = blocks[0][...].astype(F32)
-        for block in blocks[1:]:
-            total = total + block[...].astype(F32)
-        return total.astype(BF16)
-
-    rows = jnp.concatenate([added(parts[:mines]), added(parts[mines:])], axis=0)
+def scatter_body(counts, frames_ref, *refs):
+    groups, at = [], 0
+    for n in counts:
+        rows = refs[at + 1][...].astype(F32)
+        for ref in refs[at + 2 : at + 1 + n]:
+            rows = rows + ref[...].astype(F32)
+        groups.append((refs[at][...].reshape(1, refs[at].shape[0]), rows.astype(BF16)))
+        at += 1 + n
+    out_ref, *scratch = refs[at:]
     stores = []
     for i, (start, size) in enumerate(chunks_of(frames_ref.shape[0])):
         place = lax.broadcasted_iota(jnp.int32, (size, 1), 0) + start
-        onehot = jnp.where(wanted == place, 1.0, 0.0).astype(BF16)
-        put = jnp.dot(onehot, rows, preferred_element_type=F32)
-        out_ref[start : start + size, :] = (frames_ref[start : start + size, :].astype(F32) + put).astype(BF16)
+        total = frames_ref[start : start + size, :].astype(F32)
+        for wanted, rows in groups:
+            onehot = jnp.where(wanted == place, 1.0, 0.0).astype(BF16)
+            total = total + jnp.dot(onehot, rows, preferred_element_type=F32)
+        if not scratch:
+            out_ref[start : start + size, :] = total.astype(BF16)
+            continue
+        staged, sems = scratch
+        staged[start : start + size, :] = total.astype(BF16)
         cut = pl.ds(start, size)
-        store = pltpu.make_async_copy(out_ref.at[cut], out_hbm.at[cut], sems.at[i])
+        store = pltpu.make_async_copy(staged.at[cut], out_ref.at[cut], sems.at[i])
         store.start()
         stores.append(store)
     for store in stores:
         store.wait()
 
 
-def scatter_rows(name, wanted, frames, mine_parts, sib_parts):
-    slots, (frames_dev, width) = wanted.shape[0], frames.shape
-    parts = list(mine_parts) + list(sib_parts)
+def scatter_rows(name, frames, groups, last=True):
+    operands = [x for wanted, parts in groups for x in (wanted, *parts)]
+    staging = [VMEM(frames.shape, BF16), pltpu.SemaphoreType.DMA((len(chunks_of(frames.shape[0])),))]
     return pl.pallas_call(
-        functools.partial(scatter_body, len(mine_parts), len(sib_parts)),
+        functools.partial(scatter_body, [len(parts) for _, parts in groups]),
         out_shape=jax.ShapeDtypeStruct(frames.shape, BF16),
-        in_specs=[vspec(), vspec()] + [vspec()] * len(parts),
-        out_specs=ANY,
-        scratch_shapes=[VMEM(frames.shape, BF16), pltpu.SemaphoreType.DMA((len(chunks_of(frames_dev)),))],
+        in_specs=[vspec()] * (1 + len(operands)),
+        out_specs=ANY if last else vspec(),
+        scratch_shapes=staging if last else [],
         compiler_params=pltpu.CompilerParams(vmem_limit_bytes=8 * 1024 * 1024),
-        cost_estimate=pl.CostEstimate(
-            flops=2 * slots * frames_dev * width, bytes_accessed=4 * frames_dev * width, transcendentals=0
-        ),
         name=name,
-    )(wanted, frames, *parts)
+    )(frames, *operands)
 
 
 def block_start(step, side, width):
@@ -156,13 +120,14 @@
         out[...] = total_ref[:, pl.ds(start, width)]
 
 
-def forward_body(ways, width, *refs):
+def forward_body(ways, width, count_ref, picked_ref, *refs):
     n = len(ways)
     blocks = refs[:n]
     up_own, up_sib, down_own, down_sib, gain_ref, router_ref = refs[n : n + 6]
     outs = refs[n + 6 : 2 * n + 6]
     full_ref, stats_ref, hidden_ref, slope_ref = refs[2 * n + 6 : 2 * n + 10]
-    (total_ref,) = refs[2 * n + 10 :]
+    mine_ref, sib_ref, total_ref = refs[2 * n + 10 :]
+    mine_ref[...], sib_ref[...] = [x.reshape(mine_ref.shape) for x in wanted_slots(count_ref, picked_ref)]
     assemble(full_ref, blocks, ways, width)
     half, features = full_ref.shape
     hidden_dev = up_own.shape[1]
@@ -187,7 +152,7 @@
     dissect(total_ref, outs, ways, width)
 
 
-def forward(blocks, ways, weights, gain, router):
+def forward(count, picked, blocks, ways, weights, gain, router):
     half, width = blocks[0].shape
     features, hidden_dev = weights[0].shape
     piece = jax.ShapeDtypeStruct((half, width), BF16)
@@ -200,15 +165,16 @@
             jax.ShapeDtypeStruct((half, 128), F32),
             jax.ShapeDtypeStruct((half, 2 * hidden_dev), BF16),
             jax.ShapeDtypeStruct((half, 2 * hidden_dev), F32),
-        ),
-        (*blocks, *weights, gain, router),
-        [vspec()] * (len(blocks) + 6),
+        )
+        + (jax.ShapeDtypeStruct((half,), jnp.int32),) * 2,
+        (count, picked, *blocks, *weights, gain, router),
+        [vspec()] * (len(blocks) + 8),
         [VMEM((half, features), BF16)],
         1,
         1,
         16,
     )
-    return got[: len(ways)], got[len(ways) :]
+    return got[: len(ways)], got[len(ways) : -2], got[-2:]
 
 
 def backward_body(ways, width, *refs):
@@ -292,8 +258,8 @@
             return outs
         return [lax.dynamic_slice_in_dim(outs[0], block_start(k, side, width), width, 1) for k, side in pieces]
 
-    def collect(mine, sib):
-        return [mine, swap(sib)] + [send(mine, k, 0) for k in steps] + [send(sib, k, 1) for k in steps]
+    def collect(mine, sib, near):
+        return [mine, swap(near)] + [send(mine, k, 0) for k in steps] + [send(sib, k, 1) for k in steps]
 
     def deliver(parts):
         count = tensors - 1
@@ -301,25 +267,25 @@
         far_sib = [send(x, k, 1) for x, k in zip(parts[2 + count :], steps)]
         return [parts[0]] + far_mine, [swap(parts[1])] + far_sib
 
-    wanted = live_slots(picked_count, picked_rows)
     first = lax.axis_index("pair") == 0
     places_mine = jnp.where(first, picked_rows[:half], picked_rows[half:])
     places_sib = jnp.where(first, picked_rows[half:], picked_rows[:half])
     mine, sib = gather_rows(places_mine, frames), gather_rows(places_sib, frames)
-    blocks = collect(mine, sib)
+    blocks = collect(mine, sib, after(sib, mine))
     up_sib, down_sib = swap(after(up_weight, mine)), swap(after(down_weight, mine))
     weights = (up_weight, up_sib, down_weight, down_sib)
     rows = gather_rows(jnp.concatenate([places_mine, places_sib]), cotangent)
     cot_mine, cot_sib = lax.optimization_barrier((rows[:half], rows[half:]))
     cot_mine, cot_sib = lax.optimization_barrier((cot_mine, cot_sib, up_sib))[:2]
-    cot_blocks = collect(cot_mine, cot_sib)
-    parts, saved = forward(joined(blocks), ways, weights, gain, router)
+    cot_blocks = collect(cot_mine, cot_sib, cot_sib)
+    parts, saved, wanted = forward(picked_count, picked_rows, joined(blocks), ways, weights, gain, router)
     out_mine, out_sib = deliver(cut(parts))
     grads = backward(joined(cot_blocks), ways, weights, gain, router, saved)
     grad_mine, grad_sib = deliver(cut(grads))
-    mixed = scatter_rows("mixed_rows", wanted, frames, out_mine, out_sib)
+    mixed = scatter_rows("mixed_rows", frames, [(wanted[0], out_mine), (wanted[1], out_sib)])
     grad_mine[0] = after(grad_mine[0], mixed)
-    frames_grad = scatter_rows("grad_rows", wanted, cotangent, grad_mine, grad_sib)
+    started = scatter_rows("grad_rows_mine", cotangent, [(wanted[0], grad_mine)], last=False)
+    frames_grad = scatter_rows("grad_rows", started, [(wanted[1], grad_sib)])
     return (mixed, frames_grad)
 
 

time: 34.4 us -> 34.1 us (level)
  waiting for transfers between devices: 4.92 us -> 8.05 us
  starting transfers between devices: 12.5 us -> 10.9 us
  Pallas kernels: 10.8 us -> 9.79 us
  local copies, waits for them, and re-layouts: 0.74 us -> 0.07 us
    ppermute x8, waiting for transfers between devices: 4.52 us -> 7.52 us  [send(): return lax.ppermute(x, ('tensor', 'pair'), pairs)]
    pallas_call x3, Pallas kernels: 4.69 us -> 3.62 us  [scatter_rows(): pl.pallas_call(functools.partial(scatter_body, [len(parts) for _, parts i...]
    ppermute x6, starting transfers between devices: 2.28 us -> 1.24 us  [swap(): return lax.ppermute(x, 'pair', [(0, 1), (1, 0)])]
    unnamed x14 -> x16, local copies, waits for them, and re-layouts: 0.7 us -> 0.04 us
    ppermute x8, starting transfers between devices: 10.2 us -> 9.63 us  [send(): return lax.ppermute(x, ('tensor', 'pair'), pairs)]
  transfers between devices with their start and end apart: 14 -> 14, of which waited for: 6 -> 6; matrix products, arithmetic and copies ran while one was open for 5% -> 5% of each run, Pallas kernels for 27% -> 25%
where the time goes in v8:
time: 34.1 us; the launch traced here: 33.9 us
  starting transfers between devices  10.9 us (32%)
  Pallas kernels  9.79 us (29%)
  waiting for transfers between devices  8.05 us (24%)
  matrix products  3.39 us (10%)
  other arithmetic  0.94 us (3%)
  between operations  0.81 us (2%)
    ppermute x8, starting transfers between devices, send(): return lax.ppermute(x, ('tensor', 'pair'), pairs)  9.63 us
    ppermute x8, waiting for transfers between devices, send(): return lax.ppermute(x, ('tensor', 'pair'), pairs)  7.52 us
    pallas_call x2, Pallas kernels, call(): pl.pallas_call(body, out_shape=outs, in_specs=specs, out_specs=jax.tree.m...  6.17 us
    pallas_call x3, Pallas kernels, scatter_rows(): pl.pallas_call(functools.partial(scatter_body, [len(parts) for _, parts i...  3.62 us
    dot_general x3, matrix products, gather_rows(): lax.dot_general(onehot, frames, (((0,), (0,)), ((), ())), preferred_eleme...  3.39 us
    ppermute x6, starting transfers between devices, swap(): return lax.ppermute(x, 'pair', [(0, 1), (1, 0)])  1.24 us
    select_n x1, other arithmetic, per_device(): places_sib = jnp.where(first, picked_rows[half:], picked_rows[:half])  0.87 us
  transfers between devices with their start and end apart: 14, of which 6 were waited for; matrix products, arithmetic and copies ran while one was open for 5% of the time, Pallas kernels for 25%

profile of v8, /device:TPU:0, one launch (start us, length us, event | category | flops | bytes accessed | tf_op | source)
XLA Modules:
  0.0 33.9 jit_solution(5819381933105336315)
XLA Ops:
  0.6 0.0 copy-start.2
  0.6 0.9 %broadcast_select_fusion = (s32[192]{0:T(256)S(1)}, s32[192]{0:T(256)S(1)}) fusion(pred[]{:T(512)S(6)} %eq.21, s32[384]{0:T(512)} %picked_ref.1), kind=kLoop, calls=%fused_computation.13 | loop fusion | flops 384 | bytes 3073 | tf_op jit(solution)/shard_map/jit(_where)/select_n | solution.py:272
  1.5 1.9 %fusion.6.refs_0_ = bf16[192,384]{1,0:T(8,128)(2,1)S(1)} fusion(bf16[1536,384]{1,0:T(8,128)(2,1)} %frames_ref.2, s32[192]{0:T(256)S(1)} %get-tuple-element.49), kind=kOutput, calls=%fused_computation.9 | convolution fusion | flops 226861056 | bytes 1327872 | tf_op jit(solution)/shard_map/dot_general | solution.py:53
  3.4 0.0 copy-start.3
  3.4 0.5 %collective-permute-start.3 = (bf16[1536,768]{1,0:T(8,128)(2,1)}, bf16[1536,768]{1,0:T(8,128)(2,1)S(1)}, u32[]{:S(2)}, u32[]{:S(2)}) collective-permute-start(bf16[1536,768]{1,0:T(8,128)(2,1)} %refs_4_.3), channel_id=1, source_target_pairs={{0,1},{1,0},{2,3},{3,2},{4,5},{5,4},{6,7},{7,6},{8,9},{9,8},{10,11... | collective-permute-start | bytes 7077896 | tf_op jit(solution)/shard_map/ppermute | solution.py:246
  4.0 0.1 collective-permute-start.4
  4.0 2.9 %collective-permute-start.1 = (bf16[192,384]{1,0:T(8,128)(2,1)S(1)}, bf16[192,384]{1,0:T(8,128)(2,1)S(1)}, u32[]{:S(2)}, u32[]{:S(2)}) collective-permute-start(bf16[192,384]{1,0:T(8,128)(2,1)S(1)} %fusion.6.refs_0_), channel_id=1, source_target_pairs={{0,2},{1,3},{2,0},{3,1},{4,6},{5,7},{6,4},{7,5},{8,10},{9,11},{10,... | collective-permute-start | bytes 442376 | tf_op jit(solution)/shard_map/ppermute | solution.py:243
  7.0 0.0 copy-done.2
  7.0 0.0 copy-start.1
  7.0 0.6 %fusion.5 = bf16[192,384]{1,0:T(8,128)(2,1)S(1)} fusion(bf16[1536,384]{1,0:T(8,128)(2,1)S(1)} %copy-done.2, s32[192]{0:T(256)S(1)} %get-tuple-element.48), kind=kOutput, calls=%fused_computation.8 | convolution fusion | flops 226861056 | bytes 1327872 | tf_op jit(solution)/shard_map/dot_general | solution.py:53
  7.6 0.1 collective-permute-start.2
  7.7 0.1 collective-permute-start
  7.8 0.1 pad_add_fusion
  7.9 0.0 copy-done.3
  7.9 0.0 copy-start
  7.9 0.0 copy-start.4
  7.9 0.0 copy-start.5
  7.9 0.0 copy-start.6
  7.9 0.0 copy-start.7
  7.9 0.8 %fusion.3 = bf16[384,384]{1,0:T(8,128)(2,1)S(1)} fusion(bf16[1536,384]{1,0:T(8,128)(2,1)S(1)} %copy-done.3, s32[384]{0:T(512)S(1)} %pad_add_fusion), kind=kOutput, calls=%fused_computation.6 | convolution fusion | flops 453722112 | bytes 1476096 | tf_op jit(solution)/shard_map/dot_general | solution.py:53
  8.8 0.0 collective-permute-done.3.refs_5_
  8.8 2.4 %collective-permute-start.9 = (bf16[192,384]{1,0:T(8,128)(2,1)S(1)}, bf16[192,384]{1,0:T(8,128)(2,1)S(1)}, u32[]{:S(2)}, u32[]{:S(2)}) collective-permute-start(bf16[192,384]{1,0:T(8,128)(2,1)S(1)} %get-tuple-element.35.refs_0_), channel_id=1, source_target_pairs={{0,2},{1,3},{2,0},{3,1},{4,6},{5,7},{6,4},{7,5},{8,10},{9,11},{10,... | collective-permute-start | bytes 442376 | tf_op jit(solution)/shard_map/ppermute | solution.py:243
  11.2 0.5 %collective-permute-done.refs_1_ = bf16[192,384]{1,0:T(8,128)(2,1)S(1)} collective-permute-done((bf16[192,384]{1,0:T(8,128)(2,1)S(1)}, bf16[192,384]{1,0:T(8,128)(2,1)S(1)}, u32[]{:S(2)}, u32[]{:S(2)}) %collective-permute-start) | collective-permute-done | bytes 147488 | tf_op jit(solution)/shard_map/ppermute | solution.py:246
  11.7 0.0 collective-permute-start.10
  11.7 2.6 %collective-permute-done.2.refs_3_ = bf16[192,384]{1,0:T(8,128)(2,1)S(1)} collective-permute-done((bf16[192,384]{1,0:T(8,128)(2,1)S(1)}, bf16[192,384]{1,0:T(8,128)(2,1)S(1)}, u32[]{:S(2)}, u32[]{:S(2)}) %collective-permute-start.2) | collective-permute-done | bytes 147488 | tf_op jit(solution)/shard_map/ppermute | solution.py:243
  14.3 0.0 collective-permute-start.8
  14.3 0.0 collective-permute-done.1.refs_2_
  14.3 0.0 collective-permute-done.4.refs_7_
  14.4 0.0 copy-done.1
  14.4 0.0 copy-done
  14.4 0.0 copy-done.4
  14.4 0.0 copy-done.5
  14.4 0.0 copy-done.6
  14.4 0.0 copy-done.7
  14.4 2.6 %forward.1 = (bf16[192,384]{1,0:T(8,128)(2,1)S(1)}, bf16[192,384]{1,0:T(8,128)(2,1)S(1)}, bf16[192,384]{1,0:T(8,128)(2,1)S(1)}, bf16[192,384]{1,0:T(8,128)(2,1)S...) custom-call(s32[4]{0:T(128)S(1)} %copy-done.7, ...), custom_call_target="tpu_custom_call" | custom-call | flops 1 | bytes 1 | tf_op jit(solution)/shard_map/forward/pallas_call | solution.py:23
  17.0 2.4 %collective-permute-start.5 = (bf16[192,384]{1,0:T(8,128)(2,1)S(1)}, bf16[192,384]{1,0:T(8,128)(2,1)S(1)}, u32[]{:S(2)}, u32[]{:S(2)}) collective-permute-start(bf16[192,384]{1,0:T(8,128)(2,1)S(1)} %get-tuple-element.29), channel_id=1, source_target_pairs={{0,2},{1,3},{2,0},{3,1},{4,6},{5,7},{6,4},{7,5},{8,10},{9,11},{10,... | collective-permute-start | bytes 442376 | tf_op jit(solution)/shard_map/ppermute | solution.py:243
  19.4 0.0 collective-permute-start.6
  19.4 0.0 collective-permute-done.9.refs_2_
  19.4 0.2 collective-permute-start.7
  19.6 0.6 %collective-permute-done.10.refs_3_ = bf16[192,384]{1,0:T(8,128)(2,1)S(1)} collective-permute-done((bf16[192,384]{1,0:T(8,128)(2,1)S(1)}, bf16[192,384]{1,0:T(8,128)(2,1)S(1)}, u32[]{:S(2)}, u32[]{:S(2)}) %collective-permute-start.10) | collective-permute-done | bytes 147488 | tf_op jit(solution)/shard_map/ppermute | solution.py:243
  20.2 0.0 collective-permute-done.8.refs_1_
  20.2 3.6 %backward.1 = (bf16[192,384]{1,0:T(8,128)(2,1)S(1)}, bf16[192,384]{1,0:T(8,128)(2,1)S(1)}, bf16[192,384]{1,0:T(8,128)(2,1)S(1)}, bf16[192,384]{1,0:T(8,128)(2,1)S(1)}) custom-call(bf16[192,384]{1,0:T(8,128)(2,1)S(1)} %get-tuple-element.35.refs_0_, bf16[192,384]{1,0:T(8,128)(2,1)S(1)} %collective-permute-done.8.refs_1_, ...), custom_call_target="tpu_custom_call" | custom-call | flops 1 | bytes 1 | tf_op jit(solution)/shard_map/backward/pallas_call | solution.py:23
  23.8 1.4 %collective-permute-start.11 = (bf16[192,384]{1,0:T(8,128)(2,1)S(1)}, bf16[192,384]{1,0:T(8,128)(2,1)S(1)}, u32[]{:S(2)}, u32[]{:S(2)}) collective-permute-start(bf16[192,384]{1,0:T(8,128)(2,1)S(1)} %get-tuple-element.43), channel_id=1, source_target_pairs={{0,2},{1,3},{2,0},{3,1},{4,6},{5,7},{6,4},{7,5},{8,10},{9,11},{10,... | collective-permute-start | bytes 442376 | tf_op jit(solution)/shard_map/ppermute | solution.py:243
  25.2 0.5 %collective-permute-start.12 = (bf16[192,384]{1,0:T(8,128)(2,1)S(1)}, bf16[192,384]{1,0:T(8,128)(2,1)S(1)}, u32[]{:S(2)}, u32[]{:S(2)}) collective-permute-start(bf16[192,384]{1,0:T(8,128)(2,1)S(1)} %get-tuple-element.44), channel_id=1, source_target_pairs={{0,1},{1,0},{2,3},{3,2},{4,5},{5,4},{6,7},{7,6},{8,9},{9,8},{10,11... | collective-permute-start | bytes 442376 | tf_op jit(solution)/shard_map/ppermute | solution.py:246
  25.7 0.0 collective-permute-done.5.refs_2_
  25.7 0.3 collective-permute-start.13
  26.0 0.0 collective-permute-done.6.refs_4_
  26.0 0.5 %collective-permute-done.7.refs_5_ = bf16[192,384]{1,0:T(8,128)(2,1)S(1)} collective-permute-done((bf16[192,384]{1,0:T(8,128)(2,1)S(1)}, bf16[192,384]{1,0:T(8,128)(2,1)S(1)}, u32[]{:S(2)}, u32[]{:S(2)}) %collective-permute-start.7) | collective-permute-done | bytes 147488 | tf_op jit(solution)/shard_map/ppermute | solution.py:243
  26.5 1.7 %mixed_rows.1 = bf16[1536,384]{1,0:T(8,128)(2,1)} custom-call(bf16[1536,384]{1,0:T(8,128)(2,1)S(1)} %copy-done.2, s32[192]{0:T(256)S(1)} %get-tuple-element.27.refs_0_, bf16[192,384]{1,0:T(8,128)(2,1)S(1)} %get-tuple-element.28.refs_1_, bf16[192,384]{1,0:T(8,128)(2,1)S(1)} %collective-permute-done.5.refs_2_, s32[192]{0:T(256)S(1)} %get-tuple-element.30.refs_3_.refs_0_, ...), custom_call_target="tpu_custom_call" | custom-call | tf_op jit(solution)/shard_map/mixed_rows/pallas_call | solution.py:88
  28.3 2.3 %collective-permute-done.11.refs_2_ = bf16[192,384]{1,0:T(8,128)(2,1)S(1)} collective-permute-done((bf16[192,384]{1,0:T(8,128)(2,1)S(1)}, bf16[192,384]{1,0:T(8,128)(2,1)S(1)}, u32[]{:S(2)}, u32[]{:S(2)}) %collective-permute-start.11) | collective-permute-done | bytes 147488 | tf_op jit(solution)/shard_map/ppermute | solution.py:243
  30.6 0.6 %grad_rows_mine.1.frames_ref = bf16[1536,384]{1,0:T(8,128)(2,1)S(1)} custom-call(bf16[1536,384]{1,0:T(8,128)(2,1)S(1)} %copy-done.3, s32[192]{0:T(256)S(1)} %get-tuple-element.27.refs_0_, bf16[192,384]{1,0:T(8,128)(2,1)S(1)} %get-tuple-element.42.refs_1_, bf16[192,384]{1,0:T(8,128)(2,1)S(1)} %collective-permute-done.11.refs_2_), custom_call_target="tpu_custom_call" | custom-call | tf_op jit(solution)/shard_map/grad_rows_mine/pallas_call | solution.py:88
  31.1 0.0 collective-permute-done.12.refs_1_
  31.1 1.5 %collective-permute-done.13.refs_2_ = bf16[192,384]{1,0:T(8,128)(2,1)S(1)} collective-permute-done((bf16[192,384]{1,0:T(8,128)(2,1)S(1)}, bf16[192,384]{1,0:T(8,128)(2,1)S(1)}, u32[]{:S(2)}, u32[]{:S(2)}) %collective-permute-start.13) | collective-permute-done | bytes 147488 | tf_op jit(solution)/shard_map/ppermute | solution.py:243
  32.6 1.3 %grad_rows.1 = bf16[1536,384]{1,0:T(8,128)(2,1)} custom-call(bf16[1536,384]{1,0:T(8,128)(2,1)S(1)} %grad_rows_mine.1.frames_ref, s32[192]{0:T(256)S(1)} %get-tuple-element.30.refs_3_.refs_0_, bf16[192,384]{1,0:T(8,128)(2,1)S(1)} %collective-permute-done.12.refs_1_, bf16[192,384]{1,0:T(8,128)(2,1)S(1)} %collective-permute-done.13.refs_2_), custom_call_target="tpu_custom_call" | custom-call | tf_op jit(solution)/shard_map/grad_rows/pallas_call | solution.py:88
  (1 shorter events, 0.0 us)
Async XLA Ops:
  0.6 6.3 %copy-start.2 = (bf16[1536,384]{1,0:T(8,128)(2,1)S(1)}, bf16[1536,384]{1,0:T(8,128)(2,1)}, u32[]{:S(2)}) copy-start(bf16[1536,384]{1,0:T(8,128)(2,1)} %frames_ref.2) | copy-start | bytes 3538948
  3.4 4.4 %copy-start.3 = (bf16[1536,384]{1,0:T(8,128)(2,1)S(1)}, bf16[1536,384]{1,0:T(8,128)(2,1)}, u32[]{:S(2)}) copy-start(bf16[1536,384]{1,0:T(8,128)(2,1)} %frames_ref.3) | copy-start | bytes 3538948
  3.4 5.3 %collective-permute-start.3 = (bf16[1536,768]{1,0:T(8,128)(2,1)}, bf16[1536,768]{1,0:T(8,128)(2,1)S(1)}, u32[]{:S(2)}, u32[]{:S(2)}) collective-permute-start(bf16[1536,768]{1,0:T(8,128)(2,1)} %refs_4_.3), channel_id=1, source_target_pairs={{0,1},{1,0},{2,3},{3,2},{4,5},{5,4},{6,7},{7,6},{8,9},{9,8},{10,11... | collective-permute-start | bytes 7077896 | tf_op jit(solution)/shard_map/ppermute | solution.py:246
  4.0 10.4 %collective-permute-start.4 = (bf16[768,1536]{1,0:T(8,128)(2,1)}, bf16[768,1536]{1,0:T(8,128)(2,1)S(1)}, u32[]{:S(2)}, u32[]{:S(2)}) collective-permute-start(bf16[768,1536]{1,0:T(8,128)(2,1)} %refs_6_.3), channel_id=1, source_target_pairs={{0,1},{1,0},{2,3},{3,2},{4,5},{5,4},{6,7},{7,6},{8,9},{9,8},{10,11... | collective-permute-start | bytes 7077896 | tf_op jit(solution)/shard_map/ppermute | solution.py:246
  4.0 10.3 %collective-permute-start.1 = (bf16[192,384]{1,0:T(8,128)(2,1)S(1)}, bf16[192,384]{1,0:T(8,128)(2,1)S(1)}, u32[]{:S(2)}, u32[]{:S(2)}) collective-permute-start(bf16[192,384]{1,0:T(8,128)(2,1)S(1)} %fusion.6.refs_0_), channel_id=1, source_target_pairs={{0,2},{1,3},{2,0},{3,1},{4,6},{5,7},{6,4},{7,5},{8,10},{9,11},{10,... | collective-permute-start | bytes 442376 | tf_op jit(solution)/shard_map/ppermute | solution.py:243
  7.0 7.4 %copy-start.1 = (bf16[768,1536]{1,0:T(8,128)(2,1)S(1)}, bf16[768,1536]{1,0:T(8,128)(2,1)}, u32[]{:S(2)}) copy-start(bf16[768,1536]{1,0:T(8,128)(2,1)} %refs_6_.3) | copy-start | bytes 7077892
  7.6 6.7 %collective-permute-start.2 = (bf16[192,384]{1,0:T(8,128)(2,1)S(1)}, bf16[192,384]{1,0:T(8,128)(2,1)S(1)}, u32[]{:S(2)}, u32[]{:S(2)}) collective-permute-start(bf16[192,384]{1,0:T(8,128)(2,1)S(1)} %fusion.5), channel_id=1, source_target_pairs={{0,3},{1,2},{2,1},{3,0},{4,7},{5,6},{6,5},{7,4},{8,11},{9,10},{10,... | collective-permute-start | bytes 442376 | tf_op jit(solution)/shard_map/ppermute | solution.py:243
  7.7 4.0 %collective-permute-start = (bf16[192,384]{1,0:T(8,128)(2,1)S(1)}, bf16[192,384]{1,0:T(8,128)(2,1)S(1)}, u32[]{:S(2)}, u32[]{:S(2)}) collective-permute-start(bf16[192,384]{1,0:T(8,128)(2,1)S(1)} %fusion.5), channel_id=1, source_target_pairs={{0,1},{1,0},{2,3},{3,2},{4,5},{5,4},{6,7},{7,6},{8,9},{9,8},{10,11... | collective-permute-start | bytes 442376 | tf_op jit(solution)/shard_map/ppermute | solution.py:246
  7.9 6.5 %copy-start = (bf16[1536,768]{1,0:T(8,128)(2,1)S(1)}, bf16[1536,768]{1,0:T(8,128)(2,1)}, u32[]{:S(2)}) copy-start(bf16[1536,768]{1,0:T(8,128)(2,1)} %refs_4_.3) | copy-start | bytes 7077892
  7.9 6.5 %copy-start.4 = (f32[1536]{0:T(1024)S(1)}, f32[1536]{0:T(1024)}, u32[]{:S(2)}) copy-start(f32[1536]{0:T(1024)} %refs_8_.3) | copy-start | bytes 18436
  7.9 6.5 %copy-start.5 = (f32[1536]{0:T(1024)S(1)}, f32[1536]{0:T(1024)}, u32[]{:S(2)}) copy-start(f32[1536]{0:T(1024)} %refs_9_.3) | copy-start | bytes 18436
  7.9 6.5 %copy-start.6 = (s32[384]{0:T(512)S(1)}, s32[384]{0:T(512)}, u32[]{:S(2)}) copy-start(s32[384]{0:T(512)} %picked_ref.1) | copy-start | bytes 4612
  7.9 6.5 %copy-start.7 = (s32[4]{0:T(128)S(1)}, s32[4]{0:T(128)}, u32[]{:S(2)}) copy-start(s32[4]{0:T(128)} %count_ref.1) | copy-start | bytes 52
  8.8 10.6 %collective-permute-start.9 = (bf16[192,384]{1,0:T(8,128)(2,1)S(1)}, bf16[192,384]{1,0:T(8,128)(2,1)S(1)}, u32[]{:S(2)}, u32[]{:S(2)}) collective-permute-start(bf16[192,384]{1,0:T(8,128)(2,1)S(1)} %get-tuple-element.35.refs_0_), channel_id=1, source_target_pairs={{0,2},{1,3},{2,0},{3,1},{4,6},{5,7},{6,4},{7,5},{8,10},{9,11},{10,... | collective-permute-start | bytes 442376 | tf_op jit(solution)/shard_map/ppermute | solution.py:243
  11.7 8.5 %collective-permute-start.10 = (bf16[192,384]{1,0:T(8,128)(2,1)S(1)}, bf16[192,384]{1,0:T(8,128)(2,1)S(1)}, u32[]{:S(2)}, u32[]{:S(2)}) collective-permute-start(bf16[192,384]{1,0:T(8,128)(2,1)S(1)} %get-tuple-element.36), channel_id=1, source_target_pairs={{0,3},{1,2},{2,1},{3,0},{4,7},{5,6},{6,5},{7,4},{8,11},{9,10},{10,... | collective-permute-start | bytes 442376 | tf_op jit(solution)/shard_map/ppermute | solution.py:243
  14.3 5.9 %collective-permute-start.8 = (bf16[192,384]{1,0:T(8,128)(2,1)S(1)}, bf16[192,384]{1,0:T(8,128)(2,1)S(1)}, u32[]{:S(2)}, u32[]{:S(2)}) collective-permute-start(bf16[192,384]{1,0:T(8,128)(2,1)S(1)} %get-tuple-element.36), channel_id=1, source_target_pairs={{0,1},{1,0},{2,3},{3,2},{4,5},{5,4},{6,7},{7,6},{8,9},{9,8},{10,11... | collective-permute-start | bytes 442376 | tf_op jit(solution)/shard_map/ppermute | solution.py:246
  17.0 8.7 %collective-permute-start.5 = (bf16[192,384]{1,0:T(8,128)(2,1)S(1)}, bf16[192,384]{1,0:T(8,128)(2,1)S(1)}, u32[]{:S(2)}, u32[]{:S(2)}) collective-permute-start(bf16[192,384]{1,0:T(8,128)(2,1)S(1)} %get-tuple-element.29), channel_id=1, source_target_pairs={{0,2},{1,3},{2,0},{3,1},{4,6},{5,7},{6,4},{7,5},{8,10},{9,11},{10,... | collective-permute-start | bytes 442376 | tf_op jit(solution)/shard_map/ppermute | solution.py:243
  19.4 6.7 %collective-permute-start.6 = (bf16[192,384]{1,0:T(8,128)(2,1)S(1)}, bf16[192,384]{1,0:T(8,128)(2,1)S(1)}, u32[]{:S(2)}, u32[]{:S(2)}) collective-permute-start(bf16[192,384]{1,0:T(8,128)(2,1)S(1)} %get-tuple-element.31), channel_id=1, source_target_pairs={{0,1},{1,0},{2,3},{3,2},{4,5},{5,4},{6,7},{7,6},{8,9},{9,8},{10,11... | collective-permute-start | bytes 442376 | tf_op jit(solution)/shard_map/ppermute | solution.py:246
  19.4 7.1 %collective-permute-start.7 = (bf16[192,384]{1,0:T(8,128)(2,1)S(1)}, bf16[192,384]{1,0:T(8,128)(2,1)S(1)}, u32[]{:S(2)}, u32[]{:S(2)}) collective-permute-start(bf16[192,384]{1,0:T(8,128)(2,1)S(1)} %get-tuple-element.32), channel_id=1, source_target_pairs={{0,3},{1,2},{2,1},{3,0},{4,7},{5,6},{6,5},{7,4},{8,11},{9,10},{10,... | collective-permute-start | bytes 442376 | tf_op jit(solution)/shard_map/ppermute | solution.py:243
  23.8 6.7 %collective-permute-start.11 = (bf16[192,384]{1,0:T(8,128)(2,1)S(1)}, bf16[192,384]{1,0:T(8,128)(2,1)S(1)}, u32[]{:S(2)}, u32[]{:S(2)}) collective-permute-start(bf16[192,384]{1,0:T(8,128)(2,1)S(1)} %get-tuple-element.43), channel_id=1, source_target_pairs={{0,2},{1,3},{2,0},{3,1},{4,6},{5,7},{6,4},{7,5},{8,10},{9,11},{10,... | collective-permute-start | bytes 442376 | tf_op jit(solution)/shard_map/ppermute | solution.py:243
  25.2 6.0 %collective-permute-start.12 = (bf16[192,384]{1,0:T(8,128)(2,1)S(1)}, bf16[192,384]{1,0:T(8,128)(2,1)S(1)}, u32[]{:S(2)}, u32[]{:S(2)}) collective-permute-start(bf16[192,384]{1,0:T(8,128)(2,1)S(1)} %get-tuple-element.44), channel_id=1, source_target_pairs={{0,1},{1,0},{2,3},{3,2},{4,5},{5,4},{6,7},{7,6},{8,9},{9,8},{10,11... | collective-permute-start | bytes 442376 | tf_op jit(solution)/shard_map/ppermute | solution.py:246
  25.7 6.9 %collective-permute-start.13 = (bf16[192,384]{1,0:T(8,128)(2,1)S(1)}, bf16[192,384]{1,0:T(8,128)(2,1)S(1)}, u32[]{:S(2)}, u32[]{:S(2)}) collective-permute-start(bf16[192,384]{1,0:T(8,128)(2,1)S(1)} %get-tuple-element.45), channel_id=1, source_target_pairs={{0,3},{1,2},{2,1},{3,0},{4,7},{5,6},{6,5},{7,4},{8,11},{9,10},{10,... | collective-permute-start | bytes 442376 | tf_op jit(solution)/shard_map/ppermute | solution.py:243

commit v9 on v8

--- a/solution.py
+++ b/solution.py
@@ -270,13 +270,17 @@
     first = lax.axis_index("pair") == 0
     places_mine = jnp.where(first, picked_rows[:half], picked_rows[half:])
     places_sib = jnp.where(first, picked_rows[half:], picked_rows[:half])
-    mine, sib = gather_rows(places_mine, frames), gather_rows(places_sib, frames)
+    found = (lax.broadcasted_iota(jnp.int32, (frames.shape[0], 1), 0) == picked_rows).astype(BF16)
+    rows = lax.dot_general(found, frames, (((0,), (0,)), ((), ())), preferred_element_type=F32).astype(BF16)
+    mine = jnp.where(first, rows[:half], rows[half:])
+    sib = jnp.where(first, rows[half:], rows[:half])
     blocks = collect(mine, sib, after(sib, mine))
-    up_sib, down_sib = swap(after(up_weight, mine)), swap(after(down_weight, mine))
+    up_sib, down_sib = swap(up_weight), swap(after(down_weight, mine))
     weights = (up_weight, up_sib, down_weight, down_sib)
-    rows = gather_rows(jnp.concatenate([places_mine, places_sib]), cotangent)
-    cot_mine, cot_sib = lax.optimization_barrier((rows[:half], rows[half:]))
-    cot_mine, cot_sib = lax.optimization_barrier((cot_mine, cot_sib, up_sib))[:2]
+    rows = lax.dot_general(found, cotangent, (((0,), (0,)), ((), ())), preferred_element_type=F32).astype(BF16)
+    cot_mine = jnp.where(first, rows[:half], rows[half:])
+    cot_sib = jnp.where(first, rows[half:], rows[:half])
+    cot_mine, cot_sib = after(cot_mine, up_sib), after(cot_sib, up_sib, blocks[1])
     cot_blocks = collect(cot_mine, cot_sib, cot_sib)
     parts, saved, wanted = forward(picked_count, picked_rows, joined(blocks), ways, weights, gain, router)
     out_mine, out_sib = deliver(cut(parts))

time: 34.1 us -> 33.9 us (level)
  other arithmetic: 0.94 us -> 0.07 us
  waiting for transfers between devices: 8.05 us -> 8.67 us
  starting transfers between devices: 10.9 us -> 11.3 us
    ppermute x6, waiting for transfers between devices: 0.53 us -> 1.33 us  [swap(): return lax.ppermute(x, 'pair', [(0, 1), (1, 0)])]
    select_n x1 -> x2, other arithmetic: 0.87 us -> 0.07 us  [the longest x1 0.03 us: per_device(): cot_sib = jnp.where(first, rows[half:], rows[:half])]
    ppermute x6, starting transfers between devices: 1.24 us -> 1.6 us  [swap(): return lax.ppermute(x, 'pair', [(0, 1), (1, 0)])]
    dot_general x3 -> x2, matrix products: 3.39 us -> 3.08 us  [the longest x1 2.26 us: per_device(): lax.dot_general(found, frames, (((0,), (0,)), ((), ())), preferred_elemen...]
  transfers between devices with their start and end apart: 14 -> 14, of which waited for: 6 -> 6; matrix products, arithmetic and copies ran while one was open for 5% -> 9% of each run, Pallas kernels for 25% -> 25%
where the time goes in v9:
time: 33.9 us; the launch traced here: 33.8 us
  starting transfers between devices  11.3 us (33%)
  Pallas kernels  9.8 us (29%)
  waiting for transfers between devices  8.67 us (26%)
  matrix products  3.08 us (9%)
  between operations  0.76 us (2%)
    ppermute x8, starting transfers between devices, send(): return lax.ppermute(x, ('tensor', 'pair'), pairs)  9.74 us
    ppermute x8, waiting for transfers between devices, send(): return lax.ppermute(x, ('tensor', 'pair'), pairs)  7.34 us
    pallas_call x2, Pallas kernels, call(): pl.pallas_call(body, out_shape=outs, in_specs=specs, out_specs=jax.tree.m...  6.18 us
    pallas_call x3, Pallas kernels, scatter_rows(): pl.pallas_call(functools.partial(scatter_body, [len(parts) for _, parts i...  3.62 us
    dot_general x1, matrix products, per_device(): lax.dot_general(found, frames, (((0,), (0,)), ((), ())), preferred_elemen...  2.26 us
    ppermute x6, starting transfers between devices, swap(): return lax.ppermute(x, 'pair', [(0, 1), (1, 0)])  1.6 us
    ppermute x6, waiting for transfers between devices, swap(): return lax.ppermute(x, 'pair', [(0, 1), (1, 0)])  1.33 us
    dot_general x1, matrix products, per_device(): lax.dot_general(found, cotangent, (((0,), (0,)), ((), ())), preferred_ele...  0.83 us
  transfers between devices with their start and end apart: 14, of which 6 were waited for; matrix products, arithmetic and copies ran while one was open for 9% of the time, Pallas kernels for 25%

profile of v9, /device:TPU:0, one launch (start us, length us, event | category | flops | bytes accessed | tf_op | source)
XLA Modules:
  0.0 33.8 jit_solution(16038643581682984300)
XLA Ops:
  0.6 0.5 %collective-permute-start.3 = (bf16[1536,768]{1,0:T(8,128)(2,1)}, bf16[1536,768]{1,0:T(8,128)(2,1)S(1)}, u32[]{:S(2)}, u32[]{:S(2)}) collective-permute-start(bf16[1536,768]{1,0:T(8,128)(2,1)} %refs_4_.3), channel_id=1, source_target_pairs={{0,1},{1,0},{2,3},{3,2},{4,5},{5,4},{6,7},{7,6},{8,9},{9,8},{10,11... | collective-permute-start | bytes 7077896 | tf_op jit(solution)/shard_map/ppermute | solution.py:246
  1.1 0.0 copy-start.1
  1.2 0.0 copy-start.3
  1.2 0.0 copy-start.6
  1.2 2.3 %fusion.2 = bf16[384,384]{1,0:T(8,128)(2,1)S(1)} fusion(bf16[1536,384]{1,0:T(8,128)(2,1)} %frames_ref.2, s32[384]{0:T(512)} %picked_ref.1), kind=kOutput, calls=%fused_computation.3 | convolution fusion | flops 453722112 | bytes 1476096 | tf_op jit(solution)/shard_map/dot_general | solution.py:274
  3.5 0.0 copy-done.1
  3.5 0.1 collective-permute-start.4
  3.6 2.9 %collective-permute-start.1 = (bf16[192,384]{1,0:T(8,128)(2,1)S(1)}, bf16[192,384]{1,0:T(8,128)(2,1)S(1)}, u32[]{:S(2)}, u32[]{:S(2)}) collective-permute-start(bf16[192,384]{1,0:T(8,128)(2,1)S(1)} %get-tuple-element.43.refs_0_), channel_id=1, source_target_pairs={{0,2},{1,3},{2,0},{3,1},{4,6},{5,7},{6,4},{7,5},{8,10},{9,11},{10,... | collective-permute-start | bytes 442376 | tf_op jit(solution)/shard_map/ppermute | solution.py:243
  6.5 0.0 collective-permute-start.2
  6.5 0.0 copy-start.4
  6.5 0.0 copy-start.5
  6.5 0.0 copy-start.7
  6.6 0.1 collective-permute-start
  6.7 0.0 copy-done.3
  6.7 0.0 copy-done.6
  6.7 0.0 copy-start
  6.7 0.8 %fusion.3 = bf16[384,384]{1,0:T(8,128)(2,1)S(1)} fusion(bf16[1536,384]{1,0:T(8,128)(2,1)S(1)} %copy-done.3, s32[384]{0:T(512)S(1)} %copy-done.6), kind=kOutput, calls=%fused_computation.4 | convolution fusion | flops 453722112 | bytes 1476096 | tf_op jit(solution)/shard_map/dot_general | solution.py:280
  7.6 1.3 %collective-permute-done.refs_1_ = bf16[192,384]{1,0:T(8,128)(2,1)S(1)} collective-permute-done((bf16[192,384]{1,0:T(8,128)(2,1)S(1)}, bf16[192,384]{1,0:T(8,128)(2,1)S(1)}, u32[]{:S(2)}, u32[]{:S(2)}) %collective-permute-start) | collective-permute-done | bytes 147488 | tf_op jit(solution)/shard_map/ppermute | solution.py:246
  8.9 0.0 collective-permute-done.3.refs_5_
  8.9 2.9 %collective-permute-start.9 = (bf16[192,384]{1,0:T(8,128)(2,1)S(1)}, bf16[192,384]{1,0:T(8,128)(2,1)S(1)}, u32[]{:S(2)}, u32[]{:S(2)}) collective-permute-start(bf16[192,384]{1,0:T(8,128)(2,1)S(1)} %get-tuple-element.29.refs_0_), channel_id=1, source_target_pairs={{0,2},{1,3},{2,0},{3,1},{4,6},{5,7},{6,4},{7,5},{8,10},{9,11},{10,... | collective-permute-start | bytes 442376 | tf_op jit(solution)/shard_map/ppermute | solution.py:243
  11.8 0.0 collective-permute-start.10
  11.8 2.2 %collective-permute-done.2.refs_3_ = bf16[192,384]{1,0:T(8,128)(2,1)S(1)} collective-permute-done((bf16[192,384]{1,0:T(8,128)(2,1)S(1)}, bf16[192,384]{1,0:T(8,128)(2,1)S(1)}, u32[]{:S(2)}, u32[]{:S(2)}) %collective-permute-start.2) | collective-permute-done | bytes 147488 | tf_op jit(solution)/shard_map/ppermute | solution.py:243
  13.9 0.2 collective-permute-start.8
  14.2 0.0 collective-permute-done.1.refs_2_
  14.2 0.0 collective-permute-done.4.refs_7_
  14.2 0.0 copy-done.4
  14.2 0.0 copy-done.5
  14.2 0.0 copy-done.7
  14.2 0.0 copy-done
  14.2 2.6 %forward.1 = (bf16[192,384]{1,0:T(8,128)(2,1)S(1)}, bf16[192,384]{1,0:T(8,128)(2,1)S(1)}, bf16[192,384]{1,0:T(8,128)(2,1)S(1)}, bf16[192,384]{1,0:T(8,128)(2,1)S...) custom-call(s32[4]{0:T(128)S(1)} %copy-done.7, ...), custom_call_target="tpu_custom_call" | custom-call | flops 1 | bytes 1 | tf_op jit(solution)/shard_map/forward/pallas_call | solution.py:23
  16.8 2.1 %collective-permute-start.5 = (bf16[192,384]{1,0:T(8,128)(2,1)S(1)}, bf16[192,384]{1,0:T(8,128)(2,1)S(1)}, u32[]{:S(2)}, u32[]{:S(2)}) collective-permute-start(bf16[192,384]{1,0:T(8,128)(2,1)S(1)} %get-tuple-element.25), channel_id=1, source_target_pairs={{0,2},{1,3},{2,0},{3,1},{4,6},{5,7},{6,4},{7,5},{8,10},{9,11},{10,... | collective-permute-start | bytes 442376 | tf_op jit(solution)/shard_map/ppermute | solution.py:243
  18.9 0.0 collective-permute-start.6
  18.9 0.0 collective-permute-done.9.refs_2_
  18.9 0.2 collective-permute-start.7
  19.1 0.5 %collective-permute-done.10.refs_3_ = bf16[192,384]{1,0:T(8,128)(2,1)S(1)} collective-permute-done((bf16[192,384]{1,0:T(8,128)(2,1)S(1)}, bf16[192,384]{1,0:T(8,128)(2,1)S(1)}, u32[]{:S(2)}, u32[]{:S(2)}) %collective-permute-start.10) | collective-permute-done | bytes 147488 | tf_op jit(solution)/shard_map/ppermute | solution.py:243
  19.6 0.0 collective-permute-done.8.refs_1_
  19.6 0.0 copy-start.2
  19.6 3.6 %backward.1 = (bf16[192,384]{1,0:T(8,128)(2,1)S(1)}, bf16[192,384]{1,0:T(8,128)(2,1)S(1)}, bf16[192,384]{1,0:T(8,128)(2,1)S(1)}, bf16[192,384]{1,0:T(8,128)(2,1)S(1)}) custom-call(bf16[192,384]{1,0:T(8,128)(2,1)S(1)} %get-tuple-element.29.refs_0_, bf16[192,384]{1,0:T(8,128)(2,1)S(1)} %collective-permute-done.8.refs_1_, ...), custom_call_target="tpu_custom_call" | custom-call | flops 1 | bytes 1 | tf_op jit(solution)/shard_map/backward/pallas_call | solution.py:23
  23.2 1.5 %collective-permute-start.11 = (bf16[192,384]{1,0:T(8,128)(2,1)S(1)}, bf16[192,384]{1,0:T(8,128)(2,1)S(1)}, u32[]{:S(2)}, u32[]{:S(2)}) collective-permute-start(bf16[192,384]{1,0:T(8,128)(2,1)S(1)} %get-tuple-element.37), channel_id=1, source_target_pairs={{0,2},{1,3},{2,0},{3,1},{4,6},{5,7},{6,4},{7,5},{8,10},{9,11},{10,... | collective-permute-start | bytes 442376 | tf_op jit(solution)/shard_map/ppermute | solution.py:243
  24.7 0.6 %collective-permute-start.12 = (bf16[192,384]{1,0:T(8,128)(2,1)S(1)}, bf16[192,384]{1,0:T(8,128)(2,1)S(1)}, u32[]{:S(2)}, u32[]{:S(2)}) collective-permute-start(bf16[192,384]{1,0:T(8,128)(2,1)S(1)} %get-tuple-element.38), channel_id=1, source_target_pairs={{0,1},{1,0},{2,3},{3,2},{4,5},{5,4},{6,7},{7,6},{8,9},{9,8},{10,11... | collective-permute-start | bytes 442376 | tf_op jit(solution)/shard_map/ppermute | solution.py:246
  25.3 0.0 collective-permute-done.5.refs_2_
  25.3 0.1 collective-permute-start.13
  25.4 0.0 collective-permute-done.6.refs_4_
  25.4 0.7 %collective-permute-done.7.refs_5_ = bf16[192,384]{1,0:T(8,128)(2,1)S(1)} collective-permute-done((bf16[192,384]{1,0:T(8,128)(2,1)S(1)}, bf16[192,384]{1,0:T(8,128)(2,1)S(1)}, u32[]{:S(2)}, u32[]{:S(2)}) %collective-permute-start.7) | collective-permute-done | bytes 147488 | tf_op jit(solution)/shard_map/ppermute | solution.py:243
  26.1 0.0 copy-done.2
  26.1 1.7 %mixed_rows.1 = bf16[1536,384]{1,0:T(8,128)(2,1)} custom-call(bf16[1536,384]{1,0:T(8,128)(2,1)S(1)} %copy-done.2, s32[192]{0:T(256)S(1)} %get-tuple-element.23.refs_0_, bf16[192,384]{1,0:T(8,128)(2,1)S(1)} %get-tuple-element.24.refs_1_, bf16[192,384]{1,0:T(8,128)(2,1)S(1)} %collective-permute-done.5.refs_2_, s32[192]{0:T(256)S(1)} %get-tuple-element.26.refs_3_.refs_0_, ...), custom_call_target="tpu_custom_call" | custom-call | tf_op jit(solution)/shard_map/mixed_rows/pallas_call | solution.py:88
  27.9 2.1 %collective-permute-done.11.refs_2_ = bf16[192,384]{1,0:T(8,128)(2,1)S(1)} collective-permute-done((bf16[192,384]{1,0:T(8,128)(2,1)S(1)}, bf16[192,384]{1,0:T(8,128)(2,1)S(1)}, u32[]{:S(2)}, u32[]{:S(2)}) %collective-permute-start.11) | collective-permute-done | bytes 147488 | tf_op jit(solution)/shard_map/ppermute | solution.py:243
  29.9 0.6 %grad_rows_mine.1.frames_ref = bf16[1536,384]{1,0:T(8,128)(2,1)S(1)} custom-call(bf16[1536,384]{1,0:T(8,128)(2,1)S(1)} %copy-done.3, s32[192]{0:T(256)S(1)} %get-tuple-element.23.refs_0_, bf16[192,384]{1,0:T(8,128)(2,1)S(1)} %get-tuple-element.36.refs_1_, bf16[192,384]{1,0:T(8,128)(2,1)S(1)} %collective-permute-done.11.refs_2_), custom_call_target="tpu_custom_call" | custom-call | tf_op jit(solution)/shard_map/grad_rows_mine/pallas_call | solution.py:88
  30.5 0.0 collective-permute-done.12.refs_1_
  30.5 1.9 %collective-permute-done.13.refs_2_ = bf16[192,384]{1,0:T(8,128)(2,1)S(1)} collective-permute-done((bf16[192,384]{1,0:T(8,128)(2,1)S(1)}, bf16[192,384]{1,0:T(8,128)(2,1)S(1)}, u32[]{:S(2)}, u32[]{:S(2)}) %collective-permute-start.13) | collective-permute-done | bytes 147488 | tf_op jit(solution)/shard_map/ppermute | solution.py:243
  32.5 1.3 %grad_rows.1 = bf16[1536,384]{1,0:T(8,128)(2,1)} custom-call(bf16[1536,384]{1,0:T(8,128)(2,1)S(1)} %grad_rows_mine.1.frames_ref, s32[192]{0:T(256)S(1)} %get-tuple-element.26.refs_3_.refs_0_, bf16[192,384]{1,0:T(8,128)(2,1)S(1)} %collective-permute-done.12.refs_1_, bf16[192,384]{1,0:T(8,128)(2,1)S(1)} %collective-permute-done.13.refs_2_), custom_call_target="tpu_custom_call" | custom-call | tf_op jit(solution)/shard_map/grad_rows/pallas_call | solution.py:88
  (2 shorter events, 0.1 us)
Async XLA Ops:
  0.6 8.3 %collective-permute-start.3 = (bf16[1536,768]{1,0:T(8,128)(2,1)}, bf16[1536,768]{1,0:T(8,128)(2,1)S(1)}, u32[]{:S(2)}, u32[]{:S(2)}) collective-permute-start(bf16[1536,768]{1,0:T(8,128)(2,1)} %refs_4_.3), channel_id=1, source_target_pairs={{0,1},{1,0},{2,3},{3,2},{4,5},{5,4},{6,7},{7,6},{8,9},{9,8},{10,11... | collective-permute-start | bytes 7077896 | tf_op jit(solution)/shard_map/ppermute | solution.py:246
  1.1 2.3 %copy-start.1 = (bf16[768,1536]{1,0:T(8,128)(2,1)S(1)}, bf16[768,1536]{1,0:T(8,128)(2,1)}, u32[]{:S(2)}) copy-start(bf16[768,1536]{1,0:T(8,128)(2,1)} %refs_6_.3) | copy-start | bytes 7077892
  1.2 5.5 %copy-start.3 = (bf16[1536,384]{1,0:T(8,128)(2,1)S(1)}, bf16[1536,384]{1,0:T(8,128)(2,1)}, u32[]{:S(2)}) copy-start(bf16[1536,384]{1,0:T(8,128)(2,1)} %frames_ref.3) | copy-start | bytes 3538948
  1.2 5.5 %copy-start.6 = (s32[384]{0:T(512)S(1)}, s32[384]{0:T(512)}, u32[]{:S(2)}) copy-start(s32[384]{0:T(512)} %picked_ref.1) | copy-start | bytes 4612
  3.5 10.7 %collective-permute-start.4 = (bf16[768,1536]{1,0:T(8,128)(2,1)S(1)}, bf16[768,1536]{1,0:T(8,128)(2,1)S(1)}, u32[]{:S(2)}, u32[]{:S(2)}) collective-permute-start(bf16[768,1536]{1,0:T(8,128)(2,1)S(1)} %copy-done.1), channel_id=1, source_target_pairs={{0,1},{1,0},{2,3},{3,2},{4,5},{5,4},{6,7},{7,6},{8,9},{9,8},{10,11... | collective-permute-start | bytes 7077896 | tf_op jit(solution)/shard_map/ppermute | solution.py:246
  3.6 10.6 %collective-permute-start.1 = (bf16[192,384]{1,0:T(8,128)(2,1)S(1)}, bf16[192,384]{1,0:T(8,128)(2,1)S(1)}, u32[]{:S(2)}, u32[]{:S(2)}) collective-permute-start(bf16[192,384]{1,0:T(8,128)(2,1)S(1)} %get-tuple-element.43.refs_0_), channel_id=1, source_target_pairs={{0,2},{1,3},{2,0},{3,1},{4,6},{5,7},{6,4},{7,5},{8,10},{9,11},{10,... | collective-permute-start | bytes 442376 | tf_op jit(solution)/shard_map/ppermute | solution.py:243
  6.5 7.4 %collective-permute-start.2 = (bf16[192,384]{1,0:T(8,128)(2,1)S(1)}, bf16[192,384]{1,0:T(8,128)(2,1)S(1)}, u32[]{:S(2)}, u32[]{:S(2)}) collective-permute-start(bf16[192,384]{1,0:T(8,128)(2,1)S(1)} %get-tuple-element.42), channel_id=1, source_target_pairs={{0,3},{1,2},{2,1},{3,0},{4,7},{5,6},{6,5},{7,4},{8,11},{9,10},{10,... | collective-permute-start | bytes 442376 | tf_op jit(solution)/shard_map/ppermute | solution.py:243
  6.5 7.6 %copy-start.4 = (f32[1536]{0:T(1024)S(1)}, f32[1536]{0:T(1024)}, u32[]{:S(2)}) copy-start(f32[1536]{0:T(1024)} %refs_8_.3) | copy-start | bytes 18436
  6.5 7.6 %copy-start.5 = (f32[1536]{0:T(1024)S(1)}, f32[1536]{0:T(1024)}, u32[]{:S(2)}) copy-start(f32[1536]{0:T(1024)} %refs_9_.3) | copy-start | bytes 18436
  6.5 7.6 %copy-start.7 = (s32[4]{0:T(128)S(1)}, s32[4]{0:T(128)}, u32[]{:S(2)}) copy-start(s32[4]{0:T(128)} %count_ref.1) | copy-start | bytes 52
  6.6 2.3 %collective-permute-start = (bf16[192,384]{1,0:T(8,128)(2,1)S(1)}, bf16[192,384]{1,0:T(8,128)(2,1)S(1)}, u32[]{:S(2)}, u32[]{:S(2)}) collective-permute-start(bf16[192,384]{1,0:T(8,128)(2,1)S(1)} %get-tuple-element.42), channel_id=1, source_target_pairs={{0,1},{1,0},{2,3},{3,2},{4,5},{5,4},{6,7},{7,6},{8,9},{9,8},{10,11... | collective-permute-start | bytes 442376 | tf_op jit(solution)/shard_map/ppermute | solution.py:246
  6.7 7.5 %copy-start = (bf16[1536,768]{1,0:T(8,128)(2,1)S(1)}, bf16[1536,768]{1,0:T(8,128)(2,1)}, u32[]{:S(2)}) copy-start(bf16[1536,768]{1,0:T(8,128)(2,1)} %refs_4_.3) | copy-start | bytes 7077892
  8.9 10.0 %collective-permute-start.9 = (bf16[192,384]{1,0:T(8,128)(2,1)S(1)}, bf16[192,384]{1,0:T(8,128)(2,1)S(1)}, u32[]{:S(2)}, u32[]{:S(2)}) collective-permute-start(bf16[192,384]{1,0:T(8,128)(2,1)S(1)} %get-tuple-element.29.refs_0_), channel_id=1, source_target_pairs={{0,2},{1,3},{2,0},{3,1},{4,6},{5,7},{6,4},{7,5},{8,10},{9,11},{10,... | collective-permute-start | bytes 442376 | tf_op jit(solution)/shard_map/ppermute | solution.py:243
  11.8 7.9 %collective-permute-start.10 = (bf16[192,384]{1,0:T(8,128)(2,1)S(1)}, bf16[192,384]{1,0:T(8,128)(2,1)S(1)}, u32[]{:S(2)}, u32[]{:S(2)}) collective-permute-start(bf16[192,384]{1,0:T(8,128)(2,1)S(1)} %get-tuple-element.30), channel_id=1, source_target_pairs={{0,3},{1,2},{2,1},{3,0},{4,7},{5,6},{6,5},{7,4},{8,11},{9,10},{10,... | collective-permute-start | bytes 442376 | tf_op jit(solution)/shard_map/ppermute | solution.py:243
  13.9 5.7 %collective-permute-start.8 = (bf16[192,384]{1,0:T(8,128)(2,1)S(1)}, bf16[192,384]{1,0:T(8,128)(2,1)S(1)}, u32[]{:S(2)}, u32[]{:S(2)}) collective-permute-start(bf16[192,384]{1,0:T(8,128)(2,1)S(1)} %get-tuple-element.30), channel_id=1, source_target_pairs={{0,1},{1,0},{2,3},{3,2},{4,5},{5,4},{6,7},{7,6},{8,9},{9,8},{10,11... | collective-permute-start | bytes 442376 | tf_op jit(solution)/shard_map/ppermute | solution.py:246
  16.8 8.5 %collective-permute-start.5 = (bf16[192,384]{1,0:T(8,128)(2,1)S(1)}, bf16[192,384]{1,0:T(8,128)(2,1)S(1)}, u32[]{:S(2)}, u32[]{:S(2)}) collective-permute-start(bf16[192,384]{1,0:T(8,128)(2,1)S(1)} %get-tuple-element.25), channel_id=1, source_target_pairs={{0,2},{1,3},{2,0},{3,1},{4,6},{5,7},{6,4},{7,5},{8,10},{9,11},{10,... | collective-permute-start | bytes 442376 | tf_op jit(solution)/shard_map/ppermute | solution.py:243
  18.9 6.5 %collective-permute-start.6 = (bf16[192,384]{1,0:T(8,128)(2,1)S(1)}, bf16[192,384]{1,0:T(8,128)(2,1)S(1)}, u32[]{:S(2)}, u32[]{:S(2)}) collective-permute-start(bf16[192,384]{1,0:T(8,128)(2,1)S(1)} %get-tuple-element.27), channel_id=1, source_target_pairs={{0,1},{1,0},{2,3},{3,2},{4,5},{5,4},{6,7},{7,6},{8,9},{9,8},{10,11... | collective-permute-start | bytes 442376 | tf_op jit(solution)/shard_map/ppermute | solution.py:246
  18.9 7.2 %collective-permute-start.7 = (bf16[192,384]{1,0:T(8,128)(2,1)S(1)}, bf16[192,384]{1,0:T(8,128)(2,1)S(1)}, u32[]{:S(2)}, u32[]{:S(2)}) collective-permute-start(bf16[192,384]{1,0:T(8,128)(2,1)S(1)} %get-tuple-element.28), channel_id=1, source_target_pairs={{0,3},{1,2},{2,1},{3,0},{4,7},{5,6},{6,5},{7,4},{8,11},{9,10},{10,... | collective-permute-start | bytes 442376 | tf_op jit(solution)/shard_map/ppermute | solution.py:243
  19.6 6.5 %copy-start.2 = (bf16[1536,384]{1,0:T(8,128)(2,1)S(1)}, bf16[1536,384]{1,0:T(8,128)(2,1)}, u32[]{:S(2)}) copy-start(bf16[1536,384]{1,0:T(8,128)(2,1)} %frames_ref.2) | copy-start | bytes 3538948
  23.2 6.7 %collective-permute-start.11 = (bf16[192,384]{1,0:T(8,128)(2,1)S(1)}, bf16[192,384]{1,0:T(8,128)(2,1)S(1)}, u32[]{:S(2)}, u32[]{:S(2)}) collective-permute-start(bf16[192,384]{1,0:T(8,128)(2,1)S(1)} %get-tuple-element.37), channel_id=1, source_target_pairs={{0,2},{1,3},{2,0},{3,1},{4,6},{5,7},{6,4},{7,5},{8,10},{9,11},{10,... | collective-permute-start | bytes 442376 | tf_op jit(solution)/shard_map/ppermute | solution.py:243
  24.7 5.8 %collective-permute-start.12 = (bf16[192,384]{1,0:T(8,128)(2,1)S(1)}, bf16[192,384]{1,0:T(8,128)(2,1)S(1)}, u32[]{:S(2)}, u32[]{:S(2)}) collective-permute-start(bf16[192,384]{1,0:T(8,128)(2,1)S(1)} %get-tuple-element.38), channel_id=1, source_target_pairs={{0,1},{1,0},{2,3},{3,2},{4,5},{5,4},{6,7},{7,6},{8,9},{9,8},{10,11... | collective-permute-start | bytes 442376 | tf_op jit(solution)/shard_map/ppermute | solution.py:246
  25.3 7.1 %collective-permute-start.13 = (bf16[192,384]{1,0:T(8,128)(2,1)S(1)}, bf16[192,384]{1,0:T(8,128)(2,1)S(1)}, u32[]{:S(2)}, u32[]{:S(2)}) collective-permute-start(bf16[192,384]{1,0:T(8,128)(2,1)S(1)} %get-tuple-element.39), channel_id=1, source_target_pairs={{0,3},{1,2},{2,1},{3,0},{4,7},{5,6},{6,5},{7,4},{8,11},{9,10},{10,... | collective-permute-start | bytes 442376 | tf_op jit(solution)/shard_map/ppermute | solution.py:243

commit v10 on v9

--- a/solution.py
+++ b/solution.py
@@ -33,8 +33,10 @@
 
 
 def chunks_of(extent):
-    size = 256 if extent % 256 == 0 else extent
-    return [(start, size) for start in range(0, extent, size)]
+    if extent % 256:
+        return [(0, extent)]
+    sizes = [64, 192] + [256] * (extent // 256 - 1)
+    return [(sum(sizes[:i]), size) for i, size in enumerate(sizes)]
 
 
 def wanted_slots(count_ref, picked_ref):

time: 33.9 us -> 33.9 us (level)
  no operation moved by 1% of the time
where the time goes in v10:
time: 33.9 us; the launch traced here: 33.8 us
  starting transfers between devices  11.3 us (33%)
  Pallas kernels  9.87 us (29%)
  waiting for transfers between devices  8.63 us (25%)
  matrix products  3.08 us (9%)
  between operations  0.76 us (2%)
    ppermute x8, starting transfers between devices, send(): return lax.ppermute(x, ('tensor', 'pair'), pairs)  9.74 us
    ppermute x8, waiting for transfers between devices, send(): return lax.ppermute(x, ('tensor', 'pair'), pairs)  7.3 us
    pallas_call x2, Pallas kernels, call(): pl.pallas_call(body, out_shape=outs, in_specs=specs, out_specs=jax.tree.m...  6.18 us
    pallas_call x3, Pallas kernels, scatter_rows(): pl.pallas_call(functools.partial(scatter_body, [len(parts) for _, parts i...  3.69 us
    dot_general x1, matrix products, per_device(): lax.dot_general(found, frames, (((0,), (0,)), ((), ())), preferred_elemen...  2.26 us
    ppermute x6, starting transfers between devices, swap(): return lax.ppermute(x, 'pair', [(0, 1), (1, 0)])  1.6 us
    ppermute x6, waiting for transfers between devices, swap(): return lax.ppermute(x, 'pair', [(0, 1), (1, 0)])  1.33 us
    dot_general x1, matrix products, per_device(): lax.dot_general(found, cotangent, (((0,), (0,)), ((), ())), preferred_ele...  0.83 us
  transfers between devices with their start and end apart: 14, of which 6 were waited for; matrix products, arithmetic and copies ran while one was open for 9% of the time, Pallas kernels for 25%

profile of v10, /device:TPU:0, one launch (start us, length us, event | category | flops | bytes accessed | tf_op | source)
XLA Modules:
  0.0 33.8 jit_solution(10451528838879646)
XLA Ops:
  0.6 0.5 %collective-permute-start.3 = (bf16[1536,768]{1,0:T(8,128)(2,1)}, bf16[1536,768]{1,0:T(8,128)(2,1)S(1)}, u32[]{:S(2)}, u32[]{:S(2)}) collective-permute-start(bf16[1536,768]{1,0:T(8,128)(2,1)} %refs_4_.3), channel_id=1, source_target_pairs={{0,1},{1,0},{2,3},{3,2},{4,5},{5,4},{6,7},{7,6},{8,9},{9,8},{10,11... | collective-permute-start | bytes 7077896 | tf_op jit(solution)/shard_map/ppermute | solution.py:248
  1.1 0.0 copy-start.1
  1.2 0.0 copy-start.3
  1.2 0.0 copy-start.6
  1.2 2.3 %fusion.2 = bf16[384,384]{1,0:T(8,128)(2,1)S(1)} fusion(bf16[1536,384]{1,0:T(8,128)(2,1)} %frames_ref.2, s32[384]{0:T(512)} %picked_ref.1), kind=kOutput, calls=%fused_computation.3 | convolution fusion | flops 453722112 | bytes 1476096 | tf_op jit(solution)/shard_map/dot_general | solution.py:276
  3.5 0.0 copy-done.1
  3.5 0.1 collective-permute-start.4
  3.6 2.9 %collective-permute-start.1 = (bf16[192,384]{1,0:T(8,128)(2,1)S(1)}, bf16[192,384]{1,0:T(8,128)(2,1)S(1)}, u32[]{:S(2)}, u32[]{:S(2)}) collective-permute-start(bf16[192,384]{1,0:T(8,128)(2,1)S(1)} %get-tuple-element.43.refs_0_), channel_id=1, source_target_pairs={{0,2},{1,3},{2,0},{3,1},{4,6},{5,7},{6,4},{7,5},{8,10},{9,11},{10,... | collective-permute-start | bytes 442376 | tf_op jit(solution)/shard_map/ppermute | solution.py:245
  6.5 0.0 collective-permute-start.2
  6.5 0.0 copy-start.4
  6.5 0.0 copy-start.5
  6.5 0.0 copy-start.7
  6.6 0.1 collective-permute-start
  6.7 0.0 copy-done.3
  6.7 0.0 copy-done.6
  6.7 0.0 copy-start
  6.7 0.8 %fusion.3 = bf16[384,384]{1,0:T(8,128)(2,1)S(1)} fusion(bf16[1536,384]{1,0:T(8,128)(2,1)S(1)} %copy-done.3, s32[384]{0:T(512)S(1)} %copy-done.6), kind=kOutput, calls=%fused_computation.4 | convolution fusion | flops 453722112 | bytes 1476096 | tf_op jit(solution)/shard_map/dot_general | solution.py:282
  7.6 1.3 %collective-permute-done.refs_1_ = bf16[192,384]{1,0:T(8,128)(2,1)S(1)} collective-permute-done((bf16[192,384]{1,0:T(8,128)(2,1)S(1)}, bf16[192,384]{1,0:T(8,128)(2,1)S(1)}, u32[]{:S(2)}, u32[]{:S(2)}) %collective-permute-start) | collective-permute-done | bytes 147488 | tf_op jit(solution)/shard_map/ppermute | solution.py:248
  8.9 0.0 collective-permute-done.3.refs_5_
  8.9 2.9 %collective-permute-start.9 = (bf16[192,384]{1,0:T(8,128)(2,1)S(1)}, bf16[192,384]{1,0:T(8,128)(2,1)S(1)}, u32[]{:S(2)}, u32[]{:S(2)}) collective-permute-start(bf16[192,384]{1,0:T(8,128)(2,1)S(1)} %get-tuple-element.29.refs_0_), channel_id=1, source_target_pairs={{0,2},{1,3},{2,0},{3,1},{4,6},{5,7},{6,4},{7,5},{8,10},{9,11},{10,... | collective-permute-start | bytes 442376 | tf_op jit(solution)/shard_map/ppermute | solution.py:245
  11.8 0.0 collective-permute-start.10
  11.8 2.2 %collective-permute-done.2.refs_3_ = bf16[192,384]{1,0:T(8,128)(2,1)S(1)} collective-permute-done((bf16[192,384]{1,0:T(8,128)(2,1)S(1)}, bf16[192,384]{1,0:T(8,128)(2,1)S(1)}, u32[]{:S(2)}, u32[]{:S(2)}) %collective-permute-start.2) | collective-permute-done | bytes 147488 | tf_op jit(solution)/shard_map/ppermute | solution.py:245
  13.9 0.2 collective-permute-start.8
  14.2 0.0 collective-permute-done.1.refs_2_
  14.2 0.0 collective-permute-done.4.refs_7_
  14.2 0.0 copy-done.4
  14.2 0.0 copy-done.5
  14.2 0.0 copy-done.7
  14.2 0.0 copy-done
  14.2 2.6 %forward.1 = (bf16[192,384]{1,0:T(8,128)(2,1)S(1)}, bf16[192,384]{1,0:T(8,128)(2,1)S(1)}, bf16[192,384]{1,0:T(8,128)(2,1)S(1)}, bf16[192,384]{1,0:T(8,128)(2,1)S...) custom-call(s32[4]{0:T(128)S(1)} %copy-done.7, ...), custom_call_target="tpu_custom_call" | custom-call | flops 1 | bytes 1 | tf_op jit(solution)/shard_map/forward/pallas_call | solution.py:23
  16.8 2.1 %collective-permute-start.5 = (bf16[192,384]{1,0:T(8,128)(2,1)S(1)}, bf16[192,384]{1,0:T(8,128)(2,1)S(1)}, u32[]{:S(2)}, u32[]{:S(2)}) collective-permute-start(bf16[192,384]{1,0:T(8,128)(2,1)S(1)} %get-tuple-element.25), channel_id=1, source_target_pairs={{0,2},{1,3},{2,0},{3,1},{4,6},{5,7},{6,4},{7,5},{8,10},{9,11},{10,... | collective-permute-start | bytes 442376 | tf_op jit(solution)/shard_map/ppermute | solution.py:245
  18.9 0.0 collective-permute-start.6
  18.9 0.0 collective-permute-done.9.refs_2_
  18.9 0.2 collective-permute-start.7
  19.1 0.5 %collective-permute-done.10.refs_3_ = bf16[192,384]{1,0:T(8,128)(2,1)S(1)} collective-permute-done((bf16[192,384]{1,0:T(8,128)(2,1)S(1)}, bf16[192,384]{1,0:T(8,128)(2,1)S(1)}, u32[]{:S(2)}, u32[]{:S(2)}) %collective-permute-start.10) | collective-permute-done | bytes 147488 | tf_op jit(solution)/shard_map/ppermute | solution.py:245
  19.6 0.0 collective-permute-done.8.refs_1_
  19.6 0.0 copy-start.2
  19.6 3.6 %backward.1 = (bf16[192,384]{1,0:T(8,128)(2,1)S(1)}, bf16[192,384]{1,0:T(8,128)(2,1)S(1)}, bf16[192,384]{1,0:T(8,128)(2,1)S(1)}, bf16[192,384]{1,0:T(8,128)(2,1)S(1)}) custom-call(bf16[192,384]{1,0:T(8,128)(2,1)S(1)} %get-tuple-element.29.refs_0_, bf16[192,384]{1,0:T(8,128)(2,1)S(1)} %collective-permute-done.8.refs_1_, ...), custom_call_target="tpu_custom_call" | custom-call | flops 1 | bytes 1 | tf_op jit(solution)/shard_map/backward/pallas_call | solution.py:23
  23.2 1.5 %collective-permute-start.11 = (bf16[192,384]{1,0:T(8,128)(2,1)S(1)}, bf16[192,384]{1,0:T(8,128)(2,1)S(1)}, u32[]{:S(2)}, u32[]{:S(2)}) collective-permute-start(bf16[192,384]{1,0:T(8,128)(2,1)S(1)} %get-tuple-element.37), channel_id=1, source_target_pairs={{0,2},{1,3},{2,0},{3,1},{4,6},{5,7},{6,4},{7,5},{8,10},{9,11},{10,... | collective-permute-start | bytes 442376 | tf_op jit(solution)/shard_map/ppermute | solution.py:245
  24.7 0.6 %collective-permute-start.12 = (bf16[192,384]{1,0:T(8,128)(2,1)S(1)}, bf16[192,384]{1,0:T(8,128)(2,1)S(1)}, u32[]{:S(2)}, u32[]{:S(2)}) collective-permute-start(bf16[192,384]{1,0:T(8,128)(2,1)S(1)} %get-tuple-element.38), channel_id=1, source_target_pairs={{0,1},{1,0},{2,3},{3,2},{4,5},{5,4},{6,7},{7,6},{8,9},{9,8},{10,11... | collective-permute-start | bytes 442376 | tf_op jit(solution)/shard_map/ppermute | solution.py:248
  25.3 0.0 collective-permute-done.5.refs_2_
  25.3 0.1 collective-permute-start.13
  25.4 0.0 collective-permute-done.6.refs_4_
  25.4 0.7 %collective-permute-done.7.refs_5_ = bf16[192,384]{1,0:T(8,128)(2,1)S(1)} collective-permute-done((bf16[192,384]{1,0:T(8,128)(2,1)S(1)}, bf16[192,384]{1,0:T(8,128)(2,1)S(1)}, u32[]{:S(2)}, u32[]{:S(2)}) %collective-permute-start.7) | collective-permute-done | bytes 147488 | tf_op jit(solution)/shard_map/ppermute | solution.py:245
  26.1 0.0 copy-done.2
  26.1 1.8 %mixed_rows.1 = bf16[1536,384]{1,0:T(8,128)(2,1)} custom-call(bf16[1536,384]{1,0:T(8,128)(2,1)S(1)} %copy-done.2, s32[192]{0:T(256)S(1)} %get-tuple-element.23.refs_0_, bf16[192,384]{1,0:T(8,128)(2,1)S(1)} %get-tuple-element.24.refs_1_, bf16[192,384]{1,0:T(8,128)(2,1)S(1)} %collective-permute-done.5.refs_2_, s32[192]{0:T(256)S(1)} %get-tuple-element.26.refs_3_.refs_0_, ...), custom_call_target="tpu_custom_call" | custom-call | tf_op jit(solution)/shard_map/mixed_rows/pallas_call | solution.py:90
  27.9 2.0 %collective-permute-done.11.refs_2_ = bf16[192,384]{1,0:T(8,128)(2,1)S(1)} collective-permute-done((bf16[192,384]{1,0:T(8,128)(2,1)S(1)}, bf16[192,384]{1,0:T(8,128)(2,1)S(1)}, u32[]{:S(2)}, u32[]{:S(2)}) %collective-permute-start.11) | collective-permute-done | bytes 147488 | tf_op jit(solution)/shard_map/ppermute | solution.py:245
  29.9 0.6 %grad_rows_mine.1.frames_ref = bf16[1536,384]{1,0:T(8,128)(2,1)S(1)} custom-call(bf16[1536,384]{1,0:T(8,128)(2,1)S(1)} %copy-done.3, s32[192]{0:T(256)S(1)} %get-tuple-element.23.refs_0_, bf16[192,384]{1,0:T(8,128)(2,1)S(1)} %get-tuple-element.36.refs_1_, bf16[192,384]{1,0:T(8,128)(2,1)S(1)} %collective-permute-done.11.refs_2_), custom_call_target="tpu_custom_call" | custom-call | tf_op jit(solution)/shard_map/grad_rows_mine/pallas_call | solution.py:90
  30.5 0.0 collective-permute-done.12.refs_1_
  30.5 1.9 %collective-permute-done.13.refs_2_ = bf16[192,384]{1,0:T(8,128)(2,1)S(1)} collective-permute-done((bf16[192,384]{1,0:T(8,128)(2,1)S(1)}, bf16[192,384]{1,0:T(8,128)(2,1)S(1)}, u32[]{:S(2)}, u32[]{:S(2)}) %collective-permute-start.13) | collective-permute-done | bytes 147488 | tf_op jit(solution)/shard_map/ppermute | solution.py:245
  32.5 1.3 %grad_rows.1 = bf16[1536,384]{1,0:T(8,128)(2,1)} custom-call(bf16[1536,384]{1,0:T(8,128)(2,1)S(1)} %grad_rows_mine.1.frames_ref, s32[192]{0:T(256)S(1)} %get-tuple-element.26.refs_3_.refs_0_, bf16[192,384]{1,0:T(8,128)(2,1)S(1)} %collective-permute-done.12.refs_1_, bf16[192,384]{1,0:T(8,128)(2,1)S(1)} %collective-permute-done.13.refs_2_), custom_call_target="tpu_custom_call" | custom-call | tf_op jit(solution)/shard_map/grad_rows/pallas_call | solution.py:90
  (2 shorter events, 0.1 us)
Async XLA Ops:
  0.6 8.3 %collective-permute-start.3 = (bf16[1536,768]{1,0:T(8,128)(2,1)}, bf16[1536,768]{1,0:T(8,128)(2,1)S(1)}, u32[]{:S(2)}, u32[]{:S(2)}) collective-permute-start(bf16[1536,768]{1,0:T(8,128)(2,1)} %refs_4_.3), channel_id=1, source_target_pairs={{0,1},{1,0},{2,3},{3,2},{4,5},{5,4},{6,7},{7,6},{8,9},{9,8},{10,11... | collective-permute-start | bytes 7077896 | tf_op jit(solution)/shard_map/ppermute | solution.py:248
  1.1 2.3 %copy-start.1 = (bf16[768,1536]{1,0:T(8,128)(2,1)S(1)}, bf16[768,1536]{1,0:T(8,128)(2,1)}, u32[]{:S(2)}) copy-start(bf16[768,1536]{1,0:T(8,128)(2,1)} %refs_6_.3) | copy-start | bytes 7077892
  1.2 5.5 %copy-start.3 = (bf16[1536,384]{1,0:T(8,128)(2,1)S(1)}, bf16[1536,384]{1,0:T(8,128)(2,1)}, u32[]{:S(2)}) copy-start(bf16[1536,384]{1,0:T(8,128)(2,1)} %frames_ref.3) | copy-start | bytes 3538948
  1.2 5.5 %copy-start.6 = (s32[384]{0:T(512)S(1)}, s32[384]{0:T(512)}, u32[]{:S(2)}) copy-start(s32[384]{0:T(512)} %picked_ref.1) | copy-start | bytes 4612
  3.5 10.7 %collective-permute-start.4 = (bf16[768,1536]{1,0:T(8,128)(2,1)S(1)}, bf16[768,1536]{1,0:T(8,128)(2,1)S(1)}, u32[]{:S(2)}, u32[]{:S(2)}) collective-permute-start(bf16[768,1536]{1,0:T(8,128)(2,1)S(1)} %copy-done.1), channel_id=1, source_target_pairs={{0,1},{1,0},{2,3},{3,2},{4,5},{5,4},{6,7},{7,6},{8,9},{9,8},{10,11... | collective-permute-start | bytes 7077896 | tf_op jit(solution)/shard_map/ppermute | solution.py:248
  3.6 10.6 %collective-permute-start.1 = (bf16[192,384]{1,0:T(8,128)(2,1)S(1)}, bf16[192,384]{1,0:T(8,128)(2,1)S(1)}, u32[]{:S(2)}, u32[]{:S(2)}) collective-permute-start(bf16[192,384]{1,0:T(8,128)(2,1)S(1)} %get-tuple-element.43.refs_0_), channel_id=1, source_target_pairs={{0,2},{1,3},{2,0},{3,1},{4,6},{5,7},{6,4},{7,5},{8,10},{9,11},{10,... | collective-permute-start | bytes 442376 | tf_op jit(solution)/shard_map/ppermute | solution.py:245
  6.5 7.4 %collective-permute-start.2 = (bf16[192,384]{1,0:T(8,128)(2,1)S(1)}, bf16[192,384]{1,0:T(8,128)(2,1)S(1)}, u32[]{:S(2)}, u32[]{:S(2)}) collective-permute-start(bf16[192,384]{1,0:T(8,128)(2,1)S(1)} %get-tuple-element.42), channel_id=1, source_target_pairs={{0,3},{1,2},{2,1},{3,0},{4,7},{5,6},{6,5},{7,4},{8,11},{9,10},{10,... | collective-permute-start | bytes 442376 | tf_op jit(solution)/shard_map/ppermute | solution.py:245
  6.5 7.6 %copy-start.4 = (f32[1536]{0:T(1024)S(1)}, f32[1536]{0:T(1024)}, u32[]{:S(2)}) copy-start(f32[1536]{0:T(1024)} %refs_8_.3) | copy-start | bytes 18436
  6.5 7.6 %copy-start.5 = (f32[1536]{0:T(1024)S(1)}, f32[1536]{0:T(1024)}, u32[]{:S(2)}) copy-start(f32[1536]{0:T(1024)} %refs_9_.3) | copy-start | bytes 18436
  6.5 7.6 %copy-start.7 = (s32[4]{0:T(128)S(1)}, s32[4]{0:T(128)}, u32[]{:S(2)}) copy-start(s32[4]{0:T(128)} %count_ref.1) | copy-start | bytes 52
  6.6 2.3 %collective-permute-start = (bf16[192,384]{1,0:T(8,128)(2,1)S(1)}, bf16[192,384]{1,0:T(8,128)(2,1)S(1)}, u32[]{:S(2)}, u32[]{:S(2)}) collective-permute-start(bf16[192,384]{1,0:T(8,128)(2,1)S(1)} %get-tuple-element.42), channel_id=1, source_target_pairs={{0,1},{1,0},{2,3},{3,2},{4,5},{5,4},{6,7},{7,6},{8,9},{9,8},{10,11... | collective-permute-start | bytes 442376 | tf_op jit(solution)/shard_map/ppermute | solution.py:248
  6.7 7.5 %copy-start = (bf16[1536,768]{1,0:T(8,128)(2,1)S(1)}, bf16[1536,768]{1,0:T(8,128)(2,1)}, u32[]{:S(2)}) copy-start(bf16[1536,768]{1,0:T(8,128)(2,1)} %refs_4_.3) | copy-start | bytes 7077892
  8.9 10.0 %collective-permute-start.9 = (bf16[192,384]{1,0:T(8,128)(2,1)S(1)}, bf16[192,384]{1,0:T(8,128)(2,1)S(1)}, u32[]{:S(2)}, u32[]{:S(2)}) collective-permute-start(bf16[192,384]{1,0:T(8,128)(2,1)S(1)} %get-tuple-element.29.refs_0_), channel_id=1, source_target_pairs={{0,2},{1,3},{2,0},{3,1},{4,6},{5,7},{6,4},{7,5},{8,10},{9,11},{10,... | collective-permute-start | bytes 442376 | tf_op jit(solution)/shard_map/ppermute | solution.py:245
  11.8 7.9 %collective-permute-start.10 = (bf16[192,384]{1,0:T(8,128)(2,1)S(1)}, bf16[192,384]{1,0:T(8,128)(2,1)S(1)}, u32[]{:S(2)}, u32[]{:S(2)}) collective-permute-start(bf16[192,384]{1,0:T(8,128)(2,1)S(1)} %get-tuple-element.30), channel_id=1, source_target_pairs={{0,3},{1,2},{2,1},{3,0},{4,7},{5,6},{6,5},{7,4},{8,11},{9,10},{10,... | collective-permute-start | bytes 442376 | tf_op jit(solution)/shard_map/ppermute | solution.py:245
  13.9 5.7 %collective-permute-start.8 = (bf16[192,384]{1,0:T(8,128)(2,1)S(1)}, bf16[192,384]{1,0:T(8,128)(2,1)S(1)}, u32[]{:S(2)}, u32[]{:S(2)}) collective-permute-start(bf16[192,384]{1,0:T(8,128)(2,1)S(1)} %get-tuple-element.30), channel_id=1, source_target_pairs={{0,1},{1,0},{2,3},{3,2},{4,5},{5,4},{6,7},{7,6},{8,9},{9,8},{10,11... | collective-permute-start | bytes 442376 | tf_op jit(solution)/shard_map/ppermute | solution.py:248
  16.8 8.5 %collective-permute-start.5 = (bf16[192,384]{1,0:T(8,128)(2,1)S(1)}, bf16[192,384]{1,0:T(8,128)(2,1)S(1)}, u32[]{:S(2)}, u32[]{:S(2)}) collective-permute-start(bf16[192,384]{1,0:T(8,128)(2,1)S(1)} %get-tuple-element.25), channel_id=1, source_target_pairs={{0,2},{1,3},{2,0},{3,1},{4,6},{5,7},{6,4},{7,5},{8,10},{9,11},{10,... | collective-permute-start | bytes 442376 | tf_op jit(solution)/shard_map/ppermute | solution.py:245
  18.9 6.5 %collective-permute-start.6 = (bf16[192,384]{1,0:T(8,128)(2,1)S(1)}, bf16[192,384]{1,0:T(8,128)(2,1)S(1)}, u32[]{:S(2)}, u32[]{:S(2)}) collective-permute-start(bf16[192,384]{1,0:T(8,128)(2,1)S(1)} %get-tuple-element.27), channel_id=1, source_target_pairs={{0,1},{1,0},{2,3},{3,2},{4,5},{5,4},{6,7},{7,6},{8,9},{9,8},{10,11... | collective-permute-start | bytes 442376 | tf_op jit(solution)/shard_map/ppermute | solution.py:248
  18.9 7.2 %collective-permute-start.7 = (bf16[192,384]{1,0:T(8,128)(2,1)S(1)}, bf16[192,384]{1,0:T(8,128)(2,1)S(1)}, u32[]{:S(2)}, u32[]{:S(2)}) collective-permute-start(bf16[192,384]{1,0:T(8,128)(2,1)S(1)} %get-tuple-element.28), channel_id=1, source_target_pairs={{0,3},{1,2},{2,1},{3,0},{4,7},{5,6},{6,5},{7,4},{8,11},{9,10},{10,... | collective-permute-start | bytes 442376 | tf_op jit(solution)/shard_map/ppermute | solution.py:245
  19.6 6.5 %copy-start.2 = (bf16[1536,384]{1,0:T(8,128)(2,1)S(1)}, bf16[1536,384]{1,0:T(8,128)(2,1)}, u32[]{:S(2)}) copy-start(bf16[1536,384]{1,0:T(8,128)(2,1)} %frames_ref.2) | copy-start | bytes 3538948
  23.2 6.7 %collective-permute-start.11 = (bf16[192,384]{1,0:T(8,128)(2,1)S(1)}, bf16[192,384]{1,0:T(8,128)(2,1)S(1)}, u32[]{:S(2)}, u32[]{:S(2)}) collective-permute-start(bf16[192,384]{1,0:T(8,128)(2,1)S(1)} %get-tuple-element.37), channel_id=1, source_target_pairs={{0,2},{1,3},{2,0},{3,1},{4,6},{5,7},{6,4},{7,5},{8,10},{9,11},{10,... | collective-permute-start | bytes 442376 | tf_op jit(solution)/shard_map/ppermute | solution.py:245
  24.7 5.8 %collective-permute-start.12 = (bf16[192,384]{1,0:T(8,128)(2,1)S(1)}, bf16[192,384]{1,0:T(8,128)(2,1)S(1)}, u32[]{:S(2)}, u32[]{:S(2)}) collective-permute-start(bf16[192,384]{1,0:T(8,128)(2,1)S(1)} %get-tuple-element.38), channel_id=1, source_target_pairs={{0,1},{1,0},{2,3},{3,2},{4,5},{5,4},{6,7},{7,6},{8,9},{9,8},{10,11... | collective-permute-start | bytes 442376 | tf_op jit(solution)/shard_map/ppermute | solution.py:248
  25.3 7.1 %collective-permute-start.13 = (bf16[192,384]{1,0:T(8,128)(2,1)S(1)}, bf16[192,384]{1,0:T(8,128)(2,1)S(1)}, u32[]{:S(2)}, u32[]{:S(2)}) collective-permute-start(bf16[192,384]{1,0:T(8,128)(2,1)S(1)} %get-tuple-element.39), channel_id=1, source_target_pairs={{0,3},{1,2},{2,1},{3,0},{4,7},{5,6},{6,5},{7,4},{8,11},{9,10},{10,... | collective-permute-start | bytes 442376 | tf_op jit(solution)/shard_map/ppermute | solution.py:245

commit v11 on v9

--- a/solution.py
+++ b/solution.py
@@ -221,6 +221,23 @@
     )
 
 
+def in_vmem(x):
+    def body(source, target, sem):
+        copy = pltpu.make_async_copy(source, target, sem)
+        copy.start()
+        copy.wait()
+
+    return pl.pallas_call(
+        body,
+        out_shape=jax.ShapeDtypeStruct(x.shape, x.dtype),
+        in_specs=[ANY],
+        out_specs=vspec(),
+        scratch_shapes=[pltpu.SemaphoreType.DMA],
+        compiler_params=pltpu.CompilerParams(vmem_limit_bytes=6 * 1024 * 1024),
+        name="in_vmem",
+    )(x)
+
+
 def after(value, *others):
     return lax.optimization_barrier((value, *others))[0]
 
@@ -275,13 +292,13 @@
     mine = jnp.where(first, rows[:half], rows[half:])
     sib = jnp.where(first, rows[half:], rows[:half])
     blocks = collect(mine, sib, after(sib, mine))
-    up_sib, down_sib = swap(up_weight), swap(after(down_weight, mine))
+    up_sib, down_sib = swap(up_weight), in_vmem(swap(down_weight))
     weights = (up_weight, up_sib, down_weight, down_sib)
     rows = lax.dot_general(found, cotangent, (((0,), (0,)), ((), ())), preferred_element_type=F32).astype(BF16)
     cot_mine = jnp.where(first, rows[:half], rows[half:])
     cot_sib = jnp.where(first, rows[half:], rows[:half])
     cot_mine, cot_sib = after(cot_mine, up_sib), after(cot_sib, up_sib, blocks[1])
-    cot_blocks = collect(cot_mine, cot_sib, cot_sib)
+    cot_blocks = collect(cot_mine, cot_sib, after(cot_sib, down_sib))
     parts, saved, wanted = forward(picked_count, picked_rows, joined(blocks), ways, weights, gain, router)
     out_mine, out_sib = deliver(cut(parts))
     grads = backward(joined(cot_blocks), ways, weights, gain, router, saved)

time: 33.9 us -> 34.1 us (level)
  Pallas kernels: 9.8 us -> 11.6 us
  waiting for transfers between devices: 8.67 us -> 7.73 us
  starting transfers between devices: 11.3 us -> 10.7 us
    pallas_call x0 -> x1, Pallas kernels: none -> 1.82 us  [in_vmem(): pl.pallas_call(body, out_shape=jax.ShapeDtypeStruct(x.shape, x.dtype), in...]
    ppermute x8, waiting for transfers between devices: 7.34 us -> 6.44 us  [send(): return lax.ppermute(x, ('tensor', 'pair'), pairs)]
    ppermute x8, starting transfers between devices: 9.74 us -> 9.39 us  [send(): return lax.ppermute(x, ('tensor', 'pair'), pairs)]
  transfers between devices with their start and end apart: 14 -> 14, of which waited for: 6 -> 6; matrix products, arithmetic and copies ran while one was open for 9% -> 9% of each run, Pallas kernels for 25% -> 30%
where the time goes in v11:
time: 34.1 us; the launch traced here: 34 us
  Pallas kernels  11.6 us (34%)
  starting transfers between devices  10.7 us (31%)
  waiting for transfers between devices  7.73 us (23%)
  matrix products  3.03 us (9%)
  between operations  0.77 us (2%)
    ppermute x8, starting transfers between devices, send(): return lax.ppermute(x, ('tensor', 'pair'), pairs)  9.39 us
    ppermute x8, waiting for transfers between devices, send(): return lax.ppermute(x, ('tensor', 'pair'), pairs)  6.44 us
    pallas_call x2, Pallas kernels, call(): pl.pallas_call(body, out_shape=outs, in_specs=specs, out_specs=jax.tree.m...  6.16 us
    pallas_call x3, Pallas kernels, scatter_rows(): pl.pallas_call(functools.partial(scatter_body, [len(parts) for _, parts i...  3.63 us
    dot_general x1, matrix products, per_device(): lax.dot_general(found, frames, (((0,), (0,)), ((), ())), preferred_elemen...  2.21 us
    pallas_call x1, Pallas kernels, in_vmem(): pl.pallas_call(body, out_shape=jax.ShapeDtypeStruct(x.shape, x.dtype), in...  1.82 us
    ppermute x6, starting transfers between devices, swap(): return lax.ppermute(x, 'pair', [(0, 1), (1, 0)])  1.35 us
    ppermute x6, waiting for transfers between devices, swap(): return lax.ppermute(x, 'pair', [(0, 1), (1, 0)])  1.29 us
  transfers between devices with their start and end apart: 14, of which 6 were waited for; matrix products, arithmetic and copies ran while one was open for 9% of the time, Pallas kernels for 30%

profile of v11, /device:TPU:0, one launch (start us, length us, event | category | flops | bytes accessed | tf_op | source)
XLA Modules:
  0.0 34.0 jit_solution(11314963525680479845)
XLA Ops:
  0.6 0.5 %collective-permute-start.3 = (bf16[1536,768]{1,0:T(8,128)(2,1)}, bf16[1536,768]{1,0:T(8,128)(2,1)S(1)}, u32[]{:S(2)}, u32[]{:S(2)}) collective-permute-start(bf16[1536,768]{1,0:T(8,128)(2,1)} %refs_4_.3), channel_id=1, source_target_pairs={{0,1},{1,0},{2,3},{3,2},{4,5},{5,4},{6,7},{7,6},{8,9},{9,8},{10,11... | collective-permute-start | bytes 7077896 | tf_op jit(solution)/shard_map/ppermute | solution.py:263
  1.1 0.1 collective-permute-start.4
  1.2 0.0 copy-start.3
  1.2 0.0 copy-start.6
  1.2 2.2 %fusion.2 = bf16[384,384]{1,0:T(8,128)(2,1)S(1)} fusion(bf16[1536,384]{1,0:T(8,128)(2,1)} %frames_ref.2, s32[384]{0:T(512)} %picked_ref.1), kind=kOutput, calls=%fused_computation.3 | convolution fusion | flops 453722112 | bytes 1476096 | tf_op jit(solution)/shard_map/dot_general | solution.py:291
  3.5 2.7 %collective-permute-start.2 = (bf16[192,384]{1,0:T(8,128)(2,1)S(1)}, bf16[192,384]{1,0:T(8,128)(2,1)S(1)}, u32[]{:S(2)}, u32[]{:S(2)}) collective-permute-start(bf16[192,384]{1,0:T(8,128)(2,1)S(1)} %get-tuple-element.42), channel_id=1, source_target_pairs={{0,3},{1,2},{2,1},{3,0},{4,7},{5,6},{6,5},{7,4},{8,11},{9,10},{10,... | collective-permute-start | bytes 442376 | tf_op jit(solution)/shard_map/ppermute | solution.py:260
  6.2 0.4 %collective-permute-start = (bf16[192,384]{1,0:T(8,128)(2,1)S(1)}, bf16[192,384]{1,0:T(8,128)(2,1)S(1)}, u32[]{:S(2)}, u32[]{:S(2)}) collective-permute-start(bf16[192,384]{1,0:T(8,128)(2,1)S(1)} %get-tuple-element.42), channel_id=1, source_target_pairs={{0,1},{1,0},{2,3},{3,2},{4,5},{5,4},{6,7},{7,6},{8,9},{9,8},{10,11... | collective-permute-start | bytes 442376 | tf_op jit(solution)/shard_map/ppermute | solution.py:263
  6.6 0.0 collective-permute-start.1
  6.6 0.0 copy-done.3
  6.6 0.0 copy-done.6
  6.6 0.8 %fusion.3 = bf16[384,384]{1,0:T(8,128)(2,1)S(1)} fusion(bf16[1536,384]{1,0:T(8,128)(2,1)S(1)} %copy-done.3, s32[384]{0:T(512)S(1)} %copy-done.6), kind=kOutput, calls=%fused_computation.4 | convolution fusion | flops 453722112 | bytes 1476096 | tf_op jit(solution)/shard_map/dot_general | solution.py:297
  7.5 0.0 copy-start.4
  7.5 0.0 copy-start.5
  7.5 1.3 %collective-permute-done.refs_1_ = bf16[192,384]{1,0:T(8,128)(2,1)S(1)} collective-permute-done((bf16[192,384]{1,0:T(8,128)(2,1)S(1)}, bf16[192,384]{1,0:T(8,128)(2,1)S(1)}, u32[]{:S(2)}, u32[]{:S(2)}) %collective-permute-start) | collective-permute-done | bytes 147488 | tf_op jit(solution)/shard_map/ppermute | solution.py:263
  8.8 0.0 collective-permute-done.3.refs_5_
  8.8 0.0 copy-start.7
  8.8 2.3 %collective-permute-start.9 = (bf16[192,384]{1,0:T(8,128)(2,1)S(1)}, bf16[192,384]{1,0:T(8,128)(2,1)S(1)}, u32[]{:S(2)}, u32[]{:S(2)}) collective-permute-start(bf16[192,384]{1,0:T(8,128)(2,1)S(1)} %get-tuple-element.28.refs_0_), channel_id=1, source_target_pairs={{0,2},{1,3},{2,0},{3,1},{4,6},{5,7},{6,4},{7,5},{8,10},{9,11},{10,... | collective-permute-start | bytes 442376 | tf_op jit(solution)/shard_map/ppermute | solution.py:260
  11.2 0.0 collective-permute-start.10
  11.2 0.0 collective-permute-done.4.source
  11.2 0.0 copy-start
  11.2 0.0 copy-start.1
  11.2 1.8 %in_vmem.1.refs_7_ = bf16[768,1536]{1,0:T(8,128)(2,1)S(1)} custom-call(bf16[768,1536]{1,0:T(8,128)(2,1)} %collective-permute-done.4.source), custom_call_target="tpu_custom_call" | custom-call | tf_op jit(solution)/shard_map/in_vmem/pallas_call | solution.py:230
  13.0 0.2 collective-permute-start.8
  13.3 0.0 collective-permute-done.2.refs_3_
  13.3 1.0 %collective-permute-done.1.refs_2_ = bf16[192,384]{1,0:T(8,128)(2,1)S(1)} collective-permute-done((bf16[192,384]{1,0:T(8,128)(2,1)S(1)}, bf16[192,384]{1,0:T(8,128)(2,1)S(1)}, u32[]{:S(2)}, u32[]{:S(2)}) %collective-permute-start.1) | collective-permute-done | bytes 147488 | tf_op jit(solution)/shard_map/ppermute | solution.py:260
  14.3 0.0 copy-done.4
  14.3 0.0 copy-done.5
  14.3 0.0 copy-done.7
  14.3 0.0 copy-done
  14.3 0.0 copy-done.1
  14.3 2.6 %forward.1 = (bf16[192,384]{1,0:T(8,128)(2,1)S(1)}, bf16[192,384]{1,0:T(8,128)(2,1)S(1)}, bf16[192,384]{1,0:T(8,128)(2,1)S(1)}, bf16[192,384]{1,0:T(8,128)(2,1)S...) custom-call(s32[4]{0:T(128)S(1)} %copy-done.7, ...), custom_call_target="tpu_custom_call" | custom-call | flops 1 | bytes 1 | tf_op jit(solution)/shard_map/forward/pallas_call | solution.py:23
  16.9 1.8 %collective-permute-start.5 = (bf16[192,384]{1,0:T(8,128)(2,1)S(1)}, bf16[192,384]{1,0:T(8,128)(2,1)S(1)}, u32[]{:S(2)}, u32[]{:S(2)}) collective-permute-start(bf16[192,384]{1,0:T(8,128)(2,1)S(1)} %get-tuple-element.24), channel_id=1, source_target_pairs={{0,2},{1,3},{2,0},{3,1},{4,6},{5,7},{6,4},{7,5},{8,10},{9,11},{10,... | collective-permute-start | bytes 442376 | tf_op jit(solution)/shard_map/ppermute | solution.py:260
  18.7 0.0 collective-permute-start.6
  18.7 0.0 collective-permute-done.9.refs_2_
  18.7 0.4 %collective-permute-start.7 = (bf16[192,384]{1,0:T(8,128)(2,1)S(1)}, bf16[192,384]{1,0:T(8,128)(2,1)S(1)}, u32[]{:S(2)}, u32[]{:S(2)}) collective-permute-start(bf16[192,384]{1,0:T(8,128)(2,1)S(1)} %get-tuple-element.27), channel_id=1, source_target_pairs={{0,3},{1,2},{2,1},{3,0},{4,7},{5,6},{6,5},{7,4},{8,11},{9,10},{10,... | collective-permute-start | bytes 442376 | tf_op jit(solution)/shard_map/ppermute | solution.py:260
  19.1 0.8 %collective-permute-done.10.refs_3_ = bf16[192,384]{1,0:T(8,128)(2,1)S(1)} collective-permute-done((bf16[192,384]{1,0:T(8,128)(2,1)S(1)}, bf16[192,384]{1,0:T(8,128)(2,1)S(1)}, u32[]{:S(2)}, u32[]{:S(2)}) %collective-permute-start.10) | collective-permute-done | bytes 147488 | tf_op jit(solution)/shard_map/ppermute | solution.py:260
  19.9 0.0 collective-permute-done.8.refs_1_
  19.9 0.0 copy-start.2
  19.9 3.6 %backward.1 = (bf16[192,384]{1,0:T(8,128)(2,1)S(1)}, bf16[192,384]{1,0:T(8,128)(2,1)S(1)}, bf16[192,384]{1,0:T(8,128)(2,1)S(1)}, bf16[192,384]{1,0:T(8,128)(2,1)S(1)}) custom-call(bf16[192,384]{1,0:T(8,128)(2,1)S(1)} %get-tuple-element.28.refs_0_, bf16[192,384]{1,0:T(8,128)(2,1)S(1)} %collective-permute-done.8.refs_1_, ...), custom_call_target="tpu_custom_call" | custom-call | flops 1 | bytes 1 | tf_op jit(solution)/shard_map/backward/pallas_call | solution.py:23
  23.5 2.0 %collective-permute-start.11 = (bf16[192,384]{1,0:T(8,128)(2,1)S(1)}, bf16[192,384]{1,0:T(8,128)(2,1)S(1)}, u32[]{:S(2)}, u32[]{:S(2)}) collective-permute-start(bf16[192,384]{1,0:T(8,128)(2,1)S(1)} %get-tuple-element.37), channel_id=1, source_target_pairs={{0,2},{1,3},{2,0},{3,1},{4,6},{5,7},{6,4},{7,5},{8,10},{9,11},{10,... | collective-permute-start | bytes 442376 | tf_op jit(solution)/shard_map/ppermute | solution.py:260
  25.5 0.1 collective-permute-start.12
  25.6 0.0 collective-permute-done.5.refs_2_
  25.6 0.1 collective-permute-start.13
  25.7 0.0 collective-permute-done.6.refs_4_
  25.7 0.2 collective-permute-done.7.refs_5_
  25.9 0.0 copy-done.2
  25.9 1.7 %mixed_rows.1 = bf16[1536,384]{1,0:T(8,128)(2,1)} custom-call(bf16[1536,384]{1,0:T(8,128)(2,1)S(1)} %copy-done.2, s32[192]{0:T(256)S(1)} %get-tuple-element.22.refs_0_, bf16[192,384]{1,0:T(8,128)(2,1)S(1)} %get-tuple-element.23.refs_1_, bf16[192,384]{1,0:T(8,128)(2,1)S(1)} %collective-permute-done.5.refs_2_, s32[192]{0:T(256)S(1)} %get-tuple-element.25.refs_3_.refs_0_, ...), custom_call_target="tpu_custom_call" | custom-call | tf_op jit(solution)/shard_map/mixed_rows/pallas_call | solution.py:88
  27.7 2.5 %collective-permute-done.11.refs_2_ = bf16[192,384]{1,0:T(8,128)(2,1)S(1)} collective-permute-done((bf16[192,384]{1,0:T(8,128)(2,1)S(1)}, bf16[192,384]{1,0:T(8,128)(2,1)S(1)}, u32[]{:S(2)}, u32[]{:S(2)}) %collective-permute-start.11) | collective-permute-done | bytes 147488 | tf_op jit(solution)/shard_map/ppermute | solution.py:260
  30.2 0.6 %grad_rows_mine.1.frames_ref = bf16[1536,384]{1,0:T(8,128)(2,1)S(1)} custom-call(bf16[1536,384]{1,0:T(8,128)(2,1)S(1)} %copy-done.3, s32[192]{0:T(256)S(1)} %get-tuple-element.22.refs_0_, bf16[192,384]{1,0:T(8,128)(2,1)S(1)} %get-tuple-element.36.refs_1_, bf16[192,384]{1,0:T(8,128)(2,1)S(1)} %collective-permute-done.11.refs_2_), custom_call_target="tpu_custom_call" | custom-call | tf_op jit(solution)/shard_map/grad_rows_mine/pallas_call | solution.py:88
  30.8 0.0 collective-permute-done.12.refs_1_
  30.8 1.9 %collective-permute-done.13.refs_2_ = bf16[192,384]{1,0:T(8,128)(2,1)S(1)} collective-permute-done((bf16[192,384]{1,0:T(8,128)(2,1)S(1)}, bf16[192,384]{1,0:T(8,128)(2,1)S(1)}, u32[]{:S(2)}, u32[]{:S(2)}) %collective-permute-start.13) | collective-permute-done | bytes 147488 | tf_op jit(solution)/shard_map/ppermute | solution.py:260
  32.7 1.3 %grad_rows.1 = bf16[1536,384]{1,0:T(8,128)(2,1)} custom-call(bf16[1536,384]{1,0:T(8,128)(2,1)S(1)} %grad_rows_mine.1.frames_ref, s32[192]{0:T(256)S(1)} %get-tuple-element.25.refs_3_.refs_0_, bf16[192,384]{1,0:T(8,128)(2,1)S(1)} %collective-permute-done.12.refs_1_, bf16[192,384]{1,0:T(8,128)(2,1)S(1)} %collective-permute-done.13.refs_2_), custom_call_target="tpu_custom_call" | custom-call | tf_op jit(solution)/shard_map/grad_rows/pallas_call | solution.py:88
  (2 shorter events, 0.1 us)
Async XLA Ops:
  0.6 8.2 %collective-permute-start.3 = (bf16[1536,768]{1,0:T(8,128)(2,1)}, bf16[1536,768]{1,0:T(8,128)(2,1)S(1)}, u32[]{:S(2)}, u32[]{:S(2)}) collective-permute-start(bf16[1536,768]{1,0:T(8,128)(2,1)} %refs_4_.3), channel_id=1, source_target_pairs={{0,1},{1,0},{2,3},{3,2},{4,5},{5,4},{6,7},{7,6},{8,9},{9,8},{10,11... | collective-permute-start | bytes 7077896 | tf_op jit(solution)/shard_map/ppermute | solution.py:263
  1.1 10.0 %collective-permute-start.4 = (bf16[768,1536]{1,0:T(8,128)(2,1)}, bf16[768,1536]{1,0:T(8,128)(2,1)}, u32[]{:S(2)}, u32[]{:S(2)}) collective-permute-start(bf16[768,1536]{1,0:T(8,128)(2,1)} %refs_6_.3), channel_id=1, source_target_pairs={{0,1},{1,0},{2,3},{3,2},{4,5},{5,4},{6,7},{7,6},{8,9},{9,8},{10,11... | collective-permute-start | bytes 7077896 | tf_op jit(solution)/shard_map/ppermute | solution.py:263
  1.2 5.4 %copy-start.3 = (bf16[1536,384]{1,0:T(8,128)(2,1)S(1)}, bf16[1536,384]{1,0:T(8,128)(2,1)}, u32[]{:S(2)}) copy-start(bf16[1536,384]{1,0:T(8,128)(2,1)} %frames_ref.3) | copy-start | bytes 3538948
  1.2 5.4 %copy-start.6 = (s32[384]{0:T(512)S(1)}, s32[384]{0:T(512)}, u32[]{:S(2)}) copy-start(s32[384]{0:T(512)} %picked_ref.1) | copy-start | bytes 4612
  3.5 9.8 %collective-permute-start.2 = (bf16[192,384]{1,0:T(8,128)(2,1)S(1)}, bf16[192,384]{1,0:T(8,128)(2,1)S(1)}, u32[]{:S(2)}, u32[]{:S(2)}) collective-permute-start(bf16[192,384]{1,0:T(8,128)(2,1)S(1)} %get-tuple-element.42), channel_id=1, source_target_pairs={{0,3},{1,2},{2,1},{3,0},{4,7},{5,6},{6,5},{7,4},{8,11},{9,10},{10,... | collective-permute-start | bytes 442376 | tf_op jit(solution)/shard_map/ppermute | solution.py:260
  6.2 2.7 %collective-permute-start = (bf16[192,384]{1,0:T(8,128)(2,1)S(1)}, bf16[192,384]{1,0:T(8,128)(2,1)S(1)}, u32[]{:S(2)}, u32[]{:S(2)}) collective-permute-start(bf16[192,384]{1,0:T(8,128)(2,1)S(1)} %get-tuple-element.42), channel_id=1, source_target_pairs={{0,1},{1,0},{2,3},{3,2},{4,5},{5,4},{6,7},{7,6},{8,9},{9,8},{10,11... | collective-permute-start | bytes 442376 | tf_op jit(solution)/shard_map/ppermute | solution.py:263
  6.6 7.7 %collective-permute-start.1 = (bf16[192,384]{1,0:T(8,128)(2,1)S(1)}, bf16[192,384]{1,0:T(8,128)(2,1)S(1)}, u32[]{:S(2)}, u32[]{:S(2)}) collective-permute-start(bf16[192,384]{1,0:T(8,128)(2,1)S(1)} %get-tuple-element.43.refs_0_), channel_id=1, source_target_pairs={{0,2},{1,3},{2,0},{3,1},{4,6},{5,7},{6,4},{7,5},{8,10},{9,11},{10,... | collective-permute-start | bytes 442376 | tf_op jit(solution)/shard_map/ppermute | solution.py:260
  7.5 6.8 %copy-start.4 = (f32[1536]{0:T(1024)S(1)}, f32[1536]{0:T(1024)}, u32[]{:S(2)}) copy-start(f32[1536]{0:T(1024)} %refs_8_.3) | copy-start | bytes 18436
  7.5 6.8 %copy-start.5 = (f32[1536]{0:T(1024)S(1)}, f32[1536]{0:T(1024)}, u32[]{:S(2)}) copy-start(f32[1536]{0:T(1024)} %refs_9_.3) | copy-start | bytes 18436
  8.8 5.5 %copy-start.7 = (s32[4]{0:T(128)S(1)}, s32[4]{0:T(128)}, u32[]{:S(2)}) copy-start(s32[4]{0:T(128)} %count_ref.1) | copy-start | bytes 52
  8.8 9.9 %collective-permute-start.9 = (bf16[192,384]{1,0:T(8,128)(2,1)S(1)}, bf16[192,384]{1,0:T(8,128)(2,1)S(1)}, u32[]{:S(2)}, u32[]{:S(2)}) collective-permute-start(bf16[192,384]{1,0:T(8,128)(2,1)S(1)} %get-tuple-element.28.refs_0_), channel_id=1, source_target_pairs={{0,2},{1,3},{2,0},{3,1},{4,6},{5,7},{6,4},{7,5},{8,10},{9,11},{10,... | collective-permute-start | bytes 442376 | tf_op jit(solution)/shard_map/ppermute | solution.py:260
  11.2 8.7 %collective-permute-start.10 = (bf16[192,384]{1,0:T(8,128)(2,1)S(1)}, bf16[192,384]{1,0:T(8,128)(2,1)S(1)}, u32[]{:S(2)}, u32[]{:S(2)}) collective-permute-start(bf16[192,384]{1,0:T(8,128)(2,1)S(1)} %get-tuple-element.30), channel_id=1, source_target_pairs={{0,3},{1,2},{2,1},{3,0},{4,7},{5,6},{6,5},{7,4},{8,11},{9,10},{10,... | collective-permute-start | bytes 442376 | tf_op jit(solution)/shard_map/ppermute | solution.py:260
  11.2 3.1 %copy-start = (bf16[1536,768]{1,0:T(8,128)(2,1)S(1)}, bf16[1536,768]{1,0:T(8,128)(2,1)}, u32[]{:S(2)}) copy-start(bf16[1536,768]{1,0:T(8,128)(2,1)} %refs_4_.3) | copy-start | bytes 7077892
  11.2 3.1 %copy-start.1 = (bf16[768,1536]{1,0:T(8,128)(2,1)S(1)}, bf16[768,1536]{1,0:T(8,128)(2,1)}, u32[]{:S(2)}) copy-start(bf16[768,1536]{1,0:T(8,128)(2,1)} %refs_6_.3) | copy-start | bytes 7077892
  13.0 6.9 %collective-permute-start.8 = (bf16[192,384]{1,0:T(8,128)(2,1)S(1)}, bf16[192,384]{1,0:T(8,128)(2,1)S(1)}, u32[]{:S(2)}, u32[]{:S(2)}) collective-permute-start(bf16[192,384]{1,0:T(8,128)(2,1)S(1)} %get-tuple-element.30), channel_id=1, source_target_pairs={{0,1},{1,0},{2,3},{3,2},{4,5},{5,4},{6,7},{7,6},{8,9},{9,8},{10,11... | collective-permute-start | bytes 442376 | tf_op jit(solution)/shard_map/ppermute | solution.py:263
  16.9 8.7 %collective-permute-start.5 = (bf16[192,384]{1,0:T(8,128)(2,1)S(1)}, bf16[192,384]{1,0:T(8,128)(2,1)S(1)}, u32[]{:S(2)}, u32[]{:S(2)}) collective-permute-start(bf16[192,384]{1,0:T(8,128)(2,1)S(1)} %get-tuple-element.24), channel_id=1, source_target_pairs={{0,2},{1,3},{2,0},{3,1},{4,6},{5,7},{6,4},{7,5},{8,10},{9,11},{10,... | collective-permute-start | bytes 442376 | tf_op jit(solution)/shard_map/ppermute | solution.py:260
  18.7 7.0 %collective-permute-start.6 = (bf16[192,384]{1,0:T(8,128)(2,1)S(1)}, bf16[192,384]{1,0:T(8,128)(2,1)S(1)}, u32[]{:S(2)}, u32[]{:S(2)}) collective-permute-start(bf16[192,384]{1,0:T(8,128)(2,1)S(1)} %get-tuple-element.26), channel_id=1, source_target_pairs={{0,1},{1,0},{2,3},{3,2},{4,5},{5,4},{6,7},{7,6},{8,9},{9,8},{10,11... | collective-permute-start | bytes 442376 | tf_op jit(solution)/shard_map/ppermute | solution.py:263
  18.7 7.2 %collective-permute-start.7 = (bf16[192,384]{1,0:T(8,128)(2,1)S(1)}, bf16[192,384]{1,0:T(8,128)(2,1)S(1)}, u32[]{:S(2)}, u32[]{:S(2)}) collective-permute-start(bf16[192,384]{1,0:T(8,128)(2,1)S(1)} %get-tuple-element.27), channel_id=1, source_target_pairs={{0,3},{1,2},{2,1},{3,0},{4,7},{5,6},{6,5},{7,4},{8,11},{9,10},{10,... | collective-permute-start | bytes 442376 | tf_op jit(solution)/shard_map/ppermute | solution.py:260
  19.9 6.1 %copy-start.2 = (bf16[1536,384]{1,0:T(8,128)(2,1)S(1)}, bf16[1536,384]{1,0:T(8,128)(2,1)}, u32[]{:S(2)}) copy-start(bf16[1536,384]{1,0:T(8,128)(2,1)} %frames_ref.2) | copy-start | bytes 3538948
  23.5 6.7 %collective-permute-start.11 = (bf16[192,384]{1,0:T(8,128)(2,1)S(1)}, bf16[192,384]{1,0:T(8,128)(2,1)S(1)}, u32[]{:S(2)}, u32[]{:S(2)}) collective-permute-start(bf16[192,384]{1,0:T(8,128)(2,1)S(1)} %get-tuple-element.37), channel_id=1, source_target_pairs={{0,2},{1,3},{2,0},{3,1},{4,6},{5,7},{6,4},{7,5},{8,10},{9,11},{10,... | collective-permute-start | bytes 442376 | tf_op jit(solution)/shard_map/ppermute | solution.py:260
  25.5 5.3 %collective-permute-start.12 = (bf16[192,384]{1,0:T(8,128)(2,1)S(1)}, bf16[192,384]{1,0:T(8,128)(2,1)S(1)}, u32[]{:S(2)}, u32[]{:S(2)}) collective-permute-start(bf16[192,384]{1,0:T(8,128)(2,1)S(1)} %get-tuple-element.38), channel_id=1, source_target_pairs={{0,1},{1,0},{2,3},{3,2},{4,5},{5,4},{6,7},{7,6},{8,9},{9,8},{10,11... | collective-permute-start | bytes 442376 | tf_op jit(solution)/shard_map/ppermute | solution.py:263
  25.6 7.1 %collective-permute-start.13 = (bf16[192,384]{1,0:T(8,128)(2,1)S(1)}, bf16[192,384]{1,0:T(8,128)(2,1)S(1)}, u32[]{:S(2)}, u32[]{:S(2)}) collective-permute-start(bf16[192,384]{1,0:T(8,128)(2,1)S(1)} %get-tuple-element.39), channel_id=1, source_target_pairs={{0,3},{1,2},{2,1},{3,0},{4,7},{5,6},{6,5},{7,4},{8,11},{9,10},{10,... | collective-permute-start | bytes 442376 | tf_op jit(solution)/shard_map/ppermute | solution.py:260

commit v12 on v9

--- a/solution.py
+++ b/solution.py
@@ -274,13 +274,13 @@
     rows = lax.dot_general(found, frames, (((0,), (0,)), ((), ())), preferred_element_type=F32).astype(BF16)
     mine = jnp.where(first, rows[:half], rows[half:])
     sib = jnp.where(first, rows[half:], rows[:half])
-    blocks = collect(mine, sib, after(sib, mine))
     up_sib, down_sib = swap(up_weight), swap(after(down_weight, mine))
+    blocks = collect(mine, sib, after(sib, up_sib))
     weights = (up_weight, up_sib, down_weight, down_sib)
     rows = lax.dot_general(found, cotangent, (((0,), (0,)), ((), ())), preferred_element_type=F32).astype(BF16)
     cot_mine = jnp.where(first, rows[:half], rows[half:])
     cot_sib = jnp.where(first, rows[half:], rows[:half])
-    cot_mine, cot_sib = after(cot_mine, up_sib), after(cot_sib, up_sib, blocks[1])
+    cot_mine, cot_sib = after(cot_mine, up_sib), after(cot_sib, up_sib, down_sib)
     cot_blocks = collect(cot_mine, cot_sib, cot_sib)
     parts, saved, wanted = forward(picked_count, picked_rows, joined(blocks), ways, weights, gain, router)
     out_mine, out_sib = deliver(cut(parts))

time: 33.9 us -> 33.9 us (level)
  no operation moved by 1% of the time
where the time goes in v12:
time: 33.9 us; the launch traced here: 33.8 us
  starting transfers between devices  11.4 us (34%)
  Pallas kernels  9.8 us (29%)
  waiting for transfers between devices  8.56 us (25%)
  matrix products  3.09 us (9%)
  between operations  0.79 us (2%)
    ppermute x8, starting transfers between devices, send(): return lax.ppermute(x, ('tensor', 'pair'), pairs)  9.74 us
    ppermute x8, waiting for transfers between devices, send(): return lax.ppermute(x, ('tensor', 'pair'), pairs)  7.55 us
    pallas_call x2, Pallas kernels, call(): pl.pallas_call(body, out_shape=outs, in_specs=specs, out_specs=jax.tree.m...  6.18 us
    pallas_call x3, Pallas kernels, scatter_rows(): pl.pallas_call(functools.partial(scatter_body, [len(parts) for _, parts i...  3.62 us
    dot_general x1, matrix products, per_device(): lax.dot_general(found, frames, (((0,), (0,)), ((), ())), preferred_elemen...  2.26 us
    ppermute x6, starting transfers between devices, swap(): return lax.ppermute(x, 'pair', [(0, 1), (1, 0)])  1.68 us
    ppermute x6, waiting for transfers between devices, swap(): return lax.ppermute(x, 'pair', [(0, 1), (1, 0)])  1.01 us
    dot_general x1, matrix products, per_device(): lax.dot_general(found, cotangent, (((0,), (0,)), ((), ())), preferred_ele...  0.83 us
  transfers between devices with their start and end apart: 14, of which 6 were waited for; matrix products, arithmetic and copies ran while one was open for 9% of the time, Pallas kernels for 25%

profile of v12, /device:TPU:0, one launch (start us, length us, event | category | flops | bytes accessed | tf_op | source)
XLA Modules:
  0.0 33.8 jit_solution(7146684731397233610)
XLA Ops:
  0.6 0.5 %collective-permute-start = (bf16[1536,768]{1,0:T(8,128)(2,1)}, bf16[1536,768]{1,0:T(8,128)(2,1)S(1)}, u32[]{:S(2)}, u32[]{:S(2)}) collective-permute-start(bf16[1536,768]{1,0:T(8,128)(2,1)} %refs_4_.3), channel_id=1, source_target_pairs={{0,1},{1,0},{2,3},{3,2},{4,5},{5,4},{6,7},{7,6},{8,9},{9,8},{10,11... | collective-permute-start | bytes 7077896 | tf_op jit(solution)/shard_map/ppermute | solution.py:246
  1.1 0.0 copy-start.1
  1.2 0.0 copy-start.3
  1.2 0.0 copy-start.6
  1.2 2.3 %fusion.2 = bf16[384,384]{1,0:T(8,128)(2,1)S(1)} fusion(bf16[1536,384]{1,0:T(8,128)(2,1)} %frames_ref.2, s32[384]{0:T(512)} %picked_ref.1), kind=kOutput, calls=%fused_computation.3 | convolution fusion | flops 453722112 | bytes 1476096 | tf_op jit(solution)/shard_map/dot_general | solution.py:274
  3.5 0.0 copy-done.1
  3.5 0.1 collective-permute-start.4
  3.6 2.9 %collective-permute-start.2 = (bf16[192,384]{1,0:T(8,128)(2,1)S(1)}, bf16[192,384]{1,0:T(8,128)(2,1)S(1)}, u32[]{:S(2)}, u32[]{:S(2)}) collective-permute-start(bf16[192,384]{1,0:T(8,128)(2,1)S(1)} %get-tuple-element.43.refs_0_), channel_id=1, source_target_pairs={{0,2},{1,3},{2,0},{3,1},{4,6},{5,7},{6,4},{7,5},{8,10},{9,11},{10,... | collective-permute-start | bytes 442376 | tf_op jit(solution)/shard_map/ppermute | solution.py:243
  6.5 0.0 copy-start.4
  6.5 0.0 copy-start.5
  6.5 0.0 copy-start.7
  6.5 0.0 collective-permute-start.3
  6.6 0.0 copy-done.3
  6.6 0.0 copy-done.6
  6.6 0.0 copy-start
  6.6 0.8 %fusion.3 = bf16[384,384]{1,0:T(8,128)(2,1)S(1)} fusion(bf16[1536,384]{1,0:T(8,128)(2,1)S(1)} %copy-done.3, s32[384]{0:T(512)S(1)} %copy-done.6), kind=kOutput, calls=%fused_computation.4 | convolution fusion | flops 453722112 | bytes 1476096 | tf_op jit(solution)/shard_map/dot_general | solution.py:280
  7.4 0.0 collective-permute-done.refs_5_
  7.4 0.2 collective-permute-start.1
  7.7 1.0 %collective-permute-done.4.refs_7_ = bf16[768,1536]{1,0:T(8,128)(2,1)S(1)} collective-permute-done((bf16[768,1536]{1,0:T(8,128)(2,1)S(1)}, bf16[768,1536]{1,0:T(8,128)(2,1)S(1)}, u32[]{:S(2)}, u32[]{:S(2)}) %collective-permute-start.4) | collective-permute-done | bytes 2359328 | tf_op jit(solution)/shard_map/ppermute | solution.py:246
  8.7 2.9 %collective-permute-start.9 = (bf16[192,384]{1,0:T(8,128)(2,1)S(1)}, bf16[192,384]{1,0:T(8,128)(2,1)S(1)}, u32[]{:S(2)}, u32[]{:S(2)}) collective-permute-start(bf16[192,384]{1,0:T(8,128)(2,1)S(1)} %get-tuple-element.29.refs_0_), channel_id=1, source_target_pairs={{0,2},{1,3},{2,0},{3,1},{4,6},{5,7},{6,4},{7,5},{8,10},{9,11},{10,... | collective-permute-start | bytes 442376 | tf_op jit(solution)/shard_map/ppermute | solution.py:243
  11.5 0.0 collective-permute-start.10
  11.5 2.4 %collective-permute-done.3.refs_3_ = bf16[192,384]{1,0:T(8,128)(2,1)S(1)} collective-permute-done((bf16[192,384]{1,0:T(8,128)(2,1)S(1)}, bf16[192,384]{1,0:T(8,128)(2,1)S(1)}, u32[]{:S(2)}, u32[]{:S(2)}) %collective-permute-start.3) | collective-permute-done | bytes 147488 | tf_op jit(solution)/shard_map/ppermute | solution.py:243
  13.9 0.2 collective-permute-start.8
  14.2 0.0 collective-permute-done.2.refs_2_
  14.2 0.0 collective-permute-done.1.refs_1_
  14.2 0.0 copy-done.4
  14.2 0.0 copy-done.5
  14.2 0.0 copy-done.7
  14.2 0.0 copy-done
  14.2 2.6 %forward.1 = (bf16[192,384]{1,0:T(8,128)(2,1)S(1)}, bf16[192,384]{1,0:T(8,128)(2,1)S(1)}, bf16[192,384]{1,0:T(8,128)(2,1)S(1)}, bf16[192,384]{1,0:T(8,128)(2,1)S...) custom-call(s32[4]{0:T(128)S(1)} %copy-done.7, ...), custom_call_target="tpu_custom_call" | custom-call | flops 1 | bytes 1 | tf_op jit(solution)/shard_map/forward/pallas_call | solution.py:23
  16.8 2.1 %collective-permute-start.5 = (bf16[192,384]{1,0:T(8,128)(2,1)S(1)}, bf16[192,384]{1,0:T(8,128)(2,1)S(1)}, u32[]{:S(2)}, u32[]{:S(2)}) collective-permute-start(bf16[192,384]{1,0:T(8,128)(2,1)S(1)} %get-tuple-element.25), channel_id=1, source_target_pairs={{0,2},{1,3},{2,0},{3,1},{4,6},{5,7},{6,4},{7,5},{8,10},{9,11},{10,... | collective-permute-start | bytes 442376 | tf_op jit(solution)/shard_map/ppermute | solution.py:243
  18.9 0.0 collective-permute-start.6
  18.9 0.0 collective-permute-done.9.refs_2_
  18.9 0.2 collective-permute-start.7
  19.1 0.5 %collective-permute-done.10.refs_3_ = bf16[192,384]{1,0:T(8,128)(2,1)S(1)} collective-permute-done((bf16[192,384]{1,0:T(8,128)(2,1)S(1)}, bf16[192,384]{1,0:T(8,128)(2,1)S(1)}, u32[]{:S(2)}, u32[]{:S(2)}) %collective-permute-start.10) | collective-permute-done | bytes 147488 | tf_op jit(solution)/shard_map/ppermute | solution.py:243
  19.6 0.0 collective-permute-done.8.refs_1_
  19.6 0.0 copy-start.2
  19.6 3.6 %backward.1 = (bf16[192,384]{1,0:T(8,128)(2,1)S(1)}, bf16[192,384]{1,0:T(8,128)(2,1)S(1)}, bf16[192,384]{1,0:T(8,128)(2,1)S(1)}, bf16[192,384]{1,0:T(8,128)(2,1)S(1)}) custom-call(bf16[192,384]{1,0:T(8,128)(2,1)S(1)} %get-tuple-element.29.refs_0_, bf16[192,384]{1,0:T(8,128)(2,1)S(1)} %collective-permute-done.8.refs_1_, ...), custom_call_target="tpu_custom_call" | custom-call | flops 1 | bytes 1 | tf_op jit(solution)/shard_map/backward/pallas_call | solution.py:23
  23.2 1.5 %collective-permute-start.11 = (bf16[192,384]{1,0:T(8,128)(2,1)S(1)}, bf16[192,384]{1,0:T(8,128)(2,1)S(1)}, u32[]{:S(2)}, u32[]{:S(2)}) collective-permute-start(bf16[192,384]{1,0:T(8,128)(2,1)S(1)} %get-tuple-element.37), channel_id=1, source_target_pairs={{0,2},{1,3},{2,0},{3,1},{4,6},{5,7},{6,4},{7,5},{8,10},{9,11},{10,... | collective-permute-start | bytes 442376 | tf_op jit(solution)/shard_map/ppermute | solution.py:243
  24.7 0.6 %collective-permute-start.12 = (bf16[192,384]{1,0:T(8,128)(2,1)S(1)}, bf16[192,384]{1,0:T(8,128)(2,1)S(1)}, u32[]{:S(2)}, u32[]{:S(2)}) collective-permute-start(bf16[192,384]{1,0:T(8,128)(2,1)S(1)} %get-tuple-element.38), channel_id=1, source_target_pairs={{0,1},{1,0},{2,3},{3,2},{4,5},{5,4},{6,7},{7,6},{8,9},{9,8},{10,11... | collective-permute-start | bytes 442376 | tf_op jit(solution)/shard_map/ppermute | solution.py:246
  25.3 0.0 collective-permute-done.5.refs_2_
  25.3 0.1 collective-permute-start.13
  25.4 0.0 collective-permute-done.6.refs_4_
  25.4 0.7 %collective-permute-done.7.refs_5_ = bf16[192,384]{1,0:T(8,128)(2,1)S(1)} collective-permute-done((bf16[192,384]{1,0:T(8,128)(2,1)S(1)}, bf16[192,384]{1,0:T(8,128)(2,1)S(1)}, u32[]{:S(2)}, u32[]{:S(2)}) %collective-permute-start.7) | collective-permute-done | bytes 147488 | tf_op jit(solution)/shard_map/ppermute | solution.py:243
  26.1 0.0 copy-done.2
  26.1 1.7 %mixed_rows.1 = bf16[1536,384]{1,0:T(8,128)(2,1)} custom-call(bf16[1536,384]{1,0:T(8,128)(2,1)S(1)} %copy-done.2, s32[192]{0:T(256)S(1)} %get-tuple-element.23.refs_0_, bf16[192,384]{1,0:T(8,128)(2,1)S(1)} %get-tuple-element.24.refs_1_, bf16[192,384]{1,0:T(8,128)(2,1)S(1)} %collective-permute-done.5.refs_2_, s32[192]{0:T(256)S(1)} %get-tuple-element.26.refs_3_.refs_0_, ...), custom_call_target="tpu_custom_call" | custom-call | tf_op jit(solution)/shard_map/mixed_rows/pallas_call | solution.py:88
  27.9 2.1 %collective-permute-done.11.refs_2_ = bf16[192,384]{1,0:T(8,128)(2,1)S(1)} collective-permute-done((bf16[192,384]{1,0:T(8,128)(2,1)S(1)}, bf16[192,384]{1,0:T(8,128)(2,1)S(1)}, u32[]{:S(2)}, u32[]{:S(2)}) %collective-permute-start.11) | collective-permute-done | bytes 147488 | tf_op jit(solution)/shard_map/ppermute | solution.py:243
  29.9 0.6 %grad_rows_mine.1.frames_ref = bf16[1536,384]{1,0:T(8,128)(2,1)S(1)} custom-call(bf16[1536,384]{1,0:T(8,128)(2,1)S(1)} %copy-done.3, s32[192]{0:T(256)S(1)} %get-tuple-element.23.refs_0_, bf16[192,384]{1,0:T(8,128)(2,1)S(1)} %get-tuple-element.36.refs_1_, bf16[192,384]{1,0:T(8,128)(2,1)S(1)} %collective-permute-done.11.refs_2_), custom_call_target="tpu_custom_call" | custom-call | tf_op jit(solution)/shard_map/grad_rows_mine/pallas_call | solution.py:88
  30.5 0.0 collective-permute-done.12.refs_1_
  30.5 1.9 %collective-permute-done.13.refs_2_ = bf16[192,384]{1,0:T(8,128)(2,1)S(1)} collective-permute-done((bf16[192,384]{1,0:T(8,128)(2,1)S(1)}, bf16[192,384]{1,0:T(8,128)(2,1)S(1)}, u32[]{:S(2)}, u32[]{:S(2)}) %collective-permute-start.13) | collective-permute-done | bytes 147488 | tf_op jit(solution)/shard_map/ppermute | solution.py:243
  32.5 1.3 %grad_rows.1 = bf16[1536,384]{1,0:T(8,128)(2,1)} custom-call(bf16[1536,384]{1,0:T(8,128)(2,1)S(1)} %grad_rows_mine.1.frames_ref, s32[192]{0:T(256)S(1)} %get-tuple-element.26.refs_3_.refs_0_, bf16[192,384]{1,0:T(8,128)(2,1)S(1)} %collective-permute-done.12.refs_1_, bf16[192,384]{1,0:T(8,128)(2,1)S(1)} %collective-permute-done.13.refs_2_), custom_call_target="tpu_custom_call" | custom-call | tf_op jit(solution)/shard_map/grad_rows/pallas_call | solution.py:88
  (2 shorter events, 0.1 us)
Async XLA Ops:
  0.6 6.8 %collective-permute-start = (bf16[1536,768]{1,0:T(8,128)(2,1)}, bf16[1536,768]{1,0:T(8,128)(2,1)S(1)}, u32[]{:S(2)}, u32[]{:S(2)}) collective-permute-start(bf16[1536,768]{1,0:T(8,128)(2,1)} %refs_4_.3), channel_id=1, source_target_pairs={{0,1},{1,0},{2,3},{3,2},{4,5},{5,4},{6,7},{7,6},{8,9},{9,8},{10,11... | collective-permute-start | bytes 7077896 | tf_op jit(solution)/shard_map/ppermute | solution.py:246
  1.1 2.3 %copy-start.1 = (bf16[768,1536]{1,0:T(8,128)(2,1)S(1)}, bf16[768,1536]{1,0:T(8,128)(2,1)}, u32[]{:S(2)}) copy-start(bf16[768,1536]{1,0:T(8,128)(2,1)} %refs_6_.3) | copy-start | bytes 7077892
  1.2 5.4 %copy-start.3 = (bf16[1536,384]{1,0:T(8,128)(2,1)S(1)}, bf16[1536,384]{1,0:T(8,128)(2,1)}, u32[]{:S(2)}) copy-start(bf16[1536,384]{1,0:T(8,128)(2,1)} %frames_ref.3) | copy-start | bytes 3538948
  1.2 5.4 %copy-start.6 = (s32[384]{0:T(512)S(1)}, s32[384]{0:T(512)}, u32[]{:S(2)}) copy-start(s32[384]{0:T(512)} %picked_ref.1) | copy-start | bytes 4612
  3.5 5.2 %collective-permute-start.4 = (bf16[768,1536]{1,0:T(8,128)(2,1)S(1)}, bf16[768,1536]{1,0:T(8,128)(2,1)S(1)}, u32[]{:S(2)}, u32[]{:S(2)}) collective-permute-start(bf16[768,1536]{1,0:T(8,128)(2,1)S(1)} %copy-done.1), channel_id=1, source_target_pairs={{0,1},{1,0},{2,3},{3,2},{4,5},{5,4},{6,7},{7,6},{8,9},{9,8},{10,11... | collective-permute-start | bytes 7077896 | tf_op jit(solution)/shard_map/ppermute | solution.py:246
  3.6 10.6 %collective-permute-start.2 = (bf16[192,384]{1,0:T(8,128)(2,1)S(1)}, bf16[192,384]{1,0:T(8,128)(2,1)S(1)}, u32[]{:S(2)}, u32[]{:S(2)}) collective-permute-start(bf16[192,384]{1,0:T(8,128)(2,1)S(1)} %get-tuple-element.43.refs_0_), channel_id=1, source_target_pairs={{0,2},{1,3},{2,0},{3,1},{4,6},{5,7},{6,4},{7,5},{8,10},{9,11},{10,... | collective-permute-start | bytes 442376 | tf_op jit(solution)/shard_map/ppermute | solution.py:243
  6.5 7.6 %copy-start.4 = (f32[1536]{0:T(1024)S(1)}, f32[1536]{0:T(1024)}, u32[]{:S(2)}) copy-start(f32[1536]{0:T(1024)} %refs_8_.3) | copy-start | bytes 18436
  6.5 7.6 %copy-start.5 = (f32[1536]{0:T(1024)S(1)}, f32[1536]{0:T(1024)}, u32[]{:S(2)}) copy-start(f32[1536]{0:T(1024)} %refs_9_.3) | copy-start | bytes 18436
  6.5 7.6 %copy-start.7 = (s32[4]{0:T(128)S(1)}, s32[4]{0:T(128)}, u32[]{:S(2)}) copy-start(s32[4]{0:T(128)} %count_ref.1) | copy-start | bytes 52
  6.5 7.4 %collective-permute-start.3 = (bf16[192,384]{1,0:T(8,128)(2,1)S(1)}, bf16[192,384]{1,0:T(8,128)(2,1)S(1)}, u32[]{:S(2)}, u32[]{:S(2)}) collective-permute-start(bf16[192,384]{1,0:T(8,128)(2,1)S(1)} %get-tuple-element.21), channel_id=1, source_target_pairs={{0,3},{1,2},{2,1},{3,0},{4,7},{5,6},{6,5},{7,4},{8,11},{9,10},{10,... | collective-permute-start | bytes 442376 | tf_op jit(solution)/shard_map/ppermute | solution.py:243
  6.6 7.6 %copy-start = (bf16[1536,768]{1,0:T(8,128)(2,1)S(1)}, bf16[1536,768]{1,0:T(8,128)(2,1)}, u32[]{:S(2)}) copy-start(bf16[1536,768]{1,0:T(8,128)(2,1)} %refs_4_.3) | copy-start | bytes 7077892
  7.4 6.7 %collective-permute-start.1 = (bf16[192,384]{1,0:T(8,128)(2,1)S(1)}, bf16[192,384]{1,0:T(8,128)(2,1)S(1)}, u32[]{:S(2)}, u32[]{:S(2)}) collective-permute-start(bf16[192,384]{1,0:T(8,128)(2,1)S(1)} %get-tuple-element.21), channel_id=1, source_target_pairs={{0,1},{1,0},{2,3},{3,2},{4,5},{5,4},{6,7},{7,6},{8,9},{9,8},{10,11... | collective-permute-start | bytes 442376 | tf_op jit(solution)/shard_map/ppermute | solution.py:246
  8.7 10.2 %collective-permute-start.9 = (bf16[192,384]{1,0:T(8,128)(2,1)S(1)}, bf16[192,384]{1,0:T(8,128)(2,1)S(1)}, u32[]{:S(2)}, u32[]{:S(2)}) collective-permute-start(bf16[192,384]{1,0:T(8,128)(2,1)S(1)} %get-tuple-element.29.refs_0_), channel_id=1, source_target_pairs={{0,2},{1,3},{2,0},{3,1},{4,6},{5,7},{6,4},{7,5},{8,10},{9,11},{10,... | collective-permute-start | bytes 442376 | tf_op jit(solution)/shard_map/ppermute | solution.py:243
  11.5 8.1 %collective-permute-start.10 = (bf16[192,384]{1,0:T(8,128)(2,1)S(1)}, bf16[192,384]{1,0:T(8,128)(2,1)S(1)}, u32[]{:S(2)}, u32[]{:S(2)}) collective-permute-start(bf16[192,384]{1,0:T(8,128)(2,1)S(1)} %get-tuple-element.30), channel_id=1, source_target_pairs={{0,3},{1,2},{2,1},{3,0},{4,7},{5,6},{6,5},{7,4},{8,11},{9,10},{10,... | collective-permute-start | bytes 442376 | tf_op jit(solution)/shard_map/ppermute | solution.py:243
  13.9 5.7 %collective-permute-start.8 = (bf16[192,384]{1,0:T(8,128)(2,1)S(1)}, bf16[192,384]{1,0:T(8,128)(2,1)S(1)}, u32[]{:S(2)}, u32[]{:S(2)}) collective-permute-start(bf16[192,384]{1,0:T(8,128)(2,1)S(1)} %get-tuple-element.30), channel_id=1, source_target_pairs={{0,1},{1,0},{2,3},{3,2},{4,5},{5,4},{6,7},{7,6},{8,9},{9,8},{10,11... | collective-permute-start | bytes 442376 | tf_op jit(solution)/shard_map/ppermute | solution.py:246
  16.8 8.5 %collective-permute-start.5 = (bf16[192,384]{1,0:T(8,128)(2,1)S(1)}, bf16[192,384]{1,0:T(8,128)(2,1)S(1)}, u32[]{:S(2)}, u32[]{:S(2)}) collective-permute-start(bf16[192,384]{1,0:T(8,128)(2,1)S(1)} %get-tuple-element.25), channel_id=1, source_target_pairs={{0,2},{1,3},{2,0},{3,1},{4,6},{5,7},{6,4},{7,5},{8,10},{9,11},{10,... | collective-permute-start | bytes 442376 | tf_op jit(solution)/shard_map/ppermute | solution.py:243
  18.9 6.5 %collective-permute-start.6 = (bf16[192,384]{1,0:T(8,128)(2,1)S(1)}, bf16[192,384]{1,0:T(8,128)(2,1)S(1)}, u32[]{:S(2)}, u32[]{:S(2)}) collective-permute-start(bf16[192,384]{1,0:T(8,128)(2,1)S(1)} %get-tuple-element.27), channel_id=1, source_target_pairs={{0,1},{1,0},{2,3},{3,2},{4,5},{5,4},{6,7},{7,6},{8,9},{9,8},{10,11... | collective-permute-start | bytes 442376 | tf_op jit(solution)/shard_map/ppermute | solution.py:246
  18.9 7.2 %collective-permute-start.7 = (bf16[192,384]{1,0:T(8,128)(2,1)S(1)}, bf16[192,384]{1,0:T(8,128)(2,1)S(1)}, u32[]{:S(2)}, u32[]{:S(2)}) collective-permute-start(bf16[192,384]{1,0:T(8,128)(2,1)S(1)} %get-tuple-element.28), channel_id=1, source_target_pairs={{0,3},{1,2},{2,1},{3,0},{4,7},{5,6},{6,5},{7,4},{8,11},{9,10},{10,... | collective-permute-start | bytes 442376 | tf_op jit(solution)/shard_map/ppermute | solution.py:243
  19.6 6.5 %copy-start.2 = (bf16[1536,384]{1,0:T(8,128)(2,1)S(1)}, bf16[1536,384]{1,0:T(8,128)(2,1)}, u32[]{:S(2)}) copy-start(bf16[1536,384]{1,0:T(8,128)(2,1)} %frames_ref.2) | copy-start | bytes 3538948
  23.2 6.7 %collective-permute-start.11 = (bf16[192,384]{1,0:T(8,128)(2,1)S(1)}, bf16[192,384]{1,0:T(8,128)(2,1)S(1)}, u32[]{:S(2)}, u32[]{:S(2)}) collective-permute-start(bf16[192,384]{1,0:T(8,128)(2,1)S(1)} %get-tuple-element.37), channel_id=1, source_target_pairs={{0,2},{1,3},{2,0},{3,1},{4,6},{5,7},{6,4},{7,5},{8,10},{9,11},{10,... | collective-permute-start | bytes 442376 | tf_op jit(solution)/shard_map/ppermute | solution.py:243
  24.7 5.8 %collective-permute-start.12 = (bf16[192,384]{1,0:T(8,128)(2,1)S(1)}, bf16[192,384]{1,0:T(8,128)(2,1)S(1)}, u32[]{:S(2)}, u32[]{:S(2)}) collective-permute-start(bf16[192,384]{1,0:T(8,128)(2,1)S(1)} %get-tuple-element.38), channel_id=1, source_target_pairs={{0,1},{1,0},{2,3},{3,2},{4,5},{5,4},{6,7},{7,6},{8,9},{9,8},{10,11... | collective-permute-start | bytes 442376 | tf_op jit(solution)/shard_map/ppermute | solution.py:246
  25.3 7.1 %collective-permute-start.13 = (bf16[192,384]{1,0:T(8,128)(2,1)S(1)}, bf16[192,384]{1,0:T(8,128)(2,1)S(1)}, u32[]{:S(2)}, u32[]{:S(2)}) collective-permute-start(bf16[192,384]{1,0:T(8,128)(2,1)S(1)} %get-tuple-element.39), channel_id=1, source_target_pairs={{0,3},{1,2},{2,1},{3,0},{4,7},{5,6},{6,5},{7,4},{8,11},{9,10},{10,... | collective-permute-start | bytes 442376 | tf_op jit(solution)/shard_map/ppermute | solution.py:243
